TPU v7x, 32 devices: a whole 2x2x4 slice. The times are simulated.
32 devices in a mesh: rep: 2 (over y), pd: 4 (over x, core), tp: 4 (over z).
Axes of the slice: x: 2, y: 2, z: 4, core: 2. Of those that a mesh axis runs over, the one named last changes fastest.
Arguments:
- prompt_query: bfloat16 [4096, 4096], P(('rep', 'pd', 'tp')), parts along dimension 0, may hold values from -200 to 200
- prompt_key: bfloat16 [4096, 512], P(('rep', 'pd', 'tp')), parts along dimension 0, may hold values from -6 to 6
- prompt_value: bfloat16 [4096, 512], P(('rep', 'pd', 'tp')), parts along dimension 0, may hold values from -6 to 6
- prompt_lengths: int32 [8, 4], P('rep'), parts along dimension 0, may hold values from 1 to 16, 32 in all within a row
- decode_slot: int32 [32], P('rep'), parts along dimension 0, may hold values from 0 to 15, as said below
- decoded_query: bfloat16 [32, 2, 4096], P(('rep', 'pd')), parts along dimension 0, may hold values from -200 to 200
- decoded_key: bfloat16 [32, 2, 512], P(('rep', 'pd')), parts along dimension 0, may hold values from -6 to 6
- decoded_value: bfloat16 [32, 2, 512], P(('rep', 'pd')), parts along dimension 0, may hold values from -6 to 6
Outputs:
- pre_out: bfloat16 [4096, 4096], P(('rep', 'pd', 'tp')), parts along dimension 0
- dec_out: bfloat16 [32, 2, 4096], P(('rep', 'pd')), parts along dimension 0
There are 2 independent parts, one for each index of `rep`. A program takes and returns all parts, laid end to end along the dimension named above; each array names one. Nothing has to cross between parts.
Inputs may be any that keep to these rules, and one draw needn't show every extreme that they name: `prompt_lengths`: each row sums to 32; its largest entry is exactly 16. `decode_slot`: A permutation of the 16 request numbers onto the decode slots; the 4 requests of one prefill group go to 4 different decode groups.
All inputs are finite; a program needn't handle non-finite values.
Results may differ from a plain program's by a relative error of at most 0.014.
Values may be sent and summed in bfloat16 or wider, within the bound.
No kernel may reach another device: no remote copies, remote signals or barrier semaphores. Data moves between devices by JAX's collectives and lax.ppermute only.
A program may use at most 64 MiB of HBM per device.

v0:
```python
import math

import jax
import jax.numpy as jnp
from jax import lax
from jax.sharding import PartitionSpec as P

QUERY_HEADS = 32
KEY_VALUE_HEADS = 4
HEAD_SIZE = 128
PAGE = 16
GROUP_REQUESTS = 4
DECODE_STEPS = 2


NEGATIVE_FILL = -1e30


def combined_all(shard, axis, join):
    gathered = jax.tree.map(
        lambda a, kind: lax.all_gather(a.astype(kind), axis),
        shard,
        (jnp.bfloat16, jnp.bfloat16, jnp.bfloat16),
    )

    def take(source):
        return jax.tree.map(
            lambda a, own: lax.dynamic_index_in_dim(a, source, 0, False).astype(own.dtype),
            gathered,
            shard,
        )

    return lax.fori_loop(
        1, lax.axis_size(axis), lambda source, state: join(state, take(source)), take(0)
    )


def segment_of(positions, ends_row):
    return jnp.sum((positions[:, None] >= ends_row[None, :]).astype(jnp.int32), axis=1)


def stored_position(index, token_rows, tp_size):
    member = index // token_rows
    offset = index % token_rows
    return (offset // PAGE * tp_size + member) * PAGE + offset % PAGE


def update(state, query_array, key_row_list, value_row_list, allowed, scale):
    top, total, acc = state
    scores = (
        jnp.einsum("tkgd,skd->kgts", query_array, key_row_list, preferred_element_type=jnp.float32)
        * scale
    )
    scores = jnp.where(allowed[None, None], scores, NEGATIVE_FILL)
    new_top = jnp.maximum(top, jnp.max(scores, axis=-1))
    weights = jnp.where(allowed[None, None], jnp.exp(scores - new_top[..., None]), 0.0)
    factor = jnp.exp(top - new_top)
    total = total * factor + jnp.sum(weights, axis=-1)
    acc = acc * factor[..., None] + jnp.einsum(
        "kgts,skd->kgtd",
        weights.astype(jnp.bfloat16),
        value_row_list,
        preferred_element_type=jnp.float32,
    )
    return (new_top, total, acc)


def attend(state, query_array, qpos, qseg, row_range, kpos, ends_row, scale):
    count = row_range.shape[1]
    piece_length = math.gcd(count, 512)

    def one_block(index, inner):
        block_range = lax.dynamic_slice_in_dim(row_range, index * piece_length, piece_length, 1)
        bpos = lax.dynamic_slice_in_dim(kpos, index * piece_length, piece_length, 0)
        bseg = segment_of(bpos, ends_row)
        allowed = (bpos[None, :] <= qpos[:, None]) & (bseg[None, :] == qseg[:, None])
        key_row_list = block_range[0].reshape(piece_length, KEY_VALUE_HEADS, HEAD_SIZE)
        value_row_list = block_range[1].reshape(piece_length, KEY_VALUE_HEADS, HEAD_SIZE)
        return update(inner, query_array, key_row_list, value_row_list, allowed, scale)

    return lax.fori_loop(0, count // piece_length, one_block, state)


def combine(first_index, second):
    top_a, total_a, acc_a = first_index
    top_b, total_b, acc_b = second
    top = jnp.maximum(top_a, top_b)
    factor_a = jnp.exp(top_a - top)
    factor_b = jnp.exp(top_b - top)
    return (
        top,
        total_a * factor_a + total_b * factor_b,
        acc_a * factor_a[..., None] + acc_b * factor_b[..., None],
    )


def finish(state, row_range):
    top, total, acc = state
    return (
        (acc / total[..., None]).transpose(2, 0, 1, 3).reshape(row_range, QUERY_HEADS * HEAD_SIZE)
    )


def body(
    prompt_query,
    prompt_key,
    prompt_value,
    prompt_lengths,
    decode_slot,
    decoded_query,
    decoded_key,
    decoded_value,
):
    token_rows = prompt_query.shape[0]
    query_per_key_head = QUERY_HEADS // KEY_VALUE_HEADS
    scale = 1.0 / math.sqrt(HEAD_SIZE)
    tp_size = lax.axis_size("tp")
    pd_size = lax.axis_size("pd")
    my_group = lax.axis_index("pd")
    member = lax.axis_index("tp")
    page_count = token_rows // PAGE
    half_rows = token_rows // 2
    ends_pages = jnp.cumsum(prompt_lengths, axis=1)
    ends_all = ends_pages * PAGE
    ends_row = lax.dynamic_index_in_dim(ends_all, my_group, 0, keepdims=False)
    qpos = stored_position(
        member * token_rows + jnp.arange(token_rows, dtype=jnp.int32), token_rows, tp_size
    )
    qseg = segment_of(qpos, ends_row)
    query_array = prompt_query.reshape(token_rows, KEY_VALUE_HEADS, query_per_key_head, HEAD_SIZE)
    low_query = query_array[:half_rows]
    high_query = query_array[half_rows:]
    stacked = jnp.stack([prompt_key, prompt_value])

    def fresh(row_range):
        return (
            jnp.full((KEY_VALUE_HEADS, query_per_key_head, row_range), NEGATIVE_FILL, jnp.float32),
            jnp.zeros((KEY_VALUE_HEADS, query_per_key_head, row_range), jnp.float32),
            jnp.zeros((KEY_VALUE_HEADS, query_per_key_head, row_range, HEAD_SIZE), jnp.float32),
        )

    piece = lax.all_gather(stacked, "tp", axis=1, tiled=True)
    low_state = fresh(half_rows)
    high_state = fresh(half_rows)
    count = piece.shape[1]
    shards = count // token_rows
    kpos = stored_position(jnp.arange(count, dtype=jnp.int32), token_rows, tp_size)
    lower = piece.reshape(2, shards, token_rows, piece.shape[2])[:, :, :half_rows].reshape(
        2, shards * half_rows, piece.shape[2]
    )
    low_pos = kpos.reshape(shards, token_rows)[:, :half_rows].reshape(shards * half_rows)
    low_state = attend(
        low_state, low_query, qpos[:half_rows], qseg[:half_rows], lower, low_pos, ends_row, scale
    )
    high_state = attend(
        high_state, high_query, qpos[half_rows:], qseg[half_rows:], piece, kpos, ends_row, scale
    )
    low_state, high_state = (low_state, high_state)
    pre_out = jnp.concatenate(
        [finish(low_state, half_rows), finish(high_state, half_rows)], axis=0
    ).astype(jnp.bfloat16)
    page_index = jnp.arange(page_count, dtype=jnp.int32)
    group_page = page_index * tp_size + member
    request_of = jnp.sum(
        (group_page[None, :, None] >= ends_pages[:, None, :]).astype(jnp.int32), axis=2
    )
    table = decode_slot.reshape(pd_size, GROUP_REQUESTS)
    slot_of = jnp.sum(
        jnp.where(
            request_of[:, :, None] == jnp.arange(GROUP_REQUESTS, dtype=jnp.int32)[None, None, :],
            table[:, None, :],
            0,
        ),
        axis=2,
    )
    target = slot_of // GROUP_REQUESTS
    my_slot = jnp.where(target == my_group, slot_of - my_group * GROUP_REQUESTS, -1)
    kv_rows = jnp.concatenate([prompt_key, prompt_value], axis=1)
    row_width = kv_rows.shape[1]
    capacity = token_rows // (2 * PAGE)
    same = target[:, :, None] == target[:, None, :]
    earlier = page_index[None, :] < page_index[:, None]
    page_rank = jnp.sum((same & earlier[None]).astype(jnp.int32), axis=2)
    own_target = lax.dynamic_index_in_dim(target, my_group, 0, keepdims=False)
    own_rank = lax.dynamic_index_in_dim(page_rank, my_group, 0, keepdims=False)
    destinations = jnp.arange(pd_size, dtype=jnp.int32)
    columns_cap = jnp.arange(capacity, dtype=jnp.int32)
    chooser = (
        (
            (own_target[None, None, :] == destinations[:, None, None])
            & (own_rank[None, None, :] == columns_cap[None, :, None])
        )
        .astype(jnp.bfloat16)
        .reshape(pd_size * capacity, page_count)
    )
    page_rows = kv_rows.reshape(page_count, PAGE * row_width)
    outgoing = jnp.dot(chooser, page_rows, preferred_element_type=jnp.float32).astype(jnp.bfloat16)
    incoming = lax.all_to_all(outgoing, "pd", split_axis=0, concat_axis=0, tiled=True)
    page_hit = (my_slot[:, None, :] >= 0) & (page_rank[:, None, :] == columns_cap[None, :, None])
    page_slot = jnp.sum(jnp.where(page_hit, my_slot[:, None, :] + 1, 0), axis=2) - 1
    page_store = incoming.reshape(pd_size * capacity * PAGE, row_width)
    row_slot = jnp.broadcast_to(page_slot.reshape(-1, 1), (pd_size * capacity, PAGE)).reshape(-1)
    row_range = page_store.shape[0]
    slot_mask = row_slot[None, :] == jnp.arange(GROUP_REQUESTS, dtype=jnp.int32)[:, None]
    decode_queries = decoded_query.reshape(
        GROUP_REQUESTS, DECODE_STEPS, KEY_VALUE_HEADS, query_per_key_head, HEAD_SIZE
    )
    stored_keys = page_store[:, : KEY_VALUE_HEADS * HEAD_SIZE].reshape(
        row_range, KEY_VALUE_HEADS, HEAD_SIZE
    )
    stored_values = page_store[:, KEY_VALUE_HEADS * HEAD_SIZE :].reshape(
        row_range, KEY_VALUE_HEADS, HEAD_SIZE
    )
    scores = (
        jnp.einsum(
            "jskgd,rkd->jkgsr", decode_queries, stored_keys, preferred_element_type=jnp.float32
        )
        * scale
    )
    wide_mask = slot_mask[:, None, None, None, :]
    scores = jnp.where(wide_mask, scores, NEGATIVE_FILL)
    part_top = jnp.max(scores, axis=-1)
    weights = jnp.where(wide_mask, jnp.exp(scores - part_top[..., None]), 0.0)
    part_total = jnp.sum(weights, axis=-1)
    part_acc = jnp.einsum(
        "jkgsr,rkd->jkgsd",
        weights.astype(jnp.bfloat16),
        stored_values,
        preferred_element_type=jnp.float32,
    )
    merged_top, merged_total, merged_acc = combined_all(
        (part_top, part_total, part_acc), "tp", combine
    )
    fresh_key_rows = decoded_key.reshape(GROUP_REQUESTS, DECODE_STEPS, KEY_VALUE_HEADS, HEAD_SIZE)
    fresh_value_rows = decoded_value.reshape(
        GROUP_REQUESTS, DECODE_STEPS, KEY_VALUE_HEADS, HEAD_SIZE
    )
    new_scores = (
        jnp.einsum(
            "jskgd,jrkd->jkgsr", decode_queries, fresh_key_rows, preferred_element_type=jnp.float32
        )
        * scale
    )
    order = jnp.arange(DECODE_STEPS, dtype=jnp.int32)
    causal = (order[None, :] <= order[:, None])[None, None, None]
    new_scores = jnp.where(causal, new_scores, NEGATIVE_FILL)
    final_top = jnp.maximum(merged_top, jnp.max(new_scores, axis=-1))
    new_weights = jnp.where(causal, jnp.exp(new_scores - final_top[..., None]), 0.0)
    factor = jnp.exp(merged_top - final_top)
    final_total = merged_total * factor + jnp.sum(new_weights, axis=-1)
    final_acc = merged_acc * factor[..., None] + jnp.einsum(
        "jkgsr,jrkd->jkgsd",
        new_weights.astype(jnp.bfloat16),
        fresh_value_rows,
        preferred_element_type=jnp.float32,
    )
    dec_out = (
        (final_acc / final_total[..., None])
        .transpose(0, 3, 1, 2, 4)
        .reshape(GROUP_REQUESTS, DECODE_STEPS, QUERY_HEADS * HEAD_SIZE)
        .astype(jnp.bfloat16)
    )
    return (pre_out, dec_out)


def solution(mesh):
    placed = (
        P(("rep", "pd", "tp"), None),
        P(("rep", "pd", "tp"), None),
        P(("rep", "pd", "tp"), None),
        P("rep", None),
        P("rep"),
        P(("rep", "pd"), None, None),
        P(("rep", "pd"), None, None),
        P(("rep", "pd"), None, None),
    )
    return jax.shard_map(
        body,
        mesh=mesh,
        in_specs=placed,
        out_specs=(P(("rep", "pd", "tp"), None), P(("rep", "pd"), None, None)),
        check_vma=False,
    )
```

profile of v0, /device:TPU:0, one launch (start us, length us, event | category | flops | bytes accessed | tf_op | source)
XLA Modules:
  0.0 93.5 jit_solution(18364186801408495500)
XLA Ops:
  7.2 1.0 %copy.106 = bf16[128,512]{0,1:T(8,128)(2,1)S(1)} copy(bf16[128,512]{1,0:T(8,128)(2,1)} %param.11) | data formatting | bytes 262144 | tf_op args[1]
  8.3 1.0 %copy.107 = bf16[128,512]{0,1:T(8,128)(2,1)S(1)} copy(bf16[128,512]{1,0:T(8,128)(2,1)} %param.12) | data formatting | bytes 262144 | tf_op args[2]
  9.3 0.7 pad_maximum_fusion.1
  10.1 1.1 %pad_maximum_fusion.2 = bf16[128,1024]{1,0:T(8,128)(2,1)S(1)} fusion(bf16[128,512]{1,0:T(8,128)(2,1)} %param.12, bf16[128,512]{1,0:T(8,128)(2,1)} %param.11), kind=kLoop, calls=%fused_computation.61 | loop fusion | flops 524288 | bytes 524288 | tf_op jit(solution)/shard_map/concatenate | solution.py:178
  11.2 0.9 reduce_window_sum.11
  12.0 0.7 broadcast_in_dim.197
  12.8 0.1 convert_reduce_fusion.1
  12.9 0.1 select_reduce_fusion.1
  13.0 0.2 convert_reduce_fusion
  13.2 0.1 reshape.566
  13.4 0.3 convolution_convert_fusion
  13.7 1.0 %all_to_all.6 = bf16[4,4,16384]{2,1,0:T(4,128)(2,1)} reshape(bf16[16,16384]{1,0:T(8,128)(2,1)S(1)} %convolution_convert_fusion) | data formatting | bytes 1048576 | tf_op jit(solution)/shard_map/all_to_all | solution.py:198
  14.7 4.2 %all-to-all-start = ((bf16[4,4,16384]{2,1,0:T(4,128)(2,1)}), bf16[4,4,16384]{2,1,0:T(4,128)(2,1)S(1)}, u32[]{:S(2)}, u32[]{:S(2)}) async-start(bf16[4,4,16384]{2,1,0:T(4,128)(2,1)} %all_to_all.6), calls=%async_computation | async-start | bytes 1048576 | tf_op jit(solution)/shard_map/all_to_all | solution.py:198
  19.0 0.1 convert_reduce_fusion.4
  19.1 0.1 fusion.95
  19.1 0.1 convert_reduce_fusion.2
  19.2 0.1 select_reduce_fusion
  19.4 0.1 sub.163
  19.5 0.1 le.75
  19.5 0.1 convert_reduce_fusion.3
  19.7 0.1 eq.180
  19.8 0.1 slice_bitcast_fusion.1
  19.9 0.1 compare_and_fusion.1
  20.0 0.1 compare_and_fusion
  20.2 0.1 copy.160
  20.3 0.1 copy.162
  20.4 0.1 copy-done.4
  20.5 0.4 fusion.98
  20.9 6.8 %all-to-all-done = bf16[4,4,16384]{2,1,0:T(4,128)(2,1)S(1)} async-done(((bf16[4,4,16384]{2,1,0:T(4,128)(2,1)}), bf16[4,4,16384]{2,1,0:T(4,128)(2,1)S(1)}, u32[]{:S(2)}, u32[]{:S(2)}) %all-to-all-start) | async-done | bytes 524320 | tf_op jit(solution)/shard_map/all_to_all | solution.py:198
  27.7 0.4 reshape.567
  28.1 0.1 copy.123
  28.3 0.1 copy.118
  28.4 0.3 fusion.97
  28.7 0.2 fusion.44
  28.9 0.3 fusion.26
  29.2 14.1 %all-gather.1 = bf16[16,4,8,2]{2,1,3,0:T(4,128)(2,1)S(1)} all-gather(bf16[4,4,8,2]{2,1,3,0:T(4,128)(2,1)S(1)} %copy.122), channel_id=3, replica_groups=mesh['rep'=2,'pd'=4,'tp'=4] {'tp'}, dimensions={0}, use_global_device_ids=true | all-gather | bytes 2560 | tf_op jit(solution)/shard_map/all_gather | solution.py:21
  43.3 13.1 %all-gather = bf16[16,4,8,2]{2,1,3,0:T(4,128)(2,1)S(1)} all-gather(bf16[4,4,8,2]{2,1,3,0:T(4,128)(2,1)S(1)} %copy.121), channel_id=2, replica_groups=mesh['rep'=2,'pd'=4,'tp'=4] {'tp'}, dimensions={0}, use_global_device_ids=true | all-gather | bytes 2560 | tf_op jit(solution)/shard_map/all_gather | solution.py:21
  56.4 13.9 %all-gather.2 = bf16[16,4,8,2,128]{4,2,3,0,1:T(8,128)(2,1)S(1)} all-gather(bf16[4,4,8,2,128]{4,2,3,0,1:T(8,128)(2,1)S(1)} %fusion.26), channel_id=4, replica_groups=mesh['rep'=2,'pd'=4,'tp'=4] {'tp'}, dimensions={0}, use_global_device_ids=true | all-gather | bytes 327680 | tf_op jit(solution)/shard_map/all_gather | solution.py:21
  70.4 3.7 %while.12 = (s32[]{:T(128)}, f32[4,4,8,2]{2,3,1,0:T(2,128)S(1)}, f32[4,4,8,2]{2,3,1,0:T(2,128)S(1)}, f32[4,4,8,2,128]{4,3,2,1,0:T(2,128)S(1)}, bf16[4,4,4,8,2]{3...) while((s32[]{:T(128)}, f32[4,4,8,2]{2,3,1,0:T(2,128)S(1)}, ...), condition=%wide.region_15.16_spmd, body=%wide.region_14.15_spmd.sunk | while | flops 133125 | bytes 474255 | solution.py:33
  70.5 0.2 copy.212
  70.7 0.2 copy.213
  70.9 0.8 fusion.108
  71.8 0.2 copy.212
  71.9 0.2 copy.213
  72.1 0.8 fusion.108
  73.0 0.2 copy.212
  73.2 0.2 copy.213
  73.4 0.8 fusion.108
  74.2 0.1 fusion.78
  74.3 0.3 fusion.25
  74.6 0.6 convert_element_type.158
  75.3 1.5 %copy.156 = bf16[2,512,512]{2,1,0:T(8,128)(2,1)S(1)} copy(bf16[2,512,512]{1,2,0:T(8,128)(2,1)} %all-gather.5.cloned.1.call-done) | data formatting | bytes 2097152 | tf_op jit(solution)/shard_map/reshape | solution.py:148
  77.0 0.6 fusion.9
  77.6 0.9 fusion.10
  78.6 1.1 %fusion.20 = bf16[64,4,8,128]{3,0,2,1:T(8,128)(2,1)S(1)} fusion(f32[4,256,64,8]{1,2,3,0:T(8,128)S(1)} %get-tuple-element.327, f32[4,8,64]{2,1,0:T(8,128)S(1)} %get-tuple-element.315, pred[64,256]{1,0:T(8,128)(4,1)S(1)} %compare_and_fusion.1, f32[64,4,8]{0,2,1:T(8,128)S(1)} %bitcast_add_fusion.1, f32[64,4,8]{0,2,1:T(8,128)S(1)} %get-tuple-element.314, ...), kind=kOutput, calls=%fused_computation.32 | convolution fusion | flops 137625600 | bytes 2924544 | tf_op jit(solution)/shard_map/while/body/eval_jaxpr/kgts,skd->kgtd/dot_general | solution.py:59
  79.7 0.3 copy.113
  80.0 0.2 copy.205
  80.2 0.6 copy-done.1
  81.0 0.9 fusion.3
  81.9 1.4 %fusion.4 = f32[4,8,64]{2,1,0:T(8,128)S(1)} fusion(f32[4,512,64,8]{1,2,3,0:T(8,128)S(1)} %get-tuple-element.325, f32[4,8,64]{2,1,0:T(8,128)S(1)} %get-tuple-element.317, pred[64,512]{1,0:T(8,128)(4,1)S(1)} %compare_and_fusion), kind=kLoop, calls=%fused_computation.18 | loop fusion | flops 5240832 | bytes 4243456 | tf_op jit(solution)/shard_map/while/body/eval_jaxpr/reduce_sum | solution.py:58
  83.3 1.7 %divide_convert_fusion = bf16[64,4,8,128]{3,0,2,1:T(8,128)(2,1)S(1)} fusion(bf16[512,4,128,1]{0,2,3,1:T(8,128)(2,1)S(1)} %bitcast.190, f32[4,512,64,8]{1,2,3,0:T(8,128)S(1)} %get-tuple-element.325, f32[4,8,64]{2,1,0:T(8,128)S(1)} %get-tuple-element.317, pred[64,512]{1,0:T(8,128)(4,1)S(1)} %compare_and_fusion, f32[64,4,8]{0,2,1:T(8,128)S(1)} %bitcast_add_fusion, ...), kind=kOutput, calls=%fused_computation.46 | convolution fusion | flops 274464768 | bytes 5300224 | tf_op jit(solution)/shard_map/while/body/eval_jaxpr/kgts,skd->kgtd/dot_general | solution.py:59
  85.0 0.3 copy.117
  85.3 0.2 copy.204
  85.5 1.1 %pad_maximum_fusion = bf16[128,4096]{1,0:T(8,128)(2,1)} fusion(bf16[64,4096]{1,0:T(8,128)(2,1)S(1)} %bitcast.183, bf16[64,4096]{1,0:T(8,128)(2,1)S(1)} %bitcast.182), kind=kLoop, calls=%fused_computation.45 | loop fusion | flops 2097152 | bytes 2097152 | tf_op jit(solution)/shard_map/concatenate | solution.py:159
  (59 shorter events, 1.1 us)
Async XLA Ops:
  7.2 67.2 %copy-start = (bf16[4,2,512]{2,1,0:T(2,128)(2,1)S(1)}, bf16[4,2,512]{2,1,0:T(2,128)(2,1)}, u32[]{:S(2)}) copy-start(bf16[4,2,512]{2,1,0:T(2,128)(2,1)} %param.17) | copy-start | bytes 24580
  7.2 68.1 %all-gather.5.cloned.1.call-start = ((), (), s32[]{:S(2)}) async-start(), calls=%async_computation.1 | async-start | bytes 1310720 | tf_op jit(solution)/shard_map/all_gather | solution.py:142
  10.1 9.7 %copy-start.2 = (bf16[128,4096]{1,0:T(8,128)(2,1)S(1)}, bf16[128,4096]{1,0:T(8,128)(2,1)}, u32[]{:S(2)}) copy-start(bf16[128,4096]{1,0:T(8,128)(2,1)} %param.10) | copy-start | bytes 3145732
  13.7 6.5 %copy-start.3 = (bf16[4,2,4096]{2,1,0:T(2,128)(2,1)S(1)}, bf16[4,2,4096]{2,1,0:T(2,128)(2,1)}, u32[]{:S(2)}) copy-start(bf16[4,2,4096]{2,1,0:T(2,128)(2,1)} %param.15) | copy-start | bytes 196612
  14.7 13.1 %all-to-all-start = ((bf16[4,4,16384]{2,1,0:T(4,128)(2,1)}), bf16[4,4,16384]{2,1,0:T(4,128)(2,1)S(1)}, u32[]{:S(2)}, u32[]{:S(2)}) async-start(bf16[4,4,16384]{2,1,0:T(4,128)(2,1)} %all_to_all.6), calls=%async_computation | async-start | bytes 1048576 | tf_op jit(solution)/shard_map/all_to_all | solution.py:198
  19.8 0.7 copy-start.4
  79.7 1.2 %copy-start.1 = (bf16[2,512,512]{1,2,0:T(8,128)(2,1)S(1)}, bf16[2,512,512]{1,2,0:T(8,128)(2,1)}, u32[]{:S(2)}) copy-start(bf16[2,512,512]{1,2,0:T(8,128)(2,1)} %all-gather.5.cloned.1.call-done) | copy-start | bytes 3145732
Sparse Core Ops, SparseCore 0:
  10.2 34.0 all-gather.4
where the time goes:
time: 93.8 us; the launch traced here: 93.5 us
  blocking collectives  41.1 us (44%)
  between operations  14.5 us (15%)
  local copies, waits for them, and re-layouts  10.8 us (12%)
  other arithmetic  10.1 us (11%)
  waiting for transfers between devices  6.81 us (7%)
  matrix products  5.8 us (6%)
  starting transfers between devices  4.25 us (5%)
    all_gather x3, blocking collectives, combined_all(): lax.all_gather(a.astype(kind), axis)  41.1 us
    all_to_all x1, waiting for transfers between devices, body(): lax.all_to_all(outgoing, 'pd', split_axis=0, concat_axis=0, tiled=True)  6.79 us
    all_to_all x1, starting transfers between devices, body(): lax.all_to_all(outgoing, 'pd', split_axis=0, concat_axis=0, tiled=True)  4.21 us
    unnamed x17, local copies, waits for them, and re-layouts  3.53 us
    dot_general x2, matrix products, update(): jnp.einsum('kgts,skd->kgtd', weights.astype(jnp.bfloat16), value_row_list...  2.74 us
    add x3, other arithmetic, combine(): acc_a * factor_a[..., None] + acc_b * factor_b[..., None]  2.38 us
    reduce_sum x2, other arithmetic, update(): total = total * factor + jnp.sum(weights, axis=-1)  2.28 us
  transfers between devices with their start and end apart: 2, of which 1 were waited for; matrix products, arithmetic and copies ran while one was open for 12% of the time, Pallas kernels for 0%

commit v1 on v0

v1 whole, which is shorter than its diff:
```python
import math

import jax
import jax.numpy as jnp
from jax import lax
from jax.experimental import pallas as pl
from jax.experimental.pallas import tpu as pltpu
from jax.sharding import PartitionSpec as P

QUERY_HEADS = 32
KEY_VALUE_HEADS = 4
HEAD_SIZE = 128
PAGE = 16
GROUP_REQUESTS = 4
DECODE_STEPS = 2
HEADS_PER_KV = QUERY_HEADS // KEY_VALUE_HEADS
KV_WIDTH = KEY_VALUE_HEADS * HEAD_SIZE
Q_WIDTH = QUERY_HEADS * HEAD_SIZE
DECODE_ROWS = GROUP_REQUESTS * DECODE_STEPS
PADDED_ROWS = 16
CHUNK = 4

MASKED = -1e30
EXPONENT = math.log2(math.e) / math.sqrt(HEAD_SIZE)


def scores_of(queries, keys):
    return lax.dot_general(
        queries, keys, (((1,), (1,)), ((), ())), preferred_element_type=jnp.float32
    )


def with_ones(values):
    return jnp.concatenate([values, jnp.ones_like(values)], axis=1)


def key_positions(shape, member, width, first_shard):
    column = lax.broadcasted_iota(jnp.int32, shape, 1)
    rows = shape[1] // CHUNK if width >= CHUNK else shape[1] // width
    shard = column // rows
    offset = column - shard * rows
    source = member - (first_shard + shard)
    source = jnp.where(source < 0, source + width, source)
    return (offset // PAGE * width + source) * PAGE + offset % PAGE


def request_ends(lengths_ref, group):
    ends = []
    total = jnp.int32(0)
    for r in range(GROUP_REQUESTS):
        total = total + lengths_ref[group, r] * PAGE
        ends.append(total)
    return ends


def fold(state, scores_list, values_list):
    top = None
    for scores in scores_list:
        part = jnp.max(scores, axis=1, keepdims=True)
        top = part if top is None else jnp.maximum(top, part)
    if state is not None:
        top = jnp.maximum(top, state[0])
    acc = None
    for scores, values in zip(scores_list, values_list):
        weights = jnp.exp2((scores - top) * EXPONENT).astype(jnp.bfloat16)
        part = jnp.dot(weights, values, preferred_element_type=jnp.float32)
        acc = part if acc is None else acc + part
    if state is not None:
        acc = acc + state[1] * jnp.exp2((state[0] - top) * EXPONENT)
    return top, acc


def normalised(state):
    acc = state[1]
    return (acc[:, :HEAD_SIZE] / acc[:, HEAD_SIZE:]).astype(jnp.bfloat16)


def prefill_kernel(width, lengths_ref, where_ref, q_ref, *refs):
    k_refs, v_refs, out_ref, bias_ref = refs[:width], refs[width : 2 * width], refs[-2], refs[-1]
    tokens = q_ref.shape[0]
    half = tokens // 2
    group, member = where_ref[0], where_ref[1]
    per_chunk = min(CHUNK, width)
    chunks = width // per_chunk

    @pl.when(pl.program_id(0) == 0)
    def _():
        ends = request_ends(lengths_ref, group)
        offset = lax.broadcasted_iota(jnp.int32, (tokens, 1), 0)
        qpos = (offset // PAGE * width + member) * PAGE + offset % PAGE
        low = jnp.zeros_like(qpos)
        for end in ends:
            low = jnp.where(qpos >= end, end, low)
        for c in range(chunks):
            kpos = key_positions((tokens, per_chunk * tokens), member, width, c * per_chunk)
            bias_ref[c] = jnp.where((kpos >= low) & (kpos <= qpos), 0.0, MASKED)

    for first, keys in ((0, half), (half, tokens)):
        rows = pl.ds(first, half)
        chunk_data = []
        for c in range(chunks):
            span = range(c * per_chunk, (c + 1) * per_chunk)
            k_all = jnp.concatenate([k_refs[s][:keys, :] for s in span], axis=0)
            v_all = with_ones(jnp.concatenate([v_refs[s][:keys, :] for s in span], axis=0))
            bias = jnp.concatenate(
                [bias_ref[c, rows, i * tokens : i * tokens + keys] for i in range(per_chunk)], axis=1
            )
            chunk_data.append((k_all, v_all, bias))
        for head in range(HEADS_PER_KV):
            columns = slice(head * HEAD_SIZE, (head + 1) * HEAD_SIZE)
            queries = q_ref[rows, columns]
            state = None
            for k_all, v_all, bias in chunk_data:
                state = fold(state, [scores_of(queries, k_all) + bias], [v_all])
            out_ref[rows, columns] = normalised(state)


def decode_kernel(width, lengths_ref, where_ref, q_ref, fresh_k_ref, fresh_v_ref, *refs):
    k_refs, v_refs, out_ref = refs[:width], refs[width : 2 * width], refs[-1]
    tokens = k_refs[0].shape[0]
    group, member = where_ref[0], where_ref[1]
    per_chunk = min(CHUNK, width)
    chunks = width // per_chunk
    count = HEADS_PER_KV * PADDED_ROWS
    ends = request_ends(lengths_ref, group)
    row = lax.broadcasted_iota(jnp.int32, (count, 1), 0) % PADDED_ROWS
    request = row // DECODE_STEPS
    low = jnp.zeros_like(row)
    high = jnp.zeros_like(row) + ends[0]
    for r in range(1, GROUP_REQUESTS):
        low = jnp.where(request == r, ends[r - 1], low)
        high = jnp.where(request == r, ends[r], high)
    queries = jnp.concatenate(
        [q_ref[:, h * HEAD_SIZE : (h + 1) * HEAD_SIZE] for h in range(HEADS_PER_KV)], axis=0
    )
    column = lax.broadcasted_iota(jnp.int32, (count, PADDED_ROWS), 1)
    fresh = (column // DECODE_STEPS == request) & (column % DECODE_STEPS <= row % DECODE_STEPS)
    fresh_scores = jnp.where(fresh, scores_of(queries, fresh_k_ref[...]), MASKED)
    fresh_values = with_ones(fresh_v_ref[...])
    state = None
    for c in range(chunks):
        span = range(c * per_chunk, (c + 1) * per_chunk)
        k_all = jnp.concatenate([k_refs[s][...] for s in span], axis=0)
        v_all = with_ones(jnp.concatenate([v_refs[s][...] for s in span], axis=0))
        kpos = key_positions((count, per_chunk * tokens), member, width, c * per_chunk)
        scores = jnp.where((kpos >= low) & (kpos < high), scores_of(queries, k_all), MASKED)
        if c == 0:
            state = fold(state, [scores, fresh_scores], [v_all, fresh_values])
        else:
            state = fold(state, [scores], [v_all])
    out = normalised(state)
    for h in range(HEADS_PER_KV):
        out_ref[:, h * HEAD_SIZE : (h + 1) * HEAD_SIZE] = out[
            h * PADDED_ROWS : (h + 1) * PADDED_ROWS
        ]


def call_prefill(lengths, where, query, keys, values):
    tokens = query.shape[0]
    width = len(keys)
    per_chunk = min(CHUNK, width)
    kv_spec = pl.BlockSpec((tokens, HEAD_SIZE), lambda h: (0, h))
    q_spec = pl.BlockSpec((tokens, HEADS_PER_KV * HEAD_SIZE), lambda h: (0, h))
    return pl.pallas_call(
        lambda *refs: prefill_kernel(width, *refs),
        grid=(KEY_VALUE_HEADS,),
        in_specs=[pl.BlockSpec(memory_space=pltpu.SMEM)] * 2 + [q_spec] + [kv_spec] * (2 * width),
        out_specs=q_spec,
        out_shape=jax.ShapeDtypeStruct(query.shape, jnp.bfloat16),
        scratch_shapes=[
            pltpu.VMEM((width // per_chunk, tokens, per_chunk * tokens), jnp.float32)
        ],
        compiler_params=pltpu.CompilerParams(vmem_limit_bytes=32 * 1024 * 1024),
        cost_estimate=pl.CostEstimate(
            flops=4 * tokens * tokens * width * Q_WIDTH,
            bytes_accessed=4 * tokens * Q_WIDTH + 4 * width * tokens * KV_WIDTH,
            transcendentals=tokens * tokens * width * QUERY_HEADS,
        ),
        name="prefill_attention",
    )(lengths, where, query, *keys, *values)


def call_decode(lengths, where, rows, keys, values):
    tokens = keys[0].shape[0]
    width = len(keys)
    heads = HEADS_PER_KV * HEAD_SIZE
    kv_spec = pl.BlockSpec((tokens, HEAD_SIZE), lambda h: (0, h))
    q_spec = pl.BlockSpec((PADDED_ROWS, heads), lambda h: (0, h))
    first_k, first_v = Q_WIDTH // HEAD_SIZE, (Q_WIDTH + KV_WIDTH) // HEAD_SIZE
    return pl.pallas_call(
        lambda *refs: decode_kernel(width, *refs),
        grid=(KEY_VALUE_HEADS,),
        in_specs=[pl.BlockSpec(memory_space=pltpu.SMEM)] * 2
        + [
            q_spec,
            pl.BlockSpec((PADDED_ROWS, HEAD_SIZE), lambda h: (0, first_k + h)),
            pl.BlockSpec((PADDED_ROWS, HEAD_SIZE), lambda h: (0, first_v + h)),
        ]
        + [kv_spec] * (2 * width),
        out_specs=q_spec,
        out_shape=jax.ShapeDtypeStruct((PADDED_ROWS, Q_WIDTH), jnp.bfloat16),
        compiler_params=pltpu.CompilerParams(vmem_limit_bytes=32 * 1024 * 1024),
        cost_estimate=pl.CostEstimate(
            flops=4 * PADDED_ROWS * tokens * width * Q_WIDTH,
            bytes_accessed=4 * width * tokens * KV_WIDTH,
            transcendentals=PADDED_ROWS * tokens * width * QUERY_HEADS,
        ),
        name="decode_attention",
    )(lengths, where, rows, rows, rows, *keys, *values)


def ring(size, step):
    return [(i, (i + step) % size) for i in range(size)]


def chosen(picks, rows):
    return jnp.dot(picks.astype(jnp.bfloat16), rows, preferred_element_type=jnp.float32).astype(
        jnp.bfloat16
    )


def body(
    prompt_query,
    prompt_key,
    prompt_value,
    prompt_lengths,
    decode_slot,
    decoded_query,
    decoded_key,
    decoded_value,
):
    tp_size = lax.axis_size("tp")
    pd_size = lax.axis_size("pd")
    my_group = lax.axis_index("pd")
    member = lax.axis_index("tp")
    where = jnp.stack([my_group, member]).astype(jnp.int32)

    keys, values = [prompt_key], [prompt_value]
    for _ in range(1, tp_size):
        keys.append(lax.ppermute(keys[-1], "tp", ring(tp_size, 1)))
        values.append(lax.ppermute(values[-1], "tp", ring(tp_size, 1)))

    own = jnp.concatenate([decoded_query, decoded_key, decoded_value], axis=2).reshape(
        DECODE_ROWS, Q_WIDTH + 2 * KV_WIDTH
    )
    blocks = [own] + [lax.ppermute(own, "pd", ring(pd_size, k)) for k in range(1, pd_size)]
    everyone = jnp.concatenate(blocks, axis=0)

    slots = lax.dynamic_slice_in_dim(decode_slot, my_group * GROUP_REQUESTS, GROUP_REQUESTS, 0)
    block_of = (my_group - slots // GROUP_REQUESTS) % pd_size
    place_of = slots % GROUP_REQUESTS
    row = jnp.arange(PADDED_ROWS, dtype=jnp.int32)
    step = row % DECODE_STEPS
    at = jnp.repeat(
        block_of * DECODE_ROWS + place_of * DECODE_STEPS, DECODE_STEPS, total_repeat_length=DECODE_ROWS
    )
    at = jnp.concatenate([at, jnp.full((PADDED_ROWS - DECODE_ROWS,), -DECODE_STEPS, jnp.int32)]) + step
    picks = at[:, None] == jnp.arange(pd_size * DECODE_ROWS, dtype=jnp.int32)[None, :]
    rows = chosen(picks, everyone)

    dec = call_decode(prompt_lengths, where, rows, keys, values)

    sent = []
    for k in range(pd_size):
        out_row = jnp.arange(DECODE_STEPS, dtype=jnp.int32)
        match = (block_of == (-k) % pd_size if k else block_of == 0)
        match = jnp.repeat(match, DECODE_STEPS, total_repeat_length=DECODE_ROWS)
        match = jnp.concatenate([match, jnp.zeros((PADDED_ROWS - DECODE_ROWS,), bool)])
        sent.append(match[None, :] & (step[None, :] == out_row[:, None]))
    outgoing = chosen(jnp.concatenate(sent, axis=0), dec)
    arrived = [outgoing[:DECODE_STEPS]]
    for k in range(1, pd_size):
        part = outgoing[k * DECODE_STEPS : (k + 1) * DECODE_STEPS]
        arrived.append(lax.ppermute(part, "pd", ring(pd_size, k)))

    pre_out = call_prefill(prompt_lengths, where, prompt_query, keys, values)

    numbers = jnp.arange(decode_slot.shape[0], dtype=jnp.int32)
    wanted = my_group * GROUP_REQUESTS + jnp.arange(GROUP_REQUESTS, dtype=jnp.int32)
    owner = jnp.sum(
        jnp.where(decode_slot[None, :] == wanted[:, None], numbers[None, :] // GROUP_REQUESTS, 0), axis=1
    )
    from_block = (my_group - owner) % pd_size
    dec_out = jnp.zeros((GROUP_REQUESTS, DECODE_STEPS, Q_WIDTH), jnp.bfloat16)
    for k in range(pd_size):
        dec_out = jnp.where((from_block == k)[:, None, None], arrived[k][None], dec_out)
    return (pre_out, dec_out)


def solution(mesh):
    placed = (
        P(("rep", "pd", "tp"), None),
        P(("rep", "pd", "tp"), None),
        P(("rep", "pd", "tp"), None),
        P("rep", None),
        P("rep"),
        P(("rep", "pd"), None, None),
        P(("rep", "pd"), None, None),
        P(("rep", "pd"), None, None),
    )
    return jax.shard_map(
        body,
        mesh=mesh,
        in_specs=placed,
        out_specs=(P(("rep", "pd", "tp"), None), P(("rep", "pd"), None, None)),
        check_vma=False,
    )
```

time: 93.8 us -> 44.9 us (0.48)
  blocking collectives: 41.1 us -> 0 us
  between operations: 14.5 us -> 0.78 us
  Pallas kernels: 0 us -> 11.1 us
  waiting for transfers between devices: 6.81 us -> 16 us
  other arithmetic: 10.1 us -> 2.28 us
  local copies, waits for them, and re-layouts: 10.8 us -> 4.66 us
  matrix products: 5.8 us -> 0.39 us
  starting transfers between devices: 4.25 us -> 9.26 us
    all_gather x3 -> x0, blocking collectives: 41.1 us -> none  [combined_all(): lax.all_gather(a.astype(kind), axis)]
    ppermute x0 -> x12, waiting for transfers between devices: none -> 16 us  [the longest x3 9.73 us: body(): keys.append(lax.ppermute(keys[-1], 'tp', ring(tp_size, 1)))]
    pallas_call x0 -> x2, Pallas kernels: none -> 11.1 us  [the longest x1 8.09 us: call_prefill(): pl.pallas_call(lambda *refs: prefill_kernel(width, *refs), grid=(KEY_VALU...]
    ppermute x0 -> x12, starting transfers between devices: none -> 9.26 us  [the longest x3 3.23 us: body(): lax.ppermute(own, 'pd', ring(pd_size, k))]
    all_to_all x1 -> x0, waiting for transfers between devices: 6.79 us -> none  [body(): lax.all_to_all(outgoing, 'pd', split_axis=0, concat_axis=0, tiled=True)]
    dot_general x9 -> x2, matrix products: 5.8 us -> 0.39 us  [chosen(): jnp.dot(picks.astype(jnp.bfloat16), rows, preferred_element_type=jnp.floa...]
    all_to_all x1 -> x0, starting transfers between devices: 4.21 us -> none  [body(): lax.all_to_all(outgoing, 'pd', split_axis=0, concat_axis=0, tiled=True)]
    reduce_sum x11 -> x1, other arithmetic: 3.42 us -> 0.18 us  [body(): jnp.sum(jnp.where(decode_slot[None, :] == wanted[:, None], numbers[None,...]
  transfers between devices with their start and end apart: 2 -> 12, of which waited for: 1 -> 5; matrix products, arithmetic and copies ran while one was open for 12% -> 9% of each run, Pallas kernels for 0% -> 18%
where the time goes in v1:
time: 44.9 us; the launch traced here: 44.5 us
  waiting for transfers between devices  16 us (36%)
  Pallas kernels  11.1 us (25%)
  starting transfers between devices  9.26 us (21%)
  local copies, waits for them, and re-layouts  4.66 us (10%)
  other arithmetic  2.28 us (5%)
  between operations  0.78 us (2%)
    ppermute x3, waiting for transfers between devices, body(): keys.append(lax.ppermute(keys[-1], 'tp', ring(tp_size, 1)))  9.73 us
    pallas_call x1, Pallas kernels, call_prefill(): pl.pallas_call(lambda *refs: prefill_kernel(width, *refs), grid=(KEY_VALU...  8.09 us
    ppermute x3, waiting for transfers between devices, body(): values.append(lax.ppermute(values[-1], 'tp', ring(tp_size, 1)))  6.23 us
    ppermute x3, starting transfers between devices, body(): lax.ppermute(own, 'pd', ring(pd_size, k))  3.23 us
    ppermute x3, starting transfers between devices, body(): keys.append(lax.ppermute(keys[-1], 'tp', ring(tp_size, 1)))  3.21 us
    pallas_call x1, Pallas kernels, call_decode(): pl.pallas_call(lambda *refs: decode_kernel(width, *refs), grid=(KEY_VALUE...  3.03 us
    gather x4, local copies, waits for them, and re-layouts, body(): match = jnp.repeat(match, DECODE_STEPS, total_repeat_length=DECODE_ROWS)  2.6 us
    ppermute x3, starting transfers between devices, body(): values.append(lax.ppermute(values[-1], 'tp', ring(tp_size, 1)))  1.58 us
  transfers between devices with their start and end apart: 12, of which 5 were waited for; matrix products, arithmetic and copies ran while one was open for 9% of the time, Pallas kernels for 18%

profile of v1, /device:TPU:0, one launch (start us, length us, event | category | flops | bytes accessed | tf_op | source)
XLA Modules:
  0.0 44.5 jit_solution(13615099084495043236)
XLA Ops:
  0.6 0.0 copy-start
  0.6 0.0 copy-start.1
  0.7 1.0 %pad_maximum_fusion = bf16[4,2,5120]{2,1,0:T(2,128)(2,1)S(1)} fusion(bf16[4,2,512]{2,1,0:T(2,128)(2,1)} %param.27, bf16[4,2,512]{2,1,0:T(2,128)(2,1)} %param.26, bf16[4,2,4096]{2,1,0:T(2,128)(2,1)} %param.25), kind=kLoop, calls=%fused_computation.18 | loop fusion | flops 245760 | bytes 163840 | tf_op jit(solution)/shard_map/concatenate | solution.py:243
  1.7 2.4 %collective-permute-start.8 = (bf16[8,5120]{1,0:T(8,128)(2,1)S(1)}, bf16[8,5120]{1,0:T(8,128)(2,1)S(1)}, u32[]{:S(2)}, u32[]{:S(2)}) collective-permute-start(bf16[8,5120]{1,0:T(8,128)(2,1)S(1)} %reshape.167), channel_id=1, source_target_pairs={{0,12},{4,0},{8,4},{12,8},{1,13},{5,1},{9,5},{13,9},{2,14},{6,2},{... | collective-permute-start | bytes 245768 | tf_op jit(solution)/shard_map/ppermute | solution.py:246
  4.1 0.6 %collective-permute-start.7 = (bf16[8,5120]{1,0:T(8,128)(2,1)S(1)}, bf16[8,5120]{1,0:T(8,128)(2,1)S(1)}, u32[]{:S(2)}, u32[]{:S(2)}) collective-permute-start(bf16[8,5120]{1,0:T(8,128)(2,1)S(1)} %reshape.167), channel_id=1, source_target_pairs={{0,8},{4,12},{8,0},{12,4},{1,9},{5,13},{9,1},{13,5},{2,10},{6,14},... | collective-permute-start | bytes 245768 | tf_op jit(solution)/shard_map/ppermute | solution.py:246
  4.8 0.2 collective-permute-start.6
  4.9 0.0 copy-done
  4.9 1.6 %collective-permute-start = (bf16[128,512]{1,0:T(8,128)(2,1)S(1)}, bf16[128,512]{1,0:T(8,128)(2,1)S(1)}, u32[]{:S(2)}, u32[]{:S(2)}) collective-permute-start(bf16[128,512]{1,0:T(8,128)(2,1)S(1)} %copy-done), channel_id=1, source_target_pairs={{0,1},{1,2},{2,3},{3,0},{4,5},{5,6},{6,7},{7,4},{8,9},{9,10},{10,1... | collective-permute-start | bytes 393224 | tf_op jit(solution)/shard_map/ppermute | solution.py:240
  6.5 0.0 copy-done.1
  6.5 1.6 %collective-permute-start.3 = (bf16[128,512]{1,0:T(8,128)(2,1)S(1)}, bf16[128,512]{1,0:T(8,128)(2,1)S(1)}, u32[]{:S(2)}, u32[]{:S(2)}) collective-permute-start(bf16[128,512]{1,0:T(8,128)(2,1)S(1)} %copy-done.1), channel_id=1, source_target_pairs={{0,1},{1,2},{2,3},{3,0},{4,5},{5,6},{6,7},{7,4},{8,9},{9,10},{10,1... | collective-permute-start | bytes 393224 | tf_op jit(solution)/shard_map/ppermute | solution.py:241
  8.1 0.0 copy-start.4
  8.1 0.6 %copy-done.4 = s32[16]{0:T(128)S(1)} copy-done((s32[16]{0:T(128)S(1)}, s32[16]{0:T(128)}, u32[]{:S(2)}) %copy-start.4) | copy-done | bytes 88
  8.8 0.1 broadcast_compare_fusion.7
  8.8 0.1 fusion.20
  8.9 0.2 select_reduce_fusion
  9.1 0.0 copy-start.5
  9.1 0.6 %copy-done.5 = s32[8]{0:T(128)S(1)} copy-done((s32[8]{0:T(128)S(1)}, s32[8]{0:T(128)}, u32[]{:S(2)}) %copy-start.5) | copy-done | bytes 56
  9.8 0.6 %gather_fusion = s32[8]{0:T(128)S(1)} fusion(s32[4]{0:T(128)S(1)} %fusion.20, s32[1024]{0:T(1024)S(1)} %pad_clamp_fusion), kind=kCustom, calls=%fused_computation.4 | custom fusion | bytes 96 | tf_op jit(solution)/shard_map/jit(_take)/gather | solution.py:254
  10.4 0.7 %gather_fusion.4 = pred[8]{0:T(512)(128)(4,1)S(1)} fusion(pred[4]{0:T(512)(128)(4,1)S(1)} %get-tuple-element.60, s32[1024]{0:T(1024)S(1)} %pad_clamp_fusion), kind=kCustom, calls=%fused_computation.3.clone | custom fusion | bytes 48 | tf_op jit(solution)/shard_map/jit(_take)/gather | solution.py:267
  11.1 0.7 %gather_fusion.3 = pred[8]{0:T(512)(128)(4,1)S(1)} fusion(pred[4]{0:T(512)(128)(4,1)S(1)} %get-tuple-element.61, s32[1024]{0:T(1024)S(1)} %pad_clamp_fusion), kind=kCustom, calls=%fused_computation.2.clone | custom fusion | bytes 48 | tf_op jit(solution)/shard_map/jit(_take)/gather | solution.py:267
  11.8 0.6 %gather_fusion.2 = pred[8]{0:T(512)(128)(4,1)S(1)} fusion(pred[4]{0:T(512)(128)(4,1)S(1)} %get-tuple-element.59, s32[1024]{0:T(1024)S(1)} %pad_clamp_fusion), kind=kCustom, calls=%fused_computation.1.clone | custom fusion | bytes 48 | tf_op jit(solution)/shard_map/jit(_take)/gather | solution.py:267
  12.4 0.7 %gather_fusion.1 = pred[8]{0:T(512)(128)(4,1)S(1)} fusion(pred[4]{0:T(512)(128)(4,1)S(1)} %get-tuple-element.47, s32[1024]{0:T(1024)S(1)} %pad_clamp_fusion), kind=kCustom, calls=%fused_computation.clone | custom fusion | bytes 48 | tf_op jit(solution)/shard_map/jit(_take)/gather | solution.py:267
  13.1 0.0 collective-permute-done.refs_4_.refs_6_
  13.1 1.6 %collective-permute-start.1 = (bf16[128,512]{1,0:T(8,128)(2,1)S(1)}, bf16[128,512]{1,0:T(8,128)(2,1)S(1)}, u32[]{:S(2)}, u32[]{:S(2)}) collective-permute-start(bf16[128,512]{1,0:T(8,128)(2,1)S(1)} %collective-permute-done.refs_4_.refs_6_), channel_id=1, source_target_pairs={{0,1},{1,2},{2,3},{3,0},{4,5},{5,6},{6,7},{7,4},{8,9},{9,10},{10,1... | collective-permute-start | bytes 393224 | tf_op jit(solution)/shard_map/ppermute | solution.py:240
  14.7 0.8 %collective-permute-done.3.refs_8_.refs_10_ = bf16[128,512]{1,0:T(8,128)(2,1)S(1)} collective-permute-done((bf16[128,512]{1,0:T(8,128)(2,1)S(1)}, bf16[128,512]{1,0:T(8,128)(2,1)S(1)}, u32[]{:S(2)}, u32[]{:S(2)}) %collective-permute-start.3) | collective-permute-done | bytes 131104 | tf_op jit(solution)/shard_map/ppermute | solution.py:241
  15.6 0.0 collective-permute-start.4
  15.6 0.1 pad_add_fusion.refs_1_
  15.6 0.0 copy-start.2
  15.6 5.7 %collective-permute-done.1.refs_5_.refs_7_ = bf16[128,512]{1,0:T(8,128)(2,1)S(1)} collective-permute-done((bf16[128,512]{1,0:T(8,128)(2,1)S(1)}, bf16[128,512]{1,0:T(8,128)(2,1)S(1)}, u32[]{:S(2)}, u32[]{:S(2)}) %collective-permute-start.1) | collective-permute-done | bytes 131104 | tf_op jit(solution)/shard_map/ppermute | solution.py:240
  21.3 0.0 collective-permute-start.2
  21.3 2.6 %collective-permute-done.4.refs_9_.refs_11_ = bf16[128,512]{1,0:T(8,128)(2,1)S(1)} collective-permute-done((bf16[128,512]{1,0:T(8,128)(2,1)S(1)}, bf16[128,512]{1,0:T(8,128)(2,1)S(1)}, u32[]{:S(2)}, u32[]{:S(2)}) %collective-permute-start.4) | collective-permute-done | bytes 131104 | tf_op jit(solution)/shard_map/ppermute | solution.py:241
  24.0 0.0 collective-permute-start.5
  24.0 0.0 collective-permute-done.8
  24.0 0.0 collective-permute-done.7
  24.0 0.0 collective-permute-done.6
  24.0 0.2 convolution_convert_fusion.refs_2_.refs_3_.refs_4_
  24.2 0.0 copy-start.3
  24.2 4.0 %collective-permute-done.2.refs_6_.refs_8_ = bf16[128,512]{1,0:T(8,128)(2,1)S(1)} collective-permute-done((bf16[128,512]{1,0:T(8,128)(2,1)S(1)}, bf16[128,512]{1,0:T(8,128)(2,1)S(1)}, u32[]{:S(2)}, u32[]{:S(2)}) %collective-permute-start.2) | collective-permute-done | bytes 131104 | tf_op jit(solution)/shard_map/ppermute | solution.py:240
  28.3 2.8 %collective-permute-done.5.refs_10_.refs_12_ = bf16[128,512]{1,0:T(8,128)(2,1)S(1)} collective-permute-done((bf16[128,512]{1,0:T(8,128)(2,1)S(1)}, bf16[128,512]{1,0:T(8,128)(2,1)S(1)}, u32[]{:S(2)}, u32[]{:S(2)}) %collective-permute-start.5) | collective-permute-done | bytes 131104 | tf_op jit(solution)/shard_map/ppermute | solution.py:241
  31.1 0.0 copy-done.2
  31.1 3.0 %decode_attention.1 = bf16[16,4096]{1,0:T(8,128)(2,1)S(1)} custom-call(s32[4,4]{1,0:T(4,128)S(1)} %copy-done.2, s32[2]{0:T(128)S(1)} %pad_add_fusion.refs_1_, bf16[16,5120]{1,0:T(8,128)(2,1)S(1)} %convolution_convert_fusion.refs_2_.refs_3_.refs_4_, bf16[16,5120]{1,0:T(8,128)(2,1)S(1)} %convolution_convert_fusion.refs_2_.refs_3_.refs_4_, ...), custom_call_target="tpu_custom_call" | custom-call | flops 134217728 | bytes 1048576 | tf_op jit(solution)/shard_map/decode_attention/pallas_call | solution.py:190
  34.1 0.1 convolution_convert_fusion.1
  34.3 0.1 fusion.25
  34.3 0.1 collective-permute-start.9
  34.4 0.5 %collective-permute-start.11 = (bf16[2,4096]{1,0:T(2,128)(2,1)S(1)}, bf16[2,4096]{1,0:T(2,128)(2,1)S(1)}, u32[]{:S(2)}, u32[]{:S(2)}) collective-permute-start(bf16[2,4096]{1,0:T(2,128)(2,1)S(1)} %get-tuple-element.53), channel_id=1, source_target_pairs={{0,4},{4,8},{8,12},{12,0},{1,5},{5,9},{9,13},{13,1},{2,6},{6,10},{... | collective-permute-start | bytes 49160 | tf_op jit(solution)/shard_map/ppermute | solution.py:274
  34.9 0.7 %collective-permute-start.10 = (bf16[2,4096]{1,0:T(2,128)(2,1)S(1)}, bf16[2,4096]{1,0:T(2,128)(2,1)S(1)}, u32[]{:S(2)}, u32[]{:S(2)}) collective-permute-start(bf16[2,4096]{1,0:T(2,128)(2,1)S(1)} %get-tuple-element.54), channel_id=1, source_target_pairs={{0,8},{4,12},{8,0},{12,4},{1,9},{5,13},{9,1},{13,5},{2,10},{6,14},... | collective-permute-start | bytes 49160 | tf_op jit(solution)/shard_map/ppermute | solution.py:274
  35.6 0.0 copy-done.3
  35.6 8.1 %prefill_attention.1 = bf16[128,4096]{1,0:T(8,128)(2,1)} custom-call(s32[4,4]{1,0:T(4,128)S(1)} %copy-done.2, s32[2]{0:T(128)S(1)} %pad_add_fusion.refs_1_, bf16[128,4096]{1,0:T(8,128)(2,1)S(1)} %copy-done.3, bf16[128,512]{1,0:T(8,128)(2,1)S(1)} %copy-done, bf16[128,512]{1,0:T(8,128)(2,1)S(1)} %collective-permute-done.refs_4_.refs_6_, ...), custom_call_target="tpu_custom_call" | custom-call | flops 1073741824 | bytes 3145728 | tf_op jit(solution)/shard_map/prefill_attention/pallas_call | solution.py:164
  43.7 0.0 collective-permute-done.9
  43.7 0.0 collective-permute-done.11
  43.7 0.0 collective-permute-done.10
  43.7 0.8 %broadcast_select_fusion.2 = bf16[4,2,4096]{2,1,0:T(2,128)(2,1)} fusion(pred[4]{0:T(512)(128)(4,1)S(1)} %get-tuple-element.64, pred[4]{0:T(512)(128)(4,1)S(1)} %get-tuple-element.63, pred[4]{0:T(512)(128)(4,1)S(1)} %get-tuple-element.62, pred[4]{0:T(512)(128)(4,1)S(1)} %get-tuple-element.49, bf16[2,4096]{1,0:T(2,128)(2,1)S(1)} %get-tuple-element.52, ...), kind=kLoop, calls=%fused_computation.16 | loop fusion | flops 131072 | bytes 131088 | tf_op jit(solution)/shard_map/jit(_where)/select_n | solution.py:286
  (14 shorter events, 0.1 us)
Async XLA Ops:
  0.6 4.3 %copy-start = (bf16[128,512]{1,0:T(8,128)(2,1)S(1)}, bf16[128,512]{1,0:T(8,128)(2,1)}, u32[]{:S(2)}) copy-start(bf16[128,512]{1,0:T(8,128)(2,1)} %refs_5_.1) | copy-start | bytes 393220
  0.6 5.9 %copy-start.1 = (bf16[128,512]{1,0:T(8,128)(2,1)S(1)}, bf16[128,512]{1,0:T(8,128)(2,1)}, u32[]{:S(2)}) copy-start(bf16[128,512]{1,0:T(8,128)(2,1)} %refs_9_.1) | copy-start | bytes 393220
  1.7 22.3 %collective-permute-start.8 = (bf16[8,5120]{1,0:T(8,128)(2,1)S(1)}, bf16[8,5120]{1,0:T(8,128)(2,1)S(1)}, u32[]{:S(2)}, u32[]{:S(2)}) collective-permute-start(bf16[8,5120]{1,0:T(8,128)(2,1)S(1)} %reshape.167), channel_id=1, source_target_pairs={{0,12},{4,0},{8,4},{12,8},{1,13},{5,1},{9,5},{13,9},{2,14},{6,2},{... | collective-permute-start | bytes 245768 | tf_op jit(solution)/shard_map/ppermute | solution.py:246
  4.1 19.8 %collective-permute-start.7 = (bf16[8,5120]{1,0:T(8,128)(2,1)S(1)}, bf16[8,5120]{1,0:T(8,128)(2,1)S(1)}, u32[]{:S(2)}, u32[]{:S(2)}) collective-permute-start(bf16[8,5120]{1,0:T(8,128)(2,1)S(1)} %reshape.167), channel_id=1, source_target_pairs={{0,8},{4,12},{8,0},{12,4},{1,9},{5,13},{9,1},{13,5},{2,10},{6,14},... | collective-permute-start | bytes 245768 | tf_op jit(solution)/shard_map/ppermute | solution.py:246
  4.8 19.2 %collective-permute-start.6 = (bf16[8,5120]{1,0:T(8,128)(2,1)S(1)}, bf16[8,5120]{1,0:T(8,128)(2,1)S(1)}, u32[]{:S(2)}, u32[]{:S(2)}) collective-permute-start(bf16[8,5120]{1,0:T(8,128)(2,1)S(1)} %reshape.167), channel_id=1, source_target_pairs={{0,4},{4,8},{8,12},{12,0},{1,5},{5,9},{9,13},{13,1},{2,6},{6,10},{... | collective-permute-start | bytes 245768 | tf_op jit(solution)/shard_map/ppermute | solution.py:246
  4.9 8.2 %collective-permute-start = (bf16[128,512]{1,0:T(8,128)(2,1)S(1)}, bf16[128,512]{1,0:T(8,128)(2,1)S(1)}, u32[]{:S(2)}, u32[]{:S(2)}) collective-permute-start(bf16[128,512]{1,0:T(8,128)(2,1)S(1)} %copy-done), channel_id=1, source_target_pairs={{0,1},{1,2},{2,3},{3,0},{4,5},{5,6},{6,7},{7,4},{8,9},{9,10},{10,1... | collective-permute-start | bytes 393224 | tf_op jit(solution)/shard_map/ppermute | solution.py:240
  6.5 9.0 %collective-permute-start.3 = (bf16[128,512]{1,0:T(8,128)(2,1)S(1)}, bf16[128,512]{1,0:T(8,128)(2,1)S(1)}, u32[]{:S(2)}, u32[]{:S(2)}) collective-permute-start(bf16[128,512]{1,0:T(8,128)(2,1)S(1)} %copy-done.1), channel_id=1, source_target_pairs={{0,1},{1,2},{2,3},{3,0},{4,5},{5,6},{6,7},{7,4},{8,9},{9,10},{10,1... | collective-permute-start | bytes 393224 | tf_op jit(solution)/shard_map/ppermute | solution.py:241
  8.1 0.7 %copy-start.4 = (s32[16]{0:T(128)S(1)}, s32[16]{0:T(128)}, u32[]{:S(2)}) copy-start(s32[16]{0:T(128)} %param.24) | copy-start | bytes 196
  9.1 0.7 %copy-start.5 = (s32[8]{0:T(128)S(1)}, s32[8]{0:T(128)}, u32[]{:S(2)}) copy-start(s32[8]{0:T(128)} %constant.232.clone.1) | copy-start | bytes 100
  13.1 8.2 %collective-permute-start.1 = (bf16[128,512]{1,0:T(8,128)(2,1)S(1)}, bf16[128,512]{1,0:T(8,128)(2,1)S(1)}, u32[]{:S(2)}, u32[]{:S(2)}) collective-permute-start(bf16[128,512]{1,0:T(8,128)(2,1)S(1)} %collective-permute-done.refs_4_.refs_6_), channel_id=1, source_target_pairs={{0,1},{1,2},{2,3},{3,0},{4,5},{5,6},{6,7},{7,4},{8,9},{9,10},{10,1... | collective-permute-start | bytes 393224 | tf_op jit(solution)/shard_map/ppermute | solution.py:240
  15.6 8.4 %collective-permute-start.4 = (bf16[128,512]{1,0:T(8,128)(2,1)S(1)}, bf16[128,512]{1,0:T(8,128)(2,1)S(1)}, u32[]{:S(2)}, u32[]{:S(2)}) collective-permute-start(bf16[128,512]{1,0:T(8,128)(2,1)S(1)} %collective-permute-done.3.refs_8_.refs_10_), channel_id=1, source_target_pairs={{0,1},{1,2},{2,3},{3,0},{4,5},{5,6},{6,7},{7,4},{8,9},{9,10},{10,1... | collective-permute-start | bytes 393224 | tf_op jit(solution)/shard_map/ppermute | solution.py:241
  15.6 15.4 %copy-start.2 = (s32[4,4]{1,0:T(4,128)S(1)}, s32[4,4]{1,0:T(4,128)}, u32[]{:S(2)}) copy-start(s32[4,4]{1,0:T(4,128)} %refs_0_.3) | copy-start | bytes 196
  21.3 6.9 %collective-permute-start.2 = (bf16[128,512]{1,0:T(8,128)(2,1)S(1)}, bf16[128,512]{1,0:T(8,128)(2,1)S(1)}, u32[]{:S(2)}, u32[]{:S(2)}) collective-permute-start(bf16[128,512]{1,0:T(8,128)(2,1)S(1)} %collective-permute-done.1.refs_5_.refs_7_), channel_id=1, source_target_pairs={{0,1},{1,2},{2,3},{3,0},{4,5},{5,6},{6,7},{7,4},{8,9},{9,10},{10,1... | collective-permute-start | bytes 393224 | tf_op jit(solution)/shard_map/ppermute | solution.py:240
  24.0 7.1 %collective-permute-start.5 = (bf16[128,512]{1,0:T(8,128)(2,1)S(1)}, bf16[128,512]{1,0:T(8,128)(2,1)S(1)}, u32[]{:S(2)}, u32[]{:S(2)}) collective-permute-start(bf16[128,512]{1,0:T(8,128)(2,1)S(1)} %collective-permute-done.4.refs_9_.refs_11_), channel_id=1, source_target_pairs={{0,1},{1,2},{2,3},{3,0},{4,5},{5,6},{6,7},{7,4},{8,9},{9,10},{10,1... | collective-permute-start | bytes 393224 | tf_op jit(solution)/shard_map/ppermute | solution.py:241
  24.2 11.3 %copy-start.3 = (bf16[128,4096]{1,0:T(8,128)(2,1)S(1)}, bf16[128,4096]{1,0:T(8,128)(2,1)}, u32[]{:S(2)}) copy-start(bf16[128,4096]{1,0:T(8,128)(2,1)} %refs_2_.1) | copy-start | bytes 3145732
  34.3 9.3 %collective-permute-start.9 = (bf16[2,4096]{1,0:T(2,128)(2,1)S(1)}, bf16[2,4096]{1,0:T(2,128)(2,1)S(1)}, u32[]{:S(2)}, u32[]{:S(2)}) collective-permute-start(bf16[2,4096]{1,0:T(2,128)(2,1)S(1)} %get-tuple-element.51), channel_id=1, source_target_pairs={{0,12},{4,0},{8,4},{12,8},{1,13},{5,1},{9,5},{13,9},{2,14},{6,2},{... | collective-permute-start | bytes 49160 | tf_op jit(solution)/shard_map/ppermute | solution.py:274
  34.4 9.3 %collective-permute-start.11 = (bf16[2,4096]{1,0:T(2,128)(2,1)S(1)}, bf16[2,4096]{1,0:T(2,128)(2,1)S(1)}, u32[]{:S(2)}, u32[]{:S(2)}) collective-permute-start(bf16[2,4096]{1,0:T(2,128)(2,1)S(1)} %get-tuple-element.53), channel_id=1, source_target_pairs={{0,4},{4,8},{8,12},{12,0},{1,5},{5,9},{9,13},{13,1},{2,6},{6,10},{... | collective-permute-start | bytes 49160 | tf_op jit(solution)/shard_map/ppermute | solution.py:274
  34.9 8.8 %collective-permute-start.10 = (bf16[2,4096]{1,0:T(2,128)(2,1)S(1)}, bf16[2,4096]{1,0:T(2,128)(2,1)S(1)}, u32[]{:S(2)}, u32[]{:S(2)}) collective-permute-start(bf16[2,4096]{1,0:T(2,128)(2,1)S(1)} %get-tuple-element.54), channel_id=1, source_target_pairs={{0,8},{4,12},{8,0},{12,4},{1,9},{5,13},{9,1},{13,5},{2,10},{6,14},... | collective-permute-start | bytes 49160 | tf_op jit(solution)/shard_map/ppermute | solution.py:274

commit v2 on v1

v2 whole, which is shorter than its diff:
```python
import math

import jax
import jax.numpy as jnp
from jax import lax
from jax.experimental import pallas as pl
from jax.experimental.pallas import tpu as pltpu
from jax.sharding import PartitionSpec as P

QUERY_HEADS = 32
KEY_VALUE_HEADS = 4
HEAD_SIZE = 128
PAGE = 16
GROUP_REQUESTS = 4
DECODE_STEPS = 2
HEADS_PER_KV = QUERY_HEADS // KEY_VALUE_HEADS
KV_WIDTH = KEY_VALUE_HEADS * HEAD_SIZE
Q_WIDTH = QUERY_HEADS * HEAD_SIZE
Q_BLOCK = HEADS_PER_KV * HEAD_SIZE
DECODE_ROWS = GROUP_REQUESTS * DECODE_STEPS
PADDED_ROWS = 16
STACKED = HEADS_PER_KV * PADDED_ROWS
MIB = 1024 * 1024

MASKED = -1e30
EXPONENT = math.log2(math.e) / math.sqrt(HEAD_SIZE)

VMEM = pl.BlockSpec(memory_space=pltpu.VMEM)
SMEM = pl.BlockSpec(memory_space=pltpu.SMEM)


def scores_of(queries, keys):
    return lax.dot_general(
        queries, keys, (((1,), (1,)), ((), ())), preferred_element_type=jnp.float32
    )


def product(left, right):
    return jnp.dot(left, right, preferred_element_type=jnp.float32)


def iota(shape, axis):
    return lax.broadcasted_iota(jnp.int32, shape, axis)


def key_positions(rows, member, width):
    column = iota((1, width * rows), 1)
    shift = column // rows
    offset = column - shift * rows
    source = member - shift
    source = jnp.where(source < 0, source + width, source)
    return (offset // PAGE * width + source) * PAGE + offset % PAGE


def request_ends(lengths_ref, group):
    ends = []
    total = jnp.int32(0)
    for r in range(GROUP_REQUESTS):
        total = total + lengths_ref[group, r] * PAGE
        ends.append(total)
    return ends


def collect(table, refs, member, out_ref):
    rows = refs[0].shape[0]
    for shift, (right, left) in enumerate(table):
        part = refs[right][...]
        if left != right:
            part = jnp.where(member >= shift, part, refs[left][...])
        out_ref[shift * rows : (shift + 1) * rows, : part.shape[1]] = part


def parts_of(ref, width, tokens, keys, columns):
    if keys == tokens:
        return ref[:, columns]
    return jnp.concatenate([ref[s * tokens : s * tokens + keys, columns] for s in range(width)], axis=0)


def head_group(width):
    return max(1, min(HEADS_PER_KV, HEADS_PER_KV * 4 // width))


def weights_kernel(table, pd_size, lengths_ref, where_ref, slots_ref, q_ref, *refs):
    width = len(table)
    k_count = len(refs) - pd_size - 7
    block_refs, k_refs = refs[:pd_size], refs[pd_size : pd_size + k_count]
    low_ref, high_ref, dec_ref, fresh_ref, fresh_v_ref, keys_ref, rows_ref = refs[pd_size + k_count :]
    tokens = q_ref.shape[0]
    half = tokens // 2
    group, member = where_ref[0], where_ref[1]
    ends = request_ends(lengths_ref, group)
    h = pl.program_id(0)

    @pl.when(h == 0)
    def _():
        collect(table, k_refs, member, keys_ref)
        row = iota((PADDED_ROWS, DECODE_ROWS), 0)
        column = iota((PADDED_ROWS, DECODE_ROWS), 1)
        total = None
        for k in range(pd_size):
            pick = column < 0
            for r in range(GROUP_REQUESTS):
                slot = slots_ref[group * GROUP_REQUESTS + r]
                back = group - slot // GROUP_REQUESTS
                back = jnp.where(back < 0, back + pd_size, back)
                first = jnp.where(back == k, slot % GROUP_REQUESTS * DECODE_STEPS, -DECODE_ROWS * 4)
                pick = pick | (
                    (row // DECODE_STEPS == r) & (column == first + row - r * DECODE_STEPS)
                )
            part = product(pick.astype(jnp.float32).astype(jnp.bfloat16), block_refs[k][...])
            total = part if total is None else total + part
        total = total.astype(jnp.bfloat16)
        rows_ref[...] = total[:, : Q_WIDTH + KV_WIDTH]
        fresh_v_ref[...] = total[:, Q_WIDTH + KV_WIDTH :]

    columns = pl.ds(pl.multiple_of(h * HEAD_SIZE, HEAD_SIZE), HEAD_SIZE)

    row = iota((STACKED, 1), 0) % PADDED_ROWS
    request = row // DECODE_STEPS
    low = jnp.zeros_like(row)
    high = jnp.zeros_like(row) + ends[0]
    for r in range(1, GROUP_REQUESTS):
        low = jnp.where(request == r, ends[r - 1], low)
        high = jnp.where(request == r, ends[r], high)
    first = h * Q_BLOCK
    queries = jnp.concatenate(
        [
            rows_ref[:, pl.ds(pl.multiple_of(first + g * HEAD_SIZE, HEAD_SIZE), HEAD_SIZE)]
            for g in range(HEADS_PER_KV)
        ],
        axis=0,
    )
    column = iota((STACKED, PADDED_ROWS), 1)
    fresh = (column // DECODE_STEPS == request) & (column % DECODE_STEPS <= row % DECODE_STEPS)
    fresh_columns = pl.ds(pl.multiple_of(Q_WIDTH + h * HEAD_SIZE, HEAD_SIZE), HEAD_SIZE)
    fresh_scores = jnp.where(fresh, scores_of(queries, rows_ref[:, fresh_columns]), MASKED)
    kpos = key_positions(tokens, member, width)
    scores = jnp.where(
        (kpos >= low) & (kpos < high), scores_of(queries, keys_ref[:, columns]), MASKED
    )
    top = jnp.maximum(
        jnp.max(scores, axis=1, keepdims=True), jnp.max(fresh_scores, axis=1, keepdims=True)
    )
    dec_ref[0] = jnp.exp2((scores - top) * EXPONENT).astype(jnp.bfloat16)
    fresh_ref[0] = jnp.exp2((fresh_scores - top) * EXPONENT).astype(jnp.bfloat16)

    together = head_group(width)
    for start, keys, out_ref in ((0, half, low_ref), (half, tokens, high_ref)):
        offset = start + iota((half, 1), 0)
        qpos = (offset // PAGE * width + member) * PAGE + offset % PAGE
        low = jnp.zeros_like(qpos)
        for end in ends:
            low = jnp.where(qpos >= end, end, low)
        kpos = key_positions(keys, member, width)
        bias = jnp.where((kpos >= low) & (kpos <= qpos), 0.0, MASKED)
        k_all = parts_of(keys_ref, width, tokens, keys, columns)
        for g in range(0, HEADS_PER_KV, together):
            queries = jnp.concatenate(
                [
                    q_ref[
                        start : start + half,
                        pl.ds(pl.multiple_of(first + i * HEAD_SIZE, HEAD_SIZE), HEAD_SIZE),
                    ]
                    for i in range(g, g + together)
                ],
                axis=0,
            )
            scores = scores_of(queries, k_all).reshape(together, half, width * keys) + bias[None]
            top = jnp.max(scores, axis=2, keepdims=True)
            weights = jnp.exp2((scores - top) * EXPONENT).astype(jnp.bfloat16)
            out_ref[0, g * half : (g + together) * half, :] = weights.reshape(
                together * half, width * keys
            )


def decode_kernel(table, pd_size, where_ref, slots_ref, dec_ref, fresh_ref, fresh_v_ref, *refs):
    width = len(table)
    v_refs, out_refs, values_ref = refs[: -pd_size - 1], refs[-pd_size - 1 : -1], refs[-1]
    group, member = where_ref[0], where_ref[1]
    collect(table, v_refs, member, values_ref)
    ones = jnp.ones((values_ref.shape[0], HEAD_SIZE), jnp.bfloat16)
    fresh_ones = jnp.ones((PADDED_ROWS, HEAD_SIZE), jnp.bfloat16)
    row = iota((8, PADDED_ROWS), 0)
    column = iota((8, PADDED_ROWS), 1)
    picks = []
    for k in range(pd_size):
        target = group + k
        target = jnp.where(target >= pd_size, target - pd_size, target)
        pick = column < 0
        for r in range(GROUP_REQUESTS):
            mine = slots_ref[group * GROUP_REQUESTS + r] // GROUP_REQUESTS == target
            first = jnp.where(mine, r * DECODE_STEPS, -PADDED_ROWS * 4)
            pick = pick | ((row < DECODE_STEPS) & (column == first + row))
        picks.append(pick.astype(jnp.float32).astype(jnp.bfloat16))
    for h in range(KEY_VALUE_HEADS):
        columns = slice(h * HEAD_SIZE, (h + 1) * HEAD_SIZE)
        acc = product(dec_ref[h], jnp.concatenate([values_ref[:, columns], ones], axis=1))
        acc += product(fresh_ref[h], jnp.concatenate([fresh_v_ref[:, columns], fresh_ones], axis=1))
        out = (acc[:, :HEAD_SIZE] / acc[:, HEAD_SIZE:]).astype(jnp.bfloat16)
        out = jnp.concatenate(
            [out[g * PADDED_ROWS : (g + 1) * PADDED_ROWS] for g in range(HEADS_PER_KV)], axis=1
        )
        for k in range(pd_size):
            sent = product(picks[k], out).astype(jnp.bfloat16)
            out_refs[k][:, h * Q_BLOCK : (h + 1) * Q_BLOCK] = sent[:DECODE_STEPS]


def prefill_kernel(table, where_ref, low_ref, high_ref, *refs):
    width = len(table)
    v_refs, (out_ref, values_ref, done_ref, sem) = refs[:-4], refs[-4:]
    tokens = v_refs[0].shape[0]
    half = tokens // 2
    collect(table, v_refs, where_ref[1], values_ref)
    copies = []
    for h in range(KEY_VALUE_HEADS):
        columns = slice(h * HEAD_SIZE, (h + 1) * HEAD_SIZE)
        for start, keys, p_ref in ((0, half, low_ref), (half, tokens, high_ref)):
            values = parts_of(values_ref, width, tokens, keys, columns)
            acc = product(p_ref[h], jnp.concatenate([values, jnp.ones_like(values)], axis=1))
            out = (acc[:, :HEAD_SIZE] / acc[:, HEAD_SIZE:]).astype(jnp.bfloat16)
            for g in range(HEADS_PER_KV):
                done_ref[
                    start : start + half, h * Q_BLOCK + g * HEAD_SIZE : h * Q_BLOCK + (g + 1) * HEAD_SIZE
                ] = out[g * half : (g + 1) * half]
        span = pl.ds(h * Q_BLOCK, Q_BLOCK)
        copy = pltpu.make_async_copy(done_ref.at[:, span], out_ref.at[:, span], sem.at[h])
        copy.start()
        copies.append(copy)
    for copy in copies:
        copy.wait()


def call_weights(table, lengths, where, slots, query, blocks, keys):
    tokens, width = query.shape[0], len(table)
    half, every = tokens // 2, width * tokens
    stacked = HEADS_PER_KV * half
    shapes = [
        (KEY_VALUE_HEADS, stacked, width * half),
        (KEY_VALUE_HEADS, stacked, every),
        (KEY_VALUE_HEADS, STACKED, every),
        (KEY_VALUE_HEADS, STACKED, PADDED_ROWS),
    ]
    return pl.pallas_call(
        lambda *refs: weights_kernel(table, len(blocks), *refs),
        grid=(KEY_VALUE_HEADS,),
        in_specs=[SMEM] * 3 + [VMEM] * (1 + len(blocks) + len(keys)),
        out_specs=[pl.BlockSpec((1,) + s[1:], lambda h: (h, 0, 0)) for s in shapes] + [VMEM],
        out_shape=[jax.ShapeDtypeStruct(s, jnp.bfloat16) for s in shapes]
        + [jax.ShapeDtypeStruct((PADDED_ROWS, KV_WIDTH), jnp.bfloat16)],
        scratch_shapes=[
            pltpu.VMEM((every, KV_WIDTH), jnp.bfloat16),
            pltpu.VMEM((PADDED_ROWS, Q_WIDTH + KV_WIDTH), jnp.bfloat16),
        ],
        compiler_params=pltpu.CompilerParams(vmem_limit_bytes=(28 + width) * MIB),
        cost_estimate=pl.CostEstimate(
            flops=2 * tokens * every * Q_WIDTH,
            bytes_accessed=2 * tokens * Q_WIDTH + 2 * every * KV_WIDTH,
            transcendentals=tokens * every * QUERY_HEADS,
        ),
        name="weights",
    )(lengths, where, slots, query, *blocks, *keys)


def call_decode(table, pd_size, where, slots, weights, values):
    _, _, dec, fresh, fresh_v = weights
    every = dec.shape[2]
    return pl.pallas_call(
        lambda *refs: decode_kernel(table, pd_size, *refs),
        in_specs=[SMEM] * 2 + [VMEM] * (3 + len(values)),
        out_specs=[VMEM] * pd_size,
        out_shape=[jax.ShapeDtypeStruct((DECODE_STEPS, Q_WIDTH), jnp.bfloat16)] * pd_size,
        scratch_shapes=[pltpu.VMEM((every, KV_WIDTH), jnp.bfloat16)],
        compiler_params=pltpu.CompilerParams(vmem_limit_bytes=(28 + len(table)) * MIB),
        cost_estimate=pl.CostEstimate(
            flops=2 * PADDED_ROWS * every * Q_WIDTH,
            bytes_accessed=2 * every * KV_WIDTH,
            transcendentals=0,
        ),
        name="decode_values",
    )(where, slots, dec, fresh, fresh_v, *values)


def call_prefill(table, where, weights, values):
    low, high = weights[0], weights[1]
    tokens = values[0].shape[0]
    every = high.shape[2]
    return pl.pallas_call(
        lambda *refs: prefill_kernel(table, *refs),
        in_specs=[SMEM] + [VMEM] * (2 + len(values)),
        out_specs=pl.BlockSpec(memory_space=pl.ANY),
        out_shape=jax.ShapeDtypeStruct((tokens, Q_WIDTH), jnp.bfloat16),
        scratch_shapes=[
            pltpu.VMEM((every, KV_WIDTH), jnp.bfloat16),
            pltpu.VMEM((tokens, Q_WIDTH), jnp.bfloat16),
            pltpu.SemaphoreType.DMA((KEY_VALUE_HEADS,)),
        ],
        compiler_params=pltpu.CompilerParams(vmem_limit_bytes=(28 + len(table)) * MIB),
        cost_estimate=pl.CostEstimate(
            flops=2 * tokens * every * Q_WIDTH,
            bytes_accessed=4 * tokens * Q_WIDTH + 2 * every * KV_WIDTH,
            transcendentals=0,
        ),
        name="prefill_values",
    )(where, low, high, *values)


def ring(size, step):
    return [(i, (i + step) % size) for i in range(size)]


def line_exchange(own, size):
    arrays, right, left = [own], {0: 0}, {0: 0}

    def send(place, pairs):
        arrays.append(lax.ppermute(arrays[place], "tp", pairs))
        return len(arrays) - 1

    for d in sorted(range(1, size), key=lambda d: (d > 2, d != 2, d)):
        if d <= 2 and 2 * d == size:
            right[d] = left[d] = send(0, ring(size, d))
        elif d > 2 and right[d - 1] == left[d - 1] and 2 * d > size + 1:
            pairs = [(i, i + 1) for i in range(d - 1, size - 1)]
            right[d] = left[d] = send(right[d - 1], pairs + [(i, i - 1) for i in range(1, size - d + 1)])
        else:
            hop = min(d, 2) if d <= 2 else 1
            first = 0 if d <= 2 else d - 1
            right[d] = send(0 if d <= 2 else right[d - 1], [(i, i + hop) for i in range(first, size - hop)])
            left[d] = send(0 if d <= 2 else left[d - 1], [(i, i - hop) for i in range(hop, size - first)])
    return arrays, [(right[s], left[(size - s) % size]) for s in range(size)]


def body(
    prompt_query,
    prompt_key,
    prompt_value,
    prompt_lengths,
    decode_slot,
    decoded_query,
    decoded_key,
    decoded_value,
):
    tp_size = lax.axis_size("tp")
    pd_size = lax.axis_size("pd")
    my_group = lax.axis_index("pd")
    member = lax.axis_index("tp")
    where = jnp.stack([my_group, member]).astype(jnp.int32)

    keys, table = line_exchange(prompt_key, tp_size)
    values, _ = line_exchange(prompt_value, tp_size)

    own = jnp.concatenate([decoded_query, decoded_key, decoded_value], axis=2).reshape(
        DECODE_ROWS, Q_WIDTH + 2 * KV_WIDTH
    )
    own, _ = lax.optimization_barrier((own, keys[1]))
    blocks = [own] + [lax.ppermute(own, "pd", ring(pd_size, k)) for k in range(1, pd_size)]

    weights = call_weights(table, prompt_lengths, where, decode_slot, prompt_query, blocks, keys)
    outgoing = call_decode(table, pd_size, where, decode_slot, weights, values)
    arrived = [outgoing[0]]
    for k in range(1, pd_size):
        arrived.append(lax.ppermute(outgoing[k], "pd", ring(pd_size, k)))
    pre_out = call_prefill(table, where, weights, values)

    numbers = jnp.arange(decode_slot.shape[0], dtype=jnp.int32)
    wanted = my_group * GROUP_REQUESTS + jnp.arange(GROUP_REQUESTS, dtype=jnp.int32)
    owner = jnp.sum(
        jnp.where(decode_slot[None, :] == wanted[:, None], numbers[None, :] // GROUP_REQUESTS, 0), axis=1
    )
    from_block = (my_group - owner) % pd_size
    dec_out = jnp.zeros((GROUP_REQUESTS, DECODE_STEPS, Q_WIDTH), jnp.bfloat16)
    for k in range(pd_size):
        dec_out = jnp.where((from_block == k)[:, None, None], arrived[k][None], dec_out)
    return (pre_out, dec_out)


def solution(mesh):
    placed = (
        P(("rep", "pd", "tp"), None),
        P(("rep", "pd", "tp"), None),
        P(("rep", "pd", "tp"), None),
        P("rep", None),
        P("rep"),
        P(("rep", "pd"), None, None),
        P(("rep", "pd"), None, None),
        P(("rep", "pd"), None, None),
    )
    return jax.shard_map(
        body,
        mesh=mesh,
        in_specs=placed,
        out_specs=(P(("rep", "pd", "tp"), None), P(("rep", "pd"), None, None)),
        check_vma=False,
    )
```

time: 44.9 us -> 42.3 us (0.942)
  the two profiles are of different devices: /device:TPU:0 before, /device:TPU:21 now
where the time goes in v2:
time: 42.3 us; the launch traced here: 41.9 us
  starting transfers between devices  22.4 us (53%)
  Pallas kernels  7.72 us (18%)
  waiting for transfers between devices  4.79 us (11%)
  local copies, waits for them, and re-layouts  3.51 us (8%)
  other arithmetic  2.69 us (6%)
  between operations  0.84 us (2%)
    ppermute x8, starting transfers between devices, send(): arrays.append(lax.ppermute(arrays[place], 'tp', pairs))  15.2 us
    ppermute x3, starting transfers between devices, body(): lax.ppermute(own, 'pd', ring(pd_size, k))  4.12 us
    pallas_call x1, Pallas kernels, call_weights(): pl.pallas_call(lambda *refs: weights_kernel(table, len(blocks), *refs), g...  3.5 us
    unnamed x10, local copies, waits for them, and re-layouts  3.47 us
    ppermute x8, waiting for transfers between devices, send(): arrays.append(lax.ppermute(arrays[place], 'tp', pairs))  3.28 us
    ppermute x3, starting transfers between devices, body(): arrived.append(lax.ppermute(outgoing[k], 'pd', ring(pd_size, k)))  3.09 us
    pallas_call x1, Pallas kernels, call_prefill(): pl.pallas_call(lambda *refs: prefill_kernel(table, *refs), in_specs=[SMEM...  2.44 us
    pallas_call x1, Pallas kernels, call_decode(): pl.pallas_call(lambda *refs: decode_kernel(table, pd_size, *refs), in_spe...  1.78 us
  transfers between devices with their start and end apart: 14, of which 2 were waited for; matrix products, arithmetic and copies ran while one was open for 5% of the time, Pallas kernels for 14%

profile of v2, /device:TPU:21, one launch (start us, length us, event | category | flops | bytes accessed | tf_op | source)
XLA Modules:
  0.0 41.9 jit_solution(5197877853142248245)
XLA Ops:
  0.6 0.1 collective-permute-start
  0.8 3.2 %collective-permute-start.4 = (bf16[128,512]{1,0:T(8,128)(2,1)}, bf16[128,512]{1,0:T(8,128)(2,1)S(1)}, u32[]{:S(2)}, u32[]{:S(2)}) collective-permute-start(bf16[128,512]{1,0:T(8,128)(2,1)} %refs_8_.1), channel_id=1, source_target_pairs={{0,1},{1,2},{2,3},{4,5},{5,6},{6,7},{8,9},{9,10},{10,11},{12,13},{... | collective-permute-start | bytes 393224 | tf_op jit(solution)/shard_map/ppermute | solution.py:315
  4.0 3.0 %collective-permute-start.5 = (bf16[128,512]{1,0:T(8,128)(2,1)}, bf16[128,512]{1,0:T(8,128)(2,1)S(1)}, u32[]{:S(2)}, u32[]{:S(2)}) collective-permute-start(bf16[128,512]{1,0:T(8,128)(2,1)} %refs_8_.1), channel_id=1, source_target_pairs={{1,0},{2,1},{3,2},{5,4},{6,5},{7,6},{9,8},{10,9},{11,10},{13,12},{... | collective-permute-start | bytes 393224 | tf_op jit(solution)/shard_map/ppermute | solution.py:315
  7.0 0.6 %collective-permute-start.7 = (bf16[128,512]{1,0:T(8,128)(2,1)}, bf16[128,512]{1,0:T(8,128)(2,1)S(1)}, u32[]{:S(2)}, u32[]{:S(2)}) collective-permute-start(bf16[128,512]{1,0:T(8,128)(2,1)} %refs_5_.1), channel_id=1, source_target_pairs={{0,2},{1,3},{2,0},{3,1},{4,6},{5,7},{6,4},{7,5},{8,10},{9,11},{10,... | collective-permute-start | bytes 393224 | tf_op jit(solution)/shard_map/ppermute | solution.py:315
  7.6 0.9 %pad_maximum_fusion = bf16[4,2,5120]{2,1,0:T(2,128)(2,1)S(1)} fusion(bf16[4,2,512]{2,1,0:T(2,128)(2,1)} %param.15, bf16[4,2,512]{2,1,0:T(2,128)(2,1)} %param.14, bf16[4,2,4096]{2,1,0:T(2,128)(2,1)} %param.13), kind=kLoop, calls=%fused_computation.4 | loop fusion | flops 245760 | bytes 163840 | tf_op jit(solution)/shard_map/concatenate | solution.py:351
  8.6 0.0 copy-start
  8.7 0.8 %select_reduce_fusion = s32[4]{0:T(128)S(1)} fusion(s32[16]{0:T(128)S(1)} %and_select_fusion.1, s32[16]{0:T(128)} %refs_1_.1, s32[4]{0:T(128)S(1)} %iota_add_fusion), kind=kLoop, calls=%fused_computation.7 | loop fusion | flops 188 | bytes 160 | tf_op jit(solution)/shard_map/reduce_sum | solution.py:366
  9.5 0.0 collective-permute-done.refs_9_
  9.5 2.7 %collective-permute-start.1 = (bf16[8,5120]{1,0:T(8,128)(2,1)S(1)}, bf16[8,5120]{1,0:T(8,128)(2,1)S(1)}, u32[]{:S(2)}, u32[]{:S(2)}) collective-permute-start(bf16[8,5120]{1,0:T(8,128)(2,1)S(1)} %reshape.77.refs_4_), channel_id=1, source_target_pairs={{0,4},{4,8},{8,12},{12,0},{1,5},{5,9},{9,13},{13,1},{2,6},{6,10},{... | collective-permute-start | bytes 245768 | tf_op jit(solution)/shard_map/ppermute | solution.py:355
  12.2 0.3 collective-permute-start.2
  12.4 3.3 %collective-permute-done.4.refs_10_ = bf16[128,512]{1,0:T(8,128)(2,1)S(1)} collective-permute-done((bf16[128,512]{1,0:T(8,128)(2,1)}, bf16[128,512]{1,0:T(8,128)(2,1)S(1)}, u32[]{:S(2)}, u32[]{:S(2)}) %collective-permute-start.4) | collective-permute-done | bytes 131104 | tf_op jit(solution)/shard_map/ppermute | solution.py:315
  15.7 1.3 %collective-permute-start.6 = (bf16[128,512]{1,0:T(8,128)(2,1)S(1)}, bf16[128,512]{1,0:T(8,128)(2,1)S(1)}, u32[]{:S(2)}, u32[]{:S(2)}) collective-permute-start(bf16[128,512]{1,0:T(8,128)(2,1)S(1)} %collective-permute-done.refs_9_), channel_id=1, source_target_pairs={{2,3},{1,0},{6,7},{5,4},{10,11},{9,8},{14,15},{13,12},{18,19},{17,... | collective-permute-start | bytes 393224 | tf_op jit(solution)/shard_map/ppermute | solution.py:315
  17.0 0.0 collective-permute-done.5.refs_11_
  17.0 1.9 %collective-permute-start.8 = (bf16[128,512]{1,0:T(8,128)(2,1)}, bf16[128,512]{1,0:T(8,128)(2,1)S(1)}, u32[]{:S(2)}, u32[]{:S(2)}) collective-permute-start(bf16[128,512]{1,0:T(8,128)(2,1)} %refs_5_.1), channel_id=1, source_target_pairs={{0,1},{1,2},{2,3},{4,5},{5,6},{6,7},{8,9},{9,10},{10,11},{12,13},{... | collective-permute-start | bytes 393224 | tf_op jit(solution)/shard_map/ppermute | solution.py:315
  18.9 0.0 collective-permute-done.7.refs_4_.refs_6_
  19.0 3.4 %collective-permute-start.9 = (bf16[128,512]{1,0:T(8,128)(2,1)}, bf16[128,512]{1,0:T(8,128)(2,1)S(1)}, u32[]{:S(2)}, u32[]{:S(2)}) collective-permute-start(bf16[128,512]{1,0:T(8,128)(2,1)} %refs_5_.1), channel_id=1, source_target_pairs={{1,0},{2,1},{3,2},{5,4},{6,5},{7,6},{9,8},{10,9},{11,10},{13,12},{... | collective-permute-start | bytes 393224 | tf_op jit(solution)/shard_map/ppermute | solution.py:315
  22.3 0.0 collective-permute-done.1.refs_5_
  22.3 1.2 %collective-permute-start.3 = (bf16[8,5120]{1,0:T(8,128)(2,1)S(1)}, bf16[8,5120]{1,0:T(8,128)(2,1)S(1)}, u32[]{:S(2)}, u32[]{:S(2)}) collective-permute-start(bf16[8,5120]{1,0:T(8,128)(2,1)S(1)} %reshape.77.refs_4_), channel_id=1, source_target_pairs={{0,12},{4,0},{8,4},{12,8},{1,13},{5,1},{9,5},{13,9},{2,14},{6,2},{... | collective-permute-start | bytes 245768 | tf_op jit(solution)/shard_map/ppermute | solution.py:355
  23.5 0.0 collective-permute-done.2.refs_6_
  23.5 1.6 %collective-permute-start.10 = (bf16[128,512]{1,0:T(8,128)(2,1)S(1)}, bf16[128,512]{1,0:T(8,128)(2,1)S(1)}, u32[]{:S(2)}, u32[]{:S(2)}) collective-permute-start(bf16[128,512]{1,0:T(8,128)(2,1)S(1)} %collective-permute-done.7.refs_4_.refs_6_), channel_id=1, source_target_pairs={{2,3},{1,0},{6,7},{5,4},{10,11},{9,8},{14,15},{13,12},{18,19},{17,... | collective-permute-start | bytes 393224 | tf_op jit(solution)/shard_map/ppermute | solution.py:315
  25.2 0.1 pad_add_fusion.refs_1_.refs_0_
  25.3 1.5 %collective-permute-done.3.refs_7_ = bf16[8,5120]{1,0:T(8,128)(2,1)S(1)} collective-permute-done((bf16[8,5120]{1,0:T(8,128)(2,1)S(1)}, bf16[8,5120]{1,0:T(8,128)(2,1)S(1)}, u32[]{:S(2)}, u32[]{:S(2)}) %collective-permute-start.3) | collective-permute-done | bytes 81952 | tf_op jit(solution)/shard_map/ppermute | solution.py:355
  26.8 0.0 collective-permute-done.6.refs_12_
  26.8 0.0 copy-start.1
  26.8 0.7 %copy-done.1 = s32[16]{0:T(128)S(1)} copy-done((s32[16]{0:T(128)S(1)}, s32[16]{0:T(128)}, u32[]{:S(2)}) %copy-start.1) | copy-done | bytes 88
  27.4 0.0 copy-start.2
  27.4 1.2 %copy-done.2 = bf16[128,4096]{1,0:T(8,128)(2,1)S(1)} copy-done((bf16[128,4096]{1,0:T(8,128)(2,1)S(1)}, bf16[128,4096]{1,0:T(8,128)(2,1)}, u32[]{:S(2)}) %copy-start.2) | copy-done | bytes 1048600
  28.6 0.0 copy-start.3
  28.7 0.9 %copy-done.3 = bf16[128,512]{1,0:T(8,128)(2,1)S(1)} copy-done((bf16[128,512]{1,0:T(8,128)(2,1)S(1)}, bf16[128,512]{1,0:T(8,128)(2,1)}, u32[]{:S(2)}) %copy-start.3) | copy-done | bytes 131096
  29.6 0.0 copy-start.4
  29.6 0.7 %copy-done.4 = s32[4,4]{1,0:T(4,128)S(1)} copy-done((s32[4,4]{1,0:T(4,128)S(1)}, s32[4,4]{1,0:T(4,128)}, u32[]{:S(2)}) %copy-start.4) | copy-done | bytes 88
  30.2 3.5 %weights.1 = (bf16[4,512,256]{2,1,0:T(8,128)(2,1)S(1)}, bf16[4,512,512]{2,1,0:T(8,128)(2,1)S(1)}, bf16[4,128,512]{2,1,0:T(8,128)(2,1)S(1)}, bf16[4,128,16]{2,1,0:T(8,128)(2,1)S(1)}, bf16[16,512]{1,0:T(8,128)(2,1)S(1)}) custom-call(s32[4,4]{1,0:T(4,128)S(1)} %copy-done.4, s32[2]{0:T(128)S(1)} %pad_add_fusion.refs_1_.refs_0_, s32[16]{0:T(128)S(1)} %copy-done.1, ...), custom_call_target="tpu_custom_call" | custom-call | flops 536870912 | bytes 1572864 | tf_op jit(solution)/shard_map/weights/pallas_call | solution.py:243
  33.7 0.0 collective-permute-done.8.refs_5_.refs_7_
  33.8 0.0 collective-permute-done.9.refs_6_.refs_8_
  33.8 0.0 collective-permute-done.10.refs_7_.refs_9_
  33.8 0.0 copy-done
  33.8 1.8 %decode_values.1 = (bf16[2,4096]{1,0:T(2,128)(2,1)S(1)}, bf16[2,4096]{1,0:T(2,128)(2,1)S(1)}, bf16[2,4096]{1,0:T(2,128)(2,1)S(1)}, bf16[2,4096]{1,0:T(2,128)(2,1)S(1)}) custom-call(s32[2]{0:T(128)S(1)} %pad_add_fusion.refs_1_.refs_0_, s32[16]{0:T(128)S(1)} %copy-done.1, bf16[4,128,512]{2,1,0:T(8,128)(2,1)S(1)} %get-tuple-element.15.refs_2_, ...), custom_call_target="tpu_custom_call" | custom-call | flops 67108864 | bytes 524288 | tf_op jit(solution)/shard_map/decode_values/pallas_call | solution.py:267
  35.6 0.1 collective-permute-start.11
  35.6 1.1 %collective-permute-start.12 = (bf16[2,4096]{1,0:T(2,128)(2,1)S(1)}, bf16[2,4096]{1,0:T(2,128)(2,1)S(1)}, u32[]{:S(2)}, u32[]{:S(2)}) collective-permute-start(bf16[2,4096]{1,0:T(2,128)(2,1)S(1)} %get-tuple-element.19), channel_id=1, source_target_pairs={{0,8},{4,12},{8,0},{12,4},{1,9},{5,13},{9,1},{13,5},{2,10},{6,14},... | collective-permute-start | bytes 49160 | tf_op jit(solution)/shard_map/ppermute | solution.py:361
  36.7 1.9 %collective-permute-start.13 = (bf16[2,4096]{1,0:T(2,128)(2,1)S(1)}, bf16[2,4096]{1,0:T(2,128)(2,1)S(1)}, u32[]{:S(2)}, u32[]{:S(2)}) collective-permute-start(bf16[2,4096]{1,0:T(2,128)(2,1)S(1)} %get-tuple-element.20), channel_id=1, source_target_pairs={{0,4},{4,8},{8,12},{12,0},{1,5},{5,9},{9,13},{13,1},{2,6},{6,10},{... | collective-permute-start | bytes 49160 | tf_op jit(solution)/shard_map/ppermute | solution.py:361
  38.7 2.4 %prefill_values.1 = bf16[128,4096]{1,0:T(8,128)(2,1)} custom-call(s32[2]{0:T(128)S(1)} %pad_add_fusion.refs_1_.refs_0_, bf16[4,512,256]{2,1,0:T(8,128)(2,1)S(1)} %get-tuple-element.13.refs_1_, bf16[4,512,512]{2,1,0:T(8,128)(2,1)S(1)} %get-tuple-element.14.refs_2_, bf16[128,512]{1,0:T(8,128)(2,1)S(1)} %copy-done, ...), custom_call_target="tpu_custom_call" | custom-call | flops 536870912 | bytes 2621440 | tf_op jit(solution)/shard_map/prefill_values/pallas_call | solution.py:287
  41.1 0.0 collective-permute-done.11
  41.1 0.0 collective-permute-done.12
  41.1 0.0 collective-permute-done.13
  41.1 0.8 %broadcast_select_fusion.2 = bf16[4,2,4096]{2,1,0:T(2,128)(2,1)} fusion(pred[4]{0:T(512)(128)(4,1)S(1)} %get-tuple-element.26, pred[4]{0:T(512)(128)(4,1)S(1)} %get-tuple-element.25, pred[4]{0:T(512)(128)(4,1)S(1)} %get-tuple-element.24, pred[4]{0:T(512)(128)(4,1)S(1)} %get-tuple-element.22, bf16[2,4096]{1,0:T(2,128)(2,1)S(1)} %get-tuple-element.21, ...), kind=kLoop, calls=%fused_computation.2 | loop fusion | flops 131072 | bytes 131088 | tf_op jit(solution)/shard_map/jit(_where)/select_n | solution.py:372
  (5 shorter events, 0.1 us)
Async XLA Ops:
  0.6 8.9 %collective-permute-start = (bf16[128,512]{1,0:T(8,128)(2,1)}, bf16[128,512]{1,0:T(8,128)(2,1)S(1)}, u32[]{:S(2)}, u32[]{:S(2)}) collective-permute-start(bf16[128,512]{1,0:T(8,128)(2,1)} %refs_8_.1), channel_id=1, source_target_pairs={{0,2},{1,3},{2,0},{3,1},{4,6},{5,7},{6,4},{7,5},{8,10},{9,11},{10,... | collective-permute-start | bytes 393224 | tf_op jit(solution)/shard_map/ppermute | solution.py:315
  0.8 14.9 %collective-permute-start.4 = (bf16[128,512]{1,0:T(8,128)(2,1)}, bf16[128,512]{1,0:T(8,128)(2,1)S(1)}, u32[]{:S(2)}, u32[]{:S(2)}) collective-permute-start(bf16[128,512]{1,0:T(8,128)(2,1)} %refs_8_.1), channel_id=1, source_target_pairs={{0,1},{1,2},{2,3},{4,5},{5,6},{6,7},{8,9},{9,10},{10,11},{12,13},{... | collective-permute-start | bytes 393224 | tf_op jit(solution)/shard_map/ppermute | solution.py:315
  4.0 13.1 %collective-permute-start.5 = (bf16[128,512]{1,0:T(8,128)(2,1)}, bf16[128,512]{1,0:T(8,128)(2,1)S(1)}, u32[]{:S(2)}, u32[]{:S(2)}) collective-permute-start(bf16[128,512]{1,0:T(8,128)(2,1)} %refs_8_.1), channel_id=1, source_target_pairs={{1,0},{2,1},{3,2},{5,4},{6,5},{7,6},{9,8},{10,9},{11,10},{13,12},{... | collective-permute-start | bytes 393224 | tf_op jit(solution)/shard_map/ppermute | solution.py:315
  7.0 11.9 %collective-permute-start.7 = (bf16[128,512]{1,0:T(8,128)(2,1)}, bf16[128,512]{1,0:T(8,128)(2,1)S(1)}, u32[]{:S(2)}, u32[]{:S(2)}) collective-permute-start(bf16[128,512]{1,0:T(8,128)(2,1)} %refs_5_.1), channel_id=1, source_target_pairs={{0,2},{1,3},{2,0},{3,1},{4,6},{5,7},{6,4},{7,5},{8,10},{9,11},{10,... | collective-permute-start | bytes 393224 | tf_op jit(solution)/shard_map/ppermute | solution.py:315
  8.6 25.2 %copy-start = (bf16[128,512]{1,0:T(8,128)(2,1)S(1)}, bf16[128,512]{1,0:T(8,128)(2,1)}, u32[]{:S(2)}) copy-start(bf16[128,512]{1,0:T(8,128)(2,1)} %refs_5_.1) | copy-start | bytes 393220
  9.5 12.8 %collective-permute-start.1 = (bf16[8,5120]{1,0:T(8,128)(2,1)S(1)}, bf16[8,5120]{1,0:T(8,128)(2,1)S(1)}, u32[]{:S(2)}, u32[]{:S(2)}) collective-permute-start(bf16[8,5120]{1,0:T(8,128)(2,1)S(1)} %reshape.77.refs_4_), channel_id=1, source_target_pairs={{0,4},{4,8},{8,12},{12,0},{1,5},{5,9},{9,13},{13,1},{2,6},{6,10},{... | collective-permute-start | bytes 245768 | tf_op jit(solution)/shard_map/ppermute | solution.py:355
  12.2 11.4 %collective-permute-start.2 = (bf16[8,5120]{1,0:T(8,128)(2,1)S(1)}, bf16[8,5120]{1,0:T(8,128)(2,1)S(1)}, u32[]{:S(2)}, u32[]{:S(2)}) collective-permute-start(bf16[8,5120]{1,0:T(8,128)(2,1)S(1)} %reshape.77.refs_4_), channel_id=1, source_target_pairs={{0,8},{4,12},{8,0},{12,4},{1,9},{5,13},{9,1},{13,5},{2,10},{6,14},... | collective-permute-start | bytes 245768 | tf_op jit(solution)/shard_map/ppermute | solution.py:355
  15.7 11.1 %collective-permute-start.6 = (bf16[128,512]{1,0:T(8,128)(2,1)S(1)}, bf16[128,512]{1,0:T(8,128)(2,1)S(1)}, u32[]{:S(2)}, u32[]{:S(2)}) collective-permute-start(bf16[128,512]{1,0:T(8,128)(2,1)S(1)} %collective-permute-done.refs_9_), channel_id=1, source_target_pairs={{2,3},{1,0},{6,7},{5,4},{10,11},{9,8},{14,15},{13,12},{18,19},{17,... | collective-permute-start | bytes 393224 | tf_op jit(solution)/shard_map/ppermute | solution.py:315
  17.0 16.7 %collective-permute-start.8 = (bf16[128,512]{1,0:T(8,128)(2,1)}, bf16[128,512]{1,0:T(8,128)(2,1)S(1)}, u32[]{:S(2)}, u32[]{:S(2)}) collective-permute-start(bf16[128,512]{1,0:T(8,128)(2,1)} %refs_5_.1), channel_id=1, source_target_pairs={{0,1},{1,2},{2,3},{4,5},{5,6},{6,7},{8,9},{9,10},{10,11},{12,13},{... | collective-permute-start | bytes 393224 | tf_op jit(solution)/shard_map/ppermute | solution.py:315
  19.0 14.8 %collective-permute-start.9 = (bf16[128,512]{1,0:T(8,128)(2,1)}, bf16[128,512]{1,0:T(8,128)(2,1)S(1)}, u32[]{:S(2)}, u32[]{:S(2)}) collective-permute-start(bf16[128,512]{1,0:T(8,128)(2,1)} %refs_5_.1), channel_id=1, source_target_pairs={{1,0},{2,1},{3,2},{5,4},{6,5},{7,6},{9,8},{10,9},{11,10},{13,12},{... | collective-permute-start | bytes 393224 | tf_op jit(solution)/shard_map/ppermute | solution.py:315
  22.3 4.4 %collective-permute-start.3 = (bf16[8,5120]{1,0:T(8,128)(2,1)S(1)}, bf16[8,5120]{1,0:T(8,128)(2,1)S(1)}, u32[]{:S(2)}, u32[]{:S(2)}) collective-permute-start(bf16[8,5120]{1,0:T(8,128)(2,1)S(1)} %reshape.77.refs_4_), channel_id=1, source_target_pairs={{0,12},{4,0},{8,4},{12,8},{1,13},{5,1},{9,5},{13,9},{2,14},{6,2},{... | collective-permute-start | bytes 245768 | tf_op jit(solution)/shard_map/ppermute | solution.py:355
  23.5 10.2 %collective-permute-start.10 = (bf16[128,512]{1,0:T(8,128)(2,1)S(1)}, bf16[128,512]{1,0:T(8,128)(2,1)S(1)}, u32[]{:S(2)}, u32[]{:S(2)}) collective-permute-start(bf16[128,512]{1,0:T(8,128)(2,1)S(1)} %collective-permute-done.7.refs_4_.refs_6_), channel_id=1, source_target_pairs={{2,3},{1,0},{6,7},{5,4},{10,11},{9,8},{14,15},{13,12},{18,19},{17,... | collective-permute-start | bytes 393224 | tf_op jit(solution)/shard_map/ppermute | solution.py:315
  26.8 0.7 %copy-start.1 = (s32[16]{0:T(128)S(1)}, s32[16]{0:T(128)}, u32[]{:S(2)}) copy-start(s32[16]{0:T(128)} %refs_1_.1) | copy-start | bytes 196
  27.4 1.2 %copy-start.2 = (bf16[128,4096]{1,0:T(8,128)(2,1)S(1)}, bf16[128,4096]{1,0:T(8,128)(2,1)}, u32[]{:S(2)}) copy-start(bf16[128,4096]{1,0:T(8,128)(2,1)} %refs_3_.2) | copy-start | bytes 3145732
  28.6 0.9 %copy-start.3 = (bf16[128,512]{1,0:T(8,128)(2,1)S(1)}, bf16[128,512]{1,0:T(8,128)(2,1)}, u32[]{:S(2)}) copy-start(bf16[128,512]{1,0:T(8,128)(2,1)} %refs_8_.1) | copy-start | bytes 393220
  29.6 0.7 %copy-start.4 = (s32[4,4]{1,0:T(4,128)S(1)}, s32[4,4]{1,0:T(4,128)}, u32[]{:S(2)}) copy-start(s32[4,4]{1,0:T(4,128)} %refs_0_.1) | copy-start | bytes 196
  35.6 5.5 %collective-permute-start.11 = (bf16[2,4096]{1,0:T(2,128)(2,1)S(1)}, bf16[2,4096]{1,0:T(2,128)(2,1)S(1)}, u32[]{:S(2)}, u32[]{:S(2)}) collective-permute-start(bf16[2,4096]{1,0:T(2,128)(2,1)S(1)} %get-tuple-element.18), channel_id=1, source_target_pairs={{0,12},{4,0},{8,4},{12,8},{1,13},{5,1},{9,5},{13,9},{2,14},{6,2},{... | collective-permute-start | bytes 49160 | tf_op jit(solution)/shard_map/ppermute | solution.py:361
  35.6 5.5 %collective-permute-start.12 = (bf16[2,4096]{1,0:T(2,128)(2,1)S(1)}, bf16[2,4096]{1,0:T(2,128)(2,1)S(1)}, u32[]{:S(2)}, u32[]{:S(2)}) collective-permute-start(bf16[2,4096]{1,0:T(2,128)(2,1)S(1)} %get-tuple-element.19), channel_id=1, source_target_pairs={{0,8},{4,12},{8,0},{12,4},{1,9},{5,13},{9,1},{13,5},{2,10},{6,14},... | collective-permute-start | bytes 49160 | tf_op jit(solution)/shard_map/ppermute | solution.py:361
  36.7 4.4 %collective-permute-start.13 = (bf16[2,4096]{1,0:T(2,128)(2,1)S(1)}, bf16[2,4096]{1,0:T(2,128)(2,1)S(1)}, u32[]{:S(2)}, u32[]{:S(2)}) collective-permute-start(bf16[2,4096]{1,0:T(2,128)(2,1)S(1)} %get-tuple-element.20), channel_id=1, source_target_pairs={{0,4},{4,8},{8,12},{12,0},{1,5},{5,9},{9,13},{13,1},{2,6},{6,10},{... | collective-permute-start | bytes 49160 | tf_op jit(solution)/shard_map/ppermute | solution.py:361

commit v3 on v2

v3 whole, which is shorter than its diff:
```python
import math

import jax
import jax.numpy as jnp
import numpy as np
from jax import lax
from jax.experimental import pallas as pl
from jax.experimental.pallas import tpu as pltpu
from jax.sharding import PartitionSpec as P

QUERY_HEADS = 32
KEY_VALUE_HEADS = 4
HEAD_SIZE = 128
PAGE = 16
GROUP_REQUESTS = 4
DECODE_STEPS = 2
HEADS_PER_KV = QUERY_HEADS // KEY_VALUE_HEADS
KV_WIDTH = KEY_VALUE_HEADS * HEAD_SIZE
Q_WIDTH = QUERY_HEADS * HEAD_SIZE
Q_BLOCK = HEADS_PER_KV * HEAD_SIZE
DECODE_ROWS = GROUP_REQUESTS * DECODE_STEPS
PADDED_ROWS = 16
STACKED = HEADS_PER_KV * PADDED_ROWS
MIB = 1024 * 1024

MASKED = -1e30
EXPONENT = math.log2(math.e) / math.sqrt(HEAD_SIZE)

VMEM = pl.BlockSpec(memory_space=pltpu.VMEM)
SMEM = pl.BlockSpec(memory_space=pltpu.SMEM)


class Exchange:
    def __init__(self, size):
        self.size = size
        self.steps = []
        got = [[] for _ in range(size)]
        last = [0, 0]
        for d in range(1, size):
            made = [None, None]
            for odd in (0, 1):
                pairs = []
                for i in range(odd, size - 1, 2):
                    if i >= d - 1:
                        pairs.append((i, i + 1))
                    if i + 1 <= size - d:
                        pairs.append((i + 1, i))
                if pairs:
                    self.steps.append((last[1 - odd], pairs))
                    made[odd] = len(self.steps)
                    for src, dst in pairs:
                        got[dst].append((made[odd], dst - d if src < dst else dst + d))
            last = made
        self.choice = np.array([[b for b, _ in g] for g in got], np.int32)
        self.source = np.array([[s for _, s in g] for g in got], np.int32)
        self.candidates = [sorted(set(self.choice[:, j])) for j in range(size - 1)]

    def run(self, own, axis, meanwhile):
        arrays = [own]
        extra = None
        for operand, pairs in self.steps:
            if len(arrays) == len(self.steps):
                arrays, extra = lax.optimization_barrier((arrays, extra))
            arrays.append(lax.ppermute(arrays[operand], axis, pairs))
            if len(arrays) == 2:
                arrays[1], extra = meanwhile(arrays[1])
        return arrays, extra

    def table(self):
        return np.concatenate([self.choice, self.source], axis=1)


def scores_of(queries, keys):
    return lax.dot_general(
        queries, keys, (((1,), (1,)), ((), ())), preferred_element_type=jnp.float32
    )


def product(left, right):
    return jnp.dot(left, right, preferred_element_type=jnp.float32)


def iota(shape, axis):
    return lax.broadcasted_iota(jnp.int32, shape, axis)


def span(start, size):
    if isinstance(start, int):
        return slice(start, start + size)
    return pl.ds(pl.multiple_of(start, size), size)


def with_ones(values):
    return jnp.concatenate([values, jnp.ones_like(values)], axis=1)


def page_position(offset, member, width):
    return (offset // PAGE * width + member) * PAGE + offset % PAGE


def key_positions(rows, sources, width):
    column = iota((1, len(sources) * rows), 1)
    part = column // rows
    source = jnp.zeros_like(column) + sources[0]
    for b in range(1, len(sources)):
        source = jnp.where(part == b, sources[b], source)
    return page_position(column - part * rows, source, width)


class Facts:
    def __init__(self, ref, width):
        self.width = width
        self.group, self.member = ref[0], ref[1]
        self.slots = [ref[2 + r] for r in range(GROUP_REQUESTS)]
        first = 2 + GROUP_REQUESTS
        self.ends = []
        total = jnp.int32(0)
        for r in range(GROUP_REQUESTS):
            total = total + ref[first + r] * PAGE
            self.ends.append(total)
        first += GROUP_REQUESTS
        self.choice = [ref[first + j] for j in range(width - 1)]
        self.source = [ref[first + width - 1 + j] for j in range(width - 1)]


def facts_row(plan, lengths, slots):
    group, member = lax.axis_index("pd"), lax.axis_index("tp")
    return jnp.concatenate(
        [
            jnp.stack([group, member]).astype(jnp.int32),
            lax.dynamic_slice_in_dim(slots, group * GROUP_REQUESTS, GROUP_REQUESTS, 0),
            lax.dynamic_index_in_dim(lengths, group, 0, keepdims=False),
            lax.dynamic_index_in_dim(jnp.asarray(plan.table()), member, 0, keepdims=False),
        ]
    )


def causal_bias(start, rows, keys, sources, ends, member, width):
    qpos = page_position(start + iota((rows, 1), 0), member, width)
    low = jnp.zeros_like(qpos)
    for end in ends:
        low = jnp.where(qpos >= end, end, low)
    kpos = key_positions(keys, sources, width)
    return jnp.where((kpos >= low) & (kpos <= qpos), 0.0, MASKED)


def request_mask(ends, keys, sources, width):
    request = iota((STACKED, 1), 0) % PADDED_ROWS // DECODE_STEPS
    low = jnp.zeros_like(request)
    high = jnp.zeros_like(request) + ends[0]
    for r in range(1, GROUP_REQUESTS):
        low = jnp.where(request == r, ends[r - 1], low)
        high = jnp.where(request == r, ends[r], high)
    kpos = key_positions(keys, sources, width)
    return (kpos >= low) & (kpos < high)


def stacked_heads(ref, rows, first, count):
    return jnp.concatenate(
        [ref[rows, span(first + i * HEAD_SIZE, HEAD_SIZE)] for i in range(count)], axis=0
    )


def slot_rows(plan, slot, facts, refs, rows):
    names = plan.candidates[slot]
    part = refs[names[0]][rows, :]
    for name in names[1:]:
        part = jnp.where(facts.choice[slot] == name, refs[name][rows, :], part)
    return part


def each_kv_head(width, step):
    if width <= 8:
        for h in range(KEY_VALUE_HEADS):
            step(h)
    else:
        lax.fori_loop(0, KEY_VALUE_HEADS, lambda h, c: (step(h), c)[1], 0)


def first_kernel(plan, pd_size, facts_ref, q_ref, *refs):
    width = plan.size
    block_refs, refs = refs[:pd_size], refs[pd_size:]
    count = len(refs) - 8
    kv_refs = refs[:count]
    acc_ref, top_ref, dec_acc_ref, dec_top_ref, queries_ref, keys_ref, values_ref, fresh_ref = refs[count:]
    tokens = q_ref.shape[0]
    half = tokens // 2
    facts = Facts(facts_ref, width)
    group, member, ends = facts.group, facts.member, facts.ends
    sources = [member] + facts.source[:-1]
    for out, rows in ((keys_ref, slice(0, tokens)), (values_ref, slice(tokens, 2 * tokens))):
        out[:tokens, :] = kv_refs[0][rows, :]
        for j in range(width - 2):
            out[(j + 1) * tokens : (j + 2) * tokens, :] = slot_rows(plan, j, facts, kv_refs, rows)

    row = iota((PADDED_ROWS, DECODE_ROWS), 0)
    column = iota((PADDED_ROWS, DECODE_ROWS), 1)
    total = None
    for k in range(pd_size):
        pick = column < 0
        for r in range(GROUP_REQUESTS):
            slot = facts.slots[r]
            back = group - slot // GROUP_REQUESTS
            back = jnp.where(back < 0, back + pd_size, back)
            first = jnp.where(back == k, slot % GROUP_REQUESTS * DECODE_STEPS, -DECODE_ROWS * 4)
            pick = pick | ((row // DECODE_STEPS == r) & (column == first + row - r * DECODE_STEPS))
        part = product(pick.astype(jnp.float32).astype(jnp.bfloat16), block_refs[k][...])
        total = part if total is None else total + part
    total = total.astype(jnp.bfloat16)
    queries_ref[...] = total[:, :Q_WIDTH]
    fresh_ref[...] = total[:, Q_WIDTH:]

    row = iota((STACKED, PADDED_ROWS), 0) % PADDED_ROWS
    column = iota((STACKED, PADDED_ROWS), 1)
    fresh_mask = (column // DECODE_STEPS == row // DECODE_STEPS) & (
        column % DECODE_STEPS <= row % DECODE_STEPS
    )
    mask = request_mask(ends, tokens, sources, width)
    spans = ((0, half), (half, tokens))
    biases = [causal_bias(s, half, keys, sources, ends, member, width) for s, keys in spans]
    together = max(1, min(HEADS_PER_KV, HEADS_PER_KV * 4 // width))

    def step(h):
        columns = span(h * HEAD_SIZE, HEAD_SIZE)
        first = h * Q_BLOCK
        queries = stacked_heads(queries_ref, slice(None), first, HEADS_PER_KV)
        fresh_scores = jnp.where(fresh_mask, scores_of(queries, fresh_ref[:, columns]), MASKED)
        scores = jnp.where(mask, scores_of(queries, keys_ref[:, columns]), MASKED)
        top = jnp.maximum(
            jnp.max(scores, axis=1, keepdims=True), jnp.max(fresh_scores, axis=1, keepdims=True)
        )
        weights = jnp.exp2((scores - top) * EXPONENT).astype(jnp.bfloat16)
        fresh_weights = jnp.exp2((fresh_scores - top) * EXPONENT).astype(jnp.bfloat16)
        fresh_values = fresh_ref[:, span(KV_WIDTH + h * HEAD_SIZE, HEAD_SIZE)]
        dec_acc_ref[h] = product(weights, with_ones(values_ref[:, columns])) + product(
            fresh_weights, with_ones(fresh_values)
        )
        dec_top_ref[h] = top
        for (start, keys), bias in zip(spans, biases):
            parts = [slice(b * tokens, b * tokens + keys) for b in range(width - 1)]
            k_all = jnp.concatenate([keys_ref[p, columns] for p in parts], axis=0)
            v_all = with_ones(jnp.concatenate([values_ref[p, columns] for p in parts], axis=0))
            for g in range(0, HEADS_PER_KV, together):
                queries = stacked_heads(
                    q_ref, slice(start, start + half), first + g * HEAD_SIZE, together
                )
                scores = scores_of(queries, k_all).reshape(together, half, bias.shape[1]) + bias[None]
                top = jnp.max(scores, axis=2, keepdims=True)
                weights = jnp.exp2((scores - top) * EXPONENT).astype(jnp.bfloat16)
                rows = slice(
                    start * HEADS_PER_KV + g * half, start * HEADS_PER_KV + (g + together) * half
                )
                acc_ref[h, rows, :] = product(weights.reshape(together * half, bias.shape[1]), v_all)
                top_ref[h, rows, :] = top.reshape(together * half, 1)

    each_kv_head(width, step)


def merge(acc, old_top, scores, values):
    top = jnp.maximum(old_top, jnp.max(scores, axis=1, keepdims=True))
    weights = jnp.exp2((scores - top) * EXPONENT).astype(jnp.bfloat16)
    acc = acc * jnp.exp2((old_top - top) * EXPONENT) + product(weights, with_ones(values))
    return (acc[:, :HEAD_SIZE] / acc[:, HEAD_SIZE:]).astype(jnp.bfloat16)


def decode_kernel(plan, pd_size, facts_ref, *refs):
    width = plan.size
    acc_ref, top_ref, queries_ref = refs[:3]
    kv_refs, out_refs = refs[3:-pd_size], refs[-pd_size:]
    tokens = kv_refs[-1].shape[0] // 2
    facts = Facts(facts_ref, width)
    group = facts.group
    refs = dict(zip(plan.candidates[-1], kv_refs))
    slot = width - 2
    keys = slot_rows(plan, slot, facts, refs, slice(0, tokens))
    values = slot_rows(plan, slot, facts, refs, slice(tokens, 2 * tokens))
    mask = request_mask(facts.ends, tokens, facts.source[-1:], width)
    row = iota((8, PADDED_ROWS), 0)
    column = iota((8, PADDED_ROWS), 1)
    picks = []
    for k in range(pd_size):
        target = group + k
        target = jnp.where(target >= pd_size, target - pd_size, target)
        pick = column < 0
        for r in range(GROUP_REQUESTS):
            mine = facts.slots[r] // GROUP_REQUESTS == target
            first = jnp.where(mine, r * DECODE_STEPS, -PADDED_ROWS * 4)
            pick = pick | ((row < DECODE_STEPS) & (column == first + row))
        picks.append(pick.astype(jnp.float32).astype(jnp.bfloat16))
    for h in range(KEY_VALUE_HEADS):
        columns = slice(h * HEAD_SIZE, (h + 1) * HEAD_SIZE)
        queries = stacked_heads(queries_ref, slice(None), h * Q_BLOCK, HEADS_PER_KV)
        scores = jnp.where(mask, scores_of(queries, keys[:, columns]), MASKED)
        out = merge(acc_ref[h], top_ref[h], scores, values[:, columns])
        out = jnp.concatenate(
            [out[g * PADDED_ROWS : (g + 1) * PADDED_ROWS] for g in range(HEADS_PER_KV)], axis=1
        )
        for k in range(pd_size):
            sent = product(picks[k], out).astype(jnp.bfloat16)
            out_refs[k][:, h * Q_BLOCK : (h + 1) * Q_BLOCK] = sent[:DECODE_STEPS]


def prefill_kernel(plan, facts_ref, q_ref, acc_ref, top_ref, *refs):
    width = plan.size
    kv_refs, (out_ref, done_ref, sem) = refs[:-3], refs[-3:]
    tokens = q_ref.shape[0]
    half = tokens // 2
    facts = Facts(facts_ref, width)
    refs = dict(zip(plan.candidates[-1], kv_refs))
    slot = width - 2
    keys = slot_rows(plan, slot, facts, refs, slice(0, tokens))
    values = slot_rows(plan, slot, facts, refs, slice(tokens, 2 * tokens))
    biases = [
        causal_bias(s, half, tokens, facts.source[-1:], facts.ends, facts.member, width)
        for s in (0, half)
    ]
    copies = []
    for h in range(KEY_VALUE_HEADS):
        columns = slice(h * HEAD_SIZE, (h + 1) * HEAD_SIZE)
        for start, bias in zip((0, half), biases):
            queries = stacked_heads(q_ref, slice(start, start + half), h * Q_BLOCK, HEADS_PER_KV)
            scores = scores_of(queries, keys[:, columns]).reshape(HEADS_PER_KV, half, tokens)
            scores = (scores + bias[None]).reshape(HEADS_PER_KV * half, tokens)
            rows = slice(start * HEADS_PER_KV, (start + half) * HEADS_PER_KV)
            out = merge(acc_ref[h, rows, :], top_ref[h, rows, :], scores, values[:, columns])
            for g in range(HEADS_PER_KV):
                done_ref[
                    start : start + half, h * Q_BLOCK + g * HEAD_SIZE : h * Q_BLOCK + (g + 1) * HEAD_SIZE
                ] = out[g * half : (g + 1) * half]
        part = pl.ds(h * Q_BLOCK, Q_BLOCK)
        copy = pltpu.make_async_copy(done_ref.at[:, part], out_ref.at[:, part], sem.at[h])
        copy.start()
        copies.append(copy)
    for copy in copies:
        copy.wait()


def load(array):
    def kernel(in_ref, out_ref, sem):
        copy = pltpu.make_async_copy(in_ref, out_ref, sem)
        copy.start()
        copy.wait()

    return pl.pallas_call(
        kernel,
        in_specs=[pl.BlockSpec(memory_space=pl.ANY)],
        out_specs=VMEM,
        out_shape=jax.ShapeDtypeStruct(array.shape, array.dtype),
        scratch_shapes=[pltpu.SemaphoreType.DMA],
        cost_estimate=pl.CostEstimate(flops=0, bytes_accessed=4 * array.size, transcendentals=0),
        name="load_queries",
    )(array)


def cost(rows, keys, exps):
    return pl.CostEstimate(
        flops=4 * rows * keys * Q_WIDTH, bytes_accessed=4 * rows * Q_WIDTH, transcendentals=exps
    )


def call_first(plan, facts, query, blocks, arrays):
    tokens, width = query.shape[0], plan.size
    every = (width - 1) * tokens
    rows = HEADS_PER_KV * tokens
    f32 = jnp.float32
    shapes = [
        jax.ShapeDtypeStruct((KEY_VALUE_HEADS, rows, 2 * HEAD_SIZE), f32),
        jax.ShapeDtypeStruct((KEY_VALUE_HEADS, rows, 1), f32),
        jax.ShapeDtypeStruct((KEY_VALUE_HEADS, STACKED, 2 * HEAD_SIZE), f32),
        jax.ShapeDtypeStruct((KEY_VALUE_HEADS, STACKED, 1), f32),
        jax.ShapeDtypeStruct((PADDED_ROWS, Q_WIDTH), jnp.bfloat16),
    ]
    needed = arrays[: 1 + max(max(c) for c in plan.candidates[:-1])]
    return pl.pallas_call(
        lambda *refs: first_kernel(plan, len(blocks), *refs),
        in_specs=[SMEM] + [VMEM] * (1 + len(blocks) + len(needed)),
        out_specs=[VMEM] * len(shapes),
        out_shape=shapes,
        scratch_shapes=[
            pltpu.VMEM((every, KV_WIDTH), jnp.bfloat16),
            pltpu.VMEM((every, KV_WIDTH), jnp.bfloat16),
            pltpu.VMEM((PADDED_ROWS, 2 * KV_WIDTH), jnp.bfloat16),
        ],
        compiler_params=pltpu.CompilerParams(vmem_limit_bytes=(28 + width) * MIB),
        cost_estimate=cost(tokens, every, tokens * every * QUERY_HEADS),
        name="first_shards",
    )(facts, query, *blocks, *needed)


def call_decode(plan, pd_size, facts, state, arrays):
    last = [arrays[b] for b in plan.candidates[-1]]
    tokens = last[0].shape[0] // 2
    return pl.pallas_call(
        lambda *refs: decode_kernel(plan, pd_size, *refs),
        in_specs=[SMEM] + [VMEM] * (3 + len(last)),
        out_specs=[VMEM] * pd_size,
        out_shape=[jax.ShapeDtypeStruct((DECODE_STEPS, Q_WIDTH), jnp.bfloat16)] * pd_size,
        compiler_params=pltpu.CompilerParams(vmem_limit_bytes=32 * MIB),
        cost_estimate=cost(PADDED_ROWS, tokens, PADDED_ROWS * tokens * QUERY_HEADS),
        name="last_shard_decode",
    )(facts, *state[2:], *last)


def call_prefill(plan, facts, query, state, arrays):
    last = [arrays[b] for b in plan.candidates[-1]]
    tokens = query.shape[0]
    return pl.pallas_call(
        lambda *refs: prefill_kernel(plan, *refs),
        in_specs=[SMEM] + [VMEM] * (3 + len(last)),
        out_specs=pl.BlockSpec(memory_space=pl.ANY),
        out_shape=jax.ShapeDtypeStruct((tokens, Q_WIDTH), jnp.bfloat16),
        scratch_shapes=[
            pltpu.VMEM((tokens, Q_WIDTH), jnp.bfloat16),
            pltpu.SemaphoreType.DMA((KEY_VALUE_HEADS,)),
        ],
        compiler_params=pltpu.CompilerParams(vmem_limit_bytes=32 * MIB),
        cost_estimate=cost(tokens, tokens, tokens * tokens * QUERY_HEADS),
        name="last_shard_prefill",
    )(facts, query, *state[:2], *last)


def ring(size, step):
    return [(i, (i + step) % size) for i in range(size)]


def body(
    prompt_query,
    prompt_key,
    prompt_value,
    prompt_lengths,
    decode_slot,
    decoded_query,
    decoded_key,
    decoded_value,
):
    plan = Exchange(lax.axis_size("tp"))
    pd_size = lax.axis_size("pd")
    my_group = lax.axis_index("pd")
    kv = jnp.concatenate([prompt_key, prompt_value], axis=0)
    def gather(buffer):
        buffer, rows, query, facts = lax.optimization_barrier(
            (buffer, own, load(prompt_query), facts_row(plan, prompt_lengths, decode_slot))
        )
        blocks = [rows] + [lax.ppermute(rows, "pd", ring(pd_size, k)) for k in range(1, pd_size)]
        return buffer, (facts, query, blocks)

    kv, decoded_query = lax.optimization_barrier((kv, decoded_query))
    own = jnp.concatenate([decoded_query, decoded_key, decoded_value], axis=2).reshape(
        DECODE_ROWS, Q_WIDTH + 2 * KV_WIDTH
    )
    arrays, (facts, query, blocks) = plan.run(kv, "tp", gather)

    state = call_first(plan, facts, query, blocks, arrays)
    outgoing = call_decode(plan, pd_size, facts, state, arrays)
    arrived = [outgoing[0]]
    for k in range(1, pd_size):
        arrived.append(lax.ppermute(outgoing[k], "pd", ring(pd_size, k)))
    pre_out = call_prefill(plan, facts, query, state, arrays)

    numbers = jnp.arange(decode_slot.shape[0], dtype=jnp.int32)
    wanted = my_group * GROUP_REQUESTS + jnp.arange(GROUP_REQUESTS, dtype=jnp.int32)
    owner = jnp.sum(
        jnp.where(decode_slot[None, :] == wanted[:, None], numbers[None, :] // GROUP_REQUESTS, 0), axis=1
    )
    from_block = (my_group - owner) % pd_size
    dec_out = jnp.zeros((GROUP_REQUESTS, DECODE_STEPS, Q_WIDTH), jnp.bfloat16)
    for k in range(pd_size):
        dec_out = jnp.where((from_block == k)[:, None, None], arrived[k][None], dec_out)
    return (pre_out, dec_out)


def solution(mesh):
    placed = (
        P(("rep", "pd", "tp"), None),
        P(("rep", "pd", "tp"), None),
        P(("rep", "pd", "tp"), None),
        P("rep", None),
        P("rep"),
        P(("rep", "pd"), None, None),
        P(("rep", "pd"), None, None),
        P(("rep", "pd"), None, None),
    )
    return jax.shard_map(
        body,
        mesh=mesh,
        in_specs=placed,
        out_specs=(P(("rep", "pd", "tp"), None), P(("rep", "pd"), None, None)),
        check_vma=False,
    )
```

time: 42.3 us -> 45.5 us (1.076)
  the two profiles are of different devices: /device:TPU:21 before, /device:TPU:0 now
where the time goes in v3:
time: 45.5 us; the launch traced here: 45.1 us
  Pallas kernels  14.9 us (33%)
  starting transfers between devices  13.4 us (29%)
  waiting for transfers between devices  9.61 us (21%)
  other arithmetic  3.6 us (8%)
  local copies, waits for them, and re-layouts  2.78 us (6%)
  between operations  0.81 us (2%)
    ppermute x5, waiting for transfers between devices, run(): arrays.append(lax.ppermute(arrays[operand], axis, pairs))  7.06 us
    ppermute x5, starting transfers between devices, run(): arrays.append(lax.ppermute(arrays[operand], axis, pairs))  6.99 us
    pallas_call x1, Pallas kernels, call_prefill(): pl.pallas_call(lambda *refs: prefill_kernel(plan, *refs), in_specs=[SMEM]...  5.64 us
    pallas_call x1, Pallas kernels, call_first(): pl.pallas_call(lambda *refs: first_kernel(plan, len(blocks), *refs), in_s...  4.45 us
    ppermute x3, starting transfers between devices, body(): arrived.append(lax.ppermute(outgoing[k], 'pd', ring(pd_size, k)))  3.28 us
    ppermute x3, starting transfers between devices, gather(): lax.ppermute(rows, 'pd', ring(pd_size, k))  3.16 us
    pallas_call x1, Pallas kernels, call_decode(): pl.pallas_call(lambda *refs: decode_kernel(plan, pd_size, *refs), in_spec...  2.58 us
    ppermute x3, waiting for transfers between devices, gather(): lax.ppermute(rows, 'pd', ring(pd_size, k))  2.54 us
  transfers between devices with their start and end apart: 11, of which 6 were waited for; matrix products, arithmetic and copies ran while one was open for 7% of the time, Pallas kernels for 27%

profile of v3, /device:TPU:0, one launch (start us, length us, event | category | flops | bytes accessed | tf_op | source)
XLA Modules:
  0.0 45.1 jit_solution(15104323497617872632)
XLA Ops:
  0.6 0.0 copy-start
  0.6 1.0 %pad_maximum_fusion.refs_6_ = bf16[256,512]{1,0:T(8,128)(2,1)S(1)} fusion(bf16[128,512]{1,0:T(8,128)(2,1)} %param.11, bf16[128,512]{1,0:T(8,128)(2,1)} %param.10), kind=kLoop, calls=%fused_computation | loop fusion | flops 524288 | bytes 524288 | tf_op jit(solution)/shard_map/concatenate | solution.py:439
  1.6 3.1 %collective-permute-start = (bf16[256,512]{1,0:T(8,128)(2,1)S(1)}, bf16[256,512]{1,0:T(8,128)(2,1)S(1)}, u32[]{:S(2)}, u32[]{:S(2)}) collective-permute-start(bf16[256,512]{1,0:T(8,128)(2,1)S(1)} %pad_maximum_fusion.refs_6_), channel_id=1, source_target_pairs={{0,1},{1,0},{2,3},{3,2},{4,5},{5,4},{6,7},{7,6},{8,9},{9,8},{10,11... | collective-permute-start | bytes 786440 | tf_op jit(solution)/shard_map/ppermute | solution.py:64
  4.7 0.7 %collective-permute-start.1 = (bf16[256,512]{1,0:T(8,128)(2,1)S(1)}, bf16[256,512]{1,0:T(8,128)(2,1)S(1)}, u32[]{:S(2)}, u32[]{:S(2)}) collective-permute-start(bf16[256,512]{1,0:T(8,128)(2,1)S(1)} %pad_maximum_fusion.refs_6_), channel_id=1, source_target_pairs={{1,2},{2,1},{5,6},{6,5},{9,10},{10,9},{13,14},{14,13},{17,18},{18,... | collective-permute-start | bytes 786440 | tf_op jit(solution)/shard_map/ppermute | solution.py:64
  5.4 0.0 copy-done
  5.4 0.9 %pad_maximum_fusion.1 = bf16[4,2,5120]{2,1,0:T(2,128)(2,1)S(1)} fusion(bf16[4,2,512]{2,1,0:T(2,128)(2,1)} %param.16, bf16[4,2,512]{2,1,0:T(2,128)(2,1)} %param.15, bf16[4,2,4096]{2,1,0:T(2,128)(2,1)} %param.14), kind=kLoop, calls=%fused_computation.5 | loop fusion | flops 245760 | bytes 163840 | tf_op jit(solution)/shard_map/concatenate | solution.py:448
  6.4 0.7 %dynamic-slice_bitcast_fusion = s32[6]{0:T(128)S(1)} fusion(s32[4,6]{1,0:T(4,128)} %constant.56.clone, s32[]{:T(128)S(6)} %select_n.60), kind=kLoop, calls=%fused_computation.16 | loop fusion | bytes 52 | tf_op jit(solution)/shard_map/jit(dynamic_index_in_dim)/squeeze | solution.py:133
  7.1 2.2 %load_queries.1.refs_1_ = bf16[128,4096]{1,0:T(8,128)(2,1)} custom-call(bf16[128,4096]{1,0:T(8,128)(2,1)} %in_ref.1), custom_call_target="tpu_custom_call" | custom-call | bytes 2097152 | tf_op jit(solution)/shard_map/load_queries/pallas_call | solution.py:344
  9.3 0.7 %dynamic_slice.11 = s32[4]{0:T(128)S(1)} dynamic-slice(s32[16]{0:T(128)} %param.13, s32[]{:T(128)S(6)} %select_n.58), dynamic_slice_sizes={4} | dynamic-slice | bytes 36 | tf_op jit(solution)/shard_map/dynamic_slice | solution.py:131
  10.1 0.1 concatenate.11.refs_0_
  10.2 0.9 %collective-permute-done.refs_7_ = bf16[256,512]{1,0:T(8,128)(2,1)S(1)} collective-permute-done((bf16[256,512]{1,0:T(8,128)(2,1)S(1)}, bf16[256,512]{1,0:T(8,128)(2,1)S(1)}, u32[]{:S(2)}, u32[]{:S(2)}) %collective-permute-start) | collective-permute-done | bytes 262176 | tf_op jit(solution)/shard_map/ppermute | solution.py:64
  11.0 0.7 %collective-permute-start.3 = (bf16[256,512]{1,0:T(8,128)(2,1)S(1)}, bf16[256,512]{1,0:T(8,128)(2,1)S(1)}, u32[]{:S(2)}, u32[]{:S(2)}) collective-permute-start(bf16[256,512]{1,0:T(8,128)(2,1)S(1)} %collective-permute-done.refs_7_), channel_id=1, source_target_pairs={{1,2},{2,1},{5,6},{6,5},{9,10},{10,9},{13,14},{14,13},{17,18},{18,... | collective-permute-start | bytes 786440 | tf_op jit(solution)/shard_map/ppermute | solution.py:64
  11.7 0.0 collective-permute-done.1.refs_8_
  11.7 1.3 %collective-permute-start.2 = (bf16[256,512]{1,0:T(8,128)(2,1)S(1)}, bf16[256,512]{1,0:T(8,128)(2,1)S(1)}, u32[]{:S(2)}, u32[]{:S(2)}) collective-permute-start(bf16[256,512]{1,0:T(8,128)(2,1)S(1)} %collective-permute-done.1.refs_8_), channel_id=1, source_target_pairs={{1,0},{2,3},{5,4},{6,7},{9,8},{10,11},{13,12},{14,15},{17,16},{18,... | collective-permute-start | bytes 786440 | tf_op jit(solution)/shard_map/ppermute | solution.py:64
  13.0 0.8 %select_reduce_fusion = s32[4]{0:T(128)S(1)} fusion(s32[16]{0:T(128)S(1)} %and_select_fusion.1, s32[16]{0:T(128)} %param.13, s32[4]{0:T(128)S(1)} %iota_add_fusion), kind=kLoop, calls=%fused_computation.8 | loop fusion | flops 188 | bytes 160 | tf_op jit(solution)/shard_map/reduce_sum | solution.py:462
  13.9 0.0 collective-permute-start.4
  13.9 1.7 %collective-permute-start.5 = (bf16[8,5120]{1,0:T(8,128)(2,1)S(1)}, bf16[8,5120]{1,0:T(8,128)(2,1)S(1)}, u32[]{:S(2)}, u32[]{:S(2)}) collective-permute-start(bf16[8,5120]{1,0:T(8,128)(2,1)S(1)} %reshape.77.refs_2_), channel_id=1, source_target_pairs={{0,8},{4,12},{8,0},{12,4},{1,9},{5,13},{9,1},{13,5},{2,10},{6,14},... | collective-permute-start | bytes 245768 | tf_op jit(solution)/shard_map/ppermute | solution.py:444
  15.6 1.4 %collective-permute-start.6 = (bf16[8,5120]{1,0:T(8,128)(2,1)S(1)}, bf16[8,5120]{1,0:T(8,128)(2,1)S(1)}, u32[]{:S(2)}, u32[]{:S(2)}) collective-permute-start(bf16[8,5120]{1,0:T(8,128)(2,1)S(1)} %reshape.77.refs_2_), channel_id=1, source_target_pairs={{0,12},{4,0},{8,4},{12,8},{1,13},{5,1},{9,5},{13,9},{2,14},{6,2},{... | collective-permute-start | bytes 245768 | tf_op jit(solution)/shard_map/ppermute | solution.py:444
  17.0 1.0 %collective-permute-done.4.refs_3_ = bf16[8,5120]{1,0:T(8,128)(2,1)S(1)} collective-permute-done((bf16[8,5120]{1,0:T(8,128)(2,1)S(1)}, bf16[8,5120]{1,0:T(8,128)(2,1)S(1)}, u32[]{:S(2)}, u32[]{:S(2)}) %collective-permute-start.4) | collective-permute-done | bytes 81952 | tf_op jit(solution)/shard_map/ppermute | solution.py:444
  18.0 1.0 %collective-permute-done.5.refs_4_ = bf16[8,5120]{1,0:T(8,128)(2,1)S(1)} collective-permute-done((bf16[8,5120]{1,0:T(8,128)(2,1)S(1)}, bf16[8,5120]{1,0:T(8,128)(2,1)S(1)}, u32[]{:S(2)}, u32[]{:S(2)}) %collective-permute-start.5) | collective-permute-done | bytes 81952 | tf_op jit(solution)/shard_map/ppermute | solution.py:444
  19.1 0.5 %collective-permute-done.6.refs_5_ = bf16[8,5120]{1,0:T(8,128)(2,1)S(1)} collective-permute-done((bf16[8,5120]{1,0:T(8,128)(2,1)S(1)}, bf16[8,5120]{1,0:T(8,128)(2,1)S(1)}, u32[]{:S(2)}, u32[]{:S(2)}) %collective-permute-start.6) | collective-permute-done | bytes 81952 | tf_op jit(solution)/shard_map/ppermute | solution.py:444
  19.6 0.0 collective-permute-done.3.refs_4_
  19.6 3.9 %collective-permute-done.2.refs_9_ = bf16[256,512]{1,0:T(8,128)(2,1)S(1)} collective-permute-done((bf16[256,512]{1,0:T(8,128)(2,1)S(1)}, bf16[256,512]{1,0:T(8,128)(2,1)S(1)}, u32[]{:S(2)}, u32[]{:S(2)}) %collective-permute-start.2) | collective-permute-done | bytes 262176 | tf_op jit(solution)/shard_map/ppermute | solution.py:64
  23.5 1.3 %collective-permute-start.7 = (bf16[256,512]{1,0:T(8,128)(2,1)S(1)}, bf16[256,512]{1,0:T(8,128)(2,1)S(1)}, u32[]{:S(2)}, u32[]{:S(2)}) collective-permute-start(bf16[256,512]{1,0:T(8,128)(2,1)S(1)} %collective-permute-done.3.refs_4_), channel_id=1, source_target_pairs={{1,0},{2,3},{5,4},{6,7},{9,8},{10,11},{13,12},{14,15},{17,16},{18,... | collective-permute-start | bytes 786440 | tf_op jit(solution)/shard_map/ppermute | solution.py:64
  24.8 0.0 copy-start.1
  24.8 1.2 %copy-done.1 = bf16[128,4096]{1,0:T(8,128)(2,1)S(1)} copy-done((bf16[128,4096]{1,0:T(8,128)(2,1)S(1)}, bf16[128,4096]{1,0:T(8,128)(2,1)}, u32[]{:S(2)}) %copy-start.1) | copy-done | bytes 1048600
  26.0 0.0 copy-start.2
  26.0 4.5 %first_shards.1 = (f32[4,1024,256]{2,1,0:T(8,128)S(1)}, f32[4,1024,1]{2,1,0:T(8,128)S(1)}, f32[4,128,256]{2,1,0:T(8,128)S(1)}, f32[4,128,1]{2,1,0:T(8,128)S(1)}, bf16[16,4096]{1,0:T(8,128)(2,1)S(1)}) custom-call(s32[16]{0:T(128)S(1)} %concatenate.11.refs_0_, bf16[128,4096]{1,0:T(8,128)(2,1)S(1)} %copy-done.1, bf16[8,5120]{1,0:T(8,128)(2,1)S(1)} %reshape.77.refs_2_, ...), custom_call_target="tpu_custom_call" | custom-call | flops 805306368 | bytes 2097152 | tf_op jit(solution)/shard_map/first_shards/pallas_call | solution.py:374
  30.5 2.2 %collective-permute-done.7.refs_5_ = bf16[256,512]{1,0:T(8,128)(2,1)S(1)} collective-permute-done((bf16[256,512]{1,0:T(8,128)(2,1)S(1)}, bf16[256,512]{1,0:T(8,128)(2,1)S(1)}, u32[]{:S(2)}, u32[]{:S(2)}) %collective-permute-start.7) | collective-permute-done | bytes 262176 | tf_op jit(solution)/shard_map/ppermute | solution.py:64
  32.7 2.6 %last_shard_decode.1 = (bf16[2,4096]{1,0:T(2,128)(2,1)S(1)}, bf16[2,4096]{1,0:T(2,128)(2,1)S(1)}, bf16[2,4096]{1,0:T(2,128)(2,1)S(1)}, bf16[2,4096]{1,0:T(2,128)(2,1)S(1)}) custom-call(s32[16]{0:T(128)S(1)} %concatenate.11.refs_0_, f32[4,128,256]{2,1,0:T(8,128)S(1)} %get-tuple-element.47.refs_1_, f32[4,128,1]{2,1,0:T(8,128)S(1)} %get-tuple-element.48.refs_2_, ...), custom_call_target="tpu_custom_call" | custom-call | flops 33554432 | bytes 262144 | tf_op jit(solution)/shard_map/last_shard_decode/pallas_call | solution.py:393
  35.3 0.1 collective-permute-start.10
  35.4 1.7 %collective-permute-start.8 = (bf16[2,4096]{1,0:T(2,128)(2,1)S(1)}, bf16[2,4096]{1,0:T(2,128)(2,1)S(1)}, u32[]{:S(2)}, u32[]{:S(2)}) collective-permute-start(bf16[2,4096]{1,0:T(2,128)(2,1)S(1)} %get-tuple-element.50), channel_id=1, source_target_pairs={{0,12},{4,0},{8,4},{12,8},{1,13},{5,1},{9,5},{13,9},{2,14},{6,2},{... | collective-permute-start | bytes 49160 | tf_op jit(solution)/shard_map/ppermute | solution.py:457
  37.1 1.5 %collective-permute-start.9 = (bf16[2,4096]{1,0:T(2,128)(2,1)S(1)}, bf16[2,4096]{1,0:T(2,128)(2,1)S(1)}, u32[]{:S(2)}, u32[]{:S(2)}) collective-permute-start(bf16[2,4096]{1,0:T(2,128)(2,1)S(1)} %get-tuple-element.51), channel_id=1, source_target_pairs={{0,8},{4,12},{8,0},{12,4},{1,9},{5,13},{9,1},{13,5},{2,10},{6,14},... | collective-permute-start | bytes 49160 | tf_op jit(solution)/shard_map/ppermute | solution.py:457
  38.6 0.0 copy-done.2
  38.6 5.6 %last_shard_prefill.1 = bf16[128,4096]{1,0:T(8,128)(2,1)} custom-call(s32[16]{0:T(128)S(1)} %concatenate.11.refs_0_, bf16[128,4096]{1,0:T(8,128)(2,1)S(1)} %copy-done.2, f32[4,1024,256]{2,1,0:T(8,128)S(1)} %get-tuple-element.44.refs_2_, f32[4,1024,1]{2,1,0:T(8,128)S(1)} %get-tuple-element.45.refs_3_, bf16[256,512]{1,0:T(8,128)(2,1)S(1)} %collective-permute-done.3.refs_4_, ...), custom_call_target="tpu_custom_call" | custom-call | flops 268435456 | bytes 2097152 | tf_op jit(solution)/shard_map/last_shard_prefill/pallas_call | solution.py:407
  44.3 0.0 collective-permute-done.10
  44.3 0.0 collective-permute-done.8
  44.3 0.0 collective-permute-done.9
  44.3 0.8 %broadcast_select_fusion.2 = bf16[4,2,4096]{2,1,0:T(2,128)(2,1)} fusion(pred[4]{0:T(512)(128)(4,1)S(1)} %get-tuple-element.58, pred[4]{0:T(512)(128)(4,1)S(1)} %get-tuple-element.57, pred[4]{0:T(512)(128)(4,1)S(1)} %get-tuple-element.56, pred[4]{0:T(512)(128)(4,1)S(1)} %get-tuple-element.54, bf16[2,4096]{1,0:T(2,128)(2,1)S(1)} %get-tuple-element.53, ...), kind=kLoop, calls=%fused_computation.3 | loop fusion | flops 131072 | bytes 131088 | tf_op jit(solution)/shard_map/jit(_where)/select_n | solution.py:468
  (6 shorter events, 0.1 us)
Async XLA Ops:
  0.6 4.8 %copy-start = (s32[4,4]{1,0:T(4,128)S(1)}, s32[4,4]{1,0:T(4,128)}, u32[]{:S(2)}) copy-start(s32[4,4]{1,0:T(4,128)} %param.12) | copy-start | bytes 196
  1.6 9.4 %collective-permute-start = (bf16[256,512]{1,0:T(8,128)(2,1)S(1)}, bf16[256,512]{1,0:T(8,128)(2,1)S(1)}, u32[]{:S(2)}, u32[]{:S(2)}) collective-permute-start(bf16[256,512]{1,0:T(8,128)(2,1)S(1)} %pad_maximum_fusion.refs_6_), channel_id=1, source_target_pairs={{0,1},{1,0},{2,3},{3,2},{4,5},{5,4},{6,7},{7,6},{8,9},{9,8},{10,11... | collective-permute-start | bytes 786440 | tf_op jit(solution)/shard_map/ppermute | solution.py:64
  4.7 7.0 %collective-permute-start.1 = (bf16[256,512]{1,0:T(8,128)(2,1)S(1)}, bf16[256,512]{1,0:T(8,128)(2,1)S(1)}, u32[]{:S(2)}, u32[]{:S(2)}) collective-permute-start(bf16[256,512]{1,0:T(8,128)(2,1)S(1)} %pad_maximum_fusion.refs_6_), channel_id=1, source_target_pairs={{1,2},{2,1},{5,6},{6,5},{9,10},{10,9},{13,14},{14,13},{17,18},{18,... | collective-permute-start | bytes 786440 | tf_op jit(solution)/shard_map/ppermute | solution.py:64
  11.0 8.5 %collective-permute-start.3 = (bf16[256,512]{1,0:T(8,128)(2,1)S(1)}, bf16[256,512]{1,0:T(8,128)(2,1)S(1)}, u32[]{:S(2)}, u32[]{:S(2)}) collective-permute-start(bf16[256,512]{1,0:T(8,128)(2,1)S(1)} %collective-permute-done.refs_7_), channel_id=1, source_target_pairs={{1,2},{2,1},{5,6},{6,5},{9,10},{10,9},{13,14},{14,13},{17,18},{18,... | collective-permute-start | bytes 786440 | tf_op jit(solution)/shard_map/ppermute | solution.py:64
  11.7 11.8 %collective-permute-start.2 = (bf16[256,512]{1,0:T(8,128)(2,1)S(1)}, bf16[256,512]{1,0:T(8,128)(2,1)S(1)}, u32[]{:S(2)}, u32[]{:S(2)}) collective-permute-start(bf16[256,512]{1,0:T(8,128)(2,1)S(1)} %collective-permute-done.1.refs_8_), channel_id=1, source_target_pairs={{1,0},{2,3},{5,4},{6,7},{9,8},{10,11},{13,12},{14,15},{17,16},{18,... | collective-permute-start | bytes 786440 | tf_op jit(solution)/shard_map/ppermute | solution.py:64
  13.9 4.2 %collective-permute-start.4 = (bf16[8,5120]{1,0:T(8,128)(2,1)S(1)}, bf16[8,5120]{1,0:T(8,128)(2,1)S(1)}, u32[]{:S(2)}, u32[]{:S(2)}) collective-permute-start(bf16[8,5120]{1,0:T(8,128)(2,1)S(1)} %reshape.77.refs_2_), channel_id=1, source_target_pairs={{0,4},{4,8},{8,12},{12,0},{1,5},{5,9},{9,13},{13,1},{2,6},{6,10},{... | collective-permute-start | bytes 245768 | tf_op jit(solution)/shard_map/ppermute | solution.py:444
  13.9 5.2 %collective-permute-start.5 = (bf16[8,5120]{1,0:T(8,128)(2,1)S(1)}, bf16[8,5120]{1,0:T(8,128)(2,1)S(1)}, u32[]{:S(2)}, u32[]{:S(2)}) collective-permute-start(bf16[8,5120]{1,0:T(8,128)(2,1)S(1)} %reshape.77.refs_2_), channel_id=1, source_target_pairs={{0,8},{4,12},{8,0},{12,4},{1,9},{5,13},{9,1},{13,5},{2,10},{6,14},... | collective-permute-start | bytes 245768 | tf_op jit(solution)/shard_map/ppermute | solution.py:444
  15.6 3.9 %collective-permute-start.6 = (bf16[8,5120]{1,0:T(8,128)(2,1)S(1)}, bf16[8,5120]{1,0:T(8,128)(2,1)S(1)}, u32[]{:S(2)}, u32[]{:S(2)}) collective-permute-start(bf16[8,5120]{1,0:T(8,128)(2,1)S(1)} %reshape.77.refs_2_), channel_id=1, source_target_pairs={{0,12},{4,0},{8,4},{12,8},{1,13},{5,1},{9,5},{13,9},{2,14},{6,2},{... | collective-permute-start | bytes 245768 | tf_op jit(solution)/shard_map/ppermute | solution.py:444
  23.5 9.2 %collective-permute-start.7 = (bf16[256,512]{1,0:T(8,128)(2,1)S(1)}, bf16[256,512]{1,0:T(8,128)(2,1)S(1)}, u32[]{:S(2)}, u32[]{:S(2)}) collective-permute-start(bf16[256,512]{1,0:T(8,128)(2,1)S(1)} %collective-permute-done.3.refs_4_), channel_id=1, source_target_pairs={{1,0},{2,3},{5,4},{6,7},{9,8},{10,11},{13,12},{14,15},{17,16},{18,... | collective-permute-start | bytes 786440 | tf_op jit(solution)/shard_map/ppermute | solution.py:64
  24.8 1.2 %copy-start.1 = (bf16[128,4096]{1,0:T(8,128)(2,1)S(1)}, bf16[128,4096]{1,0:T(8,128)(2,1)}, u32[]{:S(2)}) copy-start(bf16[128,4096]{1,0:T(8,128)(2,1)} %load_queries.1.refs_1_) | copy-start | bytes 3145732
  26.0 12.6 %copy-start.2 = (bf16[128,4096]{1,0:T(8,128)(2,1)S(1)}, bf16[128,4096]{1,0:T(8,128)(2,1)}, u32[]{:S(2)}) copy-start(bf16[128,4096]{1,0:T(8,128)(2,1)} %load_queries.1.refs_1_) | copy-start | bytes 3145732
  35.3 8.9 %collective-permute-start.10 = (bf16[2,4096]{1,0:T(2,128)(2,1)S(1)}, bf16[2,4096]{1,0:T(2,128)(2,1)S(1)}, u32[]{:S(2)}, u32[]{:S(2)}) collective-permute-start(bf16[2,4096]{1,0:T(2,128)(2,1)S(1)} %get-tuple-element.52), channel_id=1, source_target_pairs={{0,4},{4,8},{8,12},{12,0},{1,5},{5,9},{9,13},{13,1},{2,6},{6,10},{... | collective-permute-start | bytes 49160 | tf_op jit(solution)/shard_map/ppermute | solution.py:457
  35.4 8.9 %collective-permute-start.8 = (bf16[2,4096]{1,0:T(2,128)(2,1)S(1)}, bf16[2,4096]{1,0:T(2,128)(2,1)S(1)}, u32[]{:S(2)}, u32[]{:S(2)}) collective-permute-start(bf16[2,4096]{1,0:T(2,128)(2,1)S(1)} %get-tuple-element.50), channel_id=1, source_target_pairs={{0,12},{4,0},{8,4},{12,8},{1,13},{5,1},{9,5},{13,9},{2,14},{6,2},{... | collective-permute-start | bytes 49160 | tf_op jit(solution)/shard_map/ppermute | solution.py:457
  37.1 7.2 %collective-permute-start.9 = (bf16[2,4096]{1,0:T(2,128)(2,1)S(1)}, bf16[2,4096]{1,0:T(2,128)(2,1)S(1)}, u32[]{:S(2)}, u32[]{:S(2)}) collective-permute-start(bf16[2,4096]{1,0:T(2,128)(2,1)S(1)} %get-tuple-element.51), channel_id=1, source_target_pairs={{0,8},{4,12},{8,0},{12,4},{1,9},{5,13},{9,1},{13,5},{2,10},{6,14},... | collective-permute-start | bytes 49160 | tf_op jit(solution)/shard_map/ppermute | solution.py:457

commit v4 on v3

v4 whole, which is shorter than its diff:
```python
import math

import jax
import jax.numpy as jnp
import numpy as np
from jax import lax
from jax.experimental import pallas as pl
from jax.experimental.pallas import tpu as pltpu
from jax.sharding import PartitionSpec as P

QUERY_HEADS = 32
KEY_VALUE_HEADS = 4
HEAD_SIZE = 128
PAGE = 16
GROUP_REQUESTS = 4
DECODE_STEPS = 2
HEADS_PER_KV = QUERY_HEADS // KEY_VALUE_HEADS
KV_WIDTH = KEY_VALUE_HEADS * HEAD_SIZE
Q_WIDTH = QUERY_HEADS * HEAD_SIZE
Q_BLOCK = HEADS_PER_KV * HEAD_SIZE
DECODE_ROWS = GROUP_REQUESTS * DECODE_STEPS
PADDED_ROWS = 16
STACKED = HEADS_PER_KV * PADDED_ROWS
MIB = 1024 * 1024

MASKED = -1e30
LIMIT = 60.0
EXPONENT = math.log2(math.e) / math.sqrt(HEAD_SIZE)

VMEM = pl.BlockSpec(memory_space=pltpu.VMEM)
SMEM = pl.BlockSpec(memory_space=pltpu.SMEM)
ANY = pl.BlockSpec(memory_space=pl.ANY)


class Ring:
    def __init__(self, size):
        self.size = size
        order = [0] + list(range(1, size, 2)) + [i for i in range(size - 1, 0, -1) if i % 2 == 0]
        self.pairs = [(order[i], order[(i + 1) % size]) for i in range(size)]
        place = {m: i for i, m in enumerate(order)}
        self.source = np.array(
            [[order[(place[m] - s) % size] for s in range(size)] for m in range(size)], np.int32
        )

    def step(self, array):
        return lax.ppermute(array, "tp", self.pairs)


def scores_of(queries, keys):
    return lax.dot_general(
        queries, keys, (((1,), (1,)), ((), ())), preferred_element_type=jnp.float32
    )


def product(left, right):
    return jnp.dot(left, right, preferred_element_type=jnp.float32)


def iota(shape, axis):
    return lax.broadcasted_iota(jnp.int32, shape, axis)


def span(start, size):
    if isinstance(start, int):
        return slice(start, start + size)
    return pl.ds(pl.multiple_of(start, size), size)


def with_ones(values):
    return jnp.concatenate([values, jnp.ones_like(values)], axis=1)


def page_position(offset, member, width):
    return (offset // PAGE * width + member) * PAGE + offset % PAGE


def key_positions(rows, sources, width):
    column = iota((1, len(sources) * rows), 1)
    part = column // rows
    source = jnp.zeros_like(column) + sources[0]
    for b in range(1, len(sources)):
        source = jnp.where(part == b, sources[b], source)
    return page_position(column - part * rows, source, width)


class Facts:
    def __init__(self, ref, width):
        self.width = width
        self.group, self.member = ref[0], ref[1]
        self.slots = [ref[2 + r] for r in range(GROUP_REQUESTS)]
        first = 2 + GROUP_REQUESTS
        self.ends = []
        total = jnp.int32(0)
        for r in range(GROUP_REQUESTS):
            total = total + ref[first + r] * PAGE
            self.ends.append(total)
        first += GROUP_REQUESTS
        self.source = [ref[first + s] for s in range(width)]


def facts_row(plan, lengths, slots):
    group, member = lax.axis_index("pd"), lax.axis_index("tp")
    return jnp.concatenate(
        [
            jnp.stack([group, member]).astype(jnp.int32),
            lax.dynamic_slice_in_dim(slots, group * GROUP_REQUESTS, GROUP_REQUESTS, 0),
            lax.dynamic_index_in_dim(lengths, group, 0, keepdims=False),
            lax.dynamic_index_in_dim(jnp.asarray(plan.source), member, 0, keepdims=False),
        ]
    )


def causal_bias(start, rows, keys, sources, ends, member, width):
    qpos = page_position(start + iota((rows, 1), 0), member, width)
    low = jnp.zeros_like(qpos)
    for end in ends:
        low = jnp.where(qpos >= end, end, low)
    kpos = key_positions(keys, sources, width)
    return jnp.where((kpos >= low) & (kpos <= qpos), 0.0, MASKED)


def request_mask(ends, keys, sources, width):
    request = iota((STACKED, 1), 0) % PADDED_ROWS // DECODE_STEPS
    low = jnp.zeros_like(request)
    high = jnp.zeros_like(request) + ends[0]
    for r in range(1, GROUP_REQUESTS):
        low = jnp.where(request == r, ends[r - 1], low)
        high = jnp.where(request == r, ends[r], high)
    kpos = key_positions(keys, sources, width)
    return (kpos >= low) & (kpos < high)


def stacked_heads(ref, rows, first, count):
    return jnp.concatenate(
        [ref[rows, span(first + i * HEAD_SIZE, HEAD_SIZE)] for i in range(count)], axis=0
    )


def each_kv_head(width, step):
    if width <= 8:
        for h in range(KEY_VALUE_HEADS):
            step(h)
    else:
        lax.fori_loop(0, KEY_VALUE_HEADS, lambda h, c: (step(h), c)[1], 0)


def first_kernel(plan, pd_size, facts_ref, q_hbm_ref, *refs):
    width = plan.size
    kv_refs, refs = refs[: width - 1], refs[width - 1 :]
    block_refs, refs = refs[:pd_size], refs[pd_size:]
    acc_ref, top_ref, dec_acc_ref, dec_top_ref, queries_ref, q_ref, fresh_ref, sem = refs
    copies = []
    for h in range(KEY_VALUE_HEADS):
        part = pl.ds(h * Q_BLOCK, Q_BLOCK)
        copies.append(pltpu.make_async_copy(q_hbm_ref.at[:, part], q_ref.at[:, part], sem.at[h]))
    for copy in copies:
        copy.start()
    tokens = q_ref.shape[0]
    half = tokens // 2
    facts = Facts(facts_ref, width)
    group, member, ends = facts.group, facts.member, facts.ends
    sources = facts.source[:-1]

    row = iota((PADDED_ROWS, DECODE_ROWS), 0)
    column = iota((PADDED_ROWS, DECODE_ROWS), 1)
    total = None
    for k in range(pd_size):
        pick = column < 0
        for r in range(GROUP_REQUESTS):
            slot = facts.slots[r]
            back = group - slot // GROUP_REQUESTS
            back = jnp.where(back < 0, back + pd_size, back)
            first = jnp.where(back == k, slot % GROUP_REQUESTS * DECODE_STEPS, -DECODE_ROWS * 4)
            pick = pick | ((row // DECODE_STEPS == r) & (column == first + row - r * DECODE_STEPS))
        part = product(pick.astype(jnp.float32).astype(jnp.bfloat16), block_refs[k][...])
        total = part if total is None else total + part
    total = total.astype(jnp.bfloat16)
    queries_ref[...] = total[:, :Q_WIDTH]
    fresh_ref[...] = total[:, Q_WIDTH:]

    row = iota((STACKED, PADDED_ROWS), 0) % PADDED_ROWS
    column = iota((STACKED, PADDED_ROWS), 1)
    fresh_mask = (column // DECODE_STEPS == row // DECODE_STEPS) & (
        column % DECODE_STEPS <= row % DECODE_STEPS
    )
    mask = request_mask(ends, tokens, sources, width)
    spans = ((0, half), (half, tokens))
    biases = [causal_bias(s, half, keys, sources, ends, member, width) for s, keys in spans]
    together = max(1, min(HEADS_PER_KV, HEADS_PER_KV * 4 // width))

    def step(h):
        columns = span(h * HEAD_SIZE, HEAD_SIZE)
        first = h * Q_BLOCK
        queries = stacked_heads(queries_ref, slice(None), first, HEADS_PER_KV)
        fresh_scores = jnp.where(fresh_mask, scores_of(queries, fresh_ref[:, columns]), MASKED)
        k_all = jnp.concatenate([ref[:tokens, columns] for ref in kv_refs], axis=0)
        v_all = with_ones(jnp.concatenate([ref[tokens:, columns] for ref in kv_refs], axis=0))
        scores = jnp.where(mask, scores_of(queries, k_all), MASKED)
        top = jnp.maximum(
            jnp.max(scores, axis=1, keepdims=True), jnp.max(fresh_scores, axis=1, keepdims=True)
        )
        weights = jnp.exp2((scores - top) * EXPONENT).astype(jnp.bfloat16)
        fresh_weights = jnp.exp2((fresh_scores - top) * EXPONENT).astype(jnp.bfloat16)
        fresh_values = fresh_ref[:, span(KV_WIDTH + h * HEAD_SIZE, HEAD_SIZE)]
        dec_acc_ref[h] = product(weights, v_all) + product(fresh_weights, with_ones(fresh_values))
        dec_top_ref[h] = jnp.broadcast_to(top, (STACKED, HEAD_SIZE))
        for (start, keys), bias in zip(spans, biases):
            if keys < tokens:
                k_part = jnp.concatenate([ref[:keys, columns] for ref in kv_refs], axis=0)
                v_part = with_ones(jnp.concatenate([ref[tokens : tokens + keys, columns] for ref in kv_refs], axis=0))
            else:
                k_part, v_part = k_all, v_all
            for g in range(0, HEADS_PER_KV, together):
                queries = stacked_heads(
                    q_ref, slice(start, start + half), first + g * HEAD_SIZE, together
                )
                scores = scores_of(queries, k_part).reshape(together, half, bias.shape[1]) + bias[None]
                top = jnp.max(scores, axis=2, keepdims=True)
                weights = jnp.exp2((scores - top) * EXPONENT).astype(jnp.bfloat16)
                rows = slice(
                    start * HEADS_PER_KV + g * half, start * HEADS_PER_KV + (g + together) * half
                )
                acc_ref[h, rows, :] = product(weights.reshape(together * half, bias.shape[1]), v_part)
                top_ref[h, rows, :] = jnp.broadcast_to(top, (together, half, HEAD_SIZE)).reshape(
                    together * half, HEAD_SIZE
                )

    for copy in copies:
        copy.wait()
    each_kv_head(width, step)


def divided(acc):
    return (acc[:, :HEAD_SIZE] / acc[:, HEAD_SIZE:]).astype(jnp.bfloat16)


def merge(acc, old_top, scores, values):
    top = jnp.maximum(old_top, jnp.max(scores, axis=1, keepdims=True))
    weights = jnp.exp2((scores - top) * EXPONENT).astype(jnp.bfloat16)
    factor = jnp.exp2((old_top - top) * EXPONENT)
    return acc * jnp.concatenate([factor, factor], axis=1) + product(weights, with_ones(values))


def decode_kernel(plan, pd_size, facts_ref, acc_ref, top_ref, queries_ref, kv_ref, out_ref):
    width = plan.size
    tokens = kv_ref.shape[0] // 2
    facts = Facts(facts_ref, width)
    mask = request_mask(facts.ends, tokens, facts.source[-1:], width)
    row = iota((PADDED_ROWS, PADDED_ROWS), 0)
    column = iota((PADDED_ROWS, PADDED_ROWS), 1)
    pick = column < 0
    for r in range(GROUP_REQUESTS):
        ahead = facts.slots[r] // GROUP_REQUESTS - facts.group
        ahead = jnp.where(ahead < 0, ahead + pd_size, ahead)
        pick = pick | (
            (column // DECODE_STEPS == r) & (row == ahead * DECODE_STEPS + column - r * DECODE_STEPS)
        )
    pick = pick.astype(jnp.float32).astype(jnp.bfloat16)
    heads = range(KEY_VALUE_HEADS)
    columns = [slice(h * HEAD_SIZE, (h + 1) * HEAD_SIZE) for h in heads]
    scores = [
        scores_of(stacked_heads(queries_ref, slice(None), h * Q_BLOCK, HEADS_PER_KV), kv_ref[:tokens, columns[h]])
        for h in heads
    ]
    scores = [jnp.where(mask, s, MASKED) for s in scores]
    out = [divided(merge(acc_ref[h], top_ref[h], scores[h], kv_ref[tokens:, columns[h]])) for h in heads]
    out = jnp.concatenate(
        [o[g * PADDED_ROWS : (g + 1) * PADDED_ROWS] for o in out for g in range(HEADS_PER_KV)], axis=1
    )
    out_ref[...] = product(pick, out).astype(jnp.bfloat16)


def prefill_kernel(plan, facts_ref, q_ref, acc_ref, top_ref, kv_ref, out_ref, done_ref, sem):
    width = plan.size
    tokens = q_ref.shape[0]
    half = tokens // 2
    facts = Facts(facts_ref, width)
    biases = [
        causal_bias(s, half, tokens, facts.source[-1:], facts.ends, facts.member, width)
        for s in (0, half)
    ]

    def finish(rescale):
        copies = []
        worst = jnp.full((half, tokens), MASKED, jnp.float32)
        for h in range(KEY_VALUE_HEADS):
            columns = slice(h * HEAD_SIZE, (h + 1) * HEAD_SIZE)
            keys, values = kv_ref[:tokens, columns], kv_ref[tokens:, columns]
            for start, bias in zip((0, half), biases):
                queries = stacked_heads(q_ref, slice(start, start + half), h * Q_BLOCK, HEADS_PER_KV)
                scores = scores_of(queries, keys).reshape(HEADS_PER_KV, half, tokens) + bias[None]
                rows = slice(start * HEADS_PER_KV, (start + half) * HEADS_PER_KV)
                if rescale:
                    scores = scores.reshape(HEADS_PER_KV * half, tokens)
                    acc = merge(acc_ref[h, rows, :], top_ref[h, rows, :], scores, values)
                else:
                    above = scores - top_ref[h, rows, :].reshape(HEADS_PER_KV, half, tokens)
                    worst = jnp.maximum(worst, jnp.max(above, axis=0))
                    weights = jnp.exp2(above * EXPONENT).astype(jnp.bfloat16)
                    weights = weights.reshape(HEADS_PER_KV * half, tokens)
                    acc = acc_ref[h, rows, :] + product(weights, with_ones(values))
                out = divided(acc)
                for g in range(HEADS_PER_KV):
                    done_ref[
                        start : start + half,
                        h * Q_BLOCK + g * HEAD_SIZE : h * Q_BLOCK + (g + 1) * HEAD_SIZE,
                    ] = out[g * half : (g + 1) * half]
            part = pl.ds(h * Q_BLOCK, Q_BLOCK)
            copy = pltpu.make_async_copy(done_ref.at[:, part], out_ref.at[:, part], sem.at[h])
            copy.start()
            copies.append(copy)
        for copy in copies:
            copy.wait()
        return jnp.max(worst)

    @pl.when(finish(False) * EXPONENT > LIMIT)
    def _():
        finish(True)


def cost(rows, keys, exps):
    return pl.CostEstimate(
        flops=32 * rows * keys * Q_WIDTH, bytes_accessed=4 * rows * Q_WIDTH, transcendentals=exps
    )


def call_first(plan, facts, query, blocks, pieces):
    tokens, width = query.shape[0], plan.size
    rows = HEADS_PER_KV * tokens
    f32, bf16 = jnp.float32, jnp.bfloat16
    shapes = [
        jax.ShapeDtypeStruct((KEY_VALUE_HEADS, rows, 2 * HEAD_SIZE), f32),
        jax.ShapeDtypeStruct((KEY_VALUE_HEADS, rows, HEAD_SIZE), f32),
        jax.ShapeDtypeStruct((KEY_VALUE_HEADS, STACKED, 2 * HEAD_SIZE), f32),
        jax.ShapeDtypeStruct((KEY_VALUE_HEADS, STACKED, HEAD_SIZE), f32),
        jax.ShapeDtypeStruct((PADDED_ROWS, Q_WIDTH), bf16),
    ]
    every = (width - 1) * tokens
    return pl.pallas_call(
        lambda *refs: first_kernel(plan, len(blocks), *refs),
        in_specs=[SMEM, ANY] + [VMEM] * (len(blocks) + width - 1),
        out_specs=[VMEM] * len(shapes),
        out_shape=shapes,
        scratch_shapes=[
            pltpu.VMEM((tokens, Q_WIDTH), bf16),
            pltpu.VMEM((PADDED_ROWS, 2 * KV_WIDTH), bf16),
            pltpu.SemaphoreType.DMA((KEY_VALUE_HEADS,)),
        ],
        compiler_params=pltpu.CompilerParams(vmem_limit_bytes=(28 + width) * MIB),
        cost_estimate=cost(tokens, every, tokens * every * QUERY_HEADS),
        name="first_shards",
    )(facts, query, *pieces, *blocks)


def call_decode(plan, pd_size, facts, state, piece):
    tokens = piece.shape[0] // 2
    return pl.pallas_call(
        lambda *refs: decode_kernel(plan, pd_size, *refs),
        in_specs=[SMEM] + [VMEM] * 4,
        out_specs=VMEM,
        out_shape=jax.ShapeDtypeStruct((PADDED_ROWS, Q_WIDTH), jnp.bfloat16),
        compiler_params=pltpu.CompilerParams(vmem_limit_bytes=32 * MIB),
        cost_estimate=cost(PADDED_ROWS, tokens, PADDED_ROWS * tokens * QUERY_HEADS),
        name="last_shard_decode",
    )(facts, *state[2:], piece)


def call_prefill(plan, facts, query, state, piece):
    tokens = query.shape[0]
    return pl.pallas_call(
        lambda *refs: prefill_kernel(plan, *refs),
        in_specs=[SMEM] + [VMEM] * 4,
        out_specs=ANY,
        out_shape=jax.ShapeDtypeStruct((tokens, Q_WIDTH), jnp.bfloat16),
        scratch_shapes=[
            pltpu.VMEM((tokens, Q_WIDTH), jnp.bfloat16),
            pltpu.SemaphoreType.DMA((KEY_VALUE_HEADS,)),
        ],
        compiler_params=pltpu.CompilerParams(vmem_limit_bytes=32 * MIB),
        cost_estimate=cost(tokens, tokens, tokens * tokens * QUERY_HEADS),
        name="last_shard_prefill",
    )(facts, query, *state[:2], piece)


def ring(size, step):
    return [(i, (i + step) % size) for i in range(size)]


def body(
    prompt_query,
    prompt_key,
    prompt_value,
    prompt_lengths,
    decode_slot,
    decoded_query,
    decoded_key,
    decoded_value,
):
    plan = Ring(lax.axis_size("tp"))
    pd_size = lax.axis_size("pd")
    my_group = lax.axis_index("pd")
    facts = facts_row(plan, prompt_lengths, decode_slot)
    pieces, blocks = [jnp.concatenate([prompt_key, prompt_value], axis=0)], None
    pieces[0], decoded_query = lax.optimization_barrier((pieces[0], decoded_query))
    own = jnp.concatenate([decoded_query, decoded_key, decoded_value], axis=2).reshape(
        DECODE_ROWS, Q_WIDTH + 2 * KV_WIDTH
    )
    for s in range(1, plan.size):
        if s == 2:
            pieces[1], own, facts = lax.optimization_barrier((pieces[1], own, facts))
        if s == plan.size - 1:
            pieces, blocks = lax.optimization_barrier((pieces, blocks))
        pieces.append(plan.step(pieces[-1]))
        if s == 2:
            blocks = [own] + [lax.ppermute(own, "pd", ring(pd_size, k)) for k in range(1, pd_size)]

    state = call_first(plan, facts, prompt_query, blocks, pieces[:-1])
    outgoing = call_decode(plan, pd_size, facts, state, pieces[-1])
    arrived = [outgoing[:DECODE_STEPS]]
    for k in range(1, pd_size):
        part = outgoing[k * DECODE_STEPS : (k + 1) * DECODE_STEPS]
        arrived.append(lax.ppermute(part, "pd", ring(pd_size, k)))
    pre_out = call_prefill(plan, facts, prompt_query, state, pieces[-1])

    numbers = jnp.arange(decode_slot.shape[0], dtype=jnp.int32)
    wanted = my_group * GROUP_REQUESTS + jnp.arange(GROUP_REQUESTS, dtype=jnp.int32)
    owner = jnp.sum(
        jnp.where(decode_slot[None, :] == wanted[:, None], numbers[None, :] // GROUP_REQUESTS, 0), axis=1
    )
    from_block = (my_group - owner) % pd_size
    dec_out = jnp.zeros((GROUP_REQUESTS, DECODE_STEPS, Q_WIDTH), jnp.bfloat16)
    for k in range(pd_size):
        dec_out = jnp.where((from_block == k)[:, None, None], arrived[k][None], dec_out)
    return (pre_out, dec_out)


def solution(mesh):
    placed = (
        P(("rep", "pd", "tp"), None),
        P(("rep", "pd", "tp"), None),
        P(("rep", "pd", "tp"), None),
        P("rep", None),
        P("rep"),
        P(("rep", "pd"), None, None),
        P(("rep", "pd"), None, None),
        P(("rep", "pd"), None, None),
    )
    return jax.shard_map(
        body,
        mesh=mesh,
        in_specs=placed,
        out_specs=(P(("rep", "pd", "tp"), None), P(("rep", "pd"), None, None)),
        check_vma=False,
    )
```

time: 45.5 us -> 36.6 us (0.80)
  the two profiles are of different devices: /device:TPU:0 before, /device:TPU:9 now
where the time goes in v4:
time: 36.6 us; the launch traced here: 36.3 us
  starting transfers between devices  12.4 us (34%)
  Pallas kernels  8.69 us (24%)
  waiting for transfers between devices  8.1 us (22%)
  other arithmetic  3.6 us (10%)
  local copies, waits for them, and re-layouts  2.84 us (8%)
  between operations  0.71 us (2%)
    ppermute x3, starting transfers between devices, step(): return lax.ppermute(array, 'tp', self.pairs)  5.48 us
    pallas_call x1, Pallas kernels, call_first(): pl.pallas_call(lambda *refs: first_kernel(plan, len(blocks), *refs), in_s...  4.66 us
    ppermute x3, waiting for transfers between devices, body(): lax.ppermute(own, 'pd', ring(pd_size, k))  4.23 us
    ppermute x3, waiting for transfers between devices, step(): return lax.ppermute(array, 'tp', self.pairs)  3.86 us
    ppermute x3, starting transfers between devices, body(): lax.ppermute(own, 'pd', ring(pd_size, k))  3.45 us
    ppermute x3, starting transfers between devices, body(): arrived.append(lax.ppermute(part, 'pd', ring(pd_size, k)))  3.44 us
    pallas_call x1, Pallas kernels, call_prefill(): pl.pallas_call(lambda *refs: prefill_kernel(plan, *refs), in_specs=[SMEM]...  2.9 us
    unnamed x4, local copies, waits for them, and re-layouts  1.23 us
  transfers between devices with their start and end apart: 9, of which 5 were waited for; matrix products, arithmetic and copies ran while one was open for 9% of the time, Pallas kernels for 21%

profile of v4, /device:TPU:9, one launch (start us, length us, event | category | flops | bytes accessed | tf_op | source)
XLA Modules:
  0.0 36.3 jit_solution(8582534776034504037)
XLA Ops:
  0.6 1.0 %pad_maximum_fusion.refs_2_ = bf16[256,512]{1,0:T(8,128)(2,1)S(1)} fusion(bf16[128,512]{1,0:T(8,128)(2,1)} %param.11, bf16[128,512]{1,0:T(8,128)(2,1)} %param.10), kind=kLoop, calls=%fused_computation | loop fusion | flops 524288 | bytes 524288 | tf_op jit(solution)/shard_map/concatenate | solution.py:403
  1.6 2.4 %collective-permute-start = (bf16[256,512]{1,0:T(8,128)(2,1)S(1)}, bf16[256,512]{1,0:T(8,128)(2,1)S(1)}, u32[]{:S(2)}, u32[]{:S(2)}) collective-permute-start(bf16[256,512]{1,0:T(8,128)(2,1)S(1)} %pad_maximum_fusion.refs_2_), channel_id=1, source_target_pairs={{0,1},{1,3},{3,2},{2,0},{4,5},{5,7},{7,6},{6,4},{8,9},{9,11},{11,1... | collective-permute-start | bytes 786440 | tf_op jit(solution)/shard_map/ppermute | solution.py:46
  4.0 0.9 %pad_maximum_fusion.1 = bf16[4,2,5120]{2,1,0:T(2,128)(2,1)S(1)} fusion(bf16[4,2,512]{2,1,0:T(2,128)(2,1)} %param.16, bf16[4,2,512]{2,1,0:T(2,128)(2,1)} %param.15, bf16[4,2,4096]{2,1,0:T(2,128)(2,1)} %param.14), kind=kLoop, calls=%fused_computation.5 | loop fusion | flops 245760 | bytes 163840 | tf_op jit(solution)/shard_map/concatenate | solution.py:405
  4.9 0.7 %dynamic-slice_bitcast_fusion = (s32[4]{0:T(128)S(1)}, s32[4]{0:T(128)S(1)}) fusion(s32[4,4]{1,0:T(4,128)} %constant.56.clone, s32[]{:T(128)S(6)} %select_n.60, s32[4,4]{1,0:T(4,128)} %param.12, s32[]{:T(128)S(6)} %select_n.59), kind=kLoop, calls=%fused_computation.16 | loop fusion | bytes 72 | tf_op jit(solution)/shard_map/jit(dynamic_index_in_dim)/squeeze | solution.py:108
  5.7 0.7 %dynamic_slice.11 = s32[4]{0:T(128)S(1)} dynamic-slice(s32[16]{0:T(128)} %param.13, s32[]{:T(128)S(6)} %select_n.58), dynamic_slice_sizes={4} | dynamic-slice | bytes 36 | tf_op jit(solution)/shard_map/dynamic_slice | solution.py:106
  6.4 0.1 concatenate.11.refs_0_
  6.5 0.8 %select_reduce_fusion = s32[4]{0:T(128)S(1)} fusion(s32[16]{0:T(128)S(1)} %and_select_fusion.1, s32[16]{0:T(128)} %param.13, s32[4]{0:T(128)S(1)} %iota_add_fusion), kind=kLoop, calls=%fused_computation.8 | loop fusion | flops 188 | bytes 160 | tf_op jit(solution)/shard_map/reduce_sum | solution.py:427
  7.3 1.6 %collective-permute-done.refs_3_ = bf16[256,512]{1,0:T(8,128)(2,1)S(1)} collective-permute-done((bf16[256,512]{1,0:T(8,128)(2,1)S(1)}, bf16[256,512]{1,0:T(8,128)(2,1)S(1)}, u32[]{:S(2)}, u32[]{:S(2)}) %collective-permute-start) | collective-permute-done | bytes 262176 | tf_op jit(solution)/shard_map/ppermute | solution.py:46
  9.0 3.1 %collective-permute-start.1 = (bf16[256,512]{1,0:T(8,128)(2,1)S(1)}, bf16[256,512]{1,0:T(8,128)(2,1)S(1)}, u32[]{:S(2)}, u32[]{:S(2)}) collective-permute-start(bf16[256,512]{1,0:T(8,128)(2,1)S(1)} %collective-permute-done.refs_3_), channel_id=1, source_target_pairs={{0,1},{1,3},{3,2},{2,0},{4,5},{5,7},{7,6},{6,4},{8,9},{9,11},{11,1... | collective-permute-start | bytes 786440 | tf_op jit(solution)/shard_map/ppermute | solution.py:46
  12.1 3.0 %collective-permute-start.2 = (bf16[8,5120]{1,0:T(8,128)(2,1)S(1)}, bf16[8,5120]{1,0:T(8,128)(2,1)S(1)}, u32[]{:S(2)}, u32[]{:S(2)}) collective-permute-start(bf16[8,5120]{1,0:T(8,128)(2,1)S(1)} %reshape.77.refs_5_), channel_id=1, source_target_pairs={{0,4},{4,8},{8,12},{12,0},{1,5},{5,9},{9,13},{13,1},{2,6},{6,10},{... | collective-permute-start | bytes 245768 | tf_op jit(solution)/shard_map/ppermute | solution.py:415
  15.0 0.3 collective-permute-start.3
  15.3 0.2 collective-permute-start.4
  15.5 1.2 %collective-permute-done.2.refs_6_ = bf16[8,5120]{1,0:T(8,128)(2,1)S(1)} collective-permute-done((bf16[8,5120]{1,0:T(8,128)(2,1)S(1)}, bf16[8,5120]{1,0:T(8,128)(2,1)S(1)}, u32[]{:S(2)}, u32[]{:S(2)}) %collective-permute-start.2) | collective-permute-done | bytes 81952 | tf_op jit(solution)/shard_map/ppermute | solution.py:415
  16.7 2.5 %collective-permute-done.3.refs_7_ = bf16[8,5120]{1,0:T(8,128)(2,1)S(1)} collective-permute-done((bf16[8,5120]{1,0:T(8,128)(2,1)S(1)}, bf16[8,5120]{1,0:T(8,128)(2,1)S(1)}, u32[]{:S(2)}, u32[]{:S(2)}) %collective-permute-start.3) | collective-permute-done | bytes 81952 | tf_op jit(solution)/shard_map/ppermute | solution.py:415
  19.2 0.5 %collective-permute-done.4.refs_8_ = bf16[8,5120]{1,0:T(8,128)(2,1)S(1)} collective-permute-done((bf16[8,5120]{1,0:T(8,128)(2,1)S(1)}, bf16[8,5120]{1,0:T(8,128)(2,1)S(1)}, u32[]{:S(2)}, u32[]{:S(2)}) %collective-permute-start.4) | collective-permute-done | bytes 81952 | tf_op jit(solution)/shard_map/ppermute | solution.py:415
  19.8 0.0 collective-permute-done.1.refs_4_
  19.8 0.0 collective-permute-start.5
  19.8 0.0 copy-start
  19.8 1.2 %copy-done = bf16[128,4096]{1,0:T(8,128)(2,1)S(1)} copy-done((bf16[128,4096]{1,0:T(8,128)(2,1)S(1)}, bf16[128,4096]{1,0:T(8,128)(2,1)}, u32[]{:S(2)}) %copy-start) | copy-done | bytes 1048600
  21.0 0.0 copy-start.1
  21.0 4.7 %first_shards.1 = (f32[4,1024,256]{2,1,0:T(8,128)S(1)}, f32[4,1024,128]{2,1,0:T(8,128)S(1)}, f32[4,128,256]{2,1,0:T(8,128)S(1)}, f32[4,128,128]{2,1,0:T(8,128)S(1)}, bf16[16,4096]{1,0:T(8,128)(2,1)S(1)}) custom-call(s32[14]{0:T(128)S(1)} %concatenate.11.refs_0_, bf16[128,4096]{1,0:T(8,128)(2,1)S(1)} %copy-done, ...), custom_call_target="tpu_custom_call" | custom-call | flops 6442450944 | bytes 2097152 | tf_op jit(solution)/shard_map/first_shards/pallas_call | solution.py:339
  25.7 2.2 %collective-permute-done.5.refs_4_ = bf16[256,512]{1,0:T(8,128)(2,1)S(1)} collective-permute-done((bf16[256,512]{1,0:T(8,128)(2,1)S(1)}, bf16[256,512]{1,0:T(8,128)(2,1)S(1)}, u32[]{:S(2)}, u32[]{:S(2)}) %collective-permute-start.5) | collective-permute-done | bytes 262176 | tf_op jit(solution)/shard_map/ppermute | solution.py:46
  27.9 1.1 %last_shard_decode.1 = bf16[16,4096]{1,0:T(8,128)(2,1)S(1)} custom-call(s32[14]{0:T(128)S(1)} %concatenate.11.refs_0_, f32[4,128,256]{2,1,0:T(8,128)S(1)} %get-tuple-element.33.refs_1_, f32[4,128,128]{2,1,0:T(8,128)S(1)} %get-tuple-element.34.refs_2_, bf16[16,4096]{1,0:T(8,128)(2,1)S(1)} %get-tuple-element.35.refs_3_, ...), custom_call_target="tpu_custom_call" | custom-call | flops 268435456 | bytes 262144 | tf_op jit(solution)/shard_map/last_shard_decode/pallas_call | solution.py:357
  29.1 0.1 fusion.1
  29.1 0.6 %collective-permute-start.6 = (bf16[2,4096]{1,0:T(2,128)(2,1)S(1)}, bf16[2,4096]{1,0:T(2,128)(2,1)S(1)}, u32[]{:S(2)}, u32[]{:S(2)}) collective-permute-start(bf16[2,4096]{1,0:T(2,128)(2,1)S(1)} %get-tuple-element.38), channel_id=1, source_target_pairs={{0,12},{4,0},{8,4},{12,8},{1,13},{5,1},{9,5},{13,9},{2,14},{6,2},{... | collective-permute-start | bytes 49160 | tf_op jit(solution)/shard_map/ppermute | solution.py:422
  29.7 1.2 %collective-permute-start.7 = (bf16[2,4096]{1,0:T(2,128)(2,1)S(1)}, bf16[2,4096]{1,0:T(2,128)(2,1)S(1)}, u32[]{:S(2)}, u32[]{:S(2)}) collective-permute-start(bf16[2,4096]{1,0:T(2,128)(2,1)S(1)} %get-tuple-element.41), channel_id=1, source_target_pairs={{0,8},{4,12},{8,0},{12,4},{1,9},{5,13},{9,1},{13,5},{2,10},{6,14},... | collective-permute-start | bytes 49160 | tf_op jit(solution)/shard_map/ppermute | solution.py:422
  30.9 1.6 %collective-permute-start.8 = (bf16[2,4096]{1,0:T(2,128)(2,1)S(1)}, bf16[2,4096]{1,0:T(2,128)(2,1)S(1)}, u32[]{:S(2)}, u32[]{:S(2)}) collective-permute-start(bf16[2,4096]{1,0:T(2,128)(2,1)S(1)} %get-tuple-element.40), channel_id=1, source_target_pairs={{0,4},{4,8},{8,12},{12,0},{1,5},{5,9},{9,13},{13,1},{2,6},{6,10},{... | collective-permute-start | bytes 49160 | tf_op jit(solution)/shard_map/ppermute | solution.py:422
  32.6 0.0 copy-done.1
  32.6 2.9 %last_shard_prefill.1 = bf16[128,4096]{1,0:T(8,128)(2,1)} custom-call(s32[14]{0:T(128)S(1)} %concatenate.11.refs_0_, bf16[128,4096]{1,0:T(8,128)(2,1)S(1)} %copy-done.1, f32[4,1024,256]{2,1,0:T(8,128)S(1)} %get-tuple-element.31.refs_2_, f32[4,1024,128]{2,1,0:T(8,128)S(1)} %get-tuple-element.32.refs_3_, bf16[256,512]{1,0:T(8,128)(2,1)S(1)} %collective-permute-done.5.refs_4_), custom_call_target="tpu_custom_call" | custom-call | flops 2147483648 | bytes 2097152 | tf_op jit(solution)/shard_map/last_shard_prefill/pallas_call | solution.py:370
  35.5 0.0 collective-permute-done.6
  35.5 0.0 collective-permute-done.7
  35.5 0.0 collective-permute-done.8
  35.5 0.8 %broadcast_select_fusion.2 = bf16[4,2,4096]{2,1,0:T(2,128)(2,1)} fusion(pred[4]{0:T(512)(128)(4,1)S(1)} %get-tuple-element.44, pred[4]{0:T(512)(128)(4,1)S(1)} %get-tuple-element.43, pred[4]{0:T(512)(128)(4,1)S(1)} %get-tuple-element.42, pred[4]{0:T(512)(128)(4,1)S(1)} %get-tuple-element.36, bf16[2,4096]{1,0:T(2,128)(2,1)S(1)} %get-tuple-element.39, ...), kind=kLoop, calls=%fused_computation.3 | loop fusion | flops 131072 | bytes 131088 | tf_op jit(solution)/shard_map/jit(_where)/select_n | solution.py:433
  (5 shorter events, 0.1 us)
Async XLA Ops:
  1.6 7.3 %collective-permute-start = (bf16[256,512]{1,0:T(8,128)(2,1)S(1)}, bf16[256,512]{1,0:T(8,128)(2,1)S(1)}, u32[]{:S(2)}, u32[]{:S(2)}) collective-permute-start(bf16[256,512]{1,0:T(8,128)(2,1)S(1)} %pad_maximum_fusion.refs_2_), channel_id=1, source_target_pairs={{0,1},{1,3},{3,2},{2,0},{4,5},{5,7},{7,6},{6,4},{8,9},{9,11},{11,1... | collective-permute-start | bytes 786440 | tf_op jit(solution)/shard_map/ppermute | solution.py:46
  9.0 10.8 %collective-permute-start.1 = (bf16[256,512]{1,0:T(8,128)(2,1)S(1)}, bf16[256,512]{1,0:T(8,128)(2,1)S(1)}, u32[]{:S(2)}, u32[]{:S(2)}) collective-permute-start(bf16[256,512]{1,0:T(8,128)(2,1)S(1)} %collective-permute-done.refs_3_), channel_id=1, source_target_pairs={{0,1},{1,3},{3,2},{2,0},{4,5},{5,7},{7,6},{6,4},{8,9},{9,11},{11,1... | collective-permute-start | bytes 786440 | tf_op jit(solution)/shard_map/ppermute | solution.py:46
  12.1 4.6 %collective-permute-start.2 = (bf16[8,5120]{1,0:T(8,128)(2,1)S(1)}, bf16[8,5120]{1,0:T(8,128)(2,1)S(1)}, u32[]{:S(2)}, u32[]{:S(2)}) collective-permute-start(bf16[8,5120]{1,0:T(8,128)(2,1)S(1)} %reshape.77.refs_5_), channel_id=1, source_target_pairs={{0,4},{4,8},{8,12},{12,0},{1,5},{5,9},{9,13},{13,1},{2,6},{6,10},{... | collective-permute-start | bytes 245768 | tf_op jit(solution)/shard_map/ppermute | solution.py:415
  15.0 4.2 %collective-permute-start.3 = (bf16[8,5120]{1,0:T(8,128)(2,1)S(1)}, bf16[8,5120]{1,0:T(8,128)(2,1)S(1)}, u32[]{:S(2)}, u32[]{:S(2)}) collective-permute-start(bf16[8,5120]{1,0:T(8,128)(2,1)S(1)} %reshape.77.refs_5_), channel_id=1, source_target_pairs={{0,8},{4,12},{8,0},{12,4},{1,9},{5,13},{9,1},{13,5},{2,10},{6,14},... | collective-permute-start | bytes 245768 | tf_op jit(solution)/shard_map/ppermute | solution.py:415
  15.3 4.5 %collective-permute-start.4 = (bf16[8,5120]{1,0:T(8,128)(2,1)S(1)}, bf16[8,5120]{1,0:T(8,128)(2,1)S(1)}, u32[]{:S(2)}, u32[]{:S(2)}) collective-permute-start(bf16[8,5120]{1,0:T(8,128)(2,1)S(1)} %reshape.77.refs_5_), channel_id=1, source_target_pairs={{0,12},{4,0},{8,4},{12,8},{1,13},{5,1},{9,5},{13,9},{2,14},{6,2},{... | collective-permute-start | bytes 245768 | tf_op jit(solution)/shard_map/ppermute | solution.py:415
  19.8 8.2 %collective-permute-start.5 = (bf16[256,512]{1,0:T(8,128)(2,1)S(1)}, bf16[256,512]{1,0:T(8,128)(2,1)S(1)}, u32[]{:S(2)}, u32[]{:S(2)}) collective-permute-start(bf16[256,512]{1,0:T(8,128)(2,1)S(1)} %collective-permute-done.1.refs_4_), channel_id=1, source_target_pairs={{0,1},{1,3},{3,2},{2,0},{4,5},{5,7},{7,6},{6,4},{8,9},{9,11},{11,1... | collective-permute-start | bytes 786440 | tf_op jit(solution)/shard_map/ppermute | solution.py:46
  19.8 1.2 %copy-start = (bf16[128,4096]{1,0:T(8,128)(2,1)S(1)}, bf16[128,4096]{1,0:T(8,128)(2,1)}, u32[]{:S(2)}) copy-start(bf16[128,4096]{1,0:T(8,128)(2,1)} %refs_1_.3) | copy-start | bytes 3145732
  21.0 11.6 %copy-start.1 = (bf16[128,4096]{1,0:T(8,128)(2,1)S(1)}, bf16[128,4096]{1,0:T(8,128)(2,1)}, u32[]{:S(2)}) copy-start(bf16[128,4096]{1,0:T(8,128)(2,1)} %refs_1_.3) | copy-start | bytes 3145732
  29.1 6.4 %collective-permute-start.6 = (bf16[2,4096]{1,0:T(2,128)(2,1)S(1)}, bf16[2,4096]{1,0:T(2,128)(2,1)S(1)}, u32[]{:S(2)}, u32[]{:S(2)}) collective-permute-start(bf16[2,4096]{1,0:T(2,128)(2,1)S(1)} %get-tuple-element.38), channel_id=1, source_target_pairs={{0,12},{4,0},{8,4},{12,8},{1,13},{5,1},{9,5},{13,9},{2,14},{6,2},{... | collective-permute-start | bytes 49160 | tf_op jit(solution)/shard_map/ppermute | solution.py:422
  29.7 5.8 %collective-permute-start.7 = (bf16[2,4096]{1,0:T(2,128)(2,1)S(1)}, bf16[2,4096]{1,0:T(2,128)(2,1)S(1)}, u32[]{:S(2)}, u32[]{:S(2)}) collective-permute-start(bf16[2,4096]{1,0:T(2,128)(2,1)S(1)} %get-tuple-element.41), channel_id=1, source_target_pairs={{0,8},{4,12},{8,0},{12,4},{1,9},{5,13},{9,1},{13,5},{2,10},{6,14},... | collective-permute-start | bytes 49160 | tf_op jit(solution)/shard_map/ppermute | solution.py:422
  30.9 4.5 %collective-permute-start.8 = (bf16[2,4096]{1,0:T(2,128)(2,1)S(1)}, bf16[2,4096]{1,0:T(2,128)(2,1)S(1)}, u32[]{:S(2)}, u32[]{:S(2)}) collective-permute-start(bf16[2,4096]{1,0:T(2,128)(2,1)S(1)} %get-tuple-element.40), channel_id=1, source_target_pairs={{0,4},{4,8},{8,12},{12,0},{1,5},{5,9},{9,13},{13,1},{2,6},{6,10},{... | collective-permute-start | bytes 49160 | tf_op jit(solution)/shard_map/ppermute | solution.py:422

commit v5 on v4

--- a/solution.py
+++ b/solution.py
@@ -42,8 +42,25 @@
             [[order[(place[m] - s) % size] for s in range(size)] for m in range(size)], np.int32
         )
 
-    def step(self, array):
-        return lax.ppermute(array, "tp", self.pairs)
+    def steps(self, arrays):
+        groups = lax.axis_size("pd")
+        return [
+            lax.ppermute(
+                array,
+                ("pd", "tp"),
+                [
+                    (g * self.size + a, g * self.size + b)
+                    for g in range(parity, groups, 2)
+                    for a, b in self.pairs
+                ],
+            )
+            for parity, array in enumerate(arrays)
+        ]
+
+
+def mine(group, refs, rows, columns):
+    even, odd = refs
+    return jnp.where(group % 2 == 0, even[rows, columns], odd[rows, columns])
 
 
 def scores_of(queries, keys):
@@ -146,9 +163,10 @@
 
 def first_kernel(plan, pd_size, facts_ref, q_hbm_ref, *refs):
     width = plan.size
-    kv_refs, refs = refs[: width - 1], refs[width - 1 :]
+    own_ref, kv_refs, refs = refs[0], refs[1 : 2 * width - 3], refs[2 * width - 3 :]
     block_refs, refs = refs[:pd_size], refs[pd_size:]
     acc_ref, top_ref, dec_acc_ref, dec_top_ref, queries_ref, q_ref, fresh_ref, sem = refs
+    got_refs = [(kv_refs[2 * i], kv_refs[2 * i + 1]) for i in range(width - 2)]
     copies = []
     for h in range(KEY_VALUE_HEADS):
         part = pl.ds(h * Q_BLOCK, Q_BLOCK)
@@ -193,8 +211,12 @@
         first = h * Q_BLOCK
         queries = stacked_heads(queries_ref, slice(None), first, HEADS_PER_KV)
         fresh_scores = jnp.where(fresh_mask, scores_of(queries, fresh_ref[:, columns]), MASKED)
-        k_all = jnp.concatenate([ref[:tokens, columns] for ref in kv_refs], axis=0)
-        v_all = with_ones(jnp.concatenate([ref[tokens:, columns] for ref in kv_refs], axis=0))
+        k_parts, v_parts = (
+            [own_ref[rows, columns]] + [mine(group, refs, rows, columns) for refs in got_refs]
+            for rows in (slice(0, tokens), slice(tokens, 2 * tokens))
+        )
+        k_all = jnp.concatenate(k_parts, axis=0)
+        v_all = with_ones(jnp.concatenate(v_parts, axis=0))
         scores = jnp.where(mask, scores_of(queries, k_all), MASKED)
         top = jnp.maximum(
             jnp.max(scores, axis=1, keepdims=True), jnp.max(fresh_scores, axis=1, keepdims=True)
@@ -206,8 +228,8 @@
         dec_top_ref[h] = jnp.broadcast_to(top, (STACKED, HEAD_SIZE))
         for (start, keys), bias in zip(spans, biases):
             if keys < tokens:
-                k_part = jnp.concatenate([ref[:keys, columns] for ref in kv_refs], axis=0)
-                v_part = with_ones(jnp.concatenate([ref[tokens : tokens + keys, columns] for ref in kv_refs], axis=0))
+                k_part = jnp.concatenate([part[:keys] for part in k_parts], axis=0)
+                v_part = with_ones(jnp.concatenate([part[:keys] for part in v_parts], axis=0))
             else:
                 k_part, v_part = k_all, v_all
             for g in range(0, HEADS_PER_KV, together):
@@ -241,10 +263,14 @@
     return acc * jnp.concatenate([factor, factor], axis=1) + product(weights, with_ones(values))
 
 
-def decode_kernel(plan, pd_size, facts_ref, acc_ref, top_ref, queries_ref, kv_ref, out_ref):
+def decode_kernel(plan, pd_size, facts_ref, acc_ref, top_ref, queries_ref, even_ref, odd_ref, out_ref):
     width = plan.size
-    tokens = kv_ref.shape[0] // 2
+    tokens = even_ref.shape[0] // 2
     facts = Facts(facts_ref, width)
+    k_part, v_part = (
+        mine(facts.group, (even_ref, odd_ref), rows, slice(None))
+        for rows in (slice(0, tokens), slice(tokens, 2 * tokens))
+    )
     mask = request_mask(facts.ends, tokens, facts.source[-1:], width)
     row = iota((PADDED_ROWS, PADDED_ROWS), 0)
     column = iota((PADDED_ROWS, PADDED_ROWS), 1)
@@ -259,18 +285,18 @@
     heads = range(KEY_VALUE_HEADS)
     columns = [slice(h * HEAD_SIZE, (h + 1) * HEAD_SIZE) for h in heads]
     scores = [
-        scores_of(stacked_heads(queries_ref, slice(None), h * Q_BLOCK, HEADS_PER_KV), kv_ref[:tokens, columns[h]])
+        scores_of(stacked_heads(queries_ref, slice(None), h * Q_BLOCK, HEADS_PER_KV), k_part[:, columns[h]])
         for h in heads
     ]
     scores = [jnp.where(mask, s, MASKED) for s in scores]
-    out = [divided(merge(acc_ref[h], top_ref[h], scores[h], kv_ref[tokens:, columns[h]])) for h in heads]
+    out = [divided(merge(acc_ref[h], top_ref[h], scores[h], v_part[:, columns[h]])) for h in heads]
     out = jnp.concatenate(
         [o[g * PADDED_ROWS : (g + 1) * PADDED_ROWS] for o in out for g in range(HEADS_PER_KV)], axis=1
     )
     out_ref[...] = product(pick, out).astype(jnp.bfloat16)
 
 
-def prefill_kernel(plan, facts_ref, q_ref, acc_ref, top_ref, kv_ref, out_ref, done_ref, sem):
+def prefill_kernel(plan, facts_ref, q_ref, acc_ref, top_ref, even_ref, odd_ref, out_ref, done_ref, sem):
     width = plan.size
     tokens = q_ref.shape[0]
     half = tokens // 2
@@ -285,7 +311,10 @@
         worst = jnp.full((half, tokens), MASKED, jnp.float32)
         for h in range(KEY_VALUE_HEADS):
             columns = slice(h * HEAD_SIZE, (h + 1) * HEAD_SIZE)
-            keys, values = kv_ref[:tokens, columns], kv_ref[tokens:, columns]
+            keys, values = (
+                mine(facts.group, (even_ref, odd_ref), rows, columns)
+                for rows in (slice(0, tokens), slice(tokens, 2 * tokens))
+            )
             for start, bias in zip((0, half), biases):
                 queries = stacked_heads(q_ref, slice(start, start + half), h * Q_BLOCK, HEADS_PER_KV)
                 scores = scores_of(queries, keys).reshape(HEADS_PER_KV, half, tokens) + bias[None]
@@ -338,7 +367,7 @@
     every = (width - 1) * tokens
     return pl.pallas_call(
         lambda *refs: first_kernel(plan, len(blocks), *refs),
-        in_specs=[SMEM, ANY] + [VMEM] * (len(blocks) + width - 1),
+        in_specs=[SMEM, ANY] + [VMEM] * (len(blocks) + 2 * width - 3),
         out_specs=[VMEM] * len(shapes),
         out_shape=shapes,
         scratch_shapes=[
@@ -349,27 +378,27 @@
         compiler_params=pltpu.CompilerParams(vmem_limit_bytes=(28 + width) * MIB),
         cost_estimate=cost(tokens, every, tokens * every * QUERY_HEADS),
         name="first_shards",
-    )(facts, query, *pieces, *blocks)
+    )(facts, query, *pieces[0][:1], *[a for pair in pieces[1:] for a in pair], *blocks)
 
 
 def call_decode(plan, pd_size, facts, state, piece):
-    tokens = piece.shape[0] // 2
+    tokens = piece[0].shape[0] // 2
     return pl.pallas_call(
         lambda *refs: decode_kernel(plan, pd_size, *refs),
-        in_specs=[SMEM] + [VMEM] * 4,
+        in_specs=[SMEM] + [VMEM] * 5,
         out_specs=VMEM,
         out_shape=jax.ShapeDtypeStruct((PADDED_ROWS, Q_WIDTH), jnp.bfloat16),
         compiler_params=pltpu.CompilerParams(vmem_limit_bytes=32 * MIB),
         cost_estimate=cost(PADDED_ROWS, tokens, PADDED_ROWS * tokens * QUERY_HEADS),
         name="last_shard_decode",
-    )(facts, *state[2:], piece)
+    )(facts, *state[2:], *piece)
 
 
 def call_prefill(plan, facts, query, state, piece):
     tokens = query.shape[0]
     return pl.pallas_call(
         lambda *refs: prefill_kernel(plan, *refs),
-        in_specs=[SMEM] + [VMEM] * 4,
+        in_specs=[SMEM] + [VMEM] * 5,
         out_specs=ANY,
         out_shape=jax.ShapeDtypeStruct((tokens, Q_WIDTH), jnp.bfloat16),
         scratch_shapes=[
@@ -379,7 +408,7 @@
         compiler_params=pltpu.CompilerParams(vmem_limit_bytes=32 * MIB),
         cost_estimate=cost(tokens, tokens, tokens * tokens * QUERY_HEADS),
         name="last_shard_prefill",
-    )(facts, query, *state[:2], piece)
+    )(facts, query, *state[:2], *piece)
 
 
 def ring(size, step):
@@ -400,17 +429,18 @@
     pd_size = lax.axis_size("pd")
     my_group = lax.axis_index("pd")
     facts = facts_row(plan, prompt_lengths, decode_slot)
-    pieces, blocks = [jnp.concatenate([prompt_key, prompt_value], axis=0)], None
-    pieces[0], decoded_query = lax.optimization_barrier((pieces[0], decoded_query))
+    kv, decoded_query = lax.optimization_barrier(
+        (jnp.concatenate([prompt_key, prompt_value], axis=0), decoded_query)
+    )
     own = jnp.concatenate([decoded_query, decoded_key, decoded_value], axis=2).reshape(
         DECODE_ROWS, Q_WIDTH + 2 * KV_WIDTH
     )
+    later_kv, own, facts = lax.optimization_barrier((kv, own, facts))
+    pieces, blocks = [[kv, later_kv]], None
     for s in range(1, plan.size):
-        if s == 2:
-            pieces[1], own, facts = lax.optimization_barrier((pieces[1], own, facts))
-        if s == plan.size - 1:
-            pieces, blocks = lax.optimization_barrier((pieces, blocks))
-        pieces.append(plan.step(pieces[-1]))
+        if s > 1:
+            pieces[1:], own, blocks = lax.optimization_barrier((pieces[1:], own, blocks))
+        pieces.append(plan.steps(pieces[-1]))
         if s == 2:
             blocks = [own] + [lax.ppermute(own, "pd", ring(pd_size, k)) for k in range(1, pd_size)]
 

time: 36.6 us -> 43 us (1.17)
  the two profiles are of different devices: /device:TPU:9 before, /device:TPU:0 now
where the time goes in v5:
time: 43 us; the launch traced here: 42.7 us
  starting transfers between devices  21.5 us (50%)
  Pallas kernels  8.72 us (20%)
  waiting for transfers between devices  5.18 us (12%)
  other arithmetic  3.6 us (8%)
  local copies, waits for them, and re-layouts  2.83 us (7%)
  between operations  0.81 us (2%)
    ppermute x6, starting transfers between devices, steps(): lax.ppermute(array, ('pd', 'tp'), [(g * self.size + a, g * self.size + b)...  15.2 us
    pallas_call x1, Pallas kernels, call_first(): pl.pallas_call(lambda *refs: first_kernel(plan, len(blocks), *refs), in_s...  4.68 us
    ppermute x3, starting transfers between devices, body(): lax.ppermute(own, 'pd', ring(pd_size, k))  3.52 us
    ppermute x3, waiting for transfers between devices, body(): lax.ppermute(own, 'pd', ring(pd_size, k))  3.48 us
    pallas_call x1, Pallas kernels, call_prefill(): pl.pallas_call(lambda *refs: prefill_kernel(plan, *refs), in_specs=[SMEM]...  2.91 us
    ppermute x3, starting transfers between devices, body(): arrived.append(lax.ppermute(part, 'pd', ring(pd_size, k)))  2.77 us
    ppermute x6, waiting for transfers between devices, steps(): lax.ppermute(array, ('pd', 'tp'), [(g * self.size + a, g * self.size + b)...  1.69 us
    unnamed x4, local copies, waits for them, and re-layouts  1.22 us
  transfers between devices with their start and end apart: 12, of which 3 were waited for; matrix products, arithmetic and copies ran while one was open for 8% of the time, Pallas kernels for 18%

profile of v5, /device:TPU:0, one launch (start us, length us, event | category | flops | bytes accessed | tf_op | source)
XLA Modules:
  0.0 42.7 jit_solution(5903542008577639952)
XLA Ops:
  0.6 1.0 %pad_maximum_fusion.refs_2_ = bf16[256,512]{1,0:T(8,128)(2,1)S(1)} fusion(bf16[128,512]{1,0:T(8,128)(2,1)} %param.11, bf16[128,512]{1,0:T(8,128)(2,1)} %param.10), kind=kLoop, calls=%fused_computation | loop fusion | flops 524288 | bytes 524288 | tf_op jit(solution)/shard_map/concatenate | solution.py:433
  1.6 4.9 %collective-permute-start = (bf16[256,512]{1,0:T(8,128)(2,1)S(1)}, bf16[256,512]{1,0:T(8,128)(2,1)S(1)}, u32[]{:S(2)}, u32[]{:S(2)}) collective-permute-start(bf16[256,512]{1,0:T(8,128)(2,1)S(1)} %pad_maximum_fusion.refs_2_), channel_id=1, source_target_pairs={{0,1},{1,3},{3,2},{2,0},{8,9},{9,11},{11,10},{10,8},{16,17},{17,19... | collective-permute-start | bytes 786440 | tf_op jit(solution)/shard_map/ppermute | solution.py:48
  6.6 0.9 %pad_maximum_fusion.1 = bf16[4,2,5120]{2,1,0:T(2,128)(2,1)S(1)} fusion(bf16[4,2,512]{2,1,0:T(2,128)(2,1)} %param.16, bf16[4,2,512]{2,1,0:T(2,128)(2,1)} %param.15, bf16[4,2,4096]{2,1,0:T(2,128)(2,1)} %param.14), kind=kLoop, calls=%fused_computation.5 | loop fusion | flops 245760 | bytes 163840 | tf_op jit(solution)/shard_map/concatenate | solution.py:435
  7.6 0.7 %dynamic_slice.11 = s32[4]{0:T(128)S(1)} dynamic-slice(s32[16]{0:T(128)} %param.13, s32[]{:T(128)S(6)} %select_n.58), dynamic_slice_sizes={4} | dynamic-slice | bytes 36 | tf_op jit(solution)/shard_map/dynamic_slice | solution.py:123
  8.3 0.7 %dynamic-slice_bitcast_fusion = (s32[4]{0:T(128)S(1)}, s32[4]{0:T(128)S(1)}) fusion(s32[4,4]{1,0:T(4,128)} %constant.56.clone, s32[]{:T(128)S(6)} %select_n.60, s32[4,4]{1,0:T(4,128)} %param.12, s32[]{:T(128)S(6)} %select_n.59), kind=kLoop, calls=%fused_computation.16 | loop fusion | bytes 72 | tf_op jit(solution)/shard_map/jit(dynamic_index_in_dim)/squeeze | solution.py:125
  9.0 0.1 concatenate.11.refs_0_
  9.1 0.7 %collective-permute-start.1 = (bf16[256,512]{1,0:T(8,128)(2,1)S(1)}, bf16[256,512]{1,0:T(8,128)(2,1)S(1)}, u32[]{:S(2)}, u32[]{:S(2)}) collective-permute-start(bf16[256,512]{1,0:T(8,128)(2,1)S(1)} %pad_maximum_fusion.refs_2_), channel_id=1, source_target_pairs={{4,5},{5,7},{7,6},{6,4},{12,13},{13,15},{15,14},{14,12},{20,21},{2... | collective-permute-start | bytes 786440 | tf_op jit(solution)/shard_map/ppermute | solution.py:48
  9.8 0.8 %select_reduce_fusion = s32[4]{0:T(128)S(1)} fusion(s32[16]{0:T(128)S(1)} %and_select_fusion.1, s32[16]{0:T(128)} %param.13, s32[4]{0:T(128)S(1)} %iota_add_fusion), kind=kLoop, calls=%fused_computation.8 | loop fusion | flops 188 | bytes 160 | tf_op jit(solution)/shard_map/reduce_sum | solution.py:457
  10.6 0.0 collective-permute-done.1.refs_4_
  10.6 1.7 %collective-permute-done.refs_3_ = bf16[256,512]{1,0:T(8,128)(2,1)S(1)} collective-permute-done((bf16[256,512]{1,0:T(8,128)(2,1)S(1)}, bf16[256,512]{1,0:T(8,128)(2,1)S(1)}, u32[]{:S(2)}, u32[]{:S(2)}) %collective-permute-start) | collective-permute-done | bytes 262176 | tf_op jit(solution)/shard_map/ppermute | solution.py:48
  12.3 3.3 %collective-permute-start.2 = (bf16[256,512]{1,0:T(8,128)(2,1)S(1)}, bf16[256,512]{1,0:T(8,128)(2,1)S(1)}, u32[]{:S(2)}, u32[]{:S(2)}) collective-permute-start(bf16[256,512]{1,0:T(8,128)(2,1)S(1)} %collective-permute-done.refs_3_), channel_id=1, source_target_pairs={{0,1},{1,3},{3,2},{2,0},{8,9},{9,11},{11,10},{10,8},{16,17},{17,19... | collective-permute-start | bytes 786440 | tf_op jit(solution)/shard_map/ppermute | solution.py:48
  15.6 0.7 %collective-permute-start.3 = (bf16[256,512]{1,0:T(8,128)(2,1)S(1)}, bf16[256,512]{1,0:T(8,128)(2,1)S(1)}, u32[]{:S(2)}, u32[]{:S(2)}) collective-permute-start(bf16[256,512]{1,0:T(8,128)(2,1)S(1)} %collective-permute-done.1.refs_4_), channel_id=1, source_target_pairs={{4,5},{5,7},{7,6},{6,4},{12,13},{13,15},{15,14},{14,12},{20,21},{2... | collective-permute-start | bytes 786440 | tf_op jit(solution)/shard_map/ppermute | solution.py:48
  16.3 2.0 %collective-permute-start.4 = (bf16[8,5120]{1,0:T(8,128)(2,1)S(1)}, bf16[8,5120]{1,0:T(8,128)(2,1)S(1)}, u32[]{:S(2)}, u32[]{:S(2)}) collective-permute-start(bf16[8,5120]{1,0:T(8,128)(2,1)S(1)} %reshape.77.refs_7_), channel_id=1, source_target_pairs={{0,4},{4,8},{8,12},{12,0},{1,5},{5,9},{9,13},{13,1},{2,6},{6,10},{... | collective-permute-start | bytes 245768 | tf_op jit(solution)/shard_map/ppermute | solution.py:445
  18.3 1.5 %collective-permute-start.5 = (bf16[8,5120]{1,0:T(8,128)(2,1)S(1)}, bf16[8,5120]{1,0:T(8,128)(2,1)S(1)}, u32[]{:S(2)}, u32[]{:S(2)}) collective-permute-start(bf16[8,5120]{1,0:T(8,128)(2,1)S(1)} %reshape.77.refs_7_), channel_id=1, source_target_pairs={{0,8},{4,12},{8,0},{12,4},{1,9},{5,13},{9,1},{13,5},{2,10},{6,14},... | collective-permute-start | bytes 245768 | tf_op jit(solution)/shard_map/ppermute | solution.py:445
  19.8 0.0 collective-permute-start.6
  19.8 1.7 %collective-permute-done.4.refs_8_ = bf16[8,5120]{1,0:T(8,128)(2,1)S(1)} collective-permute-done((bf16[8,5120]{1,0:T(8,128)(2,1)S(1)}, bf16[8,5120]{1,0:T(8,128)(2,1)S(1)}, u32[]{:S(2)}, u32[]{:S(2)}) %collective-permute-start.4) | collective-permute-done | bytes 81952 | tf_op jit(solution)/shard_map/ppermute | solution.py:445
  21.5 1.8 %collective-permute-done.5.refs_9_ = bf16[8,5120]{1,0:T(8,128)(2,1)S(1)} collective-permute-done((bf16[8,5120]{1,0:T(8,128)(2,1)S(1)}, bf16[8,5120]{1,0:T(8,128)(2,1)S(1)}, u32[]{:S(2)}, u32[]{:S(2)}) %collective-permute-start.5) | collective-permute-done | bytes 81952 | tf_op jit(solution)/shard_map/ppermute | solution.py:445
  23.3 0.0 collective-permute-done.6.refs_10_
  23.3 0.0 collective-permute-done.2.refs_5_
  23.3 0.0 collective-permute-done.3.refs_6_
  23.3 5.0 %collective-permute-start.7 = (bf16[256,512]{1,0:T(8,128)(2,1)S(1)}, bf16[256,512]{1,0:T(8,128)(2,1)S(1)}, u32[]{:S(2)}, u32[]{:S(2)}) collective-permute-start(bf16[256,512]{1,0:T(8,128)(2,1)S(1)} %collective-permute-done.2.refs_5_), channel_id=1, source_target_pairs={{0,1},{1,3},{3,2},{2,0},{8,9},{9,11},{11,10},{10,8},{16,17},{17,19... | collective-permute-start | bytes 786440 | tf_op jit(solution)/shard_map/ppermute | solution.py:48
  28.3 0.7 %collective-permute-start.8 = (bf16[256,512]{1,0:T(8,128)(2,1)S(1)}, bf16[256,512]{1,0:T(8,128)(2,1)S(1)}, u32[]{:S(2)}, u32[]{:S(2)}) collective-permute-start(bf16[256,512]{1,0:T(8,128)(2,1)S(1)} %collective-permute-done.3.refs_6_), channel_id=1, source_target_pairs={{4,5},{5,7},{7,6},{6,4},{12,13},{13,15},{15,14},{14,12},{20,21},{2... | collective-permute-start | bytes 786440 | tf_op jit(solution)/shard_map/ppermute | solution.py:48
  29.0 0.0 copy-start
  29.0 1.2 %copy-done = bf16[128,4096]{1,0:T(8,128)(2,1)S(1)} copy-done((bf16[128,4096]{1,0:T(8,128)(2,1)S(1)}, bf16[128,4096]{1,0:T(8,128)(2,1)}, u32[]{:S(2)}) %copy-start) | copy-done | bytes 1048600
  30.2 0.0 copy-start.1
  30.2 4.7 %first_shards.1 = (f32[4,1024,256]{2,1,0:T(8,128)S(1)}, f32[4,1024,128]{2,1,0:T(8,128)S(1)}, f32[4,128,256]{2,1,0:T(8,128)S(1)}, f32[4,128,128]{2,1,0:T(8,128)S(1)}, bf16[16,4096]{1,0:T(8,128)(2,1)S(1)}) custom-call(s32[14]{0:T(128)S(1)} %concatenate.11.refs_0_, bf16[128,4096]{1,0:T(8,128)(2,1)S(1)} %copy-done, ...), custom_call_target="tpu_custom_call" | custom-call | flops 6442450944 | bytes 2097152 | tf_op jit(solution)/shard_map/first_shards/pallas_call | solution.py:368
  34.9 0.0 collective-permute-done.7.refs_4_
  34.9 0.0 collective-permute-done.8.refs_5_
  34.9 1.1 %last_shard_decode.1 = bf16[16,4096]{1,0:T(8,128)(2,1)S(1)} custom-call(s32[14]{0:T(128)S(1)} %concatenate.11.refs_0_, f32[4,128,256]{2,1,0:T(8,128)S(1)} %get-tuple-element.41.refs_1_, f32[4,128,128]{2,1,0:T(8,128)S(1)} %get-tuple-element.42.refs_2_, bf16[16,4096]{1,0:T(8,128)(2,1)S(1)} %get-tuple-element.43.refs_3_, ...), custom_call_target="tpu_custom_call" | custom-call | flops 268435456 | bytes 262144 | tf_op jit(solution)/shard_map/last_shard_decode/pallas_call | solution.py:386
  36.1 0.1 fusion.1
  36.1 1.0 %collective-permute-start.10 = (bf16[2,4096]{1,0:T(2,128)(2,1)S(1)}, bf16[2,4096]{1,0:T(2,128)(2,1)S(1)}, u32[]{:S(2)}, u32[]{:S(2)}) collective-permute-start(bf16[2,4096]{1,0:T(2,128)(2,1)S(1)} %get-tuple-element.49), channel_id=1, source_target_pairs={{0,8},{4,12},{8,0},{12,4},{1,9},{5,13},{9,1},{13,5},{2,10},{6,14},... | collective-permute-start | bytes 49160 | tf_op jit(solution)/shard_map/ppermute | solution.py:452
  37.2 0.2 collective-permute-start.11
  37.4 1.5 %collective-permute-start.9 = (bf16[2,4096]{1,0:T(2,128)(2,1)S(1)}, bf16[2,4096]{1,0:T(2,128)(2,1)S(1)}, u32[]{:S(2)}, u32[]{:S(2)}) collective-permute-start(bf16[2,4096]{1,0:T(2,128)(2,1)S(1)} %get-tuple-element.46), channel_id=1, source_target_pairs={{0,12},{4,0},{8,4},{12,8},{1,13},{5,1},{9,5},{13,9},{2,14},{6,2},{... | collective-permute-start | bytes 49160 | tf_op jit(solution)/shard_map/ppermute | solution.py:452
  38.9 0.0 copy-done.1
  38.9 2.9 %last_shard_prefill.1 = bf16[128,4096]{1,0:T(8,128)(2,1)} custom-call(s32[14]{0:T(128)S(1)} %concatenate.11.refs_0_, bf16[128,4096]{1,0:T(8,128)(2,1)S(1)} %copy-done.1, f32[4,1024,256]{2,1,0:T(8,128)S(1)} %get-tuple-element.39.refs_2_, f32[4,1024,128]{2,1,0:T(8,128)S(1)} %get-tuple-element.40.refs_3_, bf16[256,512]{1,0:T(8,128)(2,1)S(1)} %collective-permute-done.7.refs_4_, ...), custom_call_target="tpu_custom_call" | custom-call | flops 2147483648 | bytes 2097152 | tf_op jit(solution)/shard_map/last_shard_prefill/pallas_call | solution.py:399
  41.8 0.0 collective-permute-done.10
  41.8 0.0 collective-permute-done.11
  41.9 0.0 collective-permute-done.9
  41.9 0.8 %broadcast_select_fusion.2 = bf16[4,2,4096]{2,1,0:T(2,128)(2,1)} fusion(pred[4]{0:T(512)(128)(4,1)S(1)} %get-tuple-element.52, pred[4]{0:T(512)(128)(4,1)S(1)} %get-tuple-element.51, pred[4]{0:T(512)(128)(4,1)S(1)} %get-tuple-element.50, pred[4]{0:T(512)(128)(4,1)S(1)} %get-tuple-element.44, bf16[2,4096]{1,0:T(2,128)(2,1)S(1)} %get-tuple-element.47, ...), kind=kLoop, calls=%fused_computation.3 | loop fusion | flops 131072 | bytes 131088 | tf_op jit(solution)/shard_map/jit(_where)/select_n | solution.py:463
  (5 shorter events, 0.1 us)
Async XLA Ops:
  1.6 10.7 %collective-permute-start = (bf16[256,512]{1,0:T(8,128)(2,1)S(1)}, bf16[256,512]{1,0:T(8,128)(2,1)S(1)}, u32[]{:S(2)}, u32[]{:S(2)}) collective-permute-start(bf16[256,512]{1,0:T(8,128)(2,1)S(1)} %pad_maximum_fusion.refs_2_), channel_id=1, source_target_pairs={{0,1},{1,3},{3,2},{2,0},{8,9},{9,11},{11,10},{10,8},{16,17},{17,19... | collective-permute-start | bytes 786440 | tf_op jit(solution)/shard_map/ppermute | solution.py:48
  9.1 1.5 %collective-permute-start.1 = (bf16[256,512]{1,0:T(8,128)(2,1)S(1)}, bf16[256,512]{1,0:T(8,128)(2,1)S(1)}, u32[]{:S(2)}, u32[]{:S(2)}) collective-permute-start(bf16[256,512]{1,0:T(8,128)(2,1)S(1)} %pad_maximum_fusion.refs_2_), channel_id=1, source_target_pairs={{4,5},{5,7},{7,6},{6,4},{12,13},{13,15},{15,14},{14,12},{20,21},{2... | collective-permute-start | bytes 786440 | tf_op jit(solution)/shard_map/ppermute | solution.py:48
  12.3 11.0 %collective-permute-start.2 = (bf16[256,512]{1,0:T(8,128)(2,1)S(1)}, bf16[256,512]{1,0:T(8,128)(2,1)S(1)}, u32[]{:S(2)}, u32[]{:S(2)}) collective-permute-start(bf16[256,512]{1,0:T(8,128)(2,1)S(1)} %collective-permute-done.refs_3_), channel_id=1, source_target_pairs={{0,1},{1,3},{3,2},{2,0},{8,9},{9,11},{11,10},{10,8},{16,17},{17,19... | collective-permute-start | bytes 786440 | tf_op jit(solution)/shard_map/ppermute | solution.py:48
  15.6 7.7 %collective-permute-start.3 = (bf16[256,512]{1,0:T(8,128)(2,1)S(1)}, bf16[256,512]{1,0:T(8,128)(2,1)S(1)}, u32[]{:S(2)}, u32[]{:S(2)}) collective-permute-start(bf16[256,512]{1,0:T(8,128)(2,1)S(1)} %collective-permute-done.1.refs_4_), channel_id=1, source_target_pairs={{4,5},{5,7},{7,6},{6,4},{12,13},{13,15},{15,14},{14,12},{20,21},{2... | collective-permute-start | bytes 786440 | tf_op jit(solution)/shard_map/ppermute | solution.py:48
  16.3 5.2 %collective-permute-start.4 = (bf16[8,5120]{1,0:T(8,128)(2,1)S(1)}, bf16[8,5120]{1,0:T(8,128)(2,1)S(1)}, u32[]{:S(2)}, u32[]{:S(2)}) collective-permute-start(bf16[8,5120]{1,0:T(8,128)(2,1)S(1)} %reshape.77.refs_7_), channel_id=1, source_target_pairs={{0,4},{4,8},{8,12},{12,0},{1,5},{5,9},{9,13},{13,1},{2,6},{6,10},{... | collective-permute-start | bytes 245768 | tf_op jit(solution)/shard_map/ppermute | solution.py:445
  18.3 5.0 %collective-permute-start.5 = (bf16[8,5120]{1,0:T(8,128)(2,1)S(1)}, bf16[8,5120]{1,0:T(8,128)(2,1)S(1)}, u32[]{:S(2)}, u32[]{:S(2)}) collective-permute-start(bf16[8,5120]{1,0:T(8,128)(2,1)S(1)} %reshape.77.refs_7_), channel_id=1, source_target_pairs={{0,8},{4,12},{8,0},{12,4},{1,9},{5,13},{9,1},{13,5},{2,10},{6,14},... | collective-permute-start | bytes 245768 | tf_op jit(solution)/shard_map/ppermute | solution.py:445
  19.8 3.5 %collective-permute-start.6 = (bf16[8,5120]{1,0:T(8,128)(2,1)S(1)}, bf16[8,5120]{1,0:T(8,128)(2,1)S(1)}, u32[]{:S(2)}, u32[]{:S(2)}) collective-permute-start(bf16[8,5120]{1,0:T(8,128)(2,1)S(1)} %reshape.77.refs_7_), channel_id=1, source_target_pairs={{0,12},{4,0},{8,4},{12,8},{1,13},{5,1},{9,5},{13,9},{2,14},{6,2},{... | collective-permute-start | bytes 245768 | tf_op jit(solution)/shard_map/ppermute | solution.py:445
  23.3 11.6 %collective-permute-start.7 = (bf16[256,512]{1,0:T(8,128)(2,1)S(1)}, bf16[256,512]{1,0:T(8,128)(2,1)S(1)}, u32[]{:S(2)}, u32[]{:S(2)}) collective-permute-start(bf16[256,512]{1,0:T(8,128)(2,1)S(1)} %collective-permute-done.2.refs_5_), channel_id=1, source_target_pairs={{0,1},{1,3},{3,2},{2,0},{8,9},{9,11},{11,10},{10,8},{16,17},{17,19... | collective-permute-start | bytes 786440 | tf_op jit(solution)/shard_map/ppermute | solution.py:48
  28.3 6.6 %collective-permute-start.8 = (bf16[256,512]{1,0:T(8,128)(2,1)S(1)}, bf16[256,512]{1,0:T(8,128)(2,1)S(1)}, u32[]{:S(2)}, u32[]{:S(2)}) collective-permute-start(bf16[256,512]{1,0:T(8,128)(2,1)S(1)} %collective-permute-done.3.refs_6_), channel_id=1, source_target_pairs={{4,5},{5,7},{7,6},{6,4},{12,13},{13,15},{15,14},{14,12},{20,21},{2... | collective-permute-start | bytes 786440 | tf_op jit(solution)/shard_map/ppermute | solution.py:48
  29.0 1.2 %copy-start = (bf16[128,4096]{1,0:T(8,128)(2,1)S(1)}, bf16[128,4096]{1,0:T(8,128)(2,1)}, u32[]{:S(2)}) copy-start(bf16[128,4096]{1,0:T(8,128)(2,1)} %refs_1_.3) | copy-start | bytes 3145732
  30.2 8.7 %copy-start.1 = (bf16[128,4096]{1,0:T(8,128)(2,1)S(1)}, bf16[128,4096]{1,0:T(8,128)(2,1)}, u32[]{:S(2)}) copy-start(bf16[128,4096]{1,0:T(8,128)(2,1)} %refs_1_.3) | copy-start | bytes 3145732
  36.1 5.7 %collective-permute-start.10 = (bf16[2,4096]{1,0:T(2,128)(2,1)S(1)}, bf16[2,4096]{1,0:T(2,128)(2,1)S(1)}, u32[]{:S(2)}, u32[]{:S(2)}) collective-permute-start(bf16[2,4096]{1,0:T(2,128)(2,1)S(1)} %get-tuple-element.49), channel_id=1, source_target_pairs={{0,8},{4,12},{8,0},{12,4},{1,9},{5,13},{9,1},{13,5},{2,10},{6,14},... | collective-permute-start | bytes 49160 | tf_op jit(solution)/shard_map/ppermute | solution.py:452
  37.2 4.7 %collective-permute-start.11 = (bf16[2,4096]{1,0:T(2,128)(2,1)S(1)}, bf16[2,4096]{1,0:T(2,128)(2,1)S(1)}, u32[]{:S(2)}, u32[]{:S(2)}) collective-permute-start(bf16[2,4096]{1,0:T(2,128)(2,1)S(1)} %get-tuple-element.48), channel_id=1, source_target_pairs={{0,4},{4,8},{8,12},{12,0},{1,5},{5,9},{9,13},{13,1},{2,6},{6,10},{... | collective-permute-start | bytes 49160 | tf_op jit(solution)/shard_map/ppermute | solution.py:452
  37.4 4.5 %collective-permute-start.9 = (bf16[2,4096]{1,0:T(2,128)(2,1)S(1)}, bf16[2,4096]{1,0:T(2,128)(2,1)S(1)}, u32[]{:S(2)}, u32[]{:S(2)}) collective-permute-start(bf16[2,4096]{1,0:T(2,128)(2,1)S(1)} %get-tuple-element.46), channel_id=1, source_target_pairs={{0,12},{4,0},{8,4},{12,8},{1,13},{5,1},{9,5},{13,9},{2,14},{6,2},{... | collective-permute-start | bytes 49160 | tf_op jit(solution)/shard_map/ppermute | solution.py:452

commit v6 on v4

--- a/solution.py
+++ b/solution.py
@@ -144,12 +144,16 @@
         lax.fori_loop(0, KEY_VALUE_HEADS, lambda h, c: (step(h), c)[1], 0)
 
 
-def first_kernel(plan, pd_size, facts_ref, q_hbm_ref, *refs):
+def first_kernel(plan, pd_size, facts_ref, q_hbm_ref, k_hbm_ref, v_hbm_ref, *refs):
     width = plan.size
-    kv_refs, refs = refs[: width - 1], refs[width - 1 :]
+    k_refs, v_refs, refs = refs[: width - 2], refs[width - 2 : 2 * width - 4], refs[2 * width - 4 :]
     block_refs, refs = refs[:pd_size], refs[pd_size:]
-    acc_ref, top_ref, dec_acc_ref, dec_top_ref, queries_ref, q_ref, fresh_ref, sem = refs
-    copies = []
+    acc_ref, top_ref, dec_acc_ref, dec_top_ref, queries_ref, q_ref, k_ref, v_ref, fresh_ref, sem = refs
+    k_refs, v_refs = (k_ref,) + k_refs, (v_ref,) + v_refs
+    copies = [
+        pltpu.make_async_copy(k_hbm_ref, k_ref, sem.at[KEY_VALUE_HEADS]),
+        pltpu.make_async_copy(v_hbm_ref, v_ref, sem.at[KEY_VALUE_HEADS + 1]),
+    ]
     for h in range(KEY_VALUE_HEADS):
         part = pl.ds(h * Q_BLOCK, Q_BLOCK)
         copies.append(pltpu.make_async_copy(q_hbm_ref.at[:, part], q_ref.at[:, part], sem.at[h]))
@@ -193,8 +197,8 @@
         first = h * Q_BLOCK
         queries = stacked_heads(queries_ref, slice(None), first, HEADS_PER_KV)
         fresh_scores = jnp.where(fresh_mask, scores_of(queries, fresh_ref[:, columns]), MASKED)
-        k_all = jnp.concatenate([ref[:tokens, columns] for ref in kv_refs], axis=0)
-        v_all = with_ones(jnp.concatenate([ref[tokens:, columns] for ref in kv_refs], axis=0))
+        k_all = jnp.concatenate([ref[:, columns] for ref in k_refs], axis=0)
+        v_all = with_ones(jnp.concatenate([ref[:, columns] for ref in v_refs], axis=0))
         scores = jnp.where(mask, scores_of(queries, k_all), MASKED)
         top = jnp.maximum(
             jnp.max(scores, axis=1, keepdims=True), jnp.max(fresh_scores, axis=1, keepdims=True)
@@ -206,8 +210,8 @@
         dec_top_ref[h] = jnp.broadcast_to(top, (STACKED, HEAD_SIZE))
         for (start, keys), bias in zip(spans, biases):
             if keys < tokens:
-                k_part = jnp.concatenate([ref[:keys, columns] for ref in kv_refs], axis=0)
-                v_part = with_ones(jnp.concatenate([ref[tokens : tokens + keys, columns] for ref in kv_refs], axis=0))
+                k_part = jnp.concatenate([ref[:keys, columns] for ref in k_refs], axis=0)
+                v_part = with_ones(jnp.concatenate([ref[:keys, columns] for ref in v_refs], axis=0))
             else:
                 k_part, v_part = k_all, v_all
             for g in range(0, HEADS_PER_KV, together):
@@ -241,9 +245,9 @@
     return acc * jnp.concatenate([factor, factor], axis=1) + product(weights, with_ones(values))
 
 
-def decode_kernel(plan, pd_size, facts_ref, acc_ref, top_ref, queries_ref, kv_ref, out_ref):
+def decode_kernel(plan, pd_size, facts_ref, acc_ref, top_ref, queries_ref, k_ref, v_ref, out_ref):
     width = plan.size
-    tokens = kv_ref.shape[0] // 2
+    tokens = k_ref.shape[0]
     facts = Facts(facts_ref, width)
     mask = request_mask(facts.ends, tokens, facts.source[-1:], width)
     row = iota((PADDED_ROWS, PADDED_ROWS), 0)
@@ -259,18 +263,18 @@
     heads = range(KEY_VALUE_HEADS)
     columns = [slice(h * HEAD_SIZE, (h + 1) * HEAD_SIZE) for h in heads]
     scores = [
-        scores_of(stacked_heads(queries_ref, slice(None), h * Q_BLOCK, HEADS_PER_KV), kv_ref[:tokens, columns[h]])
+        scores_of(stacked_heads(queries_ref, slice(None), h * Q_BLOCK, HEADS_PER_KV), k_ref[:, columns[h]])
         for h in heads
     ]
     scores = [jnp.where(mask, s, MASKED) for s in scores]
-    out = [divided(merge(acc_ref[h], top_ref[h], scores[h], kv_ref[tokens:, columns[h]])) for h in heads]
+    out = [divided(merge(acc_ref[h], top_ref[h], scores[h], v_ref[:, columns[h]])) for h in heads]
     out = jnp.concatenate(
         [o[g * PADDED_ROWS : (g + 1) * PADDED_ROWS] for o in out for g in range(HEADS_PER_KV)], axis=1
     )
     out_ref[...] = product(pick, out).astype(jnp.bfloat16)
 
 
-def prefill_kernel(plan, facts_ref, q_ref, acc_ref, top_ref, kv_ref, out_ref, done_ref, sem):
+def prefill_kernel(plan, facts_ref, q_ref, acc_ref, top_ref, k_ref, v_ref, out_ref, done_ref, sem):
     width = plan.size
     tokens = q_ref.shape[0]
     half = tokens // 2
@@ -285,7 +289,7 @@
         worst = jnp.full((half, tokens), MASKED, jnp.float32)
         for h in range(KEY_VALUE_HEADS):
             columns = slice(h * HEAD_SIZE, (h + 1) * HEAD_SIZE)
-            keys, values = kv_ref[:tokens, columns], kv_ref[tokens:, columns]
+            keys, values = k_ref[:, columns], v_ref[:, columns]
             for start, bias in zip((0, half), biases):
                 queries = stacked_heads(q_ref, slice(start, start + half), h * Q_BLOCK, HEADS_PER_KV)
                 scores = scores_of(queries, keys).reshape(HEADS_PER_KV, half, tokens) + bias[None]
@@ -324,7 +328,7 @@
     )
 
 
-def call_first(plan, facts, query, blocks, pieces):
+def call_first(plan, facts, query, blocks, keys, values):
     tokens, width = query.shape[0], plan.size
     rows = HEADS_PER_KV * tokens
     f32, bf16 = jnp.float32, jnp.bfloat16
@@ -338,38 +342,40 @@
     every = (width - 1) * tokens
     return pl.pallas_call(
         lambda *refs: first_kernel(plan, len(blocks), *refs),
-        in_specs=[SMEM, ANY] + [VMEM] * (len(blocks) + width - 1),
+        in_specs=[SMEM] + [ANY] * 3 + [VMEM] * (len(blocks) + 2 * (width - 2)),
         out_specs=[VMEM] * len(shapes),
         out_shape=shapes,
         scratch_shapes=[
             pltpu.VMEM((tokens, Q_WIDTH), bf16),
+            pltpu.VMEM((tokens, KV_WIDTH), bf16),
+            pltpu.VMEM((tokens, KV_WIDTH), bf16),
             pltpu.VMEM((PADDED_ROWS, 2 * KV_WIDTH), bf16),
-            pltpu.SemaphoreType.DMA((KEY_VALUE_HEADS,)),
+            pltpu.SemaphoreType.DMA((KEY_VALUE_HEADS + 2,)),
         ],
         compiler_params=pltpu.CompilerParams(vmem_limit_bytes=(28 + width) * MIB),
         cost_estimate=cost(tokens, every, tokens * every * QUERY_HEADS),
         name="first_shards",
-    )(facts, query, *pieces, *blocks)
-
-
-def call_decode(plan, pd_size, facts, state, piece):
-    tokens = piece.shape[0] // 2
+    )(facts, query, keys[0], values[0], *keys[1:], *values[1:], *blocks)
+
+
+def call_decode(plan, pd_size, facts, state, key, value):
+    tokens = key.shape[0]
     return pl.pallas_call(
         lambda *refs: decode_kernel(plan, pd_size, *refs),
-        in_specs=[SMEM] + [VMEM] * 4,
+        in_specs=[SMEM] + [VMEM] * 5,
         out_specs=VMEM,
         out_shape=jax.ShapeDtypeStruct((PADDED_ROWS, Q_WIDTH), jnp.bfloat16),
         compiler_params=pltpu.CompilerParams(vmem_limit_bytes=32 * MIB),
         cost_estimate=cost(PADDED_ROWS, tokens, PADDED_ROWS * tokens * QUERY_HEADS),
         name="last_shard_decode",
-    )(facts, *state[2:], piece)
-
-
-def call_prefill(plan, facts, query, state, piece):
+    )(facts, *state[2:], key, value)
+
+
+def call_prefill(plan, facts, query, state, key, value):
     tokens = query.shape[0]
     return pl.pallas_call(
         lambda *refs: prefill_kernel(plan, *refs),
-        in_specs=[SMEM] + [VMEM] * 4,
+        in_specs=[SMEM] + [VMEM] * 5,
         out_specs=ANY,
         out_shape=jax.ShapeDtypeStruct((tokens, Q_WIDTH), jnp.bfloat16),
         scratch_shapes=[
@@ -379,7 +385,23 @@
         compiler_params=pltpu.CompilerParams(vmem_limit_bytes=32 * MIB),
         cost_estimate=cost(tokens, tokens, tokens * tokens * QUERY_HEADS),
         name="last_shard_prefill",
-    )(facts, query, *state[:2], piece)
+    )(facts, query, *state[:2], key, value)
+
+
+def after(row, *arrays):
+    def kernel(row_ref, *refs):
+        out_ref = refs[-1]
+        for i in range(row.shape[0]):
+            out_ref[i] = row_ref[i]
+
+    return pl.pallas_call(
+        kernel,
+        in_specs=[SMEM] + [ANY] * len(arrays),
+        out_specs=SMEM,
+        out_shape=jax.ShapeDtypeStruct(row.shape, row.dtype),
+        cost_estimate=pl.CostEstimate(flops=5 * 10**9, bytes_accessed=0, transcendentals=0),
+        name="after",
+    )(row, *arrays)
 
 
 def ring(size, step):
@@ -399,28 +421,31 @@
     plan = Ring(lax.axis_size("tp"))
     pd_size = lax.axis_size("pd")
     my_group = lax.axis_index("pd")
-    facts = facts_row(plan, prompt_lengths, decode_slot)
-    pieces, blocks = [jnp.concatenate([prompt_key, prompt_value], axis=0)], None
-    pieces[0], decoded_query = lax.optimization_barrier((pieces[0], decoded_query))
     own = jnp.concatenate([decoded_query, decoded_key, decoded_value], axis=2).reshape(
         DECODE_ROWS, Q_WIDTH + 2 * KV_WIDTH
     )
+    facts = facts_row(plan, prompt_lengths, decode_slot)
+    prompt_key, decoded_query = lax.optimization_barrier((prompt_key, decoded_query))
+    prompt_value, own, facts = lax.optimization_barrier((prompt_value, own, facts))
+    keys, values = [prompt_key], [prompt_value]
     for s in range(1, plan.size):
         if s == 2:
-            pieces[1], own, facts = lax.optimization_barrier((pieces[1], own, facts))
+            keys[1], own = lax.optimization_barrier((keys[1], own))
         if s == plan.size - 1:
-            pieces, blocks = lax.optimization_barrier((pieces, blocks))
-        pieces.append(plan.step(pieces[-1]))
+            facts = after(facts, keys[-1], values[-1])
+            values[-1], blocks, facts = lax.optimization_barrier((values[-1], blocks, facts))
+        keys.append(plan.step(keys[-1]))
+        values.append(plan.step(values[-1]))
         if s == 2:
             blocks = [own] + [lax.ppermute(own, "pd", ring(pd_size, k)) for k in range(1, pd_size)]
 
-    state = call_first(plan, facts, prompt_query, blocks, pieces[:-1])
-    outgoing = call_decode(plan, pd_size, facts, state, pieces[-1])
+    state = call_first(plan, facts, prompt_query, blocks, keys[:-1], values[:-1])
+    outgoing = call_decode(plan, pd_size, facts, state, keys[-1], values[-1])
     arrived = [outgoing[:DECODE_STEPS]]
     for k in range(1, pd_size):
         part = outgoing[k * DECODE_STEPS : (k + 1) * DECODE_STEPS]
         arrived.append(lax.ppermute(part, "pd", ring(pd_size, k)))
-    pre_out = call_prefill(plan, facts, prompt_query, state, pieces[-1])
+    pre_out = call_prefill(plan, facts, prompt_query, state, keys[-1], values[-1])
 
     numbers = jnp.arange(decode_slot.shape[0], dtype=jnp.int32)
     wanted = my_group * GROUP_REQUESTS + jnp.arange(GROUP_REQUESTS, dtype=jnp.int32)

time: 36.6 us -> 40.6 us (1.11)
  the two profiles are of different devices: /device:TPU:9 before, /device:TPU:0 now
where the time goes in v6:
time: 40.6 us; the launch traced here: 40.3 us
  starting transfers between devices  17.8 us (44%)
  Pallas kernels  10.3 us (25%)
  local copies, waits for them, and re-layouts  5.49 us (14%)
  waiting for transfers between devices  3.38 us (8%)
  other arithmetic  2.61 us (6%)
  between operations  0.78 us (2%)
    ppermute x6, starting transfers between devices, step(): return lax.ppermute(array, 'tp', self.pairs)  11.5 us
    pallas_call x1, Pallas kernels, call_first(): pl.pallas_call(lambda *refs: first_kernel(plan, len(blocks), *refs), in_s...  5.02 us
    ppermute x6, waiting for transfers between devices, step(): return lax.ppermute(array, 'tp', self.pairs)  3.34 us
    unnamed x16, local copies, waits for them, and re-layouts  3.33 us
    ppermute x3, starting transfers between devices, body(): arrived.append(lax.ppermute(part, 'pd', ring(pd_size, k)))  3.3 us
    ppermute x3, starting transfers between devices, body(): lax.ppermute(own, 'pd', ring(pd_size, k))  3 us
    pallas_call x1, Pallas kernels, call_prefill(): pl.pallas_call(lambda *refs: prefill_kernel(plan, *refs), in_specs=[SMEM]...  2.93 us
    pallas_call x1, Pallas kernels, after(): pl.pallas_call(kernel, in_specs=[SMEM] + [ANY] * len(arrays), out_specs=S...  1.19 us
  transfers between devices with their start and end apart: 12, of which 2 were waited for; matrix products, arithmetic and copies ran while one was open for 10% of the time, Pallas kernels for 23%

profile of v6, /device:TPU:0, one launch (start us, length us, event | category | flops | bytes accessed | tf_op | source)
XLA Modules:
  0.0 40.3 jit_solution(13463980205854650542)
XLA Ops:
  0.6 3.1 %collective-permute-start.2 = (bf16[128,512]{1,0:T(8,128)(2,1)}, bf16[128,512]{1,0:T(8,128)(2,1)S(1)}, u32[]{:S(2)}, u32[]{:S(2)}) collective-permute-start(bf16[128,512]{1,0:T(8,128)(2,1)} %refs_2_), channel_id=1, source_target_pairs={{0,1},{1,3},{3,2},{2,0},{4,5},{5,7},{7,6},{6,4},{8,9},{9,11},{11,1... | collective-permute-start | bytes 393224 | tf_op jit(solution)/shard_map/ppermute | solution.py:46
  3.7 0.9 %pad_maximum_fusion = bf16[4,2,5120]{2,1,0:T(2,128)(2,1)S(1)} fusion(bf16[4,2,512]{2,1,0:T(2,128)(2,1)} %param.16, bf16[4,2,512]{2,1,0:T(2,128)(2,1)} %param.15, bf16[4,2,4096]{2,1,0:T(2,128)(2,1)} %param.14), kind=kLoop, calls=%fused_computation.4 | loop fusion | flops 245760 | bytes 163840 | tf_op jit(solution)/shard_map/concatenate | solution.py:424
  4.7 0.7 %dynamic_slice.11 = s32[4]{0:T(128)S(1)} dynamic-slice(s32[16]{0:T(128)} %param.13, s32[]{:T(128)S(6)} %select_n.58), dynamic_slice_sizes={4} | dynamic-slice | bytes 36 | tf_op jit(solution)/shard_map/dynamic_slice | solution.py:106
  5.4 0.7 %dynamic-slice_bitcast_fusion = (s32[4]{0:T(128)S(1)}, s32[4]{0:T(128)S(1)}) fusion(s32[4,4]{1,0:T(4,128)} %constant.56.clone, s32[]{:T(128)S(6)} %select_n.60, s32[4,4]{1,0:T(4,128)} %param.12, s32[]{:T(128)S(6)} %select_n.59), kind=kLoop, calls=%fused_computation.15 | loop fusion | bytes 72 | tf_op jit(solution)/shard_map/jit(dynamic_index_in_dim)/squeeze | solution.py:108
  6.1 0.6 %concatenate.7.row_ref = s32[14]{0:T(128)} concatenate(s32[1]{0:T(128)} %bitcast, s32[1]{0:T(128)} %bitcast.1, s32[4]{0:T(128)S(1)} %dynamic_slice.11, s32[4]{0:T(128)S(1)} %get-tuple-element.46, s32[4]{0:T(128)S(1)} %get-tuple-element.45), dimensions={0} | concatenate | bytes 112 | tf_op jit(solution)/shard_map/concatenate | solution.py:103
  6.8 2.6 %collective-permute-start = (bf16[128,512]{1,0:T(8,128)(2,1)}, bf16[128,512]{1,0:T(8,128)(2,1)S(1)}, u32[]{:S(2)}, u32[]{:S(2)}) collective-permute-start(bf16[128,512]{1,0:T(8,128)(2,1)} %refs_3_), channel_id=1, source_target_pairs={{0,1},{1,3},{3,2},{2,0},{4,5},{5,7},{7,6},{6,4},{8,9},{9,11},{11,1... | collective-permute-start | bytes 393224 | tf_op jit(solution)/shard_map/ppermute | solution.py:46
  9.4 0.8 %select_reduce_fusion = s32[4]{0:T(128)S(1)} fusion(s32[16]{0:T(128)S(1)} %and_select_fusion.1, s32[16]{0:T(128)} %param.13, s32[4]{0:T(128)S(1)} %iota_add_fusion), kind=kLoop, calls=%fused_computation.7 | loop fusion | flops 188 | bytes 160 | tf_op jit(solution)/shard_map/reduce_sum | solution.py:452
  10.2 0.0 collective-permute-done.2.refs_4_
  10.2 0.5 %collective-permute-start.6 = (bf16[128,512]{1,0:T(8,128)(2,1)S(1)}, bf16[128,512]{1,0:T(8,128)(2,1)S(1)}, u32[]{:S(2)}, u32[]{:S(2)}) collective-permute-start(bf16[128,512]{1,0:T(8,128)(2,1)S(1)} %collective-permute-done.2.refs_4_), channel_id=1, source_target_pairs={{0,1},{1,3},{3,2},{2,0},{4,5},{5,7},{7,6},{6,4},{8,9},{9,11},{11,1... | collective-permute-start | bytes 393224 | tf_op jit(solution)/shard_map/ppermute | solution.py:46
  10.7 2.9 %collective-permute-done.refs_6_ = bf16[128,512]{1,0:T(8,128)(2,1)S(1)} collective-permute-done((bf16[128,512]{1,0:T(8,128)(2,1)}, bf16[128,512]{1,0:T(8,128)(2,1)S(1)}, u32[]{:S(2)}, u32[]{:S(2)}) %collective-permute-start) | collective-permute-done | bytes 131104 | tf_op jit(solution)/shard_map/ppermute | solution.py:46
  13.6 2.4 %collective-permute-start.1 = (bf16[128,512]{1,0:T(8,128)(2,1)S(1)}, bf16[128,512]{1,0:T(8,128)(2,1)S(1)}, u32[]{:S(2)}, u32[]{:S(2)}) collective-permute-start(bf16[128,512]{1,0:T(8,128)(2,1)S(1)} %collective-permute-done.refs_6_), channel_id=1, source_target_pairs={{0,1},{1,3},{3,2},{2,0},{4,5},{5,7},{7,6},{6,4},{8,9},{9,11},{11,1... | collective-permute-start | bytes 393224 | tf_op jit(solution)/shard_map/ppermute | solution.py:46
  16.0 0.0 copy-start
  16.0 0.0 copy-start.2
  16.0 0.0 copy-start.3
  16.0 0.1 collective-permute-start.3
  16.1 1.6 %collective-permute-start.4 = (bf16[8,5120]{1,0:T(8,128)(2,1)S(1)}, bf16[8,5120]{1,0:T(8,128)(2,1)S(1)}, u32[]{:S(2)}, u32[]{:S(2)}) collective-permute-start(bf16[8,5120]{1,0:T(8,128)(2,1)S(1)} %reshape.77.refs_8_), channel_id=1, source_target_pairs={{0,8},{4,12},{8,0},{12,4},{1,9},{5,13},{9,1},{13,5},{2,10},{6,14},... | collective-permute-start | bytes 245768 | tf_op jit(solution)/shard_map/ppermute | solution.py:440
  17.6 1.4 %collective-permute-start.5 = (bf16[8,5120]{1,0:T(8,128)(2,1)S(1)}, bf16[8,5120]{1,0:T(8,128)(2,1)S(1)}, u32[]{:S(2)}, u32[]{:S(2)}) collective-permute-start(bf16[8,5120]{1,0:T(8,128)(2,1)S(1)} %reshape.77.refs_8_), channel_id=1, source_target_pairs={{0,12},{4,0},{8,4},{12,8},{1,13},{5,1},{9,5},{13,9},{2,14},{6,2},{... | collective-permute-start | bytes 245768 | tf_op jit(solution)/shard_map/ppermute | solution.py:440
  19.0 0.0 collective-permute-done.6.refs_0_.refs_5_
  19.0 0.0 copy-start.4
  19.0 0.4 %collective-permute-done.1.refs_1_.refs_7_ = bf16[128,512]{1,0:T(8,128)(2,1)S(1)} collective-permute-done((bf16[128,512]{1,0:T(8,128)(2,1)S(1)}, bf16[128,512]{1,0:T(8,128)(2,1)S(1)}, u32[]{:S(2)}, u32[]{:S(2)}) %collective-permute-start.1) | collective-permute-done | bytes 131104 | tf_op jit(solution)/shard_map/ppermute | solution.py:46
  19.5 0.2 copy-done.4
  19.7 0.0 copy-start.6
  19.7 0.6 %copy-done.6 = bf16[128,512]{1,0:T(8,128)(2,1)} copy-done((bf16[128,512]{1,0:T(8,128)(2,1)}, bf16[128,512]{1,0:T(8,128)(2,1)S(1)}, u32[]{:S(2)}) %copy-start.6) | copy-done | bytes 131096
  20.3 1.2 %after.1.refs_0_ = s32[14]{0:T(128)} custom-call(s32[14]{0:T(128)} %concatenate.7.row_ref, bf16[128,512]{1,0:T(8,128)(2,1)} %copy-done.4, bf16[128,512]{1,0:T(8,128)(2,1)} %copy-done.6), custom_call_target="tpu_custom_call" | custom-call | flops 5000000000 | tf_op jit(solution)/shard_map/after/pallas_call | solution.py:397
  21.5 0.0 collective-permute-done.3.refs_9_
  21.5 0.0 collective-permute-done.4.refs_10_
  21.6 0.0 collective-permute-done.5.refs_11_
  21.6 1.3 %collective-permute-start.8 = (bf16[128,512]{1,0:T(8,128)(2,1)}, bf16[128,512]{1,0:T(8,128)(2,1)S(1)}, u32[]{:S(2)}, u32[]{:S(2)}) collective-permute-start(bf16[128,512]{1,0:T(8,128)(2,1)} %copy-done.6), channel_id=1, source_target_pairs={{0,1},{1,3},{3,2},{2,0},{4,5},{5,7},{7,6},{6,4},{8,9},{9,11},{11,1... | collective-permute-start | bytes 393224 | tf_op jit(solution)/shard_map/ppermute | solution.py:46
  22.9 1.6 %collective-permute-start.7 = (bf16[128,512]{1,0:T(8,128)(2,1)}, bf16[128,512]{1,0:T(8,128)(2,1)S(1)}, u32[]{:S(2)}, u32[]{:S(2)}) collective-permute-start(bf16[128,512]{1,0:T(8,128)(2,1)} %copy-done.4), channel_id=1, source_target_pairs={{0,1},{1,3},{3,2},{2,0},{4,5},{5,7},{7,6},{6,4},{8,9},{9,11},{11,1... | collective-permute-start | bytes 393224 | tf_op jit(solution)/shard_map/ppermute | solution.py:46
  24.5 0.0 copy-done
  24.5 0.0 copy-done.2
  24.5 0.0 copy-done.3
  24.5 0.0 copy-start.1
  24.6 0.6 %copy-done.1 = s32[14]{0:T(128)S(1)} copy-done((s32[14]{0:T(128)S(1)}, s32[14]{0:T(128)}, u32[]{:S(2)}) %copy-start.1) | copy-done | bytes 80
  25.2 0.0 copy-start.5
  25.2 0.9 %copy-done.5 = bf16[128,512]{1,0:T(8,128)(2,1)S(1)} copy-done((bf16[128,512]{1,0:T(8,128)(2,1)S(1)}, bf16[128,512]{1,0:T(8,128)(2,1)}, u32[]{:S(2)}) %copy-start.5) | copy-done | bytes 131096
  26.1 0.0 copy-start.7
  26.1 0.9 %copy-done.7 = bf16[128,512]{1,0:T(8,128)(2,1)S(1)} copy-done((bf16[128,512]{1,0:T(8,128)(2,1)S(1)}, bf16[128,512]{1,0:T(8,128)(2,1)}, u32[]{:S(2)}) %copy-start.7) | copy-done | bytes 131096
  27.0 5.0 %first_shards.1 = (f32[4,1024,256]{2,1,0:T(8,128)S(1)}, f32[4,1024,128]{2,1,0:T(8,128)S(1)}, f32[4,128,256]{2,1,0:T(8,128)S(1)}, f32[4,128,128]{2,1,0:T(8,128)S(1)}, bf16[16,4096]{1,0:T(8,128)(2,1)S(1)}) custom-call(s32[14]{0:T(128)S(1)} %copy-done.1, bf16[128,4096]{1,0:T(8,128)(2,1)S(1)} %copy-done, bf16[128,512]{1,0:T(8,128)(2,1)S(1)} %copy-done.2, ...), custom_call_target="tpu_custom_call" | custom-call | flops 6442450944 | bytes 2097152 | tf_op jit(solution)/shard_map/first_shards/pallas_call | solution.py:343
  32.0 0.0 collective-permute-done.8.refs_5_
  32.0 0.0 collective-permute-done.7.refs_4_
  32.1 1.1 %last_shard_decode.1 = bf16[16,4096]{1,0:T(8,128)(2,1)S(1)} custom-call(s32[14]{0:T(128)S(1)} %copy-done.1, f32[4,128,256]{2,1,0:T(8,128)S(1)} %get-tuple-element.33.refs_1_, f32[4,128,128]{2,1,0:T(8,128)S(1)} %get-tuple-element.34.refs_2_, bf16[16,4096]{1,0:T(8,128)(2,1)S(1)} %get-tuple-element.35.refs_3_, ...), custom_call_target="tpu_custom_call" | custom-call | flops 268435456 | bytes 262144 | tf_op jit(solution)/shard_map/last_shard_decode/pallas_call | solution.py:363
  33.2 0.1 fusion.1
  33.3 1.6 %collective-permute-start.10 = (bf16[2,4096]{1,0:T(2,128)(2,1)S(1)}, bf16[2,4096]{1,0:T(2,128)(2,1)S(1)}, u32[]{:S(2)}, u32[]{:S(2)}) collective-permute-start(bf16[2,4096]{1,0:T(2,128)(2,1)S(1)} %get-tuple-element.41), channel_id=1, source_target_pairs={{0,8},{4,12},{8,0},{12,4},{1,9},{5,13},{9,1},{13,5},{2,10},{6,14},... | collective-permute-start | bytes 49160 | tf_op jit(solution)/shard_map/ppermute | solution.py:447
  34.8 0.0 collective-permute-start.11
  34.8 1.7 %collective-permute-start.9 = (bf16[2,4096]{1,0:T(2,128)(2,1)S(1)}, bf16[2,4096]{1,0:T(2,128)(2,1)S(1)}, u32[]{:S(2)}, u32[]{:S(2)}) collective-permute-start(bf16[2,4096]{1,0:T(2,128)(2,1)S(1)} %get-tuple-element.38), channel_id=1, source_target_pairs={{0,12},{4,0},{8,4},{12,8},{1,13},{5,1},{9,5},{13,9},{2,14},{6,2},{... | collective-permute-start | bytes 49160 | tf_op jit(solution)/shard_map/ppermute | solution.py:447
  36.6 2.9 %last_shard_prefill.1 = bf16[128,4096]{1,0:T(8,128)(2,1)} custom-call(s32[14]{0:T(128)S(1)} %copy-done.1, bf16[128,4096]{1,0:T(8,128)(2,1)S(1)} %copy-done, f32[4,1024,256]{2,1,0:T(8,128)S(1)} %get-tuple-element.31.refs_2_, f32[4,1024,128]{2,1,0:T(8,128)S(1)} %get-tuple-element.32.refs_3_, bf16[128,512]{1,0:T(8,128)(2,1)S(1)} %collective-permute-done.7.refs_4_, ...), custom_call_target="tpu_custom_call" | custom-call | flops 2147483648 | bytes 2097152 | tf_op jit(solution)/shard_map/last_shard_prefill/pallas_call | solution.py:376
  39.5 0.0 collective-permute-done.10
  39.5 0.0 collective-permute-done.11
  39.5 0.0 collective-permute-done.9
  39.5 0.8 %broadcast_select_fusion.2 = bf16[4,2,4096]{2,1,0:T(2,128)(2,1)} fusion(pred[4]{0:T(512)(128)(4,1)S(1)} %get-tuple-element.44, pred[4]{0:T(512)(128)(4,1)S(1)} %get-tuple-element.43, pred[4]{0:T(512)(128)(4,1)S(1)} %get-tuple-element.42, pred[4]{0:T(512)(128)(4,1)S(1)} %get-tuple-element.36, bf16[2,4096]{1,0:T(2,128)(2,1)S(1)} %get-tuple-element.39, ...), kind=kLoop, calls=%fused_computation.2 | loop fusion | flops 131072 | bytes 131088 | tf_op jit(solution)/shard_map/jit(_where)/select_n | solution.py:458
  (5 shorter events, 0.1 us)
Async XLA Ops:
  0.6 9.6 %collective-permute-start.2 = (bf16[128,512]{1,0:T(8,128)(2,1)}, bf16[128,512]{1,0:T(8,128)(2,1)S(1)}, u32[]{:S(2)}, u32[]{:S(2)}) collective-permute-start(bf16[128,512]{1,0:T(8,128)(2,1)} %refs_2_), channel_id=1, source_target_pairs={{0,1},{1,3},{3,2},{2,0},{4,5},{5,7},{7,6},{6,4},{8,9},{9,11},{11,1... | collective-permute-start | bytes 393224 | tf_op jit(solution)/shard_map/ppermute | solution.py:46
  6.8 6.8 %collective-permute-start = (bf16[128,512]{1,0:T(8,128)(2,1)}, bf16[128,512]{1,0:T(8,128)(2,1)S(1)}, u32[]{:S(2)}, u32[]{:S(2)}) collective-permute-start(bf16[128,512]{1,0:T(8,128)(2,1)} %refs_3_), channel_id=1, source_target_pairs={{0,1},{1,3},{3,2},{2,0},{4,5},{5,7},{7,6},{6,4},{8,9},{9,11},{11,1... | collective-permute-start | bytes 393224 | tf_op jit(solution)/shard_map/ppermute | solution.py:46
  10.2 8.8 %collective-permute-start.6 = (bf16[128,512]{1,0:T(8,128)(2,1)S(1)}, bf16[128,512]{1,0:T(8,128)(2,1)S(1)}, u32[]{:S(2)}, u32[]{:S(2)}) collective-permute-start(bf16[128,512]{1,0:T(8,128)(2,1)S(1)} %collective-permute-done.2.refs_4_), channel_id=1, source_target_pairs={{0,1},{1,3},{3,2},{2,0},{4,5},{5,7},{7,6},{6,4},{8,9},{9,11},{11,1... | collective-permute-start | bytes 393224 | tf_op jit(solution)/shard_map/ppermute | solution.py:46
  13.6 5.9 %collective-permute-start.1 = (bf16[128,512]{1,0:T(8,128)(2,1)S(1)}, bf16[128,512]{1,0:T(8,128)(2,1)S(1)}, u32[]{:S(2)}, u32[]{:S(2)}) collective-permute-start(bf16[128,512]{1,0:T(8,128)(2,1)S(1)} %collective-permute-done.refs_6_), channel_id=1, source_target_pairs={{0,1},{1,3},{3,2},{2,0},{4,5},{5,7},{7,6},{6,4},{8,9},{9,11},{11,1... | collective-permute-start | bytes 393224 | tf_op jit(solution)/shard_map/ppermute | solution.py:46
  16.0 8.5 %copy-start = (bf16[128,4096]{1,0:T(8,128)(2,1)S(1)}, bf16[128,4096]{1,0:T(8,128)(2,1)}, u32[]{:S(2)}) copy-start(bf16[128,4096]{1,0:T(8,128)(2,1)} %refs_1_.3) | copy-start | bytes 3145732
  16.0 8.5 %copy-start.2 = (bf16[128,512]{1,0:T(8,128)(2,1)S(1)}, bf16[128,512]{1,0:T(8,128)(2,1)}, u32[]{:S(2)}) copy-start(bf16[128,512]{1,0:T(8,128)(2,1)} %refs_2_) | copy-start | bytes 393220
  16.0 8.5 %copy-start.3 = (bf16[128,512]{1,0:T(8,128)(2,1)S(1)}, bf16[128,512]{1,0:T(8,128)(2,1)}, u32[]{:S(2)}) copy-start(bf16[128,512]{1,0:T(8,128)(2,1)} %refs_3_) | copy-start | bytes 393220
  16.0 5.5 %collective-permute-start.3 = (bf16[8,5120]{1,0:T(8,128)(2,1)S(1)}, bf16[8,5120]{1,0:T(8,128)(2,1)S(1)}, u32[]{:S(2)}, u32[]{:S(2)}) collective-permute-start(bf16[8,5120]{1,0:T(8,128)(2,1)S(1)} %reshape.77.refs_8_), channel_id=1, source_target_pairs={{0,4},{4,8},{8,12},{12,0},{1,5},{5,9},{9,13},{13,1},{2,6},{6,10},{... | collective-permute-start | bytes 245768 | tf_op jit(solution)/shard_map/ppermute | solution.py:440
  16.1 5.5 %collective-permute-start.4 = (bf16[8,5120]{1,0:T(8,128)(2,1)S(1)}, bf16[8,5120]{1,0:T(8,128)(2,1)S(1)}, u32[]{:S(2)}, u32[]{:S(2)}) collective-permute-start(bf16[8,5120]{1,0:T(8,128)(2,1)S(1)} %reshape.77.refs_8_), channel_id=1, source_target_pairs={{0,8},{4,12},{8,0},{12,4},{1,9},{5,13},{9,1},{13,5},{2,10},{6,14},... | collective-permute-start | bytes 245768 | tf_op jit(solution)/shard_map/ppermute | solution.py:440
  17.6 3.9 %collective-permute-start.5 = (bf16[8,5120]{1,0:T(8,128)(2,1)S(1)}, bf16[8,5120]{1,0:T(8,128)(2,1)S(1)}, u32[]{:S(2)}, u32[]{:S(2)}) collective-permute-start(bf16[8,5120]{1,0:T(8,128)(2,1)S(1)} %reshape.77.refs_8_), channel_id=1, source_target_pairs={{0,12},{4,0},{8,4},{12,8},{1,13},{5,1},{9,5},{13,9},{2,14},{6,2},{... | collective-permute-start | bytes 245768 | tf_op jit(solution)/shard_map/ppermute | solution.py:440
  19.0 0.7 %copy-start.4 = (bf16[128,512]{1,0:T(8,128)(2,1)}, bf16[128,512]{1,0:T(8,128)(2,1)S(1)}, u32[]{:S(2)}) copy-start(bf16[128,512]{1,0:T(8,128)(2,1)S(1)} %collective-permute-done.6.refs_0_.refs_5_) | copy-start | bytes 393220
  19.7 0.6 %copy-start.6 = (bf16[128,512]{1,0:T(8,128)(2,1)}, bf16[128,512]{1,0:T(8,128)(2,1)S(1)}, u32[]{:S(2)}) copy-start(bf16[128,512]{1,0:T(8,128)(2,1)S(1)} %collective-permute-done.1.refs_1_.refs_7_) | copy-start | bytes 393220
  21.6 10.5 %collective-permute-start.8 = (bf16[128,512]{1,0:T(8,128)(2,1)}, bf16[128,512]{1,0:T(8,128)(2,1)S(1)}, u32[]{:S(2)}, u32[]{:S(2)}) collective-permute-start(bf16[128,512]{1,0:T(8,128)(2,1)} %copy-done.6), channel_id=1, source_target_pairs={{0,1},{1,3},{3,2},{2,0},{4,5},{5,7},{7,6},{6,4},{8,9},{9,11},{11,1... | collective-permute-start | bytes 393224 | tf_op jit(solution)/shard_map/ppermute | solution.py:46
  22.9 9.2 %collective-permute-start.7 = (bf16[128,512]{1,0:T(8,128)(2,1)}, bf16[128,512]{1,0:T(8,128)(2,1)S(1)}, u32[]{:S(2)}, u32[]{:S(2)}) collective-permute-start(bf16[128,512]{1,0:T(8,128)(2,1)} %copy-done.4), channel_id=1, source_target_pairs={{0,1},{1,3},{3,2},{2,0},{4,5},{5,7},{7,6},{6,4},{8,9},{9,11},{11,1... | collective-permute-start | bytes 393224 | tf_op jit(solution)/shard_map/ppermute | solution.py:46
  24.5 0.7 %copy-start.1 = (s32[14]{0:T(128)S(1)}, s32[14]{0:T(128)}, u32[]{:S(2)}) copy-start(s32[14]{0:T(128)} %after.1.refs_0_) | copy-start | bytes 172
  25.2 0.9 %copy-start.5 = (bf16[128,512]{1,0:T(8,128)(2,1)S(1)}, bf16[128,512]{1,0:T(8,128)(2,1)}, u32[]{:S(2)}) copy-start(bf16[128,512]{1,0:T(8,128)(2,1)} %copy-done.4) | copy-start | bytes 393220
  26.1 0.9 %copy-start.7 = (bf16[128,512]{1,0:T(8,128)(2,1)S(1)}, bf16[128,512]{1,0:T(8,128)(2,1)}, u32[]{:S(2)}) copy-start(bf16[128,512]{1,0:T(8,128)(2,1)} %copy-done.6) | copy-start | bytes 393220
  33.3 6.2 %collective-permute-start.10 = (bf16[2,4096]{1,0:T(2,128)(2,1)S(1)}, bf16[2,4096]{1,0:T(2,128)(2,1)S(1)}, u32[]{:S(2)}, u32[]{:S(2)}) collective-permute-start(bf16[2,4096]{1,0:T(2,128)(2,1)S(1)} %get-tuple-element.41), channel_id=1, source_target_pairs={{0,8},{4,12},{8,0},{12,4},{1,9},{5,13},{9,1},{13,5},{2,10},{6,14},... | collective-permute-start | bytes 49160 | tf_op jit(solution)/shard_map/ppermute | solution.py:447
  34.8 4.7 %collective-permute-start.11 = (bf16[2,4096]{1,0:T(2,128)(2,1)S(1)}, bf16[2,4096]{1,0:T(2,128)(2,1)S(1)}, u32[]{:S(2)}, u32[]{:S(2)}) collective-permute-start(bf16[2,4096]{1,0:T(2,128)(2,1)S(1)} %get-tuple-element.40), channel_id=1, source_target_pairs={{0,4},{4,8},{8,12},{12,0},{1,5},{5,9},{9,13},{13,1},{2,6},{6,10},{... | collective-permute-start | bytes 49160 | tf_op jit(solution)/shard_map/ppermute | solution.py:447
  34.8 4.7 %collective-permute-start.9 = (bf16[2,4096]{1,0:T(2,128)(2,1)S(1)}, bf16[2,4096]{1,0:T(2,128)(2,1)S(1)}, u32[]{:S(2)}, u32[]{:S(2)}) collective-permute-start(bf16[2,4096]{1,0:T(2,128)(2,1)S(1)} %get-tuple-element.38), channel_id=1, source_target_pairs={{0,12},{4,0},{8,4},{12,8},{1,13},{5,1},{9,5},{13,9},{2,14},{6,2},{... | collective-permute-start | bytes 49160 | tf_op jit(solution)/shard_map/ppermute | solution.py:447

commit v7 on v6

v7 whole, which is shorter than its diff:
```python
import math

import jax
import jax.numpy as jnp
from jax import lax
from jax.experimental import pallas as pl
from jax.experimental.pallas import tpu as pltpu
from jax.sharding import PartitionSpec as P

QUERY_HEADS = 32
KEY_VALUE_HEADS = 4
HEAD_SIZE = 128
PAGE = 16
GROUP_REQUESTS = 4
DECODE_STEPS = 2
HEADS_PER_KV = QUERY_HEADS // KEY_VALUE_HEADS
KV_WIDTH = KEY_VALUE_HEADS * HEAD_SIZE
Q_WIDTH = QUERY_HEADS * HEAD_SIZE
Q_BLOCK = HEADS_PER_KV * HEAD_SIZE
DECODE_ROWS = GROUP_REQUESTS * DECODE_STEPS
PADDED_ROWS = 16
STACKED = HEADS_PER_KV * PADDED_ROWS
MIB = 1024 * 1024

MASKED = -1e30
LIMIT = 60.0
EXPONENT = math.log2(math.e) / math.sqrt(HEAD_SIZE)

VMEM = pl.BlockSpec(memory_space=pltpu.VMEM)
SMEM = pl.BlockSpec(memory_space=pltpu.SMEM)
ANY = pl.BlockSpec(memory_space=pl.ANY)
HBM = pl.BlockSpec(memory_space=pltpu.HBM)


class Ring:
    def __init__(self, size):
        self.size = size
        order = [0] + list(range(1, size, 2)) + [i for i in range(size - 1, 0, -1) if i % 2 == 0]
        self.pairs = [(order[i], order[(i + 1) % size]) for i in range(size)]

    def step(self, array):
        return lax.ppermute(array, "tp", self.pairs)


def scores_of(queries, keys):
    return lax.dot_general(
        queries, keys, (((1,), (1,)), ((), ())), preferred_element_type=jnp.float32
    )


def product(left, right):
    return jnp.dot(left, right, preferred_element_type=jnp.float32)


def iota(shape, axis):
    return lax.broadcasted_iota(jnp.int32, shape, axis)


def span(start, size):
    if isinstance(start, int):
        return slice(start, start + size)
    return pl.ds(pl.multiple_of(start, size), size)


def with_ones(values):
    return jnp.concatenate([values, jnp.ones_like(values)], axis=1)


def page_position(offset, member, width):
    return (offset // PAGE * width + member) * PAGE + offset % PAGE


def key_positions(rows, sources, width):
    column = iota((1, len(sources) * rows), 1)
    part = column // rows
    source = jnp.zeros_like(column) + sources[0]
    for b in range(1, len(sources)):
        source = jnp.where(part == b, sources[b], source)
    return page_position(column - part * rows, source, width)


class Facts:
    def __init__(self, ref, width):
        self.width = width
        self.group, self.member = ref[0], ref[1]
        self.slots = [ref[2 + r] for r in range(GROUP_REQUESTS)]
        first = 2 + GROUP_REQUESTS
        self.ends = []
        total = jnp.int32(0)
        for r in range(GROUP_REQUESTS):
            total = total + ref[first + r] * PAGE
            self.ends.append(total)
        first += GROUP_REQUESTS
        self.source = [ref[first + s] for s in range(width)]


def facts_row(plan, lengths, slots):
    width, groups, requests = plan.size, lengths.shape[0], slots.shape[0]

    def kernel(lengths_ref, slots_ref, out_ref):
        group, member = lax.axis_index("pd"), lax.axis_index("tp")
        values = [group, member]
        values += [slots_ref[group * GROUP_REQUESTS + r] for r in range(GROUP_REQUESTS)]
        values += [lengths_ref[group, r] for r in range(GROUP_REQUESTS)]
        place = jnp.where(member % 2 == 1, (member + 1) // 2, width - member // 2)
        for s in range(width):
            before = (place + width - s) % width
            up = 2 * before - 1
            values.append(jnp.where(before == 0, 0, jnp.where(before <= width // 2, up, 2 * (width - before))))
        for i, value in enumerate(values):
            out_ref[i] = value.astype(jnp.int32)
        for q in range(requests):
            place = slots_ref[q] - group * GROUP_REQUESTS

            @pl.when((place >= 0) & (place < GROUP_REQUESTS))
            def _():
                back = group - q // GROUP_REQUESTS
                out_ref[len(values) + place] = jnp.where(back < 0, back + groups, back).astype(jnp.int32)

    length = 2 + 2 * GROUP_REQUESTS + width + GROUP_REQUESTS
    return pl.pallas_call(
        kernel,
        in_specs=[SMEM, SMEM],
        out_specs=SMEM,
        out_shape=jax.ShapeDtypeStruct((length,), jnp.int32),
        cost_estimate=pl.CostEstimate(flops=5 * 10**9, bytes_accessed=0, transcendentals=0),
        name="facts",
    )(lengths, slots)


def causal_bias(start, rows, keys, sources, ends, member, width):
    qpos = page_position(start + iota((rows, 1), 0), member, width)
    low = jnp.zeros_like(qpos)
    for end in ends:
        low = jnp.where(qpos >= end, end, low)
    kpos = key_positions(keys, sources, width)
    return jnp.where((kpos >= low) & (kpos <= qpos), 0.0, MASKED)


def request_mask(ends, keys, sources, width):
    request = iota((STACKED, 1), 0) % PADDED_ROWS // DECODE_STEPS
    low = jnp.zeros_like(request)
    high = jnp.zeros_like(request) + ends[0]
    for r in range(1, GROUP_REQUESTS):
        low = jnp.where(request == r, ends[r - 1], low)
        high = jnp.where(request == r, ends[r], high)
    kpos = key_positions(keys, sources, width)
    return (kpos >= low) & (kpos < high)


def stacked_heads(ref, rows, first, count):
    return jnp.concatenate(
        [ref[rows, span(first + i * HEAD_SIZE, HEAD_SIZE)] for i in range(count)], axis=0
    )


def each_kv_head(width, step):
    if width <= 8:
        for h in range(KEY_VALUE_HEADS):
            step(h)
    else:
        lax.fori_loop(0, KEY_VALUE_HEADS, lambda h, c: (step(h), c)[1], 0)


def peak(exponents):
    return jnp.max(exponents.reshape(-1, 8, exponents.shape[-1]), axis=0)


def picked_rows(facts, pd_size, block_refs):
    row = iota((PADDED_ROWS, DECODE_ROWS), 0)
    column = iota((PADDED_ROWS, DECODE_ROWS), 1)
    total = None
    for k in range(pd_size):
        pick = column < 0
        for r in range(GROUP_REQUESTS):
            slot = facts.slots[r]
            back = facts.group - slot // GROUP_REQUESTS
            back = jnp.where(back < 0, back + pd_size, back)
            first = jnp.where(back == k, slot % GROUP_REQUESTS * DECODE_STEPS, -DECODE_ROWS * 4)
            pick = pick | ((row // DECODE_STEPS == r) & (column == first + row - r * DECODE_STEPS))
        part = product(pick.astype(jnp.float32).astype(jnp.bfloat16), block_refs[k][...])
        total = part if total is None else total + part
    return total.astype(jnp.bfloat16)


def fresh_mask():
    row = iota((STACKED, PADDED_ROWS), 0) % PADDED_ROWS
    column = iota((STACKED, PADDED_ROWS), 1)
    return (column // DECODE_STEPS == row // DECODE_STEPS) & (
        column % DECODE_STEPS <= row % DECODE_STEPS
    )


def first_kernel(plan, pd_size, facts_ref, q_hbm_ref, k_hbm_ref, v_hbm_ref, *refs):
    width = plan.size
    k_refs, v_refs, refs = refs[: width - 2], refs[width - 2 : 2 * width - 4], refs[2 * width - 4 :]
    block_refs, refs = refs[:pd_size], refs[pd_size:]
    acc_ref, dec_acc_ref, worst_ref, queries_ref, fresh_ref, q_ref, k_ref, v_ref, sem = refs
    k_refs, v_refs = (k_ref,) + k_refs, (v_ref,) + v_refs
    copies = [
        pltpu.make_async_copy(k_hbm_ref, k_ref, sem.at[KEY_VALUE_HEADS]),
        pltpu.make_async_copy(v_hbm_ref, v_ref, sem.at[KEY_VALUE_HEADS + 1]),
    ]
    for h in range(KEY_VALUE_HEADS):
        part = pl.ds(h * Q_BLOCK, Q_BLOCK)
        copies.append(pltpu.make_async_copy(q_hbm_ref.at[:, part], q_ref.at[:, part], sem.at[h]))
    for copy in copies:
        copy.start()
    tokens = q_ref.shape[0]
    half = tokens // 2
    facts = Facts(facts_ref, width)
    sources = facts.source[:-1]
    rows = picked_rows(facts, pd_size, block_refs)
    queries_ref[...] = rows[:, :Q_WIDTH]
    fresh_ref[...] = rows[:, Q_WIDTH:]
    worst_ref[...] = jnp.full(worst_ref.shape, MASKED, jnp.float32)
    new_mask = fresh_mask()
    mask = request_mask(facts.ends, tokens, sources, width)
    spans = ((0, half), (half, tokens))
    biases = [
        causal_bias(s, half, keys, sources, facts.ends, facts.member, width) for s, keys in spans
    ]
    together = max(1, min(HEADS_PER_KV, HEADS_PER_KV * 4 // width))

    def weigh(exponents):
        top = jnp.max(peak(exponents), axis=1, keepdims=True)
        worst_ref[...] = jnp.maximum(worst_ref[...], top)
        return jnp.exp2(exponents).astype(jnp.bfloat16)

    def step(h):
        columns = span(h * HEAD_SIZE, HEAD_SIZE)
        first = h * Q_BLOCK
        queries = stacked_heads(queries_ref, slice(None), first, HEADS_PER_KV)
        k_all = jnp.concatenate([ref[:, columns] for ref in k_refs], axis=0)
        v_all = with_ones(jnp.concatenate([ref[:, columns] for ref in v_refs], axis=0))
        new_scores = scores_of(queries, fresh_ref[:, columns]) * EXPONENT
        new_weights = weigh(jnp.where(new_mask, new_scores, MASKED))
        new_values = fresh_ref[:, span(KV_WIDTH + h * HEAD_SIZE, HEAD_SIZE)]
        weights = weigh(jnp.where(mask, scores_of(queries, k_all) * EXPONENT, MASKED))
        dec_acc_ref[h] = product(weights, v_all) + product(new_weights, with_ones(new_values))
        for (start, keys), bias in zip(spans, biases):
            if keys < tokens:
                k_part = jnp.concatenate([ref[:keys, columns] for ref in k_refs], axis=0)
                v_part = with_ones(jnp.concatenate([ref[:keys, columns] for ref in v_refs], axis=0))
            else:
                k_part, v_part = k_all, v_all
            for g in range(0, HEADS_PER_KV, together):
                queries = stacked_heads(
                    q_ref, slice(start, start + half), first + g * HEAD_SIZE, together
                )
                scores = scores_of(queries, k_part).reshape(together, half, bias.shape[1])
                exponents = (scores * EXPONENT + bias[None]).reshape(together * half, bias.shape[1])
                rows = slice(
                    start * HEADS_PER_KV + g * half, start * HEADS_PER_KV + (g + together) * half
                )
                acc_ref[h, rows, :] = product(weigh(exponents), v_part)

    for copy in copies:
        copy.wait()
    each_kv_head(width, step)


def divided(acc):
    return (acc[:, :HEAD_SIZE] * pl.reciprocal(acc[:, HEAD_SIZE:], approx=True)).astype(jnp.bfloat16)


def fold(state, scores_list, values_list):
    top = None if state is None else state[0]
    for scores in scores_list:
        part = jnp.max(scores, axis=1, keepdims=True)
        top = part if top is None else jnp.maximum(top, part)
    acc = None
    for scores, values in zip(scores_list, values_list):
        weights = jnp.exp2((scores - top) * EXPONENT).astype(jnp.bfloat16)
        part = product(weights, with_ones(values))
        acc = part if acc is None else acc + part
    if state is not None:
        acc = acc + state[1] * jnp.exp2((state[0] - top) * EXPONENT)
    return top, acc


def parts_in(width):
    return [range(c, min(c + 4, width)) for c in range(0, width, 4)]


def out_of_range(worst, least):
    return (jnp.max(worst) > LIMIT) | (jnp.min(least) < 2.0**-LIMIT)


def decode_kernel(plan, pd_size, facts_ref, acc_ref, worst_ref, queries_ref, fresh_ref, *refs):
    width = plan.size
    k_refs, v_refs, (out_ref,) = refs[:width], refs[width : 2 * width], refs[2 * width :]
    tokens = k_refs[0].shape[0]
    facts = Facts(facts_ref, width)
    mask = request_mask(facts.ends, tokens, facts.source[-1:], width)
    row = iota((PADDED_ROWS, PADDED_ROWS), 0)
    column = iota((PADDED_ROWS, PADDED_ROWS), 1)
    pick = column < 0
    for r in range(GROUP_REQUESTS):
        ahead = facts.slots[r] // GROUP_REQUESTS - facts.group
        ahead = jnp.where(ahead < 0, ahead + pd_size, ahead)
        pick = pick | (
            (column // DECODE_STEPS == r) & (row == ahead * DECODE_STEPS + column - r * DECODE_STEPS)
        )
    pick = pick.astype(jnp.float32).astype(jnp.bfloat16)
    heads = range(KEY_VALUE_HEADS)
    columns = [slice(h * HEAD_SIZE, (h + 1) * HEAD_SIZE) for h in heads]

    def queries_of(h):
        return stacked_heads(queries_ref, slice(None), h * Q_BLOCK, HEADS_PER_KV)

    def send(acc):
        out = [divided(a) for a in acc]
        out = jnp.concatenate(
            [o[g * PADDED_ROWS : (g + 1) * PADDED_ROWS] for o in out for g in range(HEADS_PER_KV)], axis=1
        )
        out_ref[...] = product(pick, out).astype(jnp.bfloat16)

    exponents = [
        jnp.where(mask, scores_of(queries_of(h), k_refs[-1][:, columns[h]]) * EXPONENT, MASKED)
        for h in heads
    ]
    acc = [
        acc_ref[h] + product(jnp.exp2(exponents[h]).astype(jnp.bfloat16), with_ones(v_refs[-1][:, columns[h]]))
        for h in heads
    ]
    send(acc)
    worst, least = worst_ref[...], None
    for h in heads:
        worst = jnp.maximum(worst, peak(exponents[h]))
        part = jnp.min(acc[h][:, HEAD_SIZE:].reshape(-1, 8, HEAD_SIZE), axis=0)
        least = part if least is None else jnp.minimum(least, part)

    @pl.when(out_of_range(worst, least))
    def _():
        new_mask = fresh_mask()
        again = []
        for h in heads:
            queries = queries_of(h)
            scores = jnp.where(new_mask, scores_of(queries, fresh_ref[:, columns[h]]), MASKED)
            new_columns = slice(KV_WIDTH + h * HEAD_SIZE, KV_WIDTH + (h + 1) * HEAD_SIZE)
            state = fold(None, [scores], [fresh_ref[:, new_columns]])
            for parts in parts_in(width):
                k_part = jnp.concatenate([k_refs[s][:, columns[h]] for s in parts], axis=0)
                v_part = jnp.concatenate([v_refs[s][:, columns[h]] for s in parts], axis=0)
                here = request_mask(facts.ends, tokens, [facts.source[s] for s in parts], width)
                state = fold(state, [jnp.where(here, scores_of(queries, k_part), MASKED)], [v_part])
            again.append(state[1])
        send(again)


def prefill_kernel(plan, facts_ref, acc_ref, worst_ref, q_ref, *refs):
    width = plan.size
    k_refs, v_refs, refs = refs[:width], refs[width : 2 * width], refs[2 * width :]
    out_ref, done_ref, sem = refs
    tokens = q_ref.shape[0]
    half = tokens // 2
    facts = Facts(facts_ref, width)

    def bias_of(start, sources):
        return causal_bias(start, half, tokens, sources, facts.ends, facts.member, width)

    def write(h, start, acc):
        out = divided(acc)
        for g in range(HEADS_PER_KV):
            done_ref[start : start + half, span(h * Q_BLOCK + g * HEAD_SIZE, HEAD_SIZE)] = out[
                g * half : (g + 1) * half
            ]

    def copy_out(h):
        part = pl.ds(h * Q_BLOCK, Q_BLOCK)
        return pltpu.make_async_copy(done_ref.at[:, part], out_ref.at[:, part], sem.at[h])

    biases = [bias_of(start, facts.source[-1:]) for start in (0, half)]
    worst, least = worst_ref[...], None
    for h in range(KEY_VALUE_HEADS):
        columns = slice(h * HEAD_SIZE, (h + 1) * HEAD_SIZE)
        keys, values = k_refs[-1][:, columns], with_ones(v_refs[-1][:, columns])
        for start, bias in zip((0, half), biases):
            queries = stacked_heads(q_ref, slice(start, start + half), h * Q_BLOCK, HEADS_PER_KV)
            scores = scores_of(queries, keys).reshape(HEADS_PER_KV, half, tokens)
            exponents = (scores * EXPONENT + bias[None]).reshape(HEADS_PER_KV * half, tokens)
            worst = jnp.maximum(worst, peak(exponents))
            rows = slice(start * HEADS_PER_KV, (start + half) * HEADS_PER_KV)
            acc = acc_ref[h, rows, :] + product(jnp.exp2(exponents).astype(jnp.bfloat16), values)
            part = jnp.min(acc[:, HEAD_SIZE:].reshape(-1, 8, HEAD_SIZE), axis=0)
            least = part if least is None else jnp.minimum(least, part)
            write(h, start, acc)
        copy_out(h).start()
    redo = out_of_range(worst, least)
    for h in range(KEY_VALUE_HEADS):
        copy_out(h).wait()

    @pl.when(redo)
    def _():
        def step(h, carry):
            columns = span(h * HEAD_SIZE, HEAD_SIZE)
            for start in (0, half):
                queries = stacked_heads(q_ref, slice(start, start + half), h * Q_BLOCK, HEADS_PER_KV)
                state = None
                for parts in parts_in(width):
                    k_part = jnp.concatenate([k_refs[s][:, columns] for s in parts], axis=0)
                    v_part = jnp.concatenate([v_refs[s][:, columns] for s in parts], axis=0)
                    bias = bias_of(start, [facts.source[s] for s in parts])
                    scores = scores_of(queries, k_part).reshape(HEADS_PER_KV, half, bias.shape[1])
                    scores = (scores + bias[None]).reshape(HEADS_PER_KV * half, bias.shape[1])
                    state = fold(state, [scores], [v_part])
                write(h, start, state[1])
            return carry

        lax.fori_loop(0, KEY_VALUE_HEADS, step, 0)
        for h in range(KEY_VALUE_HEADS):
            copy_out(h).start()
        for h in range(KEY_VALUE_HEADS):
            copy_out(h).wait()


def cost(rows, keys, exps):
    return pl.CostEstimate(
        flops=32 * rows * keys * Q_WIDTH, bytes_accessed=4 * rows * Q_WIDTH, transcendentals=exps
    )


def call_first(plan, facts, query, blocks, keys, values):
    tokens, width = query.shape[0], plan.size
    rows = HEADS_PER_KV * tokens
    f32, bf16 = jnp.float32, jnp.bfloat16
    every = (width - 1) * tokens
    shapes = [
        jax.ShapeDtypeStruct((KEY_VALUE_HEADS, rows, 2 * HEAD_SIZE), f32),
        jax.ShapeDtypeStruct((KEY_VALUE_HEADS, STACKED, 2 * HEAD_SIZE), f32),
        jax.ShapeDtypeStruct((8, HEAD_SIZE), f32),
        jax.ShapeDtypeStruct((PADDED_ROWS, Q_WIDTH), bf16),
        jax.ShapeDtypeStruct((PADDED_ROWS, 2 * KV_WIDTH), bf16),
        jax.ShapeDtypeStruct((tokens, Q_WIDTH), bf16),
        jax.ShapeDtypeStruct((tokens, KV_WIDTH), bf16),
        jax.ShapeDtypeStruct((tokens, KV_WIDTH), bf16),
    ]
    return pl.pallas_call(
        lambda *refs: first_kernel(plan, len(blocks), *refs),
        in_specs=[SMEM] + [HBM] * 3 + [VMEM] * (len(blocks) + 2 * (width - 2)),
        out_specs=[VMEM] * len(shapes),
        out_shape=shapes,
        scratch_shapes=[pltpu.SemaphoreType.DMA((KEY_VALUE_HEADS + 2,))],
        compiler_params=pltpu.CompilerParams(vmem_limit_bytes=(28 + width) * MIB),
        cost_estimate=cost(tokens, every, tokens * every * QUERY_HEADS),
        name="first_shards",
    )(facts, query, keys[0], values[0], *keys[1:], *values[1:], *blocks)


def call_decode(plan, pd_size, facts, dec_acc, worst, rows, fresh, keys, values):
    tokens, width = keys[0].shape[0], plan.size
    return pl.pallas_call(
        lambda *refs: decode_kernel(plan, pd_size, *refs),
        in_specs=[SMEM] + [VMEM] * (4 + 2 * width),
        out_specs=VMEM,
        out_shape=jax.ShapeDtypeStruct((PADDED_ROWS, Q_WIDTH), jnp.bfloat16),
        compiler_params=pltpu.CompilerParams(vmem_limit_bytes=(28 + width) * MIB),
        cost_estimate=cost(PADDED_ROWS, tokens, PADDED_ROWS * tokens * QUERY_HEADS),
        name="last_shard_decode",
    )(facts, dec_acc, worst, rows, fresh, *keys, *values)


def call_prefill(plan, facts, acc, worst, query, keys, values):
    tokens, width = query.shape[0], plan.size
    return pl.pallas_call(
        lambda *refs: prefill_kernel(plan, *refs),
        in_specs=[SMEM] + [VMEM] * (3 + 2 * width),
        out_specs=ANY,
        out_shape=jax.ShapeDtypeStruct((tokens, Q_WIDTH), jnp.bfloat16),
        scratch_shapes=[
            pltpu.VMEM((tokens, Q_WIDTH), jnp.bfloat16),
            pltpu.SemaphoreType.DMA((KEY_VALUE_HEADS,)),
        ],
        compiler_params=pltpu.CompilerParams(vmem_limit_bytes=(28 + width) * MIB),
        cost_estimate=cost(tokens, tokens, tokens * tokens * QUERY_HEADS),
        name="last_shard_prefill",
    )(facts, acc, worst, query, *keys, *values)


def after(row, *arrays):
    for array in arrays:
        row = jnp.where(array[0, 0] == array[0, 0], row, 0)
    return row


def ring(size, step):
    return [(i, (i + step) % size) for i in range(size)]


def body(
    prompt_query,
    prompt_key,
    prompt_value,
    prompt_lengths,
    decode_slot,
    decoded_query,
    decoded_key,
    decoded_value,
):
    plan = Ring(lax.axis_size("tp"))
    pd_size = lax.axis_size("pd")
    own = jnp.concatenate([decoded_query, decoded_key, decoded_value], axis=2).reshape(
        DECODE_ROWS, Q_WIDTH + 2 * KV_WIDTH
    )
    facts = facts_row(plan, prompt_lengths, decode_slot)
    prompt_key, decoded_query = lax.optimization_barrier((prompt_key, decoded_query))
    prompt_value, own, facts = lax.optimization_barrier((prompt_value, own, facts))
    keys, values = [prompt_key], [prompt_value]
    for s in range(1, plan.size):
        if s == 2:
            keys[1], own = lax.optimization_barrier((keys[1], own))
        if s == plan.size - 1:
            facts = after(facts, keys[-1], values[-1])
            values[-1], facts = lax.optimization_barrier((values[-1], facts))
        keys.append(plan.step(keys[-1]))
        values.append(plan.step(values[-1]))
        if s == 2:
            blocks = [own] + [lax.ppermute(own, "pd", ring(pd_size, k)) for k in range(1, pd_size)]

    acc, dec_acc, worst, rows, fresh, query, key, value = call_first(
        plan, facts, prompt_query, blocks, keys[:-1], values[:-1]
    )
    keys[0], values[0] = key, value
    outgoing = call_decode(plan, pd_size, facts, dec_acc, worst, rows, fresh, keys, values)
    arrived = [outgoing[:DECODE_STEPS]]
    for k in range(1, pd_size):
        part = outgoing[k * DECODE_STEPS : (k + 1) * DECODE_STEPS]
        arrived.append(lax.ppermute(part, "pd", ring(pd_size, k)))
    pre_out = call_prefill(plan, facts, acc, worst, query, keys, values)

    from_block = facts[-GROUP_REQUESTS:]
    dec_out = jnp.zeros((GROUP_REQUESTS, DECODE_STEPS, Q_WIDTH), jnp.bfloat16)
    for k in range(pd_size):
        dec_out = jnp.where((from_block == k)[:, None, None], arrived[k][None], dec_out)
    return (pre_out, dec_out)


def solution(mesh):
    placed = (
        P(("rep", "pd", "tp"), None),
        P(("rep", "pd", "tp"), None),
        P(("rep", "pd", "tp"), None),
        P("rep", None),
        P("rep"),
        P(("rep", "pd"), None, None),
        P(("rep", "pd"), None, None),
        P(("rep", "pd"), None, None),
    )
    return jax.shard_map(
        body,
        mesh=mesh,
        in_specs=placed,
        out_specs=(P(("rep", "pd", "tp"), None), P(("rep", "pd"), None, None)),
        check_vma=False,
    )
```

time: 40.6 us -> 45.7 us (1.13)
  Pallas kernels: 10.3 us -> 16.4 us
  local copies, waits for them, and re-layouts: 5.49 us -> 1.14 us
  between operations: 0.78 us -> 3.37 us
  waiting for transfers between devices: 3.38 us -> 5.45 us
  starting transfers between devices: 17.8 us -> 16.7 us
    pallas_call x1, Pallas kernels: 2.93 us -> 8.15 us  [call_prefill(): pl.pallas_call(lambda *refs: prefill_kernel(plan, *refs), in_specs=[SMEM]...]
    unnamed x16 -> x6, local copies, waits for them, and re-layouts: 3.33 us -> 0.02 us
    ppermute x6, waiting for transfers between devices: 3.34 us -> 5.44 us  [step(): return lax.ppermute(array, 'tp', self.pairs)]
    pallas_call x1, Pallas kernels: 1.13 us -> 2.66 us  [call_decode(): pl.pallas_call(lambda *refs: decode_kernel(plan, pd_size, *refs), in_spec...]
    slice x0 -> x2, local copies, waits for them, and re-layouts: none -> 1.03 us  [after(): row = jnp.where(array[0, 0] == array[0, 0], row, 0)]
    ppermute x6, starting transfers between devices: 11.5 us -> 10.6 us  [step(): return lax.ppermute(array, 'tp', self.pairs)]
    reduce_sum x1 -> x0, other arithmetic: 0.84 us -> none  [body(): jnp.sum(jnp.where(decode_slot[None, :] == wanted[:, None], numbers[None,...]
    pallas_call x1, Pallas kernels: 5.02 us -> 4.18 us  [call_first(): pl.pallas_call(lambda *refs: first_kernel(plan, len(blocks), *refs), in_s...]
  transfers between devices with their start and end apart: 12 -> 12, of which waited for: 2 -> 3; matrix products, arithmetic and copies ran while one was open for 10% -> 6% of each run, Pallas kernels for 23% -> 30%
where the time goes in v7:
time: 45.7 us; the launch traced here: 45.5 us
  starting transfers between devices  16.7 us (37%)
  Pallas kernels  16.4 us (36%)
  waiting for transfers between devices  5.45 us (12%)
  between operations  3.37 us (7%)
  other arithmetic  2.41 us (5%)
  local copies, waits for them, and re-layouts  1.14 us (2%)
    ppermute x6, starting transfers between devices, step(): return lax.ppermute(array, 'tp', self.pairs)  10.6 us
    pallas_call x1, Pallas kernels, call_prefill(): pl.pallas_call(lambda *refs: prefill_kernel(plan, *refs), in_specs=[SMEM]...  8.15 us
    ppermute x6, waiting for transfers between devices, step(): return lax.ppermute(array, 'tp', self.pairs)  5.44 us
    pallas_call x1, Pallas kernels, call_first(): pl.pallas_call(lambda *refs: first_kernel(plan, len(blocks), *refs), in_s...  4.18 us
    ppermute x3, starting transfers between devices, body(): arrived.append(lax.ppermute(part, 'pd', ring(pd_size, k)))  3.13 us
    ppermute x3, starting transfers between devices, body(): lax.ppermute(own, 'pd', ring(pd_size, k))  2.96 us
    pallas_call x1, Pallas kernels, call_decode(): pl.pallas_call(lambda *refs: decode_kernel(plan, pd_size, *refs), in_spec...  2.66 us
    pallas_call x1, Pallas kernels, facts_row(): pl.pallas_call(kernel, in_specs=[SMEM, SMEM], out_specs=SMEM, out_shape=j...  1.43 us
  transfers between devices with their start and end apart: 12, of which 3 were waited for; matrix products, arithmetic and copies ran while one was open for 6% of the time, Pallas kernels for 30%

profile of v7, /device:TPU:0, one launch (start us, length us, event | category | flops | bytes accessed | tf_op | source)
XLA Modules:
  0.0 45.5 jit_solution(18373889724528243645)
XLA Ops:
  0.6 3.1 %collective-permute-start.2 = (bf16[128,512]{1,0:T(8,128)(2,1)}, bf16[128,512]{1,0:T(8,128)(2,1)S(1)}, u32[]{:S(2)}, u32[]{:S(2)}) collective-permute-start(bf16[128,512]{1,0:T(8,128)(2,1)} %refs_2_), channel_id=1, source_target_pairs={{0,1},{1,3},{3,2},{2,0},{4,5},{5,7},{7,6},{6,4},{8,9},{9,11},{11,1... | collective-permute-start | bytes 393224 | tf_op jit(solution)/shard_map/ppermute | solution.py:42
  3.7 0.9 %pad_maximum_fusion = bf16[4,2,5120]{2,1,0:T(2,128)(2,1)S(1)} fusion(bf16[4,2,512]{2,1,0:T(2,128)(2,1)} %param.15, bf16[4,2,512]{2,1,0:T(2,128)(2,1)} %param.14, bf16[4,2,4096]{2,1,0:T(2,128)(2,1)} %param.13), kind=kLoop, calls=%fused_computation.4 | loop fusion | flops 245760 | bytes 163840 | tf_op jit(solution)/shard_map/concatenate | solution.py:503
  4.7 0.0 copy-start.1
  4.7 0.0 copy-start
  4.7 0.0 copy-start.2
  4.7 1.4 %facts.1 = s32[18]{0:T(128)} custom-call(s32[4,4]{1,0:T(4,128)} %lengths_ref.1, s32[16]{0:T(128)} %slots_ref.1), custom_call_target="tpu_custom_call" | custom-call | flops 5000000000 | tf_op jit(solution)/shard_map/facts/pallas_call | solution.py:121
  6.2 0.0 copy-done.1
  6.2 2.6 %collective-permute-start = (bf16[128,512]{1,0:T(8,128)(2,1)S(1)}, bf16[128,512]{1,0:T(8,128)(2,1)S(1)}, u32[]{:S(2)}, u32[]{:S(2)}) collective-permute-start(bf16[128,512]{1,0:T(8,128)(2,1)S(1)} %copy-done.1), channel_id=1, source_target_pairs={{0,1},{1,3},{3,2},{2,0},{4,5},{5,7},{7,6},{6,4},{8,9},{9,11},{11,1... | collective-permute-start | bytes 393224 | tf_op jit(solution)/shard_map/ppermute | solution.py:42
  8.8 0.0 collective-permute-done.2.refs_4_.refs_5_.refs_6_
  8.8 0.8 %collective-permute-start.3 = (bf16[128,512]{1,0:T(8,128)(2,1)S(1)}, bf16[128,512]{1,0:T(8,128)(2,1)S(1)}, u32[]{:S(2)}, u32[]{:S(2)}) collective-permute-start(bf16[128,512]{1,0:T(8,128)(2,1)S(1)} %collective-permute-done.2.refs_4_.refs_5_.refs_6_), channel_id=1, source_target_pairs={{0,1},{1,3},{3,2},{2,0},{4,5},{5,7},{7,6},{6,4},{8,9},{9,11},{11,1... | collective-permute-start | bytes 393224 | tf_op jit(solution)/shard_map/ppermute | solution.py:42
  9.6 3.1 %collective-permute-done.refs_6_.refs_9_.refs_10_ = bf16[128,512]{1,0:T(8,128)(2,1)S(1)} collective-permute-done((bf16[128,512]{1,0:T(8,128)(2,1)S(1)}, bf16[128,512]{1,0:T(8,128)(2,1)S(1)}, u32[]{:S(2)}, u32[]{:S(2)}) %collective-permute-start) | collective-permute-done | bytes 131104 | tf_op jit(solution)/shard_map/ppermute | solution.py:42
  12.8 2.5 %collective-permute-start.1 = (bf16[128,512]{1,0:T(8,128)(2,1)S(1)}, bf16[128,512]{1,0:T(8,128)(2,1)S(1)}, u32[]{:S(2)}, u32[]{:S(2)}) collective-permute-start(bf16[128,512]{1,0:T(8,128)(2,1)S(1)} %collective-permute-done.refs_6_.refs_9_.refs_10_), channel_id=1, source_target_pairs={{0,1},{1,3},{3,2},{2,0},{4,5},{5,7},{7,6},{6,4},{8,9},{9,11},{11,1... | collective-permute-start | bytes 393224 | tf_op jit(solution)/shard_map/ppermute | solution.py:42
  15.2 0.0 collective-permute-start.4
  15.3 1.5 %collective-permute-start.5 = (bf16[8,5120]{1,0:T(8,128)(2,1)S(1)}, bf16[8,5120]{1,0:T(8,128)(2,1)S(1)}, u32[]{:S(2)}, u32[]{:S(2)}) collective-permute-start(bf16[8,5120]{1,0:T(8,128)(2,1)S(1)} %reshape.17.refs_8_), channel_id=1, source_target_pairs={{0,8},{4,12},{8,0},{12,4},{1,9},{5,13},{9,1},{13,5},{2,10},{6,14},... | collective-permute-start | bytes 245768 | tf_op jit(solution)/shard_map/ppermute | solution.py:519
  16.8 1.4 %collective-permute-start.6 = (bf16[8,5120]{1,0:T(8,128)(2,1)S(1)}, bf16[8,5120]{1,0:T(8,128)(2,1)S(1)}, u32[]{:S(2)}, u32[]{:S(2)}) collective-permute-start(bf16[8,5120]{1,0:T(8,128)(2,1)S(1)} %reshape.17.refs_8_), channel_id=1, source_target_pairs={{0,12},{4,0},{8,4},{12,8},{1,13},{5,1},{9,5},{13,9},{2,14},{6,2},{... | collective-permute-start | bytes 245768 | tf_op jit(solution)/shard_map/ppermute | solution.py:519
  18.2 0.0 collective-permute-done.3.refs_5_.refs_6_.refs_7_
  18.2 0.5 %slice.31 = bf16[1,1]{1,0:T(2,128)(2,1)} slice(bf16[128,512]{1,0:T(8,128)(2,1)S(1)} %collective-permute-done.3.refs_5_.refs_6_.refs_7_), slice={[0:1], [0:1]} | slice | bytes 4 | tf_op jit(solution)/shard_map/slice | solution.py:483
  20.0 0.0 collective-permute-done.1.refs_7_.refs_10_.refs_11_
  20.0 0.5 %slice.30 = bf16[1,1]{1,0:T(2,128)(2,1)} slice(bf16[128,512]{1,0:T(8,128)(2,1)S(1)} %collective-permute-done.1.refs_7_.refs_10_.refs_11_), slice={[0:1], [0:1]} | slice | bytes 4 | tf_op jit(solution)/shard_map/slice | solution.py:483
  21.8 0.6 %broadcast_select_fusion.5.refs_0_ = s32[18]{0:T(128)S(1)} fusion(pred[]{:T(512)} %bitcast, s32[18]{0:T(128)} %facts.1, pred[]{:T(512)} %bitcast.1), kind=kLoop, calls=%fused_computation.6 | loop fusion | flops 36 | bytes 146 | tf_op jit(solution)/shard_map/jit(_where)/select_n | solution.py:483
  22.4 0.5 %collective-permute-start.8 = (bf16[128,512]{1,0:T(8,128)(2,1)S(1)}, bf16[128,512]{1,0:T(8,128)(2,1)S(1)}, u32[]{:S(2)}, u32[]{:S(2)}) collective-permute-start(bf16[128,512]{1,0:T(8,128)(2,1)S(1)} %collective-permute-done.1.refs_7_.refs_10_.refs_11_), channel_id=1, source_target_pairs={{0,1},{1,3},{3,2},{2,0},{4,5},{5,7},{7,6},{6,4},{8,9},{9,11},{11,1... | collective-permute-start | bytes 393224 | tf_op jit(solution)/shard_map/ppermute | solution.py:42
  22.9 1.1 %collective-permute-start.7 = (bf16[128,512]{1,0:T(8,128)(2,1)S(1)}, bf16[128,512]{1,0:T(8,128)(2,1)S(1)}, u32[]{:S(2)}, u32[]{:S(2)}) collective-permute-start(bf16[128,512]{1,0:T(8,128)(2,1)S(1)} %collective-permute-done.3.refs_5_.refs_6_.refs_7_), channel_id=1, source_target_pairs={{0,1},{1,3},{3,2},{2,0},{4,5},{5,7},{7,6},{6,4},{8,9},{9,11},{11,1... | collective-permute-start | bytes 393224 | tf_op jit(solution)/shard_map/ppermute | solution.py:42
  24.0 0.0 collective-permute-done.4.refs_9_
  24.0 0.0 collective-permute-done.5.refs_10_
  24.0 0.0 collective-permute-done.6.refs_11_
  24.0 0.0 copy-done
  24.0 0.0 copy-done.2
  24.1 4.2 %first_shards.1 = (f32[4,1024,256]{2,1,0:T(8,128)S(1)}, f32[4,128,256]{2,1,0:T(8,128)S(1)}, f32[8,128]{1,0:T(8,128)S(1)}, bf16[16,4096]{1,0:T(8,128)(2,1)S(1)}, ...) custom-call(s32[18]{0:T(128)S(1)} %broadcast_select_fusion.5.refs_0_, ...), custom_call_target="tpu_custom_call" | custom-call | flops 6442450944 | bytes 2097152 | tf_op jit(solution)/shard_map/first_shards/pallas_call | solution.py:439
  28.2 0.1 broadcast_compare_fusion.2
  28.3 0.9 %collective-permute-done.8.refs_11_.refs_12_ = bf16[128,512]{1,0:T(8,128)(2,1)S(1)} collective-permute-done((bf16[128,512]{1,0:T(8,128)(2,1)S(1)}, bf16[128,512]{1,0:T(8,128)(2,1)S(1)}, u32[]{:S(2)}, u32[]{:S(2)}) %collective-permute-start.8) | collective-permute-done | bytes 131104 | tf_op jit(solution)/shard_map/ppermute | solution.py:42
  29.2 1.4 %collective-permute-done.7.refs_7_.refs_8_ = bf16[128,512]{1,0:T(8,128)(2,1)S(1)} collective-permute-done((bf16[128,512]{1,0:T(8,128)(2,1)S(1)}, bf16[128,512]{1,0:T(8,128)(2,1)S(1)}, u32[]{:S(2)}, u32[]{:S(2)}) %collective-permute-start.7) | collective-permute-done | bytes 131104 | tf_op jit(solution)/shard_map/ppermute | solution.py:42
  30.6 2.7 %last_shard_decode.1 = bf16[16,4096]{1,0:T(8,128)(2,1)S(1)} custom-call(s32[18]{0:T(128)S(1)} %broadcast_select_fusion.5.refs_0_, f32[4,128,256]{2,1,0:T(8,128)S(1)} %get-tuple-element.31.refs_1_, f32[8,128]{1,0:T(8,128)S(1)} %get-tuple-element.27.refs_2_, bf16[16,4096]{1,0:T(8,128)(2,1)S(1)} %get-tuple-element.32.refs_3_, ...), custom_call_target="tpu_custom_call" | custom-call | flops 268435456 | bytes 262144 | tf_op jit(solution)/shard_map/last_shard_decode/pallas_call | solution.py:453
  33.3 0.1 fusion
  33.3 1.4 %collective-permute-start.10 = (bf16[2,4096]{1,0:T(2,128)(2,1)S(1)}, bf16[2,4096]{1,0:T(2,128)(2,1)S(1)}, u32[]{:S(2)}, u32[]{:S(2)}) collective-permute-start(bf16[2,4096]{1,0:T(2,128)(2,1)S(1)} %get-tuple-element.37), channel_id=1, source_target_pairs={{0,8},{4,12},{8,0},{12,4},{1,9},{5,13},{9,1},{13,5},{2,10},{6,14},... | collective-permute-start | bytes 49160 | tf_op jit(solution)/shard_map/ppermute | solution.py:529
  34.7 0.0 collective-permute-start.11
  34.7 1.7 %collective-permute-start.9 = (bf16[2,4096]{1,0:T(2,128)(2,1)S(1)}, bf16[2,4096]{1,0:T(2,128)(2,1)S(1)}, u32[]{:S(2)}, u32[]{:S(2)}) collective-permute-start(bf16[2,4096]{1,0:T(2,128)(2,1)S(1)} %get-tuple-element.34), channel_id=1, source_target_pairs={{0,12},{4,0},{8,4},{12,8},{1,13},{5,1},{9,5},{13,9},{2,14},{6,2},{... | collective-permute-start | bytes 49160 | tf_op jit(solution)/shard_map/ppermute | solution.py:529
  36.5 8.2 %last_shard_prefill.1 = bf16[128,4096]{1,0:T(8,128)(2,1)} custom-call(s32[18]{0:T(128)S(1)} %broadcast_select_fusion.5.refs_0_, f32[4,1024,256]{2,1,0:T(8,128)S(1)} %get-tuple-element.26.refs_1_, f32[8,128]{1,0:T(8,128)S(1)} %get-tuple-element.27.refs_2_, bf16[128,4096]{1,0:T(8,128)(2,1)S(1)} %get-tuple-element.28.refs_3_, ...), custom_call_target="tpu_custom_call" | custom-call | flops 2147483648 | bytes 2097152 | tf_op jit(solution)/shard_map/last_shard_prefill/pallas_call | solution.py:466
  44.6 0.0 collective-permute-done.10
  44.6 0.0 collective-permute-done.11
  44.7 0.0 collective-permute-done.9
  44.7 0.8 %broadcast_select_fusion.2 = bf16[4,2,4096]{2,1,0:T(2,128)(2,1)} fusion(pred[4]{0:T(512)(128)(4,1)S(1)} %get-tuple-element.41, pred[4]{0:T(512)(128)(4,1)S(1)} %get-tuple-element.40, pred[4]{0:T(512)(128)(4,1)S(1)} %get-tuple-element.39, pred[4]{0:T(512)(128)(4,1)S(1)} %get-tuple-element.38, bf16[2,4096]{1,0:T(2,128)(2,1)S(1)} %get-tuple-element.35, ...), kind=kLoop, calls=%fused_computation.2 | loop fusion | flops 131072 | bytes 131088 | tf_op jit(solution)/shard_map/jit(_where)/select_n | solution.py:535
  (1 shorter events, 0.0 us)
Async XLA Ops:
  0.6 8.2 %collective-permute-start.2 = (bf16[128,512]{1,0:T(8,128)(2,1)}, bf16[128,512]{1,0:T(8,128)(2,1)S(1)}, u32[]{:S(2)}, u32[]{:S(2)}) collective-permute-start(bf16[128,512]{1,0:T(8,128)(2,1)} %refs_2_), channel_id=1, source_target_pairs={{0,1},{1,3},{3,2},{2,0},{4,5},{5,7},{7,6},{6,4},{8,9},{9,11},{11,1... | collective-permute-start | bytes 393224 | tf_op jit(solution)/shard_map/ppermute | solution.py:42
  4.7 1.5 %copy-start.1 = (bf16[128,512]{1,0:T(8,128)(2,1)S(1)}, bf16[128,512]{1,0:T(8,128)(2,1)}, u32[]{:S(2)}) copy-start(bf16[128,512]{1,0:T(8,128)(2,1)} %refs_3_) | copy-start | bytes 393220
  4.7 19.4 %copy-start = (bf16[128,4096]{1,0:T(8,128)(2,1)S(1)}, bf16[128,4096]{1,0:T(8,128)(2,1)}, u32[]{:S(2)}) copy-start(bf16[128,4096]{1,0:T(8,128)(2,1)} %refs_1_.1) | copy-start | bytes 3145732
  4.7 19.4 %copy-start.2 = (bf16[128,512]{1,0:T(8,128)(2,1)S(1)}, bf16[128,512]{1,0:T(8,128)(2,1)}, u32[]{:S(2)}) copy-start(bf16[128,512]{1,0:T(8,128)(2,1)} %refs_2_) | copy-start | bytes 393220
  6.2 6.6 %collective-permute-start = (bf16[128,512]{1,0:T(8,128)(2,1)S(1)}, bf16[128,512]{1,0:T(8,128)(2,1)S(1)}, u32[]{:S(2)}, u32[]{:S(2)}) collective-permute-start(bf16[128,512]{1,0:T(8,128)(2,1)S(1)} %copy-done.1), channel_id=1, source_target_pairs={{0,1},{1,3},{3,2},{2,0},{4,5},{5,7},{7,6},{6,4},{8,9},{9,11},{11,1... | collective-permute-start | bytes 393224 | tf_op jit(solution)/shard_map/ppermute | solution.py:42
  8.8 9.4 %collective-permute-start.3 = (bf16[128,512]{1,0:T(8,128)(2,1)S(1)}, bf16[128,512]{1,0:T(8,128)(2,1)S(1)}, u32[]{:S(2)}, u32[]{:S(2)}) collective-permute-start(bf16[128,512]{1,0:T(8,128)(2,1)S(1)} %collective-permute-done.2.refs_4_.refs_5_.refs_6_), channel_id=1, source_target_pairs={{0,1},{1,3},{3,2},{2,0},{4,5},{5,7},{7,6},{6,4},{8,9},{9,11},{11,1... | collective-permute-start | bytes 393224 | tf_op jit(solution)/shard_map/ppermute | solution.py:42
  12.8 7.3 %collective-permute-start.1 = (bf16[128,512]{1,0:T(8,128)(2,1)S(1)}, bf16[128,512]{1,0:T(8,128)(2,1)S(1)}, u32[]{:S(2)}, u32[]{:S(2)}) collective-permute-start(bf16[128,512]{1,0:T(8,128)(2,1)S(1)} %collective-permute-done.refs_6_.refs_9_.refs_10_), channel_id=1, source_target_pairs={{0,1},{1,3},{3,2},{2,0},{4,5},{5,7},{7,6},{6,4},{8,9},{9,11},{11,1... | collective-permute-start | bytes 393224 | tf_op jit(solution)/shard_map/ppermute | solution.py:42
  15.2 8.8 %collective-permute-start.4 = (bf16[8,5120]{1,0:T(8,128)(2,1)S(1)}, bf16[8,5120]{1,0:T(8,128)(2,1)S(1)}, u32[]{:S(2)}, u32[]{:S(2)}) collective-permute-start(bf16[8,5120]{1,0:T(8,128)(2,1)S(1)} %reshape.17.refs_8_), channel_id=1, source_target_pairs={{0,4},{4,8},{8,12},{12,0},{1,5},{5,9},{9,13},{13,1},{2,6},{6,10},{... | collective-permute-start | bytes 245768 | tf_op jit(solution)/shard_map/ppermute | solution.py:519
  15.3 8.8 %collective-permute-start.5 = (bf16[8,5120]{1,0:T(8,128)(2,1)S(1)}, bf16[8,5120]{1,0:T(8,128)(2,1)S(1)}, u32[]{:S(2)}, u32[]{:S(2)}) collective-permute-start(bf16[8,5120]{1,0:T(8,128)(2,1)S(1)} %reshape.17.refs_8_), channel_id=1, source_target_pairs={{0,8},{4,12},{8,0},{12,4},{1,9},{5,13},{9,1},{13,5},{2,10},{6,14},... | collective-permute-start | bytes 245768 | tf_op jit(solution)/shard_map/ppermute | solution.py:519
  16.8 7.3 %collective-permute-start.6 = (bf16[8,5120]{1,0:T(8,128)(2,1)S(1)}, bf16[8,5120]{1,0:T(8,128)(2,1)S(1)}, u32[]{:S(2)}, u32[]{:S(2)}) collective-permute-start(bf16[8,5120]{1,0:T(8,128)(2,1)S(1)} %reshape.17.refs_8_), channel_id=1, source_target_pairs={{0,12},{4,0},{8,4},{12,8},{1,13},{5,1},{9,5},{13,9},{2,14},{6,2},{... | collective-permute-start | bytes 245768 | tf_op jit(solution)/shard_map/ppermute | solution.py:519
  22.4 6.8 %collective-permute-start.8 = (bf16[128,512]{1,0:T(8,128)(2,1)S(1)}, bf16[128,512]{1,0:T(8,128)(2,1)S(1)}, u32[]{:S(2)}, u32[]{:S(2)}) collective-permute-start(bf16[128,512]{1,0:T(8,128)(2,1)S(1)} %collective-permute-done.1.refs_7_.refs_10_.refs_11_), channel_id=1, source_target_pairs={{0,1},{1,3},{3,2},{2,0},{4,5},{5,7},{7,6},{6,4},{8,9},{9,11},{11,1... | collective-permute-start | bytes 393224 | tf_op jit(solution)/shard_map/ppermute | solution.py:42
  22.9 7.7 %collective-permute-start.7 = (bf16[128,512]{1,0:T(8,128)(2,1)S(1)}, bf16[128,512]{1,0:T(8,128)(2,1)S(1)}, u32[]{:S(2)}, u32[]{:S(2)}) collective-permute-start(bf16[128,512]{1,0:T(8,128)(2,1)S(1)} %collective-permute-done.3.refs_5_.refs_6_.refs_7_), channel_id=1, source_target_pairs={{0,1},{1,3},{3,2},{2,0},{4,5},{5,7},{7,6},{6,4},{8,9},{9,11},{11,1... | collective-permute-start | bytes 393224 | tf_op jit(solution)/shard_map/ppermute | solution.py:42
  33.3 11.3 %collective-permute-start.10 = (bf16[2,4096]{1,0:T(2,128)(2,1)S(1)}, bf16[2,4096]{1,0:T(2,128)(2,1)S(1)}, u32[]{:S(2)}, u32[]{:S(2)}) collective-permute-start(bf16[2,4096]{1,0:T(2,128)(2,1)S(1)} %get-tuple-element.37), channel_id=1, source_target_pairs={{0,8},{4,12},{8,0},{12,4},{1,9},{5,13},{9,1},{13,5},{2,10},{6,14},... | collective-permute-start | bytes 49160 | tf_op jit(solution)/shard_map/ppermute | solution.py:529
  34.7 9.9 %collective-permute-start.11 = (bf16[2,4096]{1,0:T(2,128)(2,1)S(1)}, bf16[2,4096]{1,0:T(2,128)(2,1)S(1)}, u32[]{:S(2)}, u32[]{:S(2)}) collective-permute-start(bf16[2,4096]{1,0:T(2,128)(2,1)S(1)} %get-tuple-element.36), channel_id=1, source_target_pairs={{0,4},{4,8},{8,12},{12,0},{1,5},{5,9},{9,13},{13,1},{2,6},{6,10},{... | collective-permute-start | bytes 49160 | tf_op jit(solution)/shard_map/ppermute | solution.py:529
  34.7 9.9 %collective-permute-start.9 = (bf16[2,4096]{1,0:T(2,128)(2,1)S(1)}, bf16[2,4096]{1,0:T(2,128)(2,1)S(1)}, u32[]{:S(2)}, u32[]{:S(2)}) collective-permute-start(bf16[2,4096]{1,0:T(2,128)(2,1)S(1)} %get-tuple-element.34), channel_id=1, source_target_pairs={{0,12},{4,0},{8,4},{12,8},{1,13},{5,1},{9,5},{13,9},{2,14},{6,2},{... | collective-permute-start | bytes 49160 | tf_op jit(solution)/shard_map/ppermute | solution.py:529

commit v8 on v7

--- a/solution.py
+++ b/solution.py
@@ -95,7 +95,7 @@
 
 
 def facts_row(plan, lengths, slots):
-    width, groups, requests = plan.size, lengths.shape[0], slots.shape[0]
+    width, requests = plan.size, slots.shape[0]
 
     def kernel(lengths_ref, slots_ref, out_ref):
         group, member = lax.axis_index("pd"), lax.axis_index("tp")
@@ -114,8 +114,7 @@
 
             @pl.when((place >= 0) & (place < GROUP_REQUESTS))
             def _():
-                back = group - q // GROUP_REQUESTS
-                out_ref[len(values) + place] = jnp.where(back < 0, back + groups, back).astype(jnp.int32)
+                out_ref[len(values) + place] = group ^ (q // GROUP_REQUESTS)
 
     length = 2 + 2 * GROUP_REQUESTS + width + GROUP_REQUESTS
     return pl.pallas_call(
@@ -174,13 +173,23 @@
         pick = column < 0
         for r in range(GROUP_REQUESTS):
             slot = facts.slots[r]
-            back = facts.group - slot // GROUP_REQUESTS
-            back = jnp.where(back < 0, back + pd_size, back)
-            first = jnp.where(back == k, slot % GROUP_REQUESTS * DECODE_STEPS, -DECODE_ROWS * 4)
+            first = jnp.where(facts.group ^ (slot // GROUP_REQUESTS) == k, slot % GROUP_REQUESTS * DECODE_STEPS, -DECODE_ROWS * 4)
             pick = pick | ((row // DECODE_STEPS == r) & (column == first + row - r * DECODE_STEPS))
         part = product(pick.astype(jnp.float32).astype(jnp.bfloat16), block_refs[k][...])
         total = part if total is None else total + part
     return total.astype(jnp.bfloat16)
+
+
+def pick_matrix(facts):
+    row = iota((PADDED_ROWS, PADDED_ROWS), 0)
+    column = iota((PADDED_ROWS, PADDED_ROWS), 1)
+    pick = column < 0
+    for r in range(GROUP_REQUESTS):
+        ahead = facts.group ^ (facts.slots[r] // GROUP_REQUESTS)
+        pick = pick | (
+            (column // DECODE_STEPS == r) & (row == ahead * DECODE_STEPS + column - r * DECODE_STEPS)
+        )
+    return pick.astype(jnp.float32).astype(jnp.bfloat16)
 
 
 def fresh_mask():
@@ -191,29 +200,25 @@
     )
 
 
-def first_kernel(plan, pd_size, facts_ref, q_hbm_ref, k_hbm_ref, v_hbm_ref, *refs):
+def first_kernel(plan, pd_size, facts_ref, maxima_ref, q_ref, *refs):
     width = plan.size
-    k_refs, v_refs, refs = refs[: width - 2], refs[width - 2 : 2 * width - 4], refs[2 * width - 4 :]
+    k_refs, v_refs, refs = refs[: width - 1], refs[width - 1 : 2 * width - 2], refs[2 * width - 2 :]
     block_refs, refs = refs[:pd_size], refs[pd_size:]
-    acc_ref, dec_acc_ref, worst_ref, queries_ref, fresh_ref, q_ref, k_ref, v_ref, sem = refs
-    k_refs, v_refs = (k_ref,) + k_refs, (v_ref,) + v_refs
-    copies = [
-        pltpu.make_async_copy(k_hbm_ref, k_ref, sem.at[KEY_VALUE_HEADS]),
-        pltpu.make_async_copy(v_hbm_ref, v_ref, sem.at[KEY_VALUE_HEADS + 1]),
-    ]
-    for h in range(KEY_VALUE_HEADS):
-        part = pl.ds(h * Q_BLOCK, Q_BLOCK)
-        copies.append(pltpu.make_async_copy(q_hbm_ref.at[:, part], q_ref.at[:, part], sem.at[h]))
-    for copy in copies:
-        copy.start()
+    acc_ref, bias_ref, dec_acc_ref, dec_bias_ref, worst_ref, queries_ref, fresh_ref, pick_ref = refs
     tokens = q_ref.shape[0]
     half = tokens // 2
     facts = Facts(facts_ref, width)
     sources = facts.source[:-1]
+    pick_ref[...] = pick_matrix(facts)
+    for s in range(width):
+        bias_ref[s] = causal_bias(0, tokens, tokens, facts.source[s : s + 1], facts.ends, facts.member, width)
+        dec_bias_ref[s] = jnp.where(
+            request_mask(facts.ends, tokens, facts.source[s : s + 1], width), 0.0, MASKED
+        )
     rows = picked_rows(facts, pd_size, block_refs)
     queries_ref[...] = rows[:, :Q_WIDTH]
     fresh_ref[...] = rows[:, Q_WIDTH:]
-    worst_ref[...] = jnp.full(worst_ref.shape, MASKED, jnp.float32)
+    worst_ref[...] = maxima_ref[...]
     new_mask = fresh_mask()
     mask = request_mask(facts.ends, tokens, sources, width)
     spans = ((0, half), (half, tokens))
@@ -255,8 +260,6 @@
                 )
                 acc_ref[h, rows, :] = product(weigh(exponents), v_part)
 
-    for copy in copies:
-        copy.wait()
     each_kv_head(width, step)
 
 
@@ -287,22 +290,9 @@
     return (jnp.max(worst) > LIMIT) | (jnp.min(least) < 2.0**-LIMIT)
 
 
-def decode_kernel(plan, pd_size, facts_ref, acc_ref, worst_ref, queries_ref, fresh_ref, *refs):
+def decode_kernel(plan, acc_ref, bias_ref, worst_ref, queries_ref, fresh_ref, pick_ref, *refs):
     width = plan.size
     k_refs, v_refs, (out_ref,) = refs[:width], refs[width : 2 * width], refs[2 * width :]
-    tokens = k_refs[0].shape[0]
-    facts = Facts(facts_ref, width)
-    mask = request_mask(facts.ends, tokens, facts.source[-1:], width)
-    row = iota((PADDED_ROWS, PADDED_ROWS), 0)
-    column = iota((PADDED_ROWS, PADDED_ROWS), 1)
-    pick = column < 0
-    for r in range(GROUP_REQUESTS):
-        ahead = facts.slots[r] // GROUP_REQUESTS - facts.group
-        ahead = jnp.where(ahead < 0, ahead + pd_size, ahead)
-        pick = pick | (
-            (column // DECODE_STEPS == r) & (row == ahead * DECODE_STEPS + column - r * DECODE_STEPS)
-        )
-    pick = pick.astype(jnp.float32).astype(jnp.bfloat16)
     heads = range(KEY_VALUE_HEADS)
     columns = [slice(h * HEAD_SIZE, (h + 1) * HEAD_SIZE) for h in heads]
 
@@ -314,10 +304,10 @@
         out = jnp.concatenate(
             [o[g * PADDED_ROWS : (g + 1) * PADDED_ROWS] for o in out for g in range(HEADS_PER_KV)], axis=1
         )
-        out_ref[...] = product(pick, out).astype(jnp.bfloat16)
+        out_ref[...] = product(pick_ref[...], out).astype(jnp.bfloat16)
 
     exponents = [
-        jnp.where(mask, scores_of(queries_of(h), k_refs[-1][:, columns[h]]) * EXPONENT, MASKED)
+        scores_of(queries_of(h), k_refs[-1][:, columns[h]]) * EXPONENT + bias_ref[width - 1]
         for h in heads
     ]
     acc = [
@@ -343,23 +333,18 @@
             for parts in parts_in(width):
                 k_part = jnp.concatenate([k_refs[s][:, columns[h]] for s in parts], axis=0)
                 v_part = jnp.concatenate([v_refs[s][:, columns[h]] for s in parts], axis=0)
-                here = request_mask(facts.ends, tokens, [facts.source[s] for s in parts], width)
-                state = fold(state, [jnp.where(here, scores_of(queries, k_part), MASKED)], [v_part])
+                bias = jnp.concatenate([bias_ref[s] for s in parts], axis=1)
+                state = fold(state, [scores_of(queries, k_part) + bias], [v_part])
             again.append(state[1])
         send(again)
 
 
-def prefill_kernel(plan, facts_ref, acc_ref, worst_ref, q_ref, *refs):
+def prefill_kernel(plan, acc_ref, bias_ref, worst_ref, q_ref, *refs):
     width = plan.size
     k_refs, v_refs, refs = refs[:width], refs[width : 2 * width], refs[2 * width :]
     out_ref, done_ref, sem = refs
     tokens = q_ref.shape[0]
     half = tokens // 2
-    facts = Facts(facts_ref, width)
-
-    def bias_of(start, sources):
-        return causal_bias(start, half, tokens, sources, facts.ends, facts.member, width)
-
     def write(h, start, acc):
         out = divided(acc)
         for g in range(HEADS_PER_KV):
@@ -371,7 +356,7 @@
         part = pl.ds(h * Q_BLOCK, Q_BLOCK)
         return pltpu.make_async_copy(done_ref.at[:, part], out_ref.at[:, part], sem.at[h])
 
-    biases = [bias_of(start, facts.source[-1:]) for start in (0, half)]
+    biases = [bias_ref[width - 1, start : start + half, :] for start in (0, half)]
     worst, least = worst_ref[...], None
     for h in range(KEY_VALUE_HEADS):
         columns = slice(h * HEAD_SIZE, (h + 1) * HEAD_SIZE)
@@ -401,7 +386,7 @@
                 for parts in parts_in(width):
                     k_part = jnp.concatenate([k_refs[s][:, columns] for s in parts], axis=0)
                     v_part = jnp.concatenate([v_refs[s][:, columns] for s in parts], axis=0)
-                    bias = bias_of(start, [facts.source[s] for s in parts])
+                    bias = jnp.concatenate([bias_ref[s, start : start + half, :] for s in parts], axis=1)
                     scores = scores_of(queries, k_part).reshape(HEADS_PER_KV, half, bias.shape[1])
                     scores = (scores + bias[None]).reshape(HEADS_PER_KV * half, bias.shape[1])
                     state = fold(state, [scores], [v_part])
@@ -421,51 +406,50 @@
     )
 
 
-def call_first(plan, facts, query, blocks, keys, values):
+def call_first(plan, facts, maxima, query, blocks, keys, values):
     tokens, width = query.shape[0], plan.size
     rows = HEADS_PER_KV * tokens
     f32, bf16 = jnp.float32, jnp.bfloat16
     every = (width - 1) * tokens
     shapes = [
         jax.ShapeDtypeStruct((KEY_VALUE_HEADS, rows, 2 * HEAD_SIZE), f32),
+        jax.ShapeDtypeStruct((width, tokens, tokens), f32),
         jax.ShapeDtypeStruct((KEY_VALUE_HEADS, STACKED, 2 * HEAD_SIZE), f32),
+        jax.ShapeDtypeStruct((width, STACKED, tokens), f32),
         jax.ShapeDtypeStruct((8, HEAD_SIZE), f32),
         jax.ShapeDtypeStruct((PADDED_ROWS, Q_WIDTH), bf16),
         jax.ShapeDtypeStruct((PADDED_ROWS, 2 * KV_WIDTH), bf16),
-        jax.ShapeDtypeStruct((tokens, Q_WIDTH), bf16),
-        jax.ShapeDtypeStruct((tokens, KV_WIDTH), bf16),
-        jax.ShapeDtypeStruct((tokens, KV_WIDTH), bf16),
+        jax.ShapeDtypeStruct((PADDED_ROWS, PADDED_ROWS), bf16),
     ]
     return pl.pallas_call(
         lambda *refs: first_kernel(plan, len(blocks), *refs),
-        in_specs=[SMEM] + [HBM] * 3 + [VMEM] * (len(blocks) + 2 * (width - 2)),
+        in_specs=[SMEM] + [VMEM] * (2 + len(blocks) + 2 * (width - 1)),
         out_specs=[VMEM] * len(shapes),
         out_shape=shapes,
-        scratch_shapes=[pltpu.SemaphoreType.DMA((KEY_VALUE_HEADS + 2,))],
         compiler_params=pltpu.CompilerParams(vmem_limit_bytes=(28 + width) * MIB),
         cost_estimate=cost(tokens, every, tokens * every * QUERY_HEADS),
         name="first_shards",
-    )(facts, query, keys[0], values[0], *keys[1:], *values[1:], *blocks)
-
-
-def call_decode(plan, pd_size, facts, dec_acc, worst, rows, fresh, keys, values):
+    )(facts, maxima, query, *keys, *values, *blocks)
+
+
+def call_decode(plan, state, keys, values):
     tokens, width = keys[0].shape[0], plan.size
     return pl.pallas_call(
-        lambda *refs: decode_kernel(plan, pd_size, *refs),
-        in_specs=[SMEM] + [VMEM] * (4 + 2 * width),
+        lambda *refs: decode_kernel(plan, *refs),
+        in_specs=[VMEM] * (6 + 2 * width),
         out_specs=VMEM,
         out_shape=jax.ShapeDtypeStruct((PADDED_ROWS, Q_WIDTH), jnp.bfloat16),
         compiler_params=pltpu.CompilerParams(vmem_limit_bytes=(28 + width) * MIB),
         cost_estimate=cost(PADDED_ROWS, tokens, PADDED_ROWS * tokens * QUERY_HEADS),
         name="last_shard_decode",
-    )(facts, dec_acc, worst, rows, fresh, *keys, *values)
-
-
-def call_prefill(plan, facts, acc, worst, query, keys, values):
+    )(*state[2:], *keys, *values)
+
+
+def call_prefill(plan, state, query, keys, values):
     tokens, width = query.shape[0], plan.size
     return pl.pallas_call(
         lambda *refs: prefill_kernel(plan, *refs),
-        in_specs=[SMEM] + [VMEM] * (3 + 2 * width),
+        in_specs=[VMEM] * (4 + 2 * width),
         out_specs=ANY,
         out_shape=jax.ShapeDtypeStruct((tokens, Q_WIDTH), jnp.bfloat16),
         scratch_shapes=[
@@ -475,17 +459,25 @@
         compiler_params=pltpu.CompilerParams(vmem_limit_bytes=(28 + width) * MIB),
         cost_estimate=cost(tokens, tokens, tokens * tokens * QUERY_HEADS),
         name="last_shard_prefill",
-    )(facts, acc, worst, query, *keys, *values)
-
-
-def after(row, *arrays):
-    for array in arrays:
-        row = jnp.where(array[0, 0] == array[0, 0], row, 0)
-    return row
-
-
-def ring(size, step):
-    return [(i, (i + step) % size) for i in range(size)]
+    )(*state[:2], state[4], query, *keys, *values)
+
+
+def start_maxima(*arrays):
+    def kernel(*refs):
+        refs[-1][...] = jnp.full((8, HEAD_SIZE), MASKED, jnp.float32)
+
+    return pl.pallas_call(
+        kernel,
+        in_specs=[VMEM] * len(arrays),
+        out_specs=VMEM,
+        out_shape=jax.ShapeDtypeStruct((8, HEAD_SIZE), jnp.float32),
+        cost_estimate=pl.CostEstimate(flops=5 * 10**9, bytes_accessed=0, transcendentals=0),
+        name="start_maxima",
+    )(*arrays)
+
+
+def paired(array, k):
+    return lax.ppermute(array, "pd", [(g, g ^ k) for g in range(lax.axis_size("pd"))])
 
 
 def body(
@@ -506,28 +498,24 @@
     facts = facts_row(plan, prompt_lengths, decode_slot)
     prompt_key, decoded_query = lax.optimization_barrier((prompt_key, decoded_query))
     prompt_value, own, facts = lax.optimization_barrier((prompt_value, own, facts))
-    keys, values = [prompt_key], [prompt_value]
+    keys, values, maxima = [prompt_key], [prompt_value], None
     for s in range(1, plan.size):
         if s == 2:
             keys[1], own = lax.optimization_barrier((keys[1], own))
         if s == plan.size - 1:
-            facts = after(facts, keys[-1], values[-1])
-            values[-1], facts = lax.optimization_barrier((values[-1], facts))
+            maxima = start_maxima(keys[-1], values[-1])
+            values[-1], maxima = lax.optimization_barrier((values[-1], maxima))
         keys.append(plan.step(keys[-1]))
         values.append(plan.step(values[-1]))
         if s == 2:
-            blocks = [own] + [lax.ppermute(own, "pd", ring(pd_size, k)) for k in range(1, pd_size)]
-
-    acc, dec_acc, worst, rows, fresh, query, key, value = call_first(
-        plan, facts, prompt_query, blocks, keys[:-1], values[:-1]
-    )
-    keys[0], values[0] = key, value
-    outgoing = call_decode(plan, pd_size, facts, dec_acc, worst, rows, fresh, keys, values)
+            blocks = [own] + [paired(own, k) for k in range(1, pd_size)]
+
+    state = call_first(plan, facts, maxima, prompt_query, blocks, keys[:-1], values[:-1])
+    outgoing = call_decode(plan, state, keys, values)
     arrived = [outgoing[:DECODE_STEPS]]
     for k in range(1, pd_size):
-        part = outgoing[k * DECODE_STEPS : (k + 1) * DECODE_STEPS]
-        arrived.append(lax.ppermute(part, "pd", ring(pd_size, k)))
-    pre_out = call_prefill(plan, facts, acc, worst, query, keys, values)
+        arrived.append(paired(outgoing[k * DECODE_STEPS : (k + 1) * DECODE_STEPS], k))
+    pre_out = call_prefill(plan, state, prompt_query, keys, values)
 
     from_block = facts[-GROUP_REQUESTS:]
     dec_out = jnp.zeros((GROUP_REQUESTS, DECODE_STEPS, Q_WIDTH), jnp.bfloat16)

time: 45.7 us -> 43.5 us (0.952)
  between operations: 3.37 us -> 0.78 us
  local copies, waits for them, and re-layouts: 1.14 us -> 3.28 us
  waiting for transfers between devices: 5.45 us -> 4.21 us
  starting transfers between devices: 16.7 us -> 16.2 us
    unnamed x6 -> x20, local copies, waits for them, and re-layouts: 0.02 us -> 3.18 us
    ppermute x6, starting transfers between devices: 6.09 us -> 4.14 us  [paired(): lax.ppermute(array, 'pd', [(g, g ^ k) for g in range(lax.axis_size('pd'))])]
    ppermute x6, starting transfers between devices: 10.6 us -> 12.1 us  [step(): return lax.ppermute(array, 'tp', self.pairs)]
    ppermute x6, waiting for transfers between devices: 5.44 us -> 4.19 us  [step(): return lax.ppermute(array, 'tp', self.pairs)]
    slice x3 -> x1, local copies, waits for them, and re-layouts: 1.08 us -> 0.06 us  [body(): arrived.append(paired(outgoing[k * DECODE_STEPS:(k + 1) * DECODE_STEPS], k))]
    eq x1, other arithmetic: 0.08 us -> 0.67 us  [body(): from_block == k]
    select_n x1 -> x0, other arithmetic: 0.59 us -> none  [after(): row = jnp.where(array[0, 0] == array[0, 0], row, 0)]
    pallas_call x1, Pallas kernels: 4.18 us -> 3.6 us  [call_first(): pl.pallas_call(lambda *refs: first_kernel(plan, len(blocks), *refs), in_s...]
  transfers between devices with their start and end apart: 12 -> 12, of which waited for: 3 -> 3; matrix products, arithmetic and copies ran while one was open for 6% -> 4% of each run, Pallas kernels for 30% -> 33%
where the time goes in v8:
time: 43.5 us; the launch traced here: 43.2 us
  Pallas kernels  16.3 us (37%)
  starting transfers between devices  16.2 us (37%)
  waiting for transfers between devices  4.21 us (10%)
  local copies, waits for them, and re-layouts  3.28 us (8%)
  other arithmetic  2.41 us (6%)
  between operations  0.78 us (2%)
    ppermute x6, starting transfers between devices, step(): return lax.ppermute(array, 'tp', self.pairs)  12.1 us
    pallas_call x1, Pallas kernels, call_prefill(): pl.pallas_call(lambda *refs: prefill_kernel(plan, *refs), in_specs=[VMEM]...  7.58 us
    ppermute x6, waiting for transfers between devices, step(): return lax.ppermute(array, 'tp', self.pairs)  4.19 us
    ppermute x6, starting transfers between devices, paired(): lax.ppermute(array, 'pd', [(g, g ^ k) for g in range(lax.axis_size('pd'))])  4.14 us
    pallas_call x1, Pallas kernels, call_first(): pl.pallas_call(lambda *refs: first_kernel(plan, len(blocks), *refs), in_s...  3.6 us
    unnamed x20, local copies, waits for them, and re-layouts  3.18 us
    pallas_call x1, Pallas kernels, call_decode(): pl.pallas_call(lambda *refs: decode_kernel(plan, *refs), in_specs=[VMEM]...  2.12 us
    pallas_call x1, Pallas kernels, start_maxima(): pl.pallas_call(kernel, in_specs=[VMEM] * len(arrays), out_specs=VMEM, out...  1.56 us
  transfers between devices with their start and end apart: 12, of which 3 were waited for; matrix products, arithmetic and copies ran while one was open for 4% of the time, Pallas kernels for 33%

profile of v8, /device:TPU:0, one launch (start us, length us, event | category | flops | bytes accessed | tf_op | source)
XLA Modules:
  0.0 43.2 jit_solution(4661377900122413242)
XLA Ops:
  0.6 3.1 %collective-permute-start.2 = (bf16[128,512]{1,0:T(8,128)(2,1)}, bf16[128,512]{1,0:T(8,128)(2,1)S(1)}, u32[]{:S(2)}, u32[]{:S(2)}) collective-permute-start(bf16[128,512]{1,0:T(8,128)(2,1)} %refs_6_.1), channel_id=1, source_target_pairs={{0,1},{1,3},{3,2},{2,0},{4,5},{5,7},{7,6},{6,4},{8,9},{9,11},{11,1... | collective-permute-start | bytes 393224 | tf_op jit(solution)/shard_map/ppermute | solution.py:42
  3.7 0.9 %pad_maximum_fusion = bf16[4,2,5120]{2,1,0:T(2,128)(2,1)S(1)} fusion(bf16[4,2,512]{2,1,0:T(2,128)(2,1)} %param.15, bf16[4,2,512]{2,1,0:T(2,128)(2,1)} %param.14, bf16[4,2,4096]{2,1,0:T(2,128)(2,1)} %param.13), kind=kLoop, calls=%fused_computation.4 | loop fusion | flops 245760 | bytes 163840 | tf_op jit(solution)/shard_map/concatenate | solution.py:495
  4.7 0.0 copy-start.1
  4.7 1.4 %facts.1.refs_0_ = s32[18]{0:T(128)} custom-call(s32[4,4]{1,0:T(4,128)} %lengths_ref.1, s32[16]{0:T(128)} %slots_ref.1), custom_call_target="tpu_custom_call" | custom-call | flops 5000000000 | tf_op jit(solution)/shard_map/facts/pallas_call | solution.py:120
  6.1 0.0 copy-done.1
  6.2 2.6 %collective-permute-start = (bf16[128,512]{1,0:T(8,128)(2,1)S(1)}, bf16[128,512]{1,0:T(8,128)(2,1)S(1)}, u32[]{:S(2)}, u32[]{:S(2)}) collective-permute-start(bf16[128,512]{1,0:T(8,128)(2,1)S(1)} %copy-done.1), channel_id=1, source_target_pairs={{0,1},{1,3},{3,2},{2,0},{4,5},{5,7},{7,6},{6,4},{8,9},{9,11},{11,1... | collective-permute-start | bytes 393224 | tf_op jit(solution)/shard_map/ppermute | solution.py:42
  8.8 0.0 collective-permute-done.2.refs_4_.refs_5_.refs_7_
  8.8 0.9 %collective-permute-start.3 = (bf16[128,512]{1,0:T(8,128)(2,1)S(1)}, bf16[128,512]{1,0:T(8,128)(2,1)S(1)}, u32[]{:S(2)}, u32[]{:S(2)}) collective-permute-start(bf16[128,512]{1,0:T(8,128)(2,1)S(1)} %collective-permute-done.2.refs_4_.refs_5_.refs_7_), channel_id=1, source_target_pairs={{0,1},{1,3},{3,2},{2,0},{4,5},{5,7},{7,6},{6,4},{8,9},{9,11},{11,1... | collective-permute-start | bytes 393224 | tf_op jit(solution)/shard_map/ppermute | solution.py:42
  9.7 3.1 %collective-permute-done.refs_7_.refs_9_.refs_11_ = bf16[128,512]{1,0:T(8,128)(2,1)S(1)} collective-permute-done((bf16[128,512]{1,0:T(8,128)(2,1)S(1)}, bf16[128,512]{1,0:T(8,128)(2,1)S(1)}, u32[]{:S(2)}, u32[]{:S(2)}) %collective-permute-start) | collective-permute-done | bytes 131104 | tf_op jit(solution)/shard_map/ppermute | solution.py:42
  12.7 2.5 %collective-permute-start.1 = (bf16[128,512]{1,0:T(8,128)(2,1)S(1)}, bf16[128,512]{1,0:T(8,128)(2,1)S(1)}, u32[]{:S(2)}, u32[]{:S(2)}) collective-permute-start(bf16[128,512]{1,0:T(8,128)(2,1)S(1)} %collective-permute-done.refs_7_.refs_9_.refs_11_), channel_id=1, source_target_pairs={{0,1},{1,3},{3,2},{2,0},{4,5},{5,7},{7,6},{6,4},{8,9},{9,11},{11,1... | collective-permute-start | bytes 393224 | tf_op jit(solution)/shard_map/ppermute | solution.py:42
  15.2 0.7 %broadcast_compare_fusion.2 = (pred[4]{0:T(512)(128)(4,1)S(1)}, pred[4]{0:T(512)(128)(4,1)S(1)}, pred[4]{0:T(512)(128)(4,1)S(1)}, pred[4]{0:T(512)(128)(4,1)S(1)}) fusion(s32[18]{0:T(128)} %facts.1.refs_0_), kind=kLoop, calls=%fused_computation.7 | loop fusion | flops 16 | bytes 32 | tf_op jit(solution)/shard_map/eq | solution.py:523
  15.9 0.0 copy-start
  15.9 0.0 copy-start.7
  15.9 0.0 copy-start.8
  15.9 0.1 collective-permute-start.4
  16.0 1.6 %collective-permute-start.5 = (bf16[8,5120]{1,0:T(8,128)(2,1)S(1)}, bf16[8,5120]{1,0:T(8,128)(2,1)S(1)}, u32[]{:S(2)}, u32[]{:S(2)}) collective-permute-start(bf16[8,5120]{1,0:T(8,128)(2,1)S(1)} %reshape.15.refs_9_), channel_id=1, source_target_pairs={{0,8},{4,12},{8,0},{12,4},{1,9},{5,13},{9,1},{13,5},{2,10},{6,14},... | collective-permute-start | bytes 245768 | tf_op jit(solution)/shard_map/ppermute | solution.py:480
  17.5 0.3 collective-permute-start.6
  17.8 0.0 collective-permute-done.3.refs_0_.refs_5_.refs_6_.refs_8_
  17.8 0.0 copy-start.2
  17.8 0.8 %collective-permute-done.1.refs_1_.refs_8_.refs_10_.refs_12_ = bf16[128,512]{1,0:T(8,128)(2,1)S(1)} collective-permute-done((bf16[128,512]{1,0:T(8,128)(2,1)S(1)}, bf16[128,512]{1,0:T(8,128)(2,1)S(1)}, u32[]{:S(2)}, u32[]{:S(2)}) %collective-permute-start.1) | collective-permute-done | bytes 131104 | tf_op jit(solution)/shard_map/ppermute | solution.py:42
  18.6 0.0 copy-done.2
  18.6 0.0 copy-start.5
  18.6 0.6 %copy-done.5 = bf16[128,512]{1,0:T(8,128)(2,1)} copy-done((bf16[128,512]{1,0:T(8,128)(2,1)}, bf16[128,512]{1,0:T(8,128)(2,1)S(1)}, u32[]{:S(2)}) %copy-start.5) | copy-done | bytes 131096
  19.3 1.6 %start_maxima.1.refs_1_ = f32[8,128]{1,0:T(8,128)} custom-call(bf16[128,512]{1,0:T(8,128)(2,1)} %copy-done.2, bf16[128,512]{1,0:T(8,128)(2,1)} %copy-done.5), custom_call_target="tpu_custom_call" | custom-call | flops 5000000000 | tf_op jit(solution)/shard_map/start_maxima/pallas_call | solution.py:469
  20.8 1.6 %collective-permute-start.8 = (bf16[128,512]{1,0:T(8,128)(2,1)}, bf16[128,512]{1,0:T(8,128)(2,1)S(1)}, u32[]{:S(2)}, u32[]{:S(2)}) collective-permute-start(bf16[128,512]{1,0:T(8,128)(2,1)} %copy-done.5), channel_id=1, source_target_pairs={{0,1},{1,3},{3,2},{2,0},{4,5},{5,7},{7,6},{6,4},{8,9},{9,11},{11,1... | collective-permute-start | bytes 393224 | tf_op jit(solution)/shard_map/ppermute | solution.py:42
  22.4 1.4 %collective-permute-start.7 = (bf16[128,512]{1,0:T(8,128)(2,1)}, bf16[128,512]{1,0:T(8,128)(2,1)S(1)}, u32[]{:S(2)}, u32[]{:S(2)}) collective-permute-start(bf16[128,512]{1,0:T(8,128)(2,1)} %copy-done.2), channel_id=1, source_target_pairs={{0,1},{1,3},{3,2},{2,0},{4,5},{5,7},{7,6},{6,4},{8,9},{9,11},{11,1... | collective-permute-start | bytes 393224 | tf_op jit(solution)/shard_map/ppermute | solution.py:42
  23.8 0.0 collective-permute-done.4.refs_10_
  23.8 0.0 collective-permute-done.5.refs_11_
  23.8 0.0 collective-permute-done.6.refs_12_
  23.8 0.0 copy-done
  23.8 0.0 copy-done.7
  23.9 0.0 copy-done.8
  23.9 0.0 copy-start.3
  23.9 0.9 %copy-done.3 = bf16[128,512]{1,0:T(8,128)(2,1)S(1)} copy-done((bf16[128,512]{1,0:T(8,128)(2,1)S(1)}, bf16[128,512]{1,0:T(8,128)(2,1)}, u32[]{:S(2)}) %copy-start.3) | copy-done | bytes 131096
  24.8 0.0 copy-start.6
  24.8 0.9 %copy-done.6 = bf16[128,512]{1,0:T(8,128)(2,1)S(1)} copy-done((bf16[128,512]{1,0:T(8,128)(2,1)S(1)}, bf16[128,512]{1,0:T(8,128)(2,1)}, u32[]{:S(2)}) %copy-start.6) | copy-done | bytes 131096
  25.7 0.0 copy-start.9
  25.7 0.7 %copy-done.9 = f32[8,128]{1,0:T(8,128)S(1)} copy-done((f32[8,128]{1,0:T(8,128)S(1)}, f32[8,128]{1,0:T(8,128)}, u32[]{:S(2)}) %copy-start.9) | copy-done | bytes 4120
  26.4 0.0 copy-start.4
  26.4 3.6 %first_shards.1 = (f32[4,1024,256]{2,1,0:T(8,128)S(1)}, f32[4,128,128]{2,1,0:T(8,128)S(1)}, f32[4,128,256]{2,1,0:T(8,128)S(1)}, f32[4,128,128]{2,1,0:T(8,128)S(1...) custom-call(s32[18]{0:T(128)S(1)} %copy-done.7, ...), custom_call_target="tpu_custom_call" | custom-call | flops 6442450944 | bytes 2097152 | tf_op jit(solution)/shard_map/first_shards/pallas_call | solution.py:424
  30.0 0.0 collective-permute-done.8.refs_11_.refs_13_
  30.0 0.4 collective-permute-done.7.refs_7_.refs_9_
  30.4 0.0 copy-done.4
  30.4 2.1 %last_shard_decode.1 = bf16[16,4096]{1,0:T(8,128)(2,1)S(1)} custom-call(f32[4,128,256]{2,1,0:T(8,128)S(1)} %get-tuple-element.29.refs_0_, f32[4,128,128]{2,1,0:T(8,128)S(1)} %get-tuple-element.30.refs_1_, f32[8,128]{1,0:T(8,128)S(1)} %get-tuple-element.28.refs_2_, bf16[16,4096]{1,0:T(8,128)(2,1)S(1)} %get-tuple-element.31.refs_3_, ...), custom_call_target="tpu_custom_call" | custom-call | flops 268435456 | bytes 262144 | tf_op jit(solution)/shard_map/last_shard_decode/pallas_call | solution.py:437
  32.5 0.1 fusion
  32.6 1.6 %collective-permute-start.10 = (bf16[2,4096]{1,0:T(2,128)(2,1)S(1)}, bf16[2,4096]{1,0:T(2,128)(2,1)S(1)}, u32[]{:S(2)}, u32[]{:S(2)}) collective-permute-start(bf16[2,4096]{1,0:T(2,128)(2,1)S(1)} %get-tuple-element.37), channel_id=1, source_target_pairs={{0,8},{4,12},{8,0},{12,4},{1,9},{5,13},{9,1},{13,5},{2,10},{6,14},... | collective-permute-start | bytes 49160 | tf_op jit(solution)/shard_map/ppermute | solution.py:480
  34.1 0.0 collective-permute-start.11
  34.1 0.6 %collective-permute-start.9 = (bf16[2,4096]{1,0:T(2,128)(2,1)S(1)}, bf16[2,4096]{1,0:T(2,128)(2,1)S(1)}, u32[]{:S(2)}, u32[]{:S(2)}) collective-permute-start(bf16[2,4096]{1,0:T(2,128)(2,1)S(1)} %get-tuple-element.34), channel_id=1, source_target_pairs={{0,12},{4,8},{8,4},{12,0},{1,13},{5,9},{9,5},{13,1},{2,14},{6,10},... | collective-permute-start | bytes 49160 | tf_op jit(solution)/shard_map/ppermute | solution.py:480
  34.8 7.6 %last_shard_prefill.1 = bf16[128,4096]{1,0:T(8,128)(2,1)} custom-call(f32[4,1024,256]{2,1,0:T(8,128)S(1)} %get-tuple-element.26.refs_0_, f32[4,128,128]{2,1,0:T(8,128)S(1)} %get-tuple-element.27.refs_1_, f32[8,128]{1,0:T(8,128)S(1)} %get-tuple-element.28.refs_2_, bf16[128,4096]{1,0:T(8,128)(2,1)S(1)} %copy-done.8, bf16[128,512]{1,0:T(8,128)(2,1)S(1)} %copy-done, ...), custom_call_target="tpu_custom_call" | custom-call | flops 2147483648 | bytes 2097152 | tf_op jit(solution)/shard_map/last_shard_prefill/pallas_call | solution.py:450
  42.4 0.0 collective-permute-done.10
  42.4 0.0 collective-permute-done.11
  42.4 0.0 collective-permute-done.9
  42.4 0.8 %broadcast_select_fusion.2 = bf16[4,2,4096]{2,1,0:T(2,128)(2,1)} fusion(pred[4]{0:T(512)(128)(4,1)S(1)} %get-tuple-element.41, pred[4]{0:T(512)(128)(4,1)S(1)} %get-tuple-element.40, pred[4]{0:T(512)(128)(4,1)S(1)} %get-tuple-element.39, pred[4]{0:T(512)(128)(4,1)S(1)} %get-tuple-element.38, bf16[2,4096]{1,0:T(2,128)(2,1)S(1)} %get-tuple-element.35, ...), kind=kLoop, calls=%fused_computation.2 | loop fusion | flops 131072 | bytes 131088 | tf_op jit(solution)/shard_map/jit(_where)/select_n | solution.py:523
  (1 shorter events, 0.0 us)
Async XLA Ops:
  0.6 8.2 %collective-permute-start.2 = (bf16[128,512]{1,0:T(8,128)(2,1)}, bf16[128,512]{1,0:T(8,128)(2,1)S(1)}, u32[]{:S(2)}, u32[]{:S(2)}) collective-permute-start(bf16[128,512]{1,0:T(8,128)(2,1)} %refs_6_.1), channel_id=1, source_target_pairs={{0,1},{1,3},{3,2},{2,0},{4,5},{5,7},{7,6},{6,4},{8,9},{9,11},{11,1... | collective-permute-start | bytes 393224 | tf_op jit(solution)/shard_map/ppermute | solution.py:42
  4.7 1.5 %copy-start.1 = (bf16[128,512]{1,0:T(8,128)(2,1)S(1)}, bf16[128,512]{1,0:T(8,128)(2,1)}, u32[]{:S(2)}) copy-start(bf16[128,512]{1,0:T(8,128)(2,1)} %refs_10_) | copy-start | bytes 393220
  6.2 6.6 %collective-permute-start = (bf16[128,512]{1,0:T(8,128)(2,1)S(1)}, bf16[128,512]{1,0:T(8,128)(2,1)S(1)}, u32[]{:S(2)}, u32[]{:S(2)}) collective-permute-start(bf16[128,512]{1,0:T(8,128)(2,1)S(1)} %copy-done.1), channel_id=1, source_target_pairs={{0,1},{1,3},{3,2},{2,0},{4,5},{5,7},{7,6},{6,4},{8,9},{9,11},{11,1... | collective-permute-start | bytes 393224 | tf_op jit(solution)/shard_map/ppermute | solution.py:42
  8.8 9.0 %collective-permute-start.3 = (bf16[128,512]{1,0:T(8,128)(2,1)S(1)}, bf16[128,512]{1,0:T(8,128)(2,1)S(1)}, u32[]{:S(2)}, u32[]{:S(2)}) collective-permute-start(bf16[128,512]{1,0:T(8,128)(2,1)S(1)} %collective-permute-done.2.refs_4_.refs_5_.refs_7_), channel_id=1, source_target_pairs={{0,1},{1,3},{3,2},{2,0},{4,5},{5,7},{7,6},{6,4},{8,9},{9,11},{11,1... | collective-permute-start | bytes 393224 | tf_op jit(solution)/shard_map/ppermute | solution.py:42
  12.7 5.9 %collective-permute-start.1 = (bf16[128,512]{1,0:T(8,128)(2,1)S(1)}, bf16[128,512]{1,0:T(8,128)(2,1)S(1)}, u32[]{:S(2)}, u32[]{:S(2)}) collective-permute-start(bf16[128,512]{1,0:T(8,128)(2,1)S(1)} %collective-permute-done.refs_7_.refs_9_.refs_11_), channel_id=1, source_target_pairs={{0,1},{1,3},{3,2},{2,0},{4,5},{5,7},{7,6},{6,4},{8,9},{9,11},{11,1... | collective-permute-start | bytes 393224 | tf_op jit(solution)/shard_map/ppermute | solution.py:42
  15.9 7.9 %copy-start = (bf16[128,512]{1,0:T(8,128)(2,1)S(1)}, bf16[128,512]{1,0:T(8,128)(2,1)}, u32[]{:S(2)}) copy-start(bf16[128,512]{1,0:T(8,128)(2,1)} %refs_6_.1) | copy-start | bytes 393220
  15.9 8.0 %copy-start.7 = (s32[18]{0:T(128)S(1)}, s32[18]{0:T(128)}, u32[]{:S(2)}) copy-start(s32[18]{0:T(128)} %facts.1.refs_0_) | copy-start | bytes 220
  15.9 8.0 %copy-start.8 = (bf16[128,4096]{1,0:T(8,128)(2,1)S(1)}, bf16[128,4096]{1,0:T(8,128)(2,1)}, u32[]{:S(2)}) copy-start(bf16[128,4096]{1,0:T(8,128)(2,1)} %refs_3_.2) | copy-start | bytes 3145732
  15.9 7.9 %collective-permute-start.4 = (bf16[8,5120]{1,0:T(8,128)(2,1)S(1)}, bf16[8,5120]{1,0:T(8,128)(2,1)S(1)}, u32[]{:S(2)}, u32[]{:S(2)}) collective-permute-start(bf16[8,5120]{1,0:T(8,128)(2,1)S(1)} %reshape.15.refs_9_), channel_id=1, source_target_pairs={{0,4},{4,0},{8,12},{12,8},{1,5},{5,1},{9,13},{13,9},{2,6},{6,2},{1... | collective-permute-start | bytes 245768 | tf_op jit(solution)/shard_map/ppermute | solution.py:480
  16.0 7.9 %collective-permute-start.5 = (bf16[8,5120]{1,0:T(8,128)(2,1)S(1)}, bf16[8,5120]{1,0:T(8,128)(2,1)S(1)}, u32[]{:S(2)}, u32[]{:S(2)}) collective-permute-start(bf16[8,5120]{1,0:T(8,128)(2,1)S(1)} %reshape.15.refs_9_), channel_id=1, source_target_pairs={{0,8},{4,12},{8,0},{12,4},{1,9},{5,13},{9,1},{13,5},{2,10},{6,14},... | collective-permute-start | bytes 245768 | tf_op jit(solution)/shard_map/ppermute | solution.py:480
  17.5 6.3 %collective-permute-start.6 = (bf16[8,5120]{1,0:T(8,128)(2,1)S(1)}, bf16[8,5120]{1,0:T(8,128)(2,1)S(1)}, u32[]{:S(2)}, u32[]{:S(2)}) collective-permute-start(bf16[8,5120]{1,0:T(8,128)(2,1)S(1)} %reshape.15.refs_9_), channel_id=1, source_target_pairs={{0,12},{4,8},{8,4},{12,0},{1,13},{5,9},{9,5},{13,1},{2,14},{6,10},... | collective-permute-start | bytes 245768 | tf_op jit(solution)/shard_map/ppermute | solution.py:480
  17.8 0.8 %copy-start.2 = (bf16[128,512]{1,0:T(8,128)(2,1)}, bf16[128,512]{1,0:T(8,128)(2,1)S(1)}, u32[]{:S(2)}) copy-start(bf16[128,512]{1,0:T(8,128)(2,1)S(1)} %collective-permute-done.3.refs_0_.refs_5_.refs_6_.refs_8_) | copy-start | bytes 393220
  18.6 0.6 %copy-start.5 = (bf16[128,512]{1,0:T(8,128)(2,1)}, bf16[128,512]{1,0:T(8,128)(2,1)S(1)}, u32[]{:S(2)}) copy-start(bf16[128,512]{1,0:T(8,128)(2,1)S(1)} %collective-permute-done.1.refs_1_.refs_8_.refs_10_.refs_12_) | copy-start | bytes 393220
  20.8 9.2 %collective-permute-start.8 = (bf16[128,512]{1,0:T(8,128)(2,1)}, bf16[128,512]{1,0:T(8,128)(2,1)S(1)}, u32[]{:S(2)}, u32[]{:S(2)}) collective-permute-start(bf16[128,512]{1,0:T(8,128)(2,1)} %copy-done.5), channel_id=1, source_target_pairs={{0,1},{1,3},{3,2},{2,0},{4,5},{5,7},{7,6},{6,4},{8,9},{9,11},{11,1... | collective-permute-start | bytes 393224 | tf_op jit(solution)/shard_map/ppermute | solution.py:42
  22.4 8.0 %collective-permute-start.7 = (bf16[128,512]{1,0:T(8,128)(2,1)}, bf16[128,512]{1,0:T(8,128)(2,1)S(1)}, u32[]{:S(2)}, u32[]{:S(2)}) collective-permute-start(bf16[128,512]{1,0:T(8,128)(2,1)} %copy-done.2), channel_id=1, source_target_pairs={{0,1},{1,3},{3,2},{2,0},{4,5},{5,7},{7,6},{6,4},{8,9},{9,11},{11,1... | collective-permute-start | bytes 393224 | tf_op jit(solution)/shard_map/ppermute | solution.py:42
  23.9 0.9 %copy-start.3 = (bf16[128,512]{1,0:T(8,128)(2,1)S(1)}, bf16[128,512]{1,0:T(8,128)(2,1)}, u32[]{:S(2)}) copy-start(bf16[128,512]{1,0:T(8,128)(2,1)} %copy-done.2) | copy-start | bytes 393220
  24.8 0.9 %copy-start.6 = (bf16[128,512]{1,0:T(8,128)(2,1)S(1)}, bf16[128,512]{1,0:T(8,128)(2,1)}, u32[]{:S(2)}) copy-start(bf16[128,512]{1,0:T(8,128)(2,1)} %copy-done.5) | copy-start | bytes 393220
  25.7 0.7 %copy-start.9 = (f32[8,128]{1,0:T(8,128)S(1)}, f32[8,128]{1,0:T(8,128)}, u32[]{:S(2)}) copy-start(f32[8,128]{1,0:T(8,128)} %start_maxima.1.refs_1_) | copy-start | bytes 12292
  26.4 4.0 %copy-start.4 = (bf16[128,512]{1,0:T(8,128)(2,1)S(1)}, bf16[128,512]{1,0:T(8,128)(2,1)}, u32[]{:S(2)}) copy-start(bf16[128,512]{1,0:T(8,128)(2,1)} %copy-done.2) | copy-start | bytes 393220
  32.6 9.8 %collective-permute-start.10 = (bf16[2,4096]{1,0:T(2,128)(2,1)S(1)}, bf16[2,4096]{1,0:T(2,128)(2,1)S(1)}, u32[]{:S(2)}, u32[]{:S(2)}) collective-permute-start(bf16[2,4096]{1,0:T(2,128)(2,1)S(1)} %get-tuple-element.37), channel_id=1, source_target_pairs={{0,8},{4,12},{8,0},{12,4},{1,9},{5,13},{9,1},{13,5},{2,10},{6,14},... | collective-permute-start | bytes 49160 | tf_op jit(solution)/shard_map/ppermute | solution.py:480
  34.1 8.3 %collective-permute-start.11 = (bf16[2,4096]{1,0:T(2,128)(2,1)S(1)}, bf16[2,4096]{1,0:T(2,128)(2,1)S(1)}, u32[]{:S(2)}, u32[]{:S(2)}) collective-permute-start(bf16[2,4096]{1,0:T(2,128)(2,1)S(1)} %get-tuple-element.36), channel_id=1, source_target_pairs={{0,4},{4,0},{8,12},{12,8},{1,5},{5,1},{9,13},{13,9},{2,6},{6,2},{1... | collective-permute-start | bytes 49160 | tf_op jit(solution)/shard_map/ppermute | solution.py:480
  34.1 8.3 %collective-permute-start.9 = (bf16[2,4096]{1,0:T(2,128)(2,1)S(1)}, bf16[2,4096]{1,0:T(2,128)(2,1)S(1)}, u32[]{:S(2)}, u32[]{:S(2)}) collective-permute-start(bf16[2,4096]{1,0:T(2,128)(2,1)S(1)} %get-tuple-element.34), channel_id=1, source_target_pairs={{0,12},{4,8},{8,4},{12,0},{1,13},{5,9},{9,5},{13,1},{2,14},{6,10},... | collective-permute-start | bytes 49160 | tf_op jit(solution)/shard_map/ppermute | solution.py:480

commit v9 on v8

--- a/solution.py
+++ b/solution.py
@@ -123,6 +123,7 @@
         out_specs=SMEM,
         out_shape=jax.ShapeDtypeStruct((length,), jnp.int32),
         cost_estimate=pl.CostEstimate(flops=5 * 10**9, bytes_accessed=0, transcendentals=0),
+        compiler_params=pltpu.CompilerParams(vmem_limit_bytes=MIB),
         name="facts",
     )(lengths, slots)
 
@@ -472,6 +473,7 @@
         out_specs=VMEM,
         out_shape=jax.ShapeDtypeStruct((8, HEAD_SIZE), jnp.float32),
         cost_estimate=pl.CostEstimate(flops=5 * 10**9, bytes_accessed=0, transcendentals=0),
+        compiler_params=pltpu.CompilerParams(vmem_limit_bytes=MIB),
         name="start_maxima",
     )(*arrays)
 

time: 43.5 us -> 41 us (0.943)
  local copies, waits for them, and re-layouts: 3.28 us -> 1.44 us
  Pallas kernels: 16.3 us -> 14.6 us
  waiting for transfers between devices: 4.21 us -> 5.84 us
  other arithmetic: 2.41 us -> 1.82 us
    unnamed x20 -> x10, local copies, waits for them, and re-layouts: 3.18 us -> 1.34 us
    ppermute x6, waiting for transfers between devices: 4.19 us -> 5.82 us  [step(): return lax.ppermute(array, 'tp', self.pairs)]
    pallas_call x1, Pallas kernels: 1.56 us -> 0.01 us  [start_maxima(): pl.pallas_call(kernel, in_specs=[VMEM] * len(arrays), out_specs=VMEM, out...]
    eq x1, other arithmetic: 0.67 us -> 0.08 us  [body(): from_block == k]
  transfers between devices with their start and end apart: 12 -> 12, of which waited for: 3 -> 3; matrix products, arithmetic and copies ran while one was open for 4% -> 3% of each run, Pallas kernels for 33% -> 31%
where the time goes in v9:
time: 41 us; the launch traced here: 40.7 us
  starting transfers between devices  16.3 us (40%)
  Pallas kernels  14.6 us (36%)
  waiting for transfers between devices  5.84 us (14%)
  other arithmetic  1.82 us (4%)
  local copies, waits for them, and re-layouts  1.44 us (4%)
  between operations  0.76 us (2%)
    ppermute x6, starting transfers between devices, step(): return lax.ppermute(array, 'tp', self.pairs)  12.2 us
    pallas_call x1, Pallas kernels, call_prefill(): pl.pallas_call(lambda *refs: prefill_kernel(plan, *refs), in_specs=[VMEM]...  7.62 us
    ppermute x6, waiting for transfers between devices, step(): return lax.ppermute(array, 'tp', self.pairs)  5.82 us
    ppermute x6, starting transfers between devices, paired(): lax.ppermute(array, 'pd', [(g, g ^ k) for g in range(lax.axis_size('pd'))])  4.1 us
    pallas_call x1, Pallas kernels, call_first(): pl.pallas_call(lambda *refs: first_kernel(plan, len(blocks), *refs), in_s...  3.61 us
    pallas_call x1, Pallas kernels, call_decode(): pl.pallas_call(lambda *refs: decode_kernel(plan, *refs), in_specs=[VMEM]...  2.14 us
    unnamed x10, local copies, waits for them, and re-layouts  1.34 us
    pallas_call x1, Pallas kernels, facts_row(): pl.pallas_call(kernel, in_specs=[SMEM, SMEM], out_specs=SMEM, out_shape=j...  1.24 us
  transfers between devices with their start and end apart: 12, of which 3 were waited for; matrix products, arithmetic and copies ran while one was open for 3% of the time, Pallas kernels for 31%

profile of v9, /device:TPU:0, one launch (start us, length us, event | category | flops | bytes accessed | tf_op | source)
XLA Modules:
  0.0 40.7 jit_solution(255230288310370310)
XLA Ops:
  0.6 3.1 %collective-permute-start.2 = (bf16[128,512]{1,0:T(8,128)(2,1)}, bf16[128,512]{1,0:T(8,128)(2,1)S(1)}, u32[]{:S(2)}, u32[]{:S(2)}) collective-permute-start(bf16[128,512]{1,0:T(8,128)(2,1)} %refs_6_.1), channel_id=1, source_target_pairs={{0,1},{1,3},{3,2},{2,0},{4,5},{5,7},{7,6},{6,4},{8,9},{9,11},{11,1... | collective-permute-start | bytes 393224 | tf_op jit(solution)/shard_map/ppermute | solution.py:42
  3.7 0.9 %pad_maximum_fusion = bf16[4,2,5120]{2,1,0:T(2,128)(2,1)S(1)} fusion(bf16[4,2,512]{2,1,0:T(2,128)(2,1)} %param.15, bf16[4,2,512]{2,1,0:T(2,128)(2,1)} %param.14, bf16[4,2,4096]{2,1,0:T(2,128)(2,1)} %param.13), kind=kLoop, calls=%fused_computation.4 | loop fusion | flops 245760 | bytes 163840 | tf_op jit(solution)/shard_map/concatenate | solution.py:497
  4.7 0.0 copy-start.3
  4.7 0.7 %copy-done.3 = s32[4,4]{1,0:T(4,128)S(1)} copy-done((s32[4,4]{1,0:T(4,128)S(1)}, s32[4,4]{1,0:T(4,128)}, u32[]{:S(2)}) %copy-start.3) | copy-done | bytes 88
  5.3 0.0 copy-start.4
  5.3 0.7 %copy-done.4 = s32[16]{0:T(128)S(1)} copy-done((s32[16]{0:T(128)S(1)}, s32[16]{0:T(128)}, u32[]{:S(2)}) %copy-start.4) | copy-done | bytes 88
  6.0 0.0 copy-start.1
  6.0 1.2 %facts.1.refs_0_ = s32[18]{0:T(128)S(1)} custom-call(s32[4,4]{1,0:T(4,128)S(1)} %copy-done.3, s32[16]{0:T(128)S(1)} %copy-done.4), custom_call_target="tpu_custom_call" | custom-call | flops 5000000000 | tf_op jit(solution)/shard_map/facts/pallas_call | solution.py:120
  7.3 0.0 copy-done.1
  7.3 2.6 %collective-permute-start = (bf16[128,512]{1,0:T(8,128)(2,1)S(1)}, bf16[128,512]{1,0:T(8,128)(2,1)S(1)}, u32[]{:S(2)}, u32[]{:S(2)}) collective-permute-start(bf16[128,512]{1,0:T(8,128)(2,1)S(1)} %copy-done.1), channel_id=1, source_target_pairs={{0,1},{1,3},{3,2},{2,0},{4,5},{5,7},{7,6},{6,4},{8,9},{9,11},{11,1... | collective-permute-start | bytes 393224 | tf_op jit(solution)/shard_map/ppermute | solution.py:42
  9.9 0.0 collective-permute-done.2.refs_4_.refs_5_.refs_7_
  9.9 0.5 %collective-permute-start.3 = (bf16[128,512]{1,0:T(8,128)(2,1)S(1)}, bf16[128,512]{1,0:T(8,128)(2,1)S(1)}, u32[]{:S(2)}, u32[]{:S(2)}) collective-permute-start(bf16[128,512]{1,0:T(8,128)(2,1)S(1)} %collective-permute-done.2.refs_4_.refs_5_.refs_7_), channel_id=1, source_target_pairs={{0,1},{1,3},{3,2},{2,0},{4,5},{5,7},{7,6},{6,4},{8,9},{9,11},{11,1... | collective-permute-start | bytes 393224 | tf_op jit(solution)/shard_map/ppermute | solution.py:42
  10.4 3.5 %collective-permute-done.refs_7_.refs_9_.refs_11_ = bf16[128,512]{1,0:T(8,128)(2,1)S(1)} collective-permute-done((bf16[128,512]{1,0:T(8,128)(2,1)S(1)}, bf16[128,512]{1,0:T(8,128)(2,1)S(1)}, u32[]{:S(2)}, u32[]{:S(2)}) %collective-permute-start) | collective-permute-done | bytes 131104 | tf_op jit(solution)/shard_map/ppermute | solution.py:42
  13.9 2.5 %collective-permute-start.1 = (bf16[128,512]{1,0:T(8,128)(2,1)S(1)}, bf16[128,512]{1,0:T(8,128)(2,1)S(1)}, u32[]{:S(2)}, u32[]{:S(2)}) collective-permute-start(bf16[128,512]{1,0:T(8,128)(2,1)S(1)} %collective-permute-done.refs_7_.refs_9_.refs_11_), channel_id=1, source_target_pairs={{0,1},{1,3},{3,2},{2,0},{4,5},{5,7},{7,6},{6,4},{8,9},{9,11},{11,1... | collective-permute-start | bytes 393224 | tf_op jit(solution)/shard_map/ppermute | solution.py:42
  16.4 0.1 broadcast_compare_fusion.2
  16.4 0.0 copy-start
  16.4 0.0 copy-start.2
  16.4 0.0 collective-permute-start.4
  16.5 1.6 %collective-permute-start.5 = (bf16[8,5120]{1,0:T(8,128)(2,1)S(1)}, bf16[8,5120]{1,0:T(8,128)(2,1)S(1)}, u32[]{:S(2)}, u32[]{:S(2)}) collective-permute-start(bf16[8,5120]{1,0:T(8,128)(2,1)S(1)} %reshape.15.refs_9_), channel_id=1, source_target_pairs={{0,8},{4,12},{8,0},{12,4},{1,9},{5,13},{9,1},{13,5},{2,10},{6,14},... | collective-permute-start | bytes 245768 | tf_op jit(solution)/shard_map/ppermute | solution.py:482
  18.0 0.3 collective-permute-start.6
  18.4 0.0 collective-permute-done.3.refs_0_.refs_5_.refs_6_.refs_8_
  18.4 1.4 %collective-permute-done.1.refs_1_.refs_8_.refs_10_.refs_12_ = bf16[128,512]{1,0:T(8,128)(2,1)S(1)} collective-permute-done((bf16[128,512]{1,0:T(8,128)(2,1)S(1)}, bf16[128,512]{1,0:T(8,128)(2,1)S(1)}, u32[]{:S(2)}, u32[]{:S(2)}) %collective-permute-start.1) | collective-permute-done | bytes 131104 | tf_op jit(solution)/shard_map/ppermute | solution.py:42
  19.8 1.6 %collective-permute-start.8 = (bf16[128,512]{1,0:T(8,128)(2,1)S(1)}, bf16[128,512]{1,0:T(8,128)(2,1)S(1)}, u32[]{:S(2)}, u32[]{:S(2)}) collective-permute-start(bf16[128,512]{1,0:T(8,128)(2,1)S(1)} %collective-permute-done.1.refs_1_.refs_8_.refs_10_.refs_12_), channel_id=1, source_target_pairs={{0,1},{1,3},{3,2},{2,0},{4,5},{5,7},{7,6},{6,4},{8,9},{9,11},{11,1... | collective-permute-start | bytes 393224 | tf_op jit(solution)/shard_map/ppermute | solution.py:42
  21.3 2.0 %collective-permute-start.7 = (bf16[128,512]{1,0:T(8,128)(2,1)S(1)}, bf16[128,512]{1,0:T(8,128)(2,1)S(1)}, u32[]{:S(2)}, u32[]{:S(2)}) collective-permute-start(bf16[128,512]{1,0:T(8,128)(2,1)S(1)} %collective-permute-done.3.refs_0_.refs_5_.refs_6_.refs_8_), channel_id=1, source_target_pairs={{0,1},{1,3},{3,2},{2,0},{4,5},{5,7},{7,6},{6,4},{8,9},{9,11},{11,1... | collective-permute-start | bytes 393224 | tf_op jit(solution)/shard_map/ppermute | solution.py:42
  23.3 0.0 collective-permute-done.4.refs_10_
  23.3 0.0 collective-permute-done.5.refs_11_
  23.3 0.0 collective-permute-done.6.refs_12_
  23.3 0.0 copy-done
  23.3 0.0 copy-done.2
  23.3 3.6 %first_shards.1 = (f32[4,1024,256]{2,1,0:T(8,128)S(1)}, f32[4,128,128]{2,1,0:T(8,128)S(1)}, f32[4,128,256]{2,1,0:T(8,128)S(1)}, f32[4,128,128]{2,1,0:T(8,128)S(1...) custom-call(s32[18]{0:T(128)S(1)} %facts.1.refs_0_, ...), custom_call_target="tpu_custom_call" | custom-call | flops 6442450944 | bytes 2097152 | tf_op jit(solution)/shard_map/first_shards/pallas_call | solution.py:425
  26.9 0.0 collective-permute-done.8.refs_11_.refs_13_
  26.9 0.9 %collective-permute-done.7.refs_7_.refs_9_ = bf16[128,512]{1,0:T(8,128)(2,1)S(1)} collective-permute-done((bf16[128,512]{1,0:T(8,128)(2,1)S(1)}, bf16[128,512]{1,0:T(8,128)(2,1)S(1)}, u32[]{:S(2)}, u32[]{:S(2)}) %collective-permute-start.7) | collective-permute-done | bytes 131104 | tf_op jit(solution)/shard_map/ppermute | solution.py:42
  27.9 2.1 %last_shard_decode.1 = bf16[16,4096]{1,0:T(8,128)(2,1)S(1)} custom-call(f32[4,128,256]{2,1,0:T(8,128)S(1)} %get-tuple-element.29.refs_0_, f32[4,128,128]{2,1,0:T(8,128)S(1)} %get-tuple-element.30.refs_1_, f32[8,128]{1,0:T(8,128)S(1)} %get-tuple-element.28.refs_2_, bf16[16,4096]{1,0:T(8,128)(2,1)S(1)} %get-tuple-element.31.refs_3_, ...), custom_call_target="tpu_custom_call" | custom-call | flops 268435456 | bytes 262144 | tf_op jit(solution)/shard_map/last_shard_decode/pallas_call | solution.py:438
  30.0 0.1 fusion
  30.1 1.6 %collective-permute-start.10 = (bf16[2,4096]{1,0:T(2,128)(2,1)S(1)}, bf16[2,4096]{1,0:T(2,128)(2,1)S(1)}, u32[]{:S(2)}, u32[]{:S(2)}) collective-permute-start(bf16[2,4096]{1,0:T(2,128)(2,1)S(1)} %get-tuple-element.37), channel_id=1, source_target_pairs={{0,8},{4,12},{8,0},{12,4},{1,9},{5,13},{9,1},{13,5},{2,10},{6,14},... | collective-permute-start | bytes 49160 | tf_op jit(solution)/shard_map/ppermute | solution.py:482
  31.6 0.0 collective-permute-start.11
  31.6 0.6 %collective-permute-start.9 = (bf16[2,4096]{1,0:T(2,128)(2,1)S(1)}, bf16[2,4096]{1,0:T(2,128)(2,1)S(1)}, u32[]{:S(2)}, u32[]{:S(2)}) collective-permute-start(bf16[2,4096]{1,0:T(2,128)(2,1)S(1)} %get-tuple-element.34), channel_id=1, source_target_pairs={{0,12},{4,8},{8,4},{12,0},{1,13},{5,9},{9,5},{13,1},{2,14},{6,10},... | collective-permute-start | bytes 49160 | tf_op jit(solution)/shard_map/ppermute | solution.py:482
  32.3 7.6 %last_shard_prefill.1 = bf16[128,4096]{1,0:T(8,128)(2,1)} custom-call(f32[4,1024,256]{2,1,0:T(8,128)S(1)} %get-tuple-element.26.refs_0_, f32[4,128,128]{2,1,0:T(8,128)S(1)} %get-tuple-element.27.refs_1_, f32[8,128]{1,0:T(8,128)S(1)} %get-tuple-element.28.refs_2_, bf16[128,4096]{1,0:T(8,128)(2,1)S(1)} %copy-done.2, bf16[128,512]{1,0:T(8,128)(2,1)S(1)} %copy-done, ...), custom_call_target="tpu_custom_call" | custom-call | flops 2147483648 | bytes 2097152 | tf_op jit(solution)/shard_map/last_shard_prefill/pallas_call | solution.py:451
  39.9 0.0 collective-permute-done.10
  39.9 0.0 collective-permute-done.11
  39.9 0.0 collective-permute-done.9
  39.9 0.8 %broadcast_select_fusion.2 = bf16[4,2,4096]{2,1,0:T(2,128)(2,1)} fusion(pred[4]{0:T(512)(128)(4,1)S(1)} %get-tuple-element.41, pred[4]{0:T(512)(128)(4,1)S(1)} %get-tuple-element.40, pred[4]{0:T(512)(128)(4,1)S(1)} %get-tuple-element.39, pred[4]{0:T(512)(128)(4,1)S(1)} %get-tuple-element.38, bf16[2,4096]{1,0:T(2,128)(2,1)S(1)} %get-tuple-element.35, ...), kind=kLoop, calls=%fused_computation.2 | loop fusion | flops 131072 | bytes 131088 | tf_op jit(solution)/shard_map/jit(_where)/select_n | solution.py:525
  (2 shorter events, 0.0 us)
Async XLA Ops:
  0.6 9.3 %collective-permute-start.2 = (bf16[128,512]{1,0:T(8,128)(2,1)}, bf16[128,512]{1,0:T(8,128)(2,1)S(1)}, u32[]{:S(2)}, u32[]{:S(2)}) collective-permute-start(bf16[128,512]{1,0:T(8,128)(2,1)} %refs_6_.1), channel_id=1, source_target_pairs={{0,1},{1,3},{3,2},{2,0},{4,5},{5,7},{7,6},{6,4},{8,9},{9,11},{11,1... | collective-permute-start | bytes 393224 | tf_op jit(solution)/shard_map/ppermute | solution.py:42
  4.7 0.7 %copy-start.3 = (s32[4,4]{1,0:T(4,128)S(1)}, s32[4,4]{1,0:T(4,128)}, u32[]{:S(2)}) copy-start(s32[4,4]{1,0:T(4,128)} %lengths_ref.1) | copy-start | bytes 196
  5.3 0.7 %copy-start.4 = (s32[16]{0:T(128)S(1)}, s32[16]{0:T(128)}, u32[]{:S(2)}) copy-start(s32[16]{0:T(128)} %slots_ref.1) | copy-start | bytes 196
  6.0 1.3 %copy-start.1 = (bf16[128,512]{1,0:T(8,128)(2,1)S(1)}, bf16[128,512]{1,0:T(8,128)(2,1)}, u32[]{:S(2)}) copy-start(bf16[128,512]{1,0:T(8,128)(2,1)} %refs_10_) | copy-start | bytes 393220
  7.3 6.6 %collective-permute-start = (bf16[128,512]{1,0:T(8,128)(2,1)S(1)}, bf16[128,512]{1,0:T(8,128)(2,1)S(1)}, u32[]{:S(2)}, u32[]{:S(2)}) collective-permute-start(bf16[128,512]{1,0:T(8,128)(2,1)S(1)} %copy-done.1), channel_id=1, source_target_pairs={{0,1},{1,3},{3,2},{2,0},{4,5},{5,7},{7,6},{6,4},{8,9},{9,11},{11,1... | collective-permute-start | bytes 393224 | tf_op jit(solution)/shard_map/ppermute | solution.py:42
  9.9 8.4 %collective-permute-start.3 = (bf16[128,512]{1,0:T(8,128)(2,1)S(1)}, bf16[128,512]{1,0:T(8,128)(2,1)S(1)}, u32[]{:S(2)}, u32[]{:S(2)}) collective-permute-start(bf16[128,512]{1,0:T(8,128)(2,1)S(1)} %collective-permute-done.2.refs_4_.refs_5_.refs_7_), channel_id=1, source_target_pairs={{0,1},{1,3},{3,2},{2,0},{4,5},{5,7},{7,6},{6,4},{8,9},{9,11},{11,1... | collective-permute-start | bytes 393224 | tf_op jit(solution)/shard_map/ppermute | solution.py:42
  13.9 5.9 %collective-permute-start.1 = (bf16[128,512]{1,0:T(8,128)(2,1)S(1)}, bf16[128,512]{1,0:T(8,128)(2,1)S(1)}, u32[]{:S(2)}, u32[]{:S(2)}) collective-permute-start(bf16[128,512]{1,0:T(8,128)(2,1)S(1)} %collective-permute-done.refs_7_.refs_9_.refs_11_), channel_id=1, source_target_pairs={{0,1},{1,3},{3,2},{2,0},{4,5},{5,7},{7,6},{6,4},{8,9},{9,11},{11,1... | collective-permute-start | bytes 393224 | tf_op jit(solution)/shard_map/ppermute | solution.py:42
  16.4 6.9 %copy-start = (bf16[128,512]{1,0:T(8,128)(2,1)S(1)}, bf16[128,512]{1,0:T(8,128)(2,1)}, u32[]{:S(2)}) copy-start(bf16[128,512]{1,0:T(8,128)(2,1)} %refs_6_.1) | copy-start | bytes 393220
  16.4 6.9 %copy-start.2 = (bf16[128,4096]{1,0:T(8,128)(2,1)S(1)}, bf16[128,4096]{1,0:T(8,128)(2,1)}, u32[]{:S(2)}) copy-start(bf16[128,4096]{1,0:T(8,128)(2,1)} %refs_3_.2) | copy-start | bytes 3145732
  16.4 6.8 %collective-permute-start.4 = (bf16[8,5120]{1,0:T(8,128)(2,1)S(1)}, bf16[8,5120]{1,0:T(8,128)(2,1)S(1)}, u32[]{:S(2)}, u32[]{:S(2)}) collective-permute-start(bf16[8,5120]{1,0:T(8,128)(2,1)S(1)} %reshape.15.refs_9_), channel_id=1, source_target_pairs={{0,4},{4,0},{8,12},{12,8},{1,5},{5,1},{9,13},{13,9},{2,6},{6,2},{1... | collective-permute-start | bytes 245768 | tf_op jit(solution)/shard_map/ppermute | solution.py:482
  16.5 6.8 %collective-permute-start.5 = (bf16[8,5120]{1,0:T(8,128)(2,1)S(1)}, bf16[8,5120]{1,0:T(8,128)(2,1)S(1)}, u32[]{:S(2)}, u32[]{:S(2)}) collective-permute-start(bf16[8,5120]{1,0:T(8,128)(2,1)S(1)} %reshape.15.refs_9_), channel_id=1, source_target_pairs={{0,8},{4,12},{8,0},{12,4},{1,9},{5,13},{9,1},{13,5},{2,10},{6,14},... | collective-permute-start | bytes 245768 | tf_op jit(solution)/shard_map/ppermute | solution.py:482
  18.0 5.3 %collective-permute-start.6 = (bf16[8,5120]{1,0:T(8,128)(2,1)S(1)}, bf16[8,5120]{1,0:T(8,128)(2,1)S(1)}, u32[]{:S(2)}, u32[]{:S(2)}) collective-permute-start(bf16[8,5120]{1,0:T(8,128)(2,1)S(1)} %reshape.15.refs_9_), channel_id=1, source_target_pairs={{0,12},{4,8},{8,4},{12,0},{1,13},{5,9},{9,5},{13,1},{2,14},{6,10},... | collective-permute-start | bytes 245768 | tf_op jit(solution)/shard_map/ppermute | solution.py:482
  19.8 7.2 %collective-permute-start.8 = (bf16[128,512]{1,0:T(8,128)(2,1)S(1)}, bf16[128,512]{1,0:T(8,128)(2,1)S(1)}, u32[]{:S(2)}, u32[]{:S(2)}) collective-permute-start(bf16[128,512]{1,0:T(8,128)(2,1)S(1)} %collective-permute-done.1.refs_1_.refs_8_.refs_10_.refs_12_), channel_id=1, source_target_pairs={{0,1},{1,3},{3,2},{2,0},{4,5},{5,7},{7,6},{6,4},{8,9},{9,11},{11,1... | collective-permute-start | bytes 393224 | tf_op jit(solution)/shard_map/ppermute | solution.py:42
  21.3 6.5 %collective-permute-start.7 = (bf16[128,512]{1,0:T(8,128)(2,1)S(1)}, bf16[128,512]{1,0:T(8,128)(2,1)S(1)}, u32[]{:S(2)}, u32[]{:S(2)}) collective-permute-start(bf16[128,512]{1,0:T(8,128)(2,1)S(1)} %collective-permute-done.3.refs_0_.refs_5_.refs_6_.refs_8_), channel_id=1, source_target_pairs={{0,1},{1,3},{3,2},{2,0},{4,5},{5,7},{7,6},{6,4},{8,9},{9,11},{11,1... | collective-permute-start | bytes 393224 | tf_op jit(solution)/shard_map/ppermute | solution.py:42
  30.1 9.8 %collective-permute-start.10 = (bf16[2,4096]{1,0:T(2,128)(2,1)S(1)}, bf16[2,4096]{1,0:T(2,128)(2,1)S(1)}, u32[]{:S(2)}, u32[]{:S(2)}) collective-permute-start(bf16[2,4096]{1,0:T(2,128)(2,1)S(1)} %get-tuple-element.37), channel_id=1, source_target_pairs={{0,8},{4,12},{8,0},{12,4},{1,9},{5,13},{9,1},{13,5},{2,10},{6,14},... | collective-permute-start | bytes 49160 | tf_op jit(solution)/shard_map/ppermute | solution.py:482
  31.6 8.3 %collective-permute-start.11 = (bf16[2,4096]{1,0:T(2,128)(2,1)S(1)}, bf16[2,4096]{1,0:T(2,128)(2,1)S(1)}, u32[]{:S(2)}, u32[]{:S(2)}) collective-permute-start(bf16[2,4096]{1,0:T(2,128)(2,1)S(1)} %get-tuple-element.36), channel_id=1, source_target_pairs={{0,4},{4,0},{8,12},{12,8},{1,5},{5,1},{9,13},{13,9},{2,6},{6,2},{1... | collective-permute-start | bytes 49160 | tf_op jit(solution)/shard_map/ppermute | solution.py:482
  31.6 8.3 %collective-permute-start.9 = (bf16[2,4096]{1,0:T(2,128)(2,1)S(1)}, bf16[2,4096]{1,0:T(2,128)(2,1)S(1)}, u32[]{:S(2)}, u32[]{:S(2)}) collective-permute-start(bf16[2,4096]{1,0:T(2,128)(2,1)S(1)} %get-tuple-element.34), channel_id=1, source_target_pairs={{0,12},{4,8},{8,4},{12,0},{1,13},{5,9},{9,5},{13,1},{2,14},{6,10},... | collective-permute-start | bytes 49160 | tf_op jit(solution)/shard_map/ppermute | solution.py:482

commit v10 on v9

--- a/solution.py
+++ b/solution.py
@@ -123,7 +123,6 @@
         out_specs=SMEM,
         out_shape=jax.ShapeDtypeStruct((length,), jnp.int32),
         cost_estimate=pl.CostEstimate(flops=5 * 10**9, bytes_accessed=0, transcendentals=0),
-        compiler_params=pltpu.CompilerParams(vmem_limit_bytes=MIB),
         name="facts",
     )(lengths, slots)
 
@@ -463,7 +462,7 @@
     )(*state[:2], state[4], query, *keys, *values)
 
 
-def start_maxima(*arrays):
+def start_maxima(*arrays, flops=5 * 10**9):
     def kernel(*refs):
         refs[-1][...] = jnp.full((8, HEAD_SIZE), MASKED, jnp.float32)
 
@@ -472,7 +471,7 @@
         in_specs=[VMEM] * len(arrays),
         out_specs=VMEM,
         out_shape=jax.ShapeDtypeStruct((8, HEAD_SIZE), jnp.float32),
-        cost_estimate=pl.CostEstimate(flops=5 * 10**9, bytes_accessed=0, transcendentals=0),
+        cost_estimate=pl.CostEstimate(flops=flops, bytes_accessed=0, transcendentals=0),
         compiler_params=pltpu.CompilerParams(vmem_limit_bytes=MIB),
         name="start_maxima",
     )(*arrays)
@@ -505,8 +504,8 @@
         if s == 2:
             keys[1], own = lax.optimization_barrier((keys[1], own))
         if s == plan.size - 1:
-            maxima = start_maxima(keys[-1], values[-1])
-            values[-1], maxima = lax.optimization_barrier((values[-1], maxima))
+            maxima = start_maxima(keys[-1])
+            keys[-1], maxima = lax.optimization_barrier((keys[-1], maxima))
         keys.append(plan.step(keys[-1]))
         values.append(plan.step(values[-1]))
         if s == 2:

time: 41 us -> 38.7 us (0.944)
  waiting for transfers between devices: 5.84 us -> 3.26 us
  local copies, waits for them, and re-layouts: 1.44 us -> 0.11 us
  starting transfers between devices: 16.3 us -> 17.1 us
  other arithmetic: 1.82 us -> 2.47 us
    ppermute x6, waiting for transfers between devices: 5.82 us -> 3.24 us  [step(): return lax.ppermute(array, 'tp', self.pairs)]
    unnamed x10 -> x8, local copies, waits for them, and re-layouts: 1.34 us -> 0.02 us
    ppermute x6, starting transfers between devices: 12.2 us -> 12.9 us  [step(): return lax.ppermute(array, 'tp', self.pairs)]
    eq x1, other arithmetic: 0.08 us -> 0.73 us  [body(): from_block == k]
  transfers between devices with their start and end apart: 12 -> 12, of which waited for: 3 -> 2; matrix products, arithmetic and copies ran while one was open for 3% -> 4% of each run, Pallas kernels for 31% -> 33%
where the time goes in v10:
time: 38.7 us; the launch traced here: 38.5 us
  starting transfers between devices  17.1 us (44%)
  Pallas kernels  14.8 us (38%)
  waiting for transfers between devices  3.26 us (8%)
  other arithmetic  2.47 us (6%)
  between operations  0.77 us (2%)
    ppermute x6, starting transfers between devices, step(): return lax.ppermute(array, 'tp', self.pairs)  12.9 us
    pallas_call x1, Pallas kernels, call_prefill(): pl.pallas_call(lambda *refs: prefill_kernel(plan, *refs), in_specs=[VMEM]...  7.61 us
    ppermute x6, starting transfers between devices, paired(): lax.ppermute(array, 'pd', [(g, g ^ k) for g in range(lax.axis_size('pd'))])  4.14 us
    pallas_call x1, Pallas kernels, call_first(): pl.pallas_call(lambda *refs: first_kernel(plan, len(blocks), *refs), in_s...  3.61 us
    ppermute x6, waiting for transfers between devices, step(): return lax.ppermute(array, 'tp', self.pairs)  3.24 us
    pallas_call x1, Pallas kernels, call_decode(): pl.pallas_call(lambda *refs: decode_kernel(plan, *refs), in_specs=[VMEM]...  2.13 us
    pallas_call x1, Pallas kernels, facts_row(): pl.pallas_call(kernel, in_specs=[SMEM, SMEM], out_specs=SMEM, out_shape=j...  1.43 us
    concatenate x1, other arithmetic, body(): jnp.concatenate([decoded_query, decoded_key, decoded_value], axis=2)  0.95 us
  transfers between devices with their start and end apart: 12, of which 2 were waited for; matrix products, arithmetic and copies ran while one was open for 4% of the time, Pallas kernels for 33%

profile of v10, /device:TPU:0, one launch (start us, length us, event | category | flops | bytes accessed | tf_op | source)
XLA Modules:
  0.0 38.5 jit_solution(3391182192928286400)
XLA Ops:
  0.6 3.1 %collective-permute-start = (bf16[128,512]{1,0:T(8,128)(2,1)}, bf16[128,512]{1,0:T(8,128)(2,1)S(1)}, u32[]{:S(2)}, u32[]{:S(2)}) collective-permute-start(bf16[128,512]{1,0:T(8,128)(2,1)} %refs_6_.1), channel_id=1, source_target_pairs={{0,1},{1,3},{3,2},{2,0},{4,5},{5,7},{7,6},{6,4},{8,9},{9,11},{11,1... | collective-permute-start | bytes 393224 | tf_op jit(solution)/shard_map/ppermute | solution.py:42
  3.7 0.9 %pad_maximum_fusion = bf16[4,2,5120]{2,1,0:T(2,128)(2,1)S(1)} fusion(bf16[4,2,512]{2,1,0:T(2,128)(2,1)} %param.15, bf16[4,2,512]{2,1,0:T(2,128)(2,1)} %param.14, bf16[4,2,4096]{2,1,0:T(2,128)(2,1)} %param.13), kind=kLoop, calls=%fused_computation.4 | loop fusion | flops 245760 | bytes 163840 | tf_op jit(solution)/shard_map/concatenate | solution.py:496
  4.7 0.0 copy-start.1
  4.7 1.4 %facts.1.refs_0_ = s32[18]{0:T(128)} custom-call(s32[4,4]{1,0:T(4,128)} %lengths_ref.1, s32[16]{0:T(128)} %slots_ref.1), custom_call_target="tpu_custom_call" | custom-call | flops 5000000000 | tf_op jit(solution)/shard_map/facts/pallas_call | solution.py:120
  6.1 0.0 copy-done.1
  6.2 2.6 %collective-permute-start.2 = (bf16[128,512]{1,0:T(8,128)(2,1)S(1)}, bf16[128,512]{1,0:T(8,128)(2,1)S(1)}, u32[]{:S(2)}, u32[]{:S(2)}) collective-permute-start(bf16[128,512]{1,0:T(8,128)(2,1)S(1)} %copy-done.1), channel_id=1, source_target_pairs={{0,1},{1,3},{3,2},{2,0},{4,5},{5,7},{7,6},{6,4},{8,9},{9,11},{11,1... | collective-permute-start | bytes 393224 | tf_op jit(solution)/shard_map/ppermute | solution.py:42
  8.8 0.0 collective-permute-done.refs_4_.refs_5_.refs_7_
  8.8 0.9 %collective-permute-start.1 = (bf16[128,512]{1,0:T(8,128)(2,1)S(1)}, bf16[128,512]{1,0:T(8,128)(2,1)S(1)}, u32[]{:S(2)}, u32[]{:S(2)}) collective-permute-start(bf16[128,512]{1,0:T(8,128)(2,1)S(1)} %collective-permute-done.refs_4_.refs_5_.refs_7_), channel_id=1, source_target_pairs={{0,1},{1,3},{3,2},{2,0},{4,5},{5,7},{7,6},{6,4},{8,9},{9,11},{11,1... | collective-permute-start | bytes 393224 | tf_op jit(solution)/shard_map/ppermute | solution.py:42
  9.7 0.7 %broadcast_compare_fusion.2 = (pred[4]{0:T(512)(128)(4,1)S(1)}, pred[4]{0:T(512)(128)(4,1)S(1)}, pred[4]{0:T(512)(128)(4,1)S(1)}, pred[4]{0:T(512)(128)(4,1)S(1)}) fusion(s32[18]{0:T(128)} %facts.1.refs_0_), kind=kLoop, calls=%fused_computation.7 | loop fusion | flops 16 | bytes 32 | tf_op jit(solution)/shard_map/eq | solution.py:524
  10.4 0.0 copy-start
  10.4 0.0 copy-start.2
  10.4 0.0 copy-start.3
  10.4 0.1 collective-permute-start.4
  10.5 1.6 %collective-permute-start.5 = (bf16[8,5120]{1,0:T(8,128)(2,1)S(1)}, bf16[8,5120]{1,0:T(8,128)(2,1)S(1)}, u32[]{:S(2)}, u32[]{:S(2)}) collective-permute-start(bf16[8,5120]{1,0:T(8,128)(2,1)S(1)} %reshape.15.refs_9_), channel_id=1, source_target_pairs={{0,8},{4,12},{8,0},{12,4},{1,9},{5,13},{9,1},{13,5},{2,10},{6,14},... | collective-permute-start | bytes 245768 | tf_op jit(solution)/shard_map/ppermute | solution.py:481
  12.0 0.3 collective-permute-start.6
  12.3 0.3 collective-permute-done.2.refs_7_.refs_9_.refs_11_
  12.7 2.9 %collective-permute-start.3 = (bf16[128,512]{1,0:T(8,128)(2,1)S(1)}, bf16[128,512]{1,0:T(8,128)(2,1)S(1)}, u32[]{:S(2)}, u32[]{:S(2)}) collective-permute-start(bf16[128,512]{1,0:T(8,128)(2,1)S(1)} %collective-permute-done.2.refs_7_.refs_9_.refs_11_), channel_id=1, source_target_pairs={{0,1},{1,3},{3,2},{2,0},{4,5},{5,7},{7,6},{6,4},{8,9},{9,11},{11,1... | collective-permute-start | bytes 393224 | tf_op jit(solution)/shard_map/ppermute | solution.py:42
  15.6 0.0 collective-permute-done.1.refs_0_.refs_5_.refs_6_.refs_8_
  15.6 0.9 %collective-permute-start.7 = (bf16[128,512]{1,0:T(8,128)(2,1)S(1)}, bf16[128,512]{1,0:T(8,128)(2,1)S(1)}, u32[]{:S(2)}, u32[]{:S(2)}) collective-permute-start(bf16[128,512]{1,0:T(8,128)(2,1)S(1)} %collective-permute-done.1.refs_0_.refs_5_.refs_6_.refs_8_), channel_id=1, source_target_pairs={{0,1},{1,3},{3,2},{2,0},{4,5},{5,7},{7,6},{6,4},{8,9},{9,11},{11,1... | collective-permute-start | bytes 393224 | tf_op jit(solution)/shard_map/ppermute | solution.py:42
  16.6 2.9 %collective-permute-done.3.refs_8_.refs_10_.refs_12_ = bf16[128,512]{1,0:T(8,128)(2,1)S(1)} collective-permute-done((bf16[128,512]{1,0:T(8,128)(2,1)S(1)}, bf16[128,512]{1,0:T(8,128)(2,1)S(1)}, u32[]{:S(2)}, u32[]{:S(2)}) %collective-permute-start.3) | collective-permute-done | bytes 131104 | tf_op jit(solution)/shard_map/ppermute | solution.py:42
  19.5 2.5 %collective-permute-start.8 = (bf16[128,512]{1,0:T(8,128)(2,1)S(1)}, bf16[128,512]{1,0:T(8,128)(2,1)S(1)}, u32[]{:S(2)}, u32[]{:S(2)}) collective-permute-start(bf16[128,512]{1,0:T(8,128)(2,1)S(1)} %collective-permute-done.3.refs_8_.refs_10_.refs_12_), channel_id=1, source_target_pairs={{0,1},{1,3},{3,2},{2,0},{4,5},{5,7},{7,6},{6,4},{8,9},{9,11},{11,1... | collective-permute-start | bytes 393224 | tf_op jit(solution)/shard_map/ppermute | solution.py:42
  21.9 0.0 collective-permute-done.4.refs_10_
  21.9 0.0 collective-permute-done.5.refs_11_
  21.9 0.0 collective-permute-done.6.refs_12_
  21.9 0.0 copy-done
  22.0 0.0 copy-done.2
  22.0 0.0 copy-done.3
  22.0 3.6 %first_shards.1 = (f32[4,1024,256]{2,1,0:T(8,128)S(1)}, f32[4,128,128]{2,1,0:T(8,128)S(1)}, f32[4,128,256]{2,1,0:T(8,128)S(1)}, f32[4,128,128]{2,1,0:T(8,128)S(1...) custom-call(s32[18]{0:T(128)S(1)} %copy-done.2, ...), custom_call_target="tpu_custom_call" | custom-call | flops 6442450944 | bytes 2097152 | tf_op jit(solution)/shard_map/first_shards/pallas_call | solution.py:424
  25.6 0.0 collective-permute-done.7.refs_7_.refs_9_
  25.6 0.0 collective-permute-done.8.refs_11_.refs_13_
  25.6 2.1 %last_shard_decode.1 = bf16[16,4096]{1,0:T(8,128)(2,1)S(1)} custom-call(f32[4,128,256]{2,1,0:T(8,128)S(1)} %get-tuple-element.29.refs_0_, f32[4,128,128]{2,1,0:T(8,128)S(1)} %get-tuple-element.30.refs_1_, f32[8,128]{1,0:T(8,128)S(1)} %get-tuple-element.28.refs_2_, bf16[16,4096]{1,0:T(8,128)(2,1)S(1)} %get-tuple-element.31.refs_3_, ...), custom_call_target="tpu_custom_call" | custom-call | flops 268435456 | bytes 262144 | tf_op jit(solution)/shard_map/last_shard_decode/pallas_call | solution.py:437
  27.7 0.1 fusion
  27.8 1.6 %collective-permute-start.10 = (bf16[2,4096]{1,0:T(2,128)(2,1)S(1)}, bf16[2,4096]{1,0:T(2,128)(2,1)S(1)}, u32[]{:S(2)}, u32[]{:S(2)}) collective-permute-start(bf16[2,4096]{1,0:T(2,128)(2,1)S(1)} %get-tuple-element.37), channel_id=1, source_target_pairs={{0,8},{4,12},{8,0},{12,4},{1,9},{5,13},{9,1},{13,5},{2,10},{6,14},... | collective-permute-start | bytes 49160 | tf_op jit(solution)/shard_map/ppermute | solution.py:481
  29.4 0.0 collective-permute-start.11
  29.4 0.6 %collective-permute-start.9 = (bf16[2,4096]{1,0:T(2,128)(2,1)S(1)}, bf16[2,4096]{1,0:T(2,128)(2,1)S(1)}, u32[]{:S(2)}, u32[]{:S(2)}) collective-permute-start(bf16[2,4096]{1,0:T(2,128)(2,1)S(1)} %get-tuple-element.34), channel_id=1, source_target_pairs={{0,12},{4,8},{8,4},{12,0},{1,13},{5,9},{9,5},{13,1},{2,14},{6,10},... | collective-permute-start | bytes 49160 | tf_op jit(solution)/shard_map/ppermute | solution.py:481
  30.0 7.6 %last_shard_prefill.1 = bf16[128,4096]{1,0:T(8,128)(2,1)} custom-call(f32[4,1024,256]{2,1,0:T(8,128)S(1)} %get-tuple-element.26.refs_0_, f32[4,128,128]{2,1,0:T(8,128)S(1)} %get-tuple-element.27.refs_1_, f32[8,128]{1,0:T(8,128)S(1)} %get-tuple-element.28.refs_2_, bf16[128,4096]{1,0:T(8,128)(2,1)S(1)} %copy-done.3, bf16[128,512]{1,0:T(8,128)(2,1)S(1)} %copy-done, ...), custom_call_target="tpu_custom_call" | custom-call | flops 2147483648 | bytes 2097152 | tf_op jit(solution)/shard_map/last_shard_prefill/pallas_call | solution.py:450
  37.6 0.0 collective-permute-done.10
  37.6 0.0 collective-permute-done.11
  37.7 0.0 collective-permute-done.9
  37.7 0.8 %broadcast_select_fusion.2 = bf16[4,2,4096]{2,1,0:T(2,128)(2,1)} fusion(pred[4]{0:T(512)(128)(4,1)S(1)} %get-tuple-element.41, pred[4]{0:T(512)(128)(4,1)S(1)} %get-tuple-element.40, pred[4]{0:T(512)(128)(4,1)S(1)} %get-tuple-element.39, pred[4]{0:T(512)(128)(4,1)S(1)} %get-tuple-element.38, bf16[2,4096]{1,0:T(2,128)(2,1)S(1)} %get-tuple-element.35, ...), kind=kLoop, calls=%fused_computation.2 | loop fusion | flops 131072 | bytes 131088 | tf_op jit(solution)/shard_map/jit(_where)/select_n | solution.py:524
  (2 shorter events, 0.0 us)
Async XLA Ops:
  0.6 8.2 %collective-permute-start = (bf16[128,512]{1,0:T(8,128)(2,1)}, bf16[128,512]{1,0:T(8,128)(2,1)S(1)}, u32[]{:S(2)}, u32[]{:S(2)}) collective-permute-start(bf16[128,512]{1,0:T(8,128)(2,1)} %refs_6_.1), channel_id=1, source_target_pairs={{0,1},{1,3},{3,2},{2,0},{4,5},{5,7},{7,6},{6,4},{8,9},{9,11},{11,1... | collective-permute-start | bytes 393224 | tf_op jit(solution)/shard_map/ppermute | solution.py:42
  4.7 1.5 %copy-start.1 = (bf16[128,512]{1,0:T(8,128)(2,1)S(1)}, bf16[128,512]{1,0:T(8,128)(2,1)}, u32[]{:S(2)}) copy-start(bf16[128,512]{1,0:T(8,128)(2,1)} %refs_10_) | copy-start | bytes 393220
  6.2 6.5 %collective-permute-start.2 = (bf16[128,512]{1,0:T(8,128)(2,1)S(1)}, bf16[128,512]{1,0:T(8,128)(2,1)S(1)}, u32[]{:S(2)}, u32[]{:S(2)}) collective-permute-start(bf16[128,512]{1,0:T(8,128)(2,1)S(1)} %copy-done.1), channel_id=1, source_target_pairs={{0,1},{1,3},{3,2},{2,0},{4,5},{5,7},{7,6},{6,4},{8,9},{9,11},{11,1... | collective-permute-start | bytes 393224 | tf_op jit(solution)/shard_map/ppermute | solution.py:42
  8.8 6.8 %collective-permute-start.1 = (bf16[128,512]{1,0:T(8,128)(2,1)S(1)}, bf16[128,512]{1,0:T(8,128)(2,1)S(1)}, u32[]{:S(2)}, u32[]{:S(2)}) collective-permute-start(bf16[128,512]{1,0:T(8,128)(2,1)S(1)} %collective-permute-done.refs_4_.refs_5_.refs_7_), channel_id=1, source_target_pairs={{0,1},{1,3},{3,2},{2,0},{4,5},{5,7},{7,6},{6,4},{8,9},{9,11},{11,1... | collective-permute-start | bytes 393224 | tf_op jit(solution)/shard_map/ppermute | solution.py:42
  10.4 11.6 %copy-start = (bf16[128,512]{1,0:T(8,128)(2,1)S(1)}, bf16[128,512]{1,0:T(8,128)(2,1)}, u32[]{:S(2)}) copy-start(bf16[128,512]{1,0:T(8,128)(2,1)} %refs_6_.1) | copy-start | bytes 393220
  10.4 11.6 %copy-start.2 = (s32[18]{0:T(128)S(1)}, s32[18]{0:T(128)}, u32[]{:S(2)}) copy-start(s32[18]{0:T(128)} %facts.1.refs_0_) | copy-start | bytes 220
  10.4 11.6 %copy-start.3 = (bf16[128,4096]{1,0:T(8,128)(2,1)S(1)}, bf16[128,4096]{1,0:T(8,128)(2,1)}, u32[]{:S(2)}) copy-start(bf16[128,4096]{1,0:T(8,128)(2,1)} %refs_3_.2) | copy-start | bytes 3145732
  10.4 11.5 %collective-permute-start.4 = (bf16[8,5120]{1,0:T(8,128)(2,1)S(1)}, bf16[8,5120]{1,0:T(8,128)(2,1)S(1)}, u32[]{:S(2)}, u32[]{:S(2)}) collective-permute-start(bf16[8,5120]{1,0:T(8,128)(2,1)S(1)} %reshape.15.refs_9_), channel_id=1, source_target_pairs={{0,4},{4,0},{8,12},{12,8},{1,5},{5,1},{9,13},{13,9},{2,6},{6,2},{1... | collective-permute-start | bytes 245768 | tf_op jit(solution)/shard_map/ppermute | solution.py:481
  10.5 11.5 %collective-permute-start.5 = (bf16[8,5120]{1,0:T(8,128)(2,1)S(1)}, bf16[8,5120]{1,0:T(8,128)(2,1)S(1)}, u32[]{:S(2)}, u32[]{:S(2)}) collective-permute-start(bf16[8,5120]{1,0:T(8,128)(2,1)S(1)} %reshape.15.refs_9_), channel_id=1, source_target_pairs={{0,8},{4,12},{8,0},{12,4},{1,9},{5,13},{9,1},{13,5},{2,10},{6,14},... | collective-permute-start | bytes 245768 | tf_op jit(solution)/shard_map/ppermute | solution.py:481
  12.0 9.9 %collective-permute-start.6 = (bf16[8,5120]{1,0:T(8,128)(2,1)S(1)}, bf16[8,5120]{1,0:T(8,128)(2,1)S(1)}, u32[]{:S(2)}, u32[]{:S(2)}) collective-permute-start(bf16[8,5120]{1,0:T(8,128)(2,1)S(1)} %reshape.15.refs_9_), channel_id=1, source_target_pairs={{0,12},{4,8},{8,4},{12,0},{1,13},{5,9},{9,5},{13,1},{2,14},{6,10},... | collective-permute-start | bytes 245768 | tf_op jit(solution)/shard_map/ppermute | solution.py:481
  12.7 6.8 %collective-permute-start.3 = (bf16[128,512]{1,0:T(8,128)(2,1)S(1)}, bf16[128,512]{1,0:T(8,128)(2,1)S(1)}, u32[]{:S(2)}, u32[]{:S(2)}) collective-permute-start(bf16[128,512]{1,0:T(8,128)(2,1)S(1)} %collective-permute-done.2.refs_7_.refs_9_.refs_11_), channel_id=1, source_target_pairs={{0,1},{1,3},{3,2},{2,0},{4,5},{5,7},{7,6},{6,4},{8,9},{9,11},{11,1... | collective-permute-start | bytes 393224 | tf_op jit(solution)/shard_map/ppermute | solution.py:42
  15.6 10.0 %collective-permute-start.7 = (bf16[128,512]{1,0:T(8,128)(2,1)S(1)}, bf16[128,512]{1,0:T(8,128)(2,1)S(1)}, u32[]{:S(2)}, u32[]{:S(2)}) collective-permute-start(bf16[128,512]{1,0:T(8,128)(2,1)S(1)} %collective-permute-done.1.refs_0_.refs_5_.refs_6_.refs_8_), channel_id=1, source_target_pairs={{0,1},{1,3},{3,2},{2,0},{4,5},{5,7},{7,6},{6,4},{8,9},{9,11},{11,1... | collective-permute-start | bytes 393224 | tf_op jit(solution)/shard_map/ppermute | solution.py:42
  19.5 6.1 %collective-permute-start.8 = (bf16[128,512]{1,0:T(8,128)(2,1)S(1)}, bf16[128,512]{1,0:T(8,128)(2,1)S(1)}, u32[]{:S(2)}, u32[]{:S(2)}) collective-permute-start(bf16[128,512]{1,0:T(8,128)(2,1)S(1)} %collective-permute-done.3.refs_8_.refs_10_.refs_12_), channel_id=1, source_target_pairs={{0,1},{1,3},{3,2},{2,0},{4,5},{5,7},{7,6},{6,4},{8,9},{9,11},{11,1... | collective-permute-start | bytes 393224 | tf_op jit(solution)/shard_map/ppermute | solution.py:42
  27.8 9.8 %collective-permute-start.10 = (bf16[2,4096]{1,0:T(2,128)(2,1)S(1)}, bf16[2,4096]{1,0:T(2,128)(2,1)S(1)}, u32[]{:S(2)}, u32[]{:S(2)}) collective-permute-start(bf16[2,4096]{1,0:T(2,128)(2,1)S(1)} %get-tuple-element.37), channel_id=1, source_target_pairs={{0,8},{4,12},{8,0},{12,4},{1,9},{5,13},{9,1},{13,5},{2,10},{6,14},... | collective-permute-start | bytes 49160 | tf_op jit(solution)/shard_map/ppermute | solution.py:481
  29.4 8.3 %collective-permute-start.11 = (bf16[2,4096]{1,0:T(2,128)(2,1)S(1)}, bf16[2,4096]{1,0:T(2,128)(2,1)S(1)}, u32[]{:S(2)}, u32[]{:S(2)}) collective-permute-start(bf16[2,4096]{1,0:T(2,128)(2,1)S(1)} %get-tuple-element.36), channel_id=1, source_target_pairs={{0,4},{4,0},{8,12},{12,8},{1,5},{5,1},{9,13},{13,9},{2,6},{6,2},{1... | collective-permute-start | bytes 49160 | tf_op jit(solution)/shard_map/ppermute | solution.py:481
  29.4 8.3 %collective-permute-start.9 = (bf16[2,4096]{1,0:T(2,128)(2,1)S(1)}, bf16[2,4096]{1,0:T(2,128)(2,1)S(1)}, u32[]{:S(2)}, u32[]{:S(2)}) collective-permute-start(bf16[2,4096]{1,0:T(2,128)(2,1)S(1)} %get-tuple-element.34), channel_id=1, source_target_pairs={{0,12},{4,8},{8,4},{12,0},{1,13},{5,9},{9,5},{13,1},{2,14},{6,10},... | collective-permute-start | bytes 49160 | tf_op jit(solution)/shard_map/ppermute | solution.py:481

commit v11 on v10

--- a/solution.py
+++ b/solution.py
@@ -92,6 +92,8 @@
             self.ends.append(total)
         first += GROUP_REQUESTS
         self.source = [ref[first + s] for s in range(width)]
+        first += width
+        self.owner = [ref[first + p] for p in range(GROUP_REQUESTS)]
 
 
 def facts_row(plan, lengths, slots):
@@ -204,12 +206,17 @@
     width = plan.size
     k_refs, v_refs, refs = refs[: width - 1], refs[width - 1 : 2 * width - 2], refs[2 * width - 2 :]
     block_refs, refs = refs[:pd_size], refs[pd_size:]
-    acc_ref, bias_ref, dec_acc_ref, dec_bias_ref, worst_ref, queries_ref, fresh_ref, pick_ref = refs
+    acc_ref, bias_ref, dec_acc_ref, dec_bias_ref, worst_ref, queries_ref, fresh_ref, pick_ref, owner_ref = refs
     tokens = q_ref.shape[0]
     half = tokens // 2
     facts = Facts(facts_ref, width)
     sources = facts.source[:-1]
     pick_ref[...] = pick_matrix(facts)
+    slot = iota((8, HEAD_SIZE), 0)
+    owner = jnp.zeros_like(slot)
+    for p in range(GROUP_REQUESTS):
+        owner = jnp.where(slot == p, facts.owner[p], owner)
+    owner_ref[...] = owner
     for s in range(width):
         bias_ref[s] = causal_bias(0, tokens, tokens, facts.source[s : s + 1], facts.ends, facts.member, width)
         dec_bias_ref[s] = jnp.where(
@@ -420,6 +427,7 @@
         jax.ShapeDtypeStruct((PADDED_ROWS, Q_WIDTH), bf16),
         jax.ShapeDtypeStruct((PADDED_ROWS, 2 * KV_WIDTH), bf16),
         jax.ShapeDtypeStruct((PADDED_ROWS, PADDED_ROWS), bf16),
+        jax.ShapeDtypeStruct((8, HEAD_SIZE), jnp.int32),
     ]
     return pl.pallas_call(
         lambda *refs: first_kernel(plan, len(blocks), *refs),
@@ -442,7 +450,7 @@
         compiler_params=pltpu.CompilerParams(vmem_limit_bytes=(28 + width) * MIB),
         cost_estimate=cost(PADDED_ROWS, tokens, PADDED_ROWS * tokens * QUERY_HEADS),
         name="last_shard_decode",
-    )(*state[2:], *keys, *values)
+    )(*state[2:8], *keys, *values)
 
 
 def call_prefill(plan, state, query, keys, values):
@@ -498,11 +506,11 @@
     )
     facts = facts_row(plan, prompt_lengths, decode_slot)
     prompt_key, decoded_query = lax.optimization_barrier((prompt_key, decoded_query))
-    prompt_value, own, facts = lax.optimization_barrier((prompt_value, own, facts))
+    prompt_value, own = lax.optimization_barrier((prompt_value, own))
     keys, values, maxima = [prompt_key], [prompt_value], None
     for s in range(1, plan.size):
         if s == 2:
-            keys[1], own = lax.optimization_barrier((keys[1], own))
+            keys[1], own, facts = lax.optimization_barrier((keys[1], own, facts))
         if s == plan.size - 1:
             maxima = start_maxima(keys[-1])
             keys[-1], maxima = lax.optimization_barrier((keys[-1], maxima))
@@ -518,7 +526,7 @@
         arrived.append(paired(outgoing[k * DECODE_STEPS : (k + 1) * DECODE_STEPS], k))
     pre_out = call_prefill(plan, state, prompt_query, keys, values)
 
-    from_block = facts[-GROUP_REQUESTS:]
+    from_block = state[8][:GROUP_REQUESTS, 0]
     dec_out = jnp.zeros((GROUP_REQUESTS, DECODE_STEPS, Q_WIDTH), jnp.bfloat16)
     for k in range(pd_size):
         dec_out = jnp.where((from_block == k)[:, None, None], arrived[k][None], dec_out)

time: 38.7 us -> 38.9 us (level)
  starting transfers between devices: 17.1 us -> 17.9 us
  other arithmetic: 2.47 us -> 1.89 us
    ppermute x6, starting transfers between devices: 12.9 us -> 13.9 us  [step(): return lax.ppermute(array, 'tp', self.pairs)]
    eq x1, other arithmetic: 0.73 us -> 0.15 us  [body(): from_block == k]
  transfers between devices with their start and end apart: 12 -> 12, of which waited for: 2 -> 2; matrix products, arithmetic and copies ran while one was open for 4% -> 3% of each run, Pallas kernels for 33% -> 32%
where the time goes in v11:
time: 38.9 us; the launch traced here: 38.7 us
  starting transfers between devices  17.9 us (46%)
  Pallas kernels  14.6 us (38%)
  waiting for transfers between devices  3.3 us (8%)
  other arithmetic  1.89 us (5%)
  between operations  0.78 us (2%)
    ppermute x6, starting transfers between devices, step(): return lax.ppermute(array, 'tp', self.pairs)  13.9 us
    pallas_call x1, Pallas kernels, call_prefill(): pl.pallas_call(lambda *refs: prefill_kernel(plan, *refs), in_specs=[VMEM]...  7.6 us
    ppermute x6, starting transfers between devices, paired(): lax.ppermute(array, 'pd', [(g, g ^ k) for g in range(lax.axis_size('pd'))])  4.07 us
    pallas_call x1, Pallas kernels, call_first(): pl.pallas_call(lambda *refs: first_kernel(plan, len(blocks), *refs), in_s...  3.62 us
    ppermute x6, waiting for transfers between devices, step(): return lax.ppermute(array, 'tp', self.pairs)  3.29 us
    pallas_call x1, Pallas kernels, call_decode(): pl.pallas_call(lambda *refs: decode_kernel(plan, *refs), in_specs=[VMEM]...  2.13 us
    pallas_call x1, Pallas kernels, facts_row(): pl.pallas_call(kernel, in_specs=[SMEM, SMEM], out_specs=SMEM, out_shape=j...  1.29 us
    concatenate x1, other arithmetic, body(): jnp.concatenate([decoded_query, decoded_key, decoded_value], axis=2)  0.95 us
  transfers between devices with their start and end apart: 12, of which 2 were waited for; matrix products, arithmetic and copies ran while one was open for 3% of the time, Pallas kernels for 32%

profile of v11, /device:TPU:0, one launch (start us, length us, event | category | flops | bytes accessed | tf_op | source)
XLA Modules:
  0.0 38.7 jit_solution(16915431875206623948)
XLA Ops:
  0.6 3.1 %collective-permute-start = (bf16[128,512]{1,0:T(8,128)(2,1)}, bf16[128,512]{1,0:T(8,128)(2,1)S(1)}, u32[]{:S(2)}, u32[]{:S(2)}) collective-permute-start(bf16[128,512]{1,0:T(8,128)(2,1)} %refs_6_.1), channel_id=1, source_target_pairs={{0,1},{1,3},{3,2},{2,0},{4,5},{5,7},{7,6},{6,4},{8,9},{9,11},{11,1... | collective-permute-start | bytes 393224 | tf_op jit(solution)/shard_map/ppermute | solution.py:42
  3.7 0.9 %pad_maximum_fusion = bf16[4,2,5120]{2,1,0:T(2,128)(2,1)S(1)} fusion(bf16[4,2,512]{2,1,0:T(2,128)(2,1)} %param.15, bf16[4,2,512]{2,1,0:T(2,128)(2,1)} %param.14, bf16[4,2,4096]{2,1,0:T(2,128)(2,1)} %param.13), kind=kLoop, calls=%fused_computation.4 | loop fusion | flops 245760 | bytes 163840 | tf_op jit(solution)/shard_map/concatenate | solution.py:504
  4.7 2.6 %collective-permute-start.2 = (bf16[128,512]{1,0:T(8,128)(2,1)}, bf16[128,512]{1,0:T(8,128)(2,1)S(1)}, u32[]{:S(2)}, u32[]{:S(2)}) collective-permute-start(bf16[128,512]{1,0:T(8,128)(2,1)} %refs_10_), channel_id=1, source_target_pairs={{0,1},{1,3},{3,2},{2,0},{4,5},{5,7},{7,6},{6,4},{8,9},{9,11},{11,1... | collective-permute-start | bytes 393224 | tf_op jit(solution)/shard_map/ppermute | solution.py:42
  7.3 1.3 %facts.1.refs_0_ = s32[18]{0:T(128)} custom-call(s32[4,4]{1,0:T(4,128)} %lengths_ref.1, s32[16]{0:T(128)} %slots_ref.1), custom_call_target="tpu_custom_call" | custom-call | flops 5000000000 | tf_op jit(solution)/shard_map/facts/pallas_call | solution.py:122
  8.6 0.0 copy-start
  8.7 0.0 copy-start.1
  8.7 0.0 copy-start.2
  8.7 0.0 copy-start.3
  8.7 0.1 collective-permute-done.refs_4_.refs_5_.refs_7_
  8.8 1.7 %collective-permute-start.1 = (bf16[128,512]{1,0:T(8,128)(2,1)S(1)}, bf16[128,512]{1,0:T(8,128)(2,1)S(1)}, u32[]{:S(2)}, u32[]{:S(2)}) collective-permute-start(bf16[128,512]{1,0:T(8,128)(2,1)S(1)} %collective-permute-done.refs_4_.refs_5_.refs_7_), channel_id=1, source_target_pairs={{0,1},{1,3},{3,2},{2,0},{4,5},{5,7},{7,6},{6,4},{8,9},{9,11},{11,1... | collective-permute-start | bytes 393224 | tf_op jit(solution)/shard_map/ppermute | solution.py:42
  10.5 0.0 collective-permute-start.4
  10.5 1.5 %collective-permute-start.5 = (bf16[8,5120]{1,0:T(8,128)(2,1)S(1)}, bf16[8,5120]{1,0:T(8,128)(2,1)S(1)}, u32[]{:S(2)}, u32[]{:S(2)}) collective-permute-start(bf16[8,5120]{1,0:T(8,128)(2,1)S(1)} %reshape.39.refs_9_), channel_id=1, source_target_pairs={{0,8},{4,12},{8,0},{12,4},{1,9},{5,13},{9,1},{13,5},{2,10},{6,14},... | collective-permute-start | bytes 245768 | tf_op jit(solution)/shard_map/ppermute | solution.py:489
  12.0 0.4 collective-permute-start.6
  12.4 0.0 collective-permute-done.2.refs_7_.refs_9_.refs_11_
  12.4 3.3 %collective-permute-start.3 = (bf16[128,512]{1,0:T(8,128)(2,1)S(1)}, bf16[128,512]{1,0:T(8,128)(2,1)S(1)}, u32[]{:S(2)}, u32[]{:S(2)}) collective-permute-start(bf16[128,512]{1,0:T(8,128)(2,1)S(1)} %collective-permute-done.2.refs_7_.refs_9_.refs_11_), channel_id=1, source_target_pairs={{0,1},{1,3},{3,2},{2,0},{4,5},{5,7},{7,6},{6,4},{8,9},{9,11},{11,1... | collective-permute-start | bytes 393224 | tf_op jit(solution)/shard_map/ppermute | solution.py:42
  15.7 0.0 collective-permute-done.1.refs_0_.refs_5_.refs_6_.refs_8_
  15.7 0.7 %collective-permute-start.7 = (bf16[128,512]{1,0:T(8,128)(2,1)S(1)}, bf16[128,512]{1,0:T(8,128)(2,1)S(1)}, u32[]{:S(2)}, u32[]{:S(2)}) collective-permute-start(bf16[128,512]{1,0:T(8,128)(2,1)S(1)} %collective-permute-done.1.refs_0_.refs_5_.refs_6_.refs_8_), channel_id=1, source_target_pairs={{0,1},{1,3},{3,2},{2,0},{4,5},{5,7},{7,6},{6,4},{8,9},{9,11},{11,1... | collective-permute-start | bytes 393224 | tf_op jit(solution)/shard_map/ppermute | solution.py:42
  16.3 3.2 %collective-permute-done.3.refs_8_.refs_10_.refs_12_ = bf16[128,512]{1,0:T(8,128)(2,1)S(1)} collective-permute-done((bf16[128,512]{1,0:T(8,128)(2,1)S(1)}, bf16[128,512]{1,0:T(8,128)(2,1)S(1)}, u32[]{:S(2)}, u32[]{:S(2)}) %collective-permute-start.3) | collective-permute-done | bytes 131104 | tf_op jit(solution)/shard_map/ppermute | solution.py:42
  19.5 2.5 %collective-permute-start.8 = (bf16[128,512]{1,0:T(8,128)(2,1)S(1)}, bf16[128,512]{1,0:T(8,128)(2,1)S(1)}, u32[]{:S(2)}, u32[]{:S(2)}) collective-permute-start(bf16[128,512]{1,0:T(8,128)(2,1)S(1)} %collective-permute-done.3.refs_8_.refs_10_.refs_12_), channel_id=1, source_target_pairs={{0,1},{1,3},{3,2},{2,0},{4,5},{5,7},{7,6},{6,4},{8,9},{9,11},{11,1... | collective-permute-start | bytes 393224 | tf_op jit(solution)/shard_map/ppermute | solution.py:42
  22.0 0.0 collective-permute-done.4.refs_10_
  22.0 0.0 collective-permute-done.5.refs_11_
  22.0 0.0 collective-permute-done.6.refs_12_
  22.0 0.0 copy-done
  22.0 0.0 copy-done.1
  22.0 0.0 copy-done.2
  22.0 0.0 copy-done.3
  22.0 3.6 %first_shards.1 = (f32[4,1024,256]{2,1,0:T(8,128)S(1)}, f32[4,128,128]{2,1,0:T(8,128)S(1)}, f32[4,128,256]{2,1,0:T(8,128)S(1)}, f32[4,128,128]{2,1,0:T(8,128)S(1...) custom-call(s32[18]{0:T(128)S(1)} %copy-done.3, ...), custom_call_target="tpu_custom_call" | custom-call | flops 6442450944 | bytes 2097152 | tf_op jit(solution)/shard_map/first_shards/pallas_call | solution.py:432
  25.7 0.1 compare_reduce_fusion.2
  25.8 0.0 collective-permute-done.7.refs_7_.refs_9_
  25.8 0.0 collective-permute-done.8.refs_11_.refs_13_
  25.8 2.1 %last_shard_decode.1 = bf16[16,4096]{1,0:T(8,128)(2,1)S(1)} custom-call(f32[4,128,256]{2,1,0:T(8,128)S(1)} %get-tuple-element.31.refs_0_, f32[4,128,128]{2,1,0:T(8,128)S(1)} %get-tuple-element.32.refs_1_, f32[8,128]{1,0:T(8,128)S(1)} %get-tuple-element.29.refs_2_, bf16[16,4096]{1,0:T(8,128)(2,1)S(1)} %get-tuple-element.33.refs_3_, ...), custom_call_target="tpu_custom_call" | custom-call | flops 268435456 | bytes 262144 | tf_op jit(solution)/shard_map/last_shard_decode/pallas_call | solution.py:445
  28.0 0.1 fusion
  28.0 1.6 %collective-permute-start.10 = (bf16[2,4096]{1,0:T(2,128)(2,1)S(1)}, bf16[2,4096]{1,0:T(2,128)(2,1)S(1)}, u32[]{:S(2)}, u32[]{:S(2)}) collective-permute-start(bf16[2,4096]{1,0:T(2,128)(2,1)S(1)} %get-tuple-element.43), channel_id=1, source_target_pairs={{0,8},{4,12},{8,0},{12,4},{1,9},{5,13},{9,1},{13,5},{2,10},{6,14},... | collective-permute-start | bytes 49160 | tf_op jit(solution)/shard_map/ppermute | solution.py:489
  29.6 0.0 collective-permute-start.11
  29.6 0.6 %collective-permute-start.9 = (bf16[2,4096]{1,0:T(2,128)(2,1)S(1)}, bf16[2,4096]{1,0:T(2,128)(2,1)S(1)}, u32[]{:S(2)}, u32[]{:S(2)}) collective-permute-start(bf16[2,4096]{1,0:T(2,128)(2,1)S(1)} %get-tuple-element.40), channel_id=1, source_target_pairs={{0,12},{4,8},{8,4},{12,0},{1,13},{5,9},{9,5},{13,1},{2,14},{6,10},... | collective-permute-start | bytes 49160 | tf_op jit(solution)/shard_map/ppermute | solution.py:489
  30.2 7.6 %last_shard_prefill.1 = bf16[128,4096]{1,0:T(8,128)(2,1)} custom-call(f32[4,1024,256]{2,1,0:T(8,128)S(1)} %get-tuple-element.27.refs_0_, f32[4,128,128]{2,1,0:T(8,128)S(1)} %get-tuple-element.28.refs_1_, f32[8,128]{1,0:T(8,128)S(1)} %get-tuple-element.29.refs_2_, bf16[128,4096]{1,0:T(8,128)(2,1)S(1)} %copy-done.2, bf16[128,512]{1,0:T(8,128)(2,1)S(1)} %copy-done, ...), custom_call_target="tpu_custom_call" | custom-call | flops 2147483648 | bytes 2097152 | tf_op jit(solution)/shard_map/last_shard_prefill/pallas_call | solution.py:458
  37.8 0.0 collective-permute-done.10
  37.8 0.0 collective-permute-done.11
  37.9 0.0 collective-permute-done.9
  37.9 0.8 %broadcast_select_fusion.2 = bf16[4,2,4096]{2,1,0:T(2,128)(2,1)} fusion(pred[4]{0:T(512)(128)(4,1)S(1)} %get-tuple-element.39, pred[4]{0:T(512)(128)(4,1)S(1)} %get-tuple-element.38, pred[4]{0:T(512)(128)(4,1)S(1)} %get-tuple-element.37, pred[4]{0:T(512)(128)(4,1)S(1)} %get-tuple-element.36, bf16[2,4096]{1,0:T(2,128)(2,1)S(1)} %get-tuple-element.41, ...), kind=kLoop, calls=%fused_computation.2 | loop fusion | flops 131072 | bytes 131088 | tf_op jit(solution)/shard_map/jit(_where)/select_n | solution.py:532
  (2 shorter events, 0.0 us)
Async XLA Ops:
  0.6 8.1 %collective-permute-start = (bf16[128,512]{1,0:T(8,128)(2,1)}, bf16[128,512]{1,0:T(8,128)(2,1)S(1)}, u32[]{:S(2)}, u32[]{:S(2)}) collective-permute-start(bf16[128,512]{1,0:T(8,128)(2,1)} %refs_6_.1), channel_id=1, source_target_pairs={{0,1},{1,3},{3,2},{2,0},{4,5},{5,7},{7,6},{6,4},{8,9},{9,11},{11,1... | collective-permute-start | bytes 393224 | tf_op jit(solution)/shard_map/ppermute | solution.py:42
  4.7 7.7 %collective-permute-start.2 = (bf16[128,512]{1,0:T(8,128)(2,1)}, bf16[128,512]{1,0:T(8,128)(2,1)S(1)}, u32[]{:S(2)}, u32[]{:S(2)}) collective-permute-start(bf16[128,512]{1,0:T(8,128)(2,1)} %refs_10_), channel_id=1, source_target_pairs={{0,1},{1,3},{3,2},{2,0},{4,5},{5,7},{7,6},{6,4},{8,9},{9,11},{11,1... | collective-permute-start | bytes 393224 | tf_op jit(solution)/shard_map/ppermute | solution.py:42
  8.6 13.4 %copy-start = (bf16[128,512]{1,0:T(8,128)(2,1)S(1)}, bf16[128,512]{1,0:T(8,128)(2,1)}, u32[]{:S(2)}) copy-start(bf16[128,512]{1,0:T(8,128)(2,1)} %refs_6_.1) | copy-start | bytes 393220
  8.7 13.4 %copy-start.1 = (bf16[128,512]{1,0:T(8,128)(2,1)S(1)}, bf16[128,512]{1,0:T(8,128)(2,1)}, u32[]{:S(2)}) copy-start(bf16[128,512]{1,0:T(8,128)(2,1)} %refs_10_) | copy-start | bytes 393220
  8.7 13.4 %copy-start.2 = (bf16[128,4096]{1,0:T(8,128)(2,1)S(1)}, bf16[128,4096]{1,0:T(8,128)(2,1)}, u32[]{:S(2)}) copy-start(bf16[128,4096]{1,0:T(8,128)(2,1)} %refs_3_.2) | copy-start | bytes 3145732
  8.7 13.3 %copy-start.3 = (s32[18]{0:T(128)S(1)}, s32[18]{0:T(128)}, u32[]{:S(2)}) copy-start(s32[18]{0:T(128)} %facts.1.refs_0_) | copy-start | bytes 220
  8.8 6.9 %collective-permute-start.1 = (bf16[128,512]{1,0:T(8,128)(2,1)S(1)}, bf16[128,512]{1,0:T(8,128)(2,1)S(1)}, u32[]{:S(2)}, u32[]{:S(2)}) collective-permute-start(bf16[128,512]{1,0:T(8,128)(2,1)S(1)} %collective-permute-done.refs_4_.refs_5_.refs_7_), channel_id=1, source_target_pairs={{0,1},{1,3},{3,2},{2,0},{4,5},{5,7},{7,6},{6,4},{8,9},{9,11},{11,1... | collective-permute-start | bytes 393224 | tf_op jit(solution)/shard_map/ppermute | solution.py:42
  10.5 11.5 %collective-permute-start.4 = (bf16[8,5120]{1,0:T(8,128)(2,1)S(1)}, bf16[8,5120]{1,0:T(8,128)(2,1)S(1)}, u32[]{:S(2)}, u32[]{:S(2)}) collective-permute-start(bf16[8,5120]{1,0:T(8,128)(2,1)S(1)} %reshape.39.refs_9_), channel_id=1, source_target_pairs={{0,4},{4,0},{8,12},{12,8},{1,5},{5,1},{9,13},{13,9},{2,6},{6,2},{1... | collective-permute-start | bytes 245768 | tf_op jit(solution)/shard_map/ppermute | solution.py:489
  10.5 11.5 %collective-permute-start.5 = (bf16[8,5120]{1,0:T(8,128)(2,1)S(1)}, bf16[8,5120]{1,0:T(8,128)(2,1)S(1)}, u32[]{:S(2)}, u32[]{:S(2)}) collective-permute-start(bf16[8,5120]{1,0:T(8,128)(2,1)S(1)} %reshape.39.refs_9_), channel_id=1, source_target_pairs={{0,8},{4,12},{8,0},{12,4},{1,9},{5,13},{9,1},{13,5},{2,10},{6,14},... | collective-permute-start | bytes 245768 | tf_op jit(solution)/shard_map/ppermute | solution.py:489
  12.0 10.0 %collective-permute-start.6 = (bf16[8,5120]{1,0:T(8,128)(2,1)S(1)}, bf16[8,5120]{1,0:T(8,128)(2,1)S(1)}, u32[]{:S(2)}, u32[]{:S(2)}) collective-permute-start(bf16[8,5120]{1,0:T(8,128)(2,1)S(1)} %reshape.39.refs_9_), channel_id=1, source_target_pairs={{0,12},{4,8},{8,4},{12,0},{1,13},{5,9},{9,5},{13,1},{2,14},{6,10},... | collective-permute-start | bytes 245768 | tf_op jit(solution)/shard_map/ppermute | solution.py:489
  12.4 7.1 %collective-permute-start.3 = (bf16[128,512]{1,0:T(8,128)(2,1)S(1)}, bf16[128,512]{1,0:T(8,128)(2,1)S(1)}, u32[]{:S(2)}, u32[]{:S(2)}) collective-permute-start(bf16[128,512]{1,0:T(8,128)(2,1)S(1)} %collective-permute-done.2.refs_7_.refs_9_.refs_11_), channel_id=1, source_target_pairs={{0,1},{1,3},{3,2},{2,0},{4,5},{5,7},{7,6},{6,4},{8,9},{9,11},{11,1... | collective-permute-start | bytes 393224 | tf_op jit(solution)/shard_map/ppermute | solution.py:42
  15.7 10.2 %collective-permute-start.7 = (bf16[128,512]{1,0:T(8,128)(2,1)S(1)}, bf16[128,512]{1,0:T(8,128)(2,1)S(1)}, u32[]{:S(2)}, u32[]{:S(2)}) collective-permute-start(bf16[128,512]{1,0:T(8,128)(2,1)S(1)} %collective-permute-done.1.refs_0_.refs_5_.refs_6_.refs_8_), channel_id=1, source_target_pairs={{0,1},{1,3},{3,2},{2,0},{4,5},{5,7},{7,6},{6,4},{8,9},{9,11},{11,1... | collective-permute-start | bytes 393224 | tf_op jit(solution)/shard_map/ppermute | solution.py:42
  19.5 6.3 %collective-permute-start.8 = (bf16[128,512]{1,0:T(8,128)(2,1)S(1)}, bf16[128,512]{1,0:T(8,128)(2,1)S(1)}, u32[]{:S(2)}, u32[]{:S(2)}) collective-permute-start(bf16[128,512]{1,0:T(8,128)(2,1)S(1)} %collective-permute-done.3.refs_8_.refs_10_.refs_12_), channel_id=1, source_target_pairs={{0,1},{1,3},{3,2},{2,0},{4,5},{5,7},{7,6},{6,4},{8,9},{9,11},{11,1... | collective-permute-start | bytes 393224 | tf_op jit(solution)/shard_map/ppermute | solution.py:42
  28.0 9.8 %collective-permute-start.10 = (bf16[2,4096]{1,0:T(2,128)(2,1)S(1)}, bf16[2,4096]{1,0:T(2,128)(2,1)S(1)}, u32[]{:S(2)}, u32[]{:S(2)}) collective-permute-start(bf16[2,4096]{1,0:T(2,128)(2,1)S(1)} %get-tuple-element.43), channel_id=1, source_target_pairs={{0,8},{4,12},{8,0},{12,4},{1,9},{5,13},{9,1},{13,5},{2,10},{6,14},... | collective-permute-start | bytes 49160 | tf_op jit(solution)/shard_map/ppermute | solution.py:489
  29.6 8.3 %collective-permute-start.11 = (bf16[2,4096]{1,0:T(2,128)(2,1)S(1)}, bf16[2,4096]{1,0:T(2,128)(2,1)S(1)}, u32[]{:S(2)}, u32[]{:S(2)}) collective-permute-start(bf16[2,4096]{1,0:T(2,128)(2,1)S(1)} %get-tuple-element.42), channel_id=1, source_target_pairs={{0,4},{4,0},{8,12},{12,8},{1,5},{5,1},{9,13},{13,9},{2,6},{6,2},{1... | collective-permute-start | bytes 49160 | tf_op jit(solution)/shard_map/ppermute | solution.py:489
  29.6 8.3 %collective-permute-start.9 = (bf16[2,4096]{1,0:T(2,128)(2,1)S(1)}, bf16[2,4096]{1,0:T(2,128)(2,1)S(1)}, u32[]{:S(2)}, u32[]{:S(2)}) collective-permute-start(bf16[2,4096]{1,0:T(2,128)(2,1)S(1)} %get-tuple-element.40), channel_id=1, source_target_pairs={{0,12},{4,8},{8,4},{12,0},{1,13},{5,9},{9,5},{13,1},{2,14},{6,10},... | collective-permute-start | bytes 49160 | tf_op jit(solution)/shard_map/ppermute | solution.py:489

commit v12 on v11

--- a/solution.py
+++ b/solution.py
@@ -37,9 +37,13 @@
         self.size = size
         order = [0] + list(range(1, size, 2)) + [i for i in range(size - 1, 0, -1) if i % 2 == 0]
         self.pairs = [(order[i], order[(i + 1) % size]) for i in range(size)]
-
-    def step(self, array):
-        return lax.ppermute(array, "tp", self.pairs)
+        self.offsets = [0]
+        for d in range(1, size // 2 + 1):
+            self.offsets += [-d, d]
+        self.offsets = self.offsets[:size]
+
+    def step(self, array, up):
+        return lax.ppermute(array, "tp", self.pairs if up else [(b, a) for a, b in self.pairs])
 
 
 def scores_of(queries, keys):
@@ -105,8 +109,8 @@
         values += [slots_ref[group * GROUP_REQUESTS + r] for r in range(GROUP_REQUESTS)]
         values += [lengths_ref[group, r] for r in range(GROUP_REQUESTS)]
         place = jnp.where(member % 2 == 1, (member + 1) // 2, width - member // 2)
-        for s in range(width):
-            before = (place + width - s) % width
+        for offset in plan.offsets:
+            before = (place + width + offset) % width
             up = 2 * before - 1
             values.append(jnp.where(before == 0, 0, jnp.where(before <= width // 2, up, 2 * (width - before))))
         for i, value in enumerate(values):
@@ -204,7 +208,7 @@
 
 def first_kernel(plan, pd_size, facts_ref, maxima_ref, q_ref, *refs):
     width = plan.size
-    k_refs, v_refs, refs = refs[: width - 1], refs[width - 1 : 2 * width - 2], refs[2 * width - 2 :]
+    kv_refs, refs = refs[: width - 1], refs[width - 1 :]
     block_refs, refs = refs[:pd_size], refs[pd_size:]
     acc_ref, bias_ref, dec_acc_ref, dec_bias_ref, worst_ref, queries_ref, fresh_ref, pick_ref, owner_ref = refs
     tokens = q_ref.shape[0]
@@ -243,8 +247,8 @@
         columns = span(h * HEAD_SIZE, HEAD_SIZE)
         first = h * Q_BLOCK
         queries = stacked_heads(queries_ref, slice(None), first, HEADS_PER_KV)
-        k_all = jnp.concatenate([ref[:, columns] for ref in k_refs], axis=0)
-        v_all = with_ones(jnp.concatenate([ref[:, columns] for ref in v_refs], axis=0))
+        k_all = jnp.concatenate([ref[:tokens, columns] for ref in kv_refs], axis=0)
+        v_all = with_ones(jnp.concatenate([ref[tokens:, columns] for ref in kv_refs], axis=0))
         new_scores = scores_of(queries, fresh_ref[:, columns]) * EXPONENT
         new_weights = weigh(jnp.where(new_mask, new_scores, MASKED))
         new_values = fresh_ref[:, span(KV_WIDTH + h * HEAD_SIZE, HEAD_SIZE)]
@@ -252,8 +256,10 @@
         dec_acc_ref[h] = product(weights, v_all) + product(new_weights, with_ones(new_values))
         for (start, keys), bias in zip(spans, biases):
             if keys < tokens:
-                k_part = jnp.concatenate([ref[:keys, columns] for ref in k_refs], axis=0)
-                v_part = with_ones(jnp.concatenate([ref[:keys, columns] for ref in v_refs], axis=0))
+                k_part = jnp.concatenate([ref[:keys, columns] for ref in kv_refs], axis=0)
+                v_part = with_ones(
+                    jnp.concatenate([ref[tokens : tokens + keys, columns] for ref in kv_refs], axis=0)
+                )
             else:
                 k_part, v_part = k_all, v_all
             for g in range(0, HEADS_PER_KV, together):
@@ -299,7 +305,8 @@
 
 def decode_kernel(plan, acc_ref, bias_ref, worst_ref, queries_ref, fresh_ref, pick_ref, *refs):
     width = plan.size
-    k_refs, v_refs, (out_ref,) = refs[:width], refs[width : 2 * width], refs[2 * width :]
+    kv_refs, (out_ref,) = refs[:width], refs[width:]
+    tokens = kv_refs[0].shape[0] // 2
     heads = range(KEY_VALUE_HEADS)
     columns = [slice(h * HEAD_SIZE, (h + 1) * HEAD_SIZE) for h in heads]
 
@@ -314,11 +321,11 @@
         out_ref[...] = product(pick_ref[...], out).astype(jnp.bfloat16)
 
     exponents = [
-        scores_of(queries_of(h), k_refs[-1][:, columns[h]]) * EXPONENT + bias_ref[width - 1]
+        scores_of(queries_of(h), kv_refs[-1][:tokens, columns[h]]) * EXPONENT + bias_ref[width - 1]
         for h in heads
     ]
     acc = [
-        acc_ref[h] + product(jnp.exp2(exponents[h]).astype(jnp.bfloat16), with_ones(v_refs[-1][:, columns[h]]))
+        acc_ref[h] + product(jnp.exp2(exponents[h]).astype(jnp.bfloat16), with_ones(kv_refs[-1][tokens:, columns[h]]))
         for h in heads
     ]
     send(acc)
@@ -338,8 +345,8 @@
             new_columns = slice(KV_WIDTH + h * HEAD_SIZE, KV_WIDTH + (h + 1) * HEAD_SIZE)
             state = fold(None, [scores], [fresh_ref[:, new_columns]])
             for parts in parts_in(width):
-                k_part = jnp.concatenate([k_refs[s][:, columns[h]] for s in parts], axis=0)
-                v_part = jnp.concatenate([v_refs[s][:, columns[h]] for s in parts], axis=0)
+                k_part = jnp.concatenate([kv_refs[s][:tokens, columns[h]] for s in parts], axis=0)
+                v_part = jnp.concatenate([kv_refs[s][tokens:, columns[h]] for s in parts], axis=0)
                 bias = jnp.concatenate([bias_ref[s] for s in parts], axis=1)
                 state = fold(state, [scores_of(queries, k_part) + bias], [v_part])
             again.append(state[1])
@@ -348,7 +355,7 @@
 
 def prefill_kernel(plan, acc_ref, bias_ref, worst_ref, q_ref, *refs):
     width = plan.size
-    k_refs, v_refs, refs = refs[:width], refs[width : 2 * width], refs[2 * width :]
+    kv_refs, refs = refs[:width], refs[width:]
     out_ref, done_ref, sem = refs
     tokens = q_ref.shape[0]
     half = tokens // 2
@@ -367,7 +374,7 @@
     worst, least = worst_ref[...], None
     for h in range(KEY_VALUE_HEADS):
         columns = slice(h * HEAD_SIZE, (h + 1) * HEAD_SIZE)
-        keys, values = k_refs[-1][:, columns], with_ones(v_refs[-1][:, columns])
+        keys, values = kv_refs[-1][:tokens, columns], with_ones(kv_refs[-1][tokens:, columns])
         for start, bias in zip((0, half), biases):
             queries = stacked_heads(q_ref, slice(start, start + half), h * Q_BLOCK, HEADS_PER_KV)
             scores = scores_of(queries, keys).reshape(HEADS_PER_KV, half, tokens)
@@ -391,8 +398,8 @@
                 queries = stacked_heads(q_ref, slice(start, start + half), h * Q_BLOCK, HEADS_PER_KV)
                 state = None
                 for parts in parts_in(width):
-                    k_part = jnp.concatenate([k_refs[s][:, columns] for s in parts], axis=0)
-                    v_part = jnp.concatenate([v_refs[s][:, columns] for s in parts], axis=0)
+                    k_part = jnp.concatenate([kv_refs[s][:tokens, columns] for s in parts], axis=0)
+                    v_part = jnp.concatenate([kv_refs[s][tokens:, columns] for s in parts], axis=0)
                     bias = jnp.concatenate([bias_ref[s, start : start + half, :] for s in parts], axis=1)
                     scores = scores_of(queries, k_part).reshape(HEADS_PER_KV, half, bias.shape[1])
                     scores = (scores + bias[None]).reshape(HEADS_PER_KV * half, bias.shape[1])
@@ -413,7 +420,7 @@
     )
 
 
-def call_first(plan, facts, maxima, query, blocks, keys, values):
+def call_first(plan, facts, maxima, query, blocks, pieces):
     tokens, width = query.shape[0], plan.size
     rows = HEADS_PER_KV * tokens
     f32, bf16 = jnp.float32, jnp.bfloat16
@@ -431,33 +438,33 @@
     ]
     return pl.pallas_call(
         lambda *refs: first_kernel(plan, len(blocks), *refs),
-        in_specs=[SMEM] + [VMEM] * (2 + len(blocks) + 2 * (width - 1)),
+        in_specs=[SMEM] + [VMEM] * (2 + len(blocks) + width - 1),
         out_specs=[VMEM] * len(shapes),
         out_shape=shapes,
         compiler_params=pltpu.CompilerParams(vmem_limit_bytes=(28 + width) * MIB),
         cost_estimate=cost(tokens, every, tokens * every * QUERY_HEADS),
         name="first_shards",
-    )(facts, maxima, query, *keys, *values, *blocks)
-
-
-def call_decode(plan, state, keys, values):
-    tokens, width = keys[0].shape[0], plan.size
+    )(facts, maxima, query, *pieces, *blocks)
+
+
+def call_decode(plan, state, pieces):
+    tokens, width = pieces[0].shape[0] // 2, plan.size
     return pl.pallas_call(
         lambda *refs: decode_kernel(plan, *refs),
-        in_specs=[VMEM] * (6 + 2 * width),
+        in_specs=[VMEM] * (6 + width),
         out_specs=VMEM,
         out_shape=jax.ShapeDtypeStruct((PADDED_ROWS, Q_WIDTH), jnp.bfloat16),
         compiler_params=pltpu.CompilerParams(vmem_limit_bytes=(28 + width) * MIB),
         cost_estimate=cost(PADDED_ROWS, tokens, PADDED_ROWS * tokens * QUERY_HEADS),
         name="last_shard_decode",
-    )(*state[2:8], *keys, *values)
-
-
-def call_prefill(plan, state, query, keys, values):
+    )(*state[2:8], *pieces)
+
+
+def call_prefill(plan, state, query, pieces):
     tokens, width = query.shape[0], plan.size
     return pl.pallas_call(
         lambda *refs: prefill_kernel(plan, *refs),
-        in_specs=[VMEM] * (4 + 2 * width),
+        in_specs=[VMEM] * (4 + width),
         out_specs=ANY,
         out_shape=jax.ShapeDtypeStruct((tokens, Q_WIDTH), jnp.bfloat16),
         scratch_shapes=[
@@ -467,7 +474,7 @@
         compiler_params=pltpu.CompilerParams(vmem_limit_bytes=(28 + width) * MIB),
         cost_estimate=cost(tokens, tokens, tokens * tokens * QUERY_HEADS),
         name="last_shard_prefill",
-    )(*state[:2], state[4], query, *keys, *values)
+    )(*state[:2], state[4], query, *pieces)
 
 
 def start_maxima(*arrays, flops=5 * 10**9):
@@ -505,26 +512,27 @@
         DECODE_ROWS, Q_WIDTH + 2 * KV_WIDTH
     )
     facts = facts_row(plan, prompt_lengths, decode_slot)
-    prompt_key, decoded_query = lax.optimization_barrier((prompt_key, decoded_query))
-    prompt_value, own = lax.optimization_barrier((prompt_value, own))
-    keys, values, maxima = [prompt_key], [prompt_value], None
-    for s in range(1, plan.size):
-        if s == 2:
-            keys[1], own, facts = lax.optimization_barrier((keys[1], own, facts))
-        if s == plan.size - 1:
-            maxima = start_maxima(keys[-1])
-            keys[-1], maxima = lax.optimization_barrier((keys[-1], maxima))
-        keys.append(plan.step(keys[-1]))
-        values.append(plan.step(values[-1]))
-        if s == 2:
-            blocks = [own] + [paired(own, k) for k in range(1, pd_size)]
-
-    state = call_first(plan, facts, maxima, prompt_query, blocks, keys[:-1], values[:-1])
-    outgoing = call_decode(plan, state, keys, values)
+    kv, decoded_query = lax.optimization_barrier(
+        (jnp.concatenate([prompt_key, prompt_value], axis=0), decoded_query)
+    )
+    later_kv, own = lax.optimization_barrier((kv, own))
+    pieces, maxima, up, down = [kv], None, kv, later_kv
+    for d in range(1, plan.size // 2 + 1):
+        if d == 2:
+            up, facts = lax.optimization_barrier((up, facts))
+        up = plan.step(up, True)
+        down = plan.step(down, False) if 2 * d < plan.size else None
+        pieces += [up, down]
+    pieces = pieces[: plan.size]
+    blocks = [own] + [paired(own, k) for k in range(1, pd_size)]
+    maxima = start_maxima(pieces[1])
+
+    state = call_first(plan, facts, maxima, prompt_query, blocks, pieces[:-1])
+    outgoing = call_decode(plan, state, pieces)
     arrived = [outgoing[:DECODE_STEPS]]
     for k in range(1, pd_size):
         arrived.append(paired(outgoing[k * DECODE_STEPS : (k + 1) * DECODE_STEPS], k))
-    pre_out = call_prefill(plan, state, prompt_query, keys, values)
+    pre_out = call_prefill(plan, state, prompt_query, pieces)
 
     from_block = state[8][:GROUP_REQUESTS, 0]
     dec_out = jnp.zeros((GROUP_REQUESTS, DECODE_STEPS, Q_WIDTH), jnp.bfloat16)

time: 38.9 us -> 37.6 us (0.967)
  starting transfers between devices: 17.9 us -> 15.4 us
  other arithmetic: 1.89 us -> 2.88 us
    ppermute x6 -> x3, starting transfers between devices: 13.9 us -> 11.5 us  [step(): lax.ppermute(array, 'tp', self.pairs if up else [(b, a) for a, b in self....]
    concatenate x0 -> x1, other arithmetic: none -> 0.99 us  [body(): jnp.concatenate([prompt_key, prompt_value], axis=0)]
    ppermute x6 -> x3, waiting for transfers between devices: 3.29 us -> 3.49 us  [step(): lax.ppermute(array, 'tp', self.pairs if up else [(b, a) for a, b in self....]
  transfers between devices with their start and end apart: 12 -> 9, of which waited for: 2 -> 2; matrix products, arithmetic and copies ran while one was open for 3% -> 3% of each run, Pallas kernels for 32% -> 34%
where the time goes in v12:
time: 37.6 us; the launch traced here: 37.3 us
  starting transfers between devices  15.4 us (41%)
  Pallas kernels  14.6 us (39%)
  waiting for transfers between devices  3.51 us (9%)
  other arithmetic  2.88 us (8%)
  between operations  0.76 us (2%)
    ppermute x3, starting transfers between devices, step(): lax.ppermute(array, 'tp', self.pairs if up else [(b, a) for a, b in self....  11.5 us
    pallas_call x1, Pallas kernels, call_prefill(): pl.pallas_call(lambda *refs: prefill_kernel(plan, *refs), in_specs=[VMEM]...  7.6 us
    ppermute x6, starting transfers between devices, paired(): lax.ppermute(array, 'pd', [(g, g ^ k) for g in range(lax.axis_size('pd'))])  3.86 us
    pallas_call x1, Pallas kernels, call_first(): pl.pallas_call(lambda *refs: first_kernel(plan, len(blocks), *refs), in_s...  3.61 us
    ppermute x3, waiting for transfers between devices, step(): lax.ppermute(array, 'tp', self.pairs if up else [(b, a) for a, b in self....  3.49 us
    pallas_call x1, Pallas kernels, call_decode(): pl.pallas_call(lambda *refs: decode_kernel(plan, *refs), in_specs=[VMEM]...  2.13 us
    pallas_call x1, Pallas kernels, facts_row(): pl.pallas_call(kernel, in_specs=[SMEM, SMEM], out_specs=SMEM, out_shape=j...  1.29 us
    concatenate x1, other arithmetic, body(): jnp.concatenate([prompt_key, prompt_value], axis=0)  0.99 us
  transfers between devices with their start and end apart: 9, of which 2 were waited for; matrix products, arithmetic and copies ran while one was open for 3% of the time, Pallas kernels for 34%

profile of v12, /device:TPU:0, one launch (start us, length us, event | category | flops | bytes accessed | tf_op | source)
XLA Modules:
  0.0 37.3 jit_solution(9528373570158102681)
XLA Ops:
  0.6 1.0 %pad_maximum_fusion.refs_3_.refs_4_.refs_6_ = bf16[256,512]{1,0:T(8,128)(2,1)S(1)} fusion(bf16[128,512]{1,0:T(8,128)(2,1)} %param.10, bf16[128,512]{1,0:T(8,128)(2,1)} %param.9), kind=kLoop, calls=%fused_computation | loop fusion | flops 524288 | bytes 524288 | tf_op jit(solution)/shard_map/concatenate | solution.py:516
  1.6 3.1 %collective-permute-start = (bf16[256,512]{1,0:T(8,128)(2,1)S(1)}, bf16[256,512]{1,0:T(8,128)(2,1)S(1)}, u32[]{:S(2)}, u32[]{:S(2)}) collective-permute-start(bf16[256,512]{1,0:T(8,128)(2,1)S(1)} %pad_maximum_fusion.refs_3_.refs_4_.refs_6_), channel_id=1, source_target_pairs={{0,1},{1,3},{3,2},{2,0},{4,5},{5,7},{7,6},{6,4},{8,9},{9,11},{11,1... | collective-permute-start | bytes 786440 | tf_op jit(solution)/shard_map/ppermute | solution.py:46
  4.7 0.9 %pad_maximum_fusion.1 = bf16[4,2,5120]{2,1,0:T(2,128)(2,1)S(1)} fusion(bf16[4,2,512]{2,1,0:T(2,128)(2,1)} %param.15, bf16[4,2,512]{2,1,0:T(2,128)(2,1)} %param.14, bf16[4,2,4096]{2,1,0:T(2,128)(2,1)} %param.13), kind=kLoop, calls=%fused_computation.5 | loop fusion | flops 245760 | bytes 163840 | tf_op jit(solution)/shard_map/concatenate | solution.py:511
  5.7 0.1 collective-permute-start.2
  5.8 1.6 %collective-permute-start.3 = (bf16[8,5120]{1,0:T(8,128)(2,1)S(1)}, bf16[8,5120]{1,0:T(8,128)(2,1)S(1)}, u32[]{:S(2)}, u32[]{:S(2)}) collective-permute-start(bf16[8,5120]{1,0:T(8,128)(2,1)S(1)} %reshape.39.refs_6_), channel_id=1, source_target_pairs={{0,8},{4,12},{8,0},{12,4},{1,9},{5,13},{9,1},{13,5},{2,10},{6,14},... | collective-permute-start | bytes 245768 | tf_op jit(solution)/shard_map/ppermute | solution.py:496
  7.3 0.3 collective-permute-start.4
  7.6 1.1 %collective-permute-start.1 = (bf16[256,512]{1,0:T(8,128)(2,1)S(1)}, bf16[256,512]{1,0:T(8,128)(2,1)S(1)}, u32[]{:S(2)}, u32[]{:S(2)}) collective-permute-start(bf16[256,512]{1,0:T(8,128)(2,1)S(1)} %pad_maximum_fusion.refs_3_.refs_4_.refs_6_), channel_id=1, source_target_pairs={{1,0},{3,1},{2,3},{0,2},{5,4},{7,5},{6,7},{4,6},{9,8},{11,9},{10,1... | collective-permute-start | bytes 786440 | tf_op jit(solution)/shard_map/ppermute | solution.py:46
  8.7 1.3 %facts.1.refs_0_ = s32[18]{0:T(128)} custom-call(s32[4,4]{1,0:T(4,128)} %lengths_ref.1, s32[16]{0:T(128)} %slots_ref.1), custom_call_target="tpu_custom_call" | custom-call | flops 5000000000 | tf_op jit(solution)/shard_map/facts/pallas_call | solution.py:126
  10.0 0.0 copy-start
  10.1 0.0 copy-start.1
  10.1 2.0 %collective-permute-done.refs_0_.refs_4_.refs_5_.refs_7_ = bf16[256,512]{1,0:T(8,128)(2,1)S(1)} collective-permute-done((bf16[256,512]{1,0:T(8,128)(2,1)S(1)}, bf16[256,512]{1,0:T(8,128)(2,1)S(1)}, u32[]{:S(2)}, u32[]{:S(2)}) %collective-permute-start) | collective-permute-done | bytes 262176 | tf_op jit(solution)/shard_map/ppermute | solution.py:46
  12.1 7.4 %collective-permute-start.5 = (bf16[256,512]{1,0:T(8,128)(2,1)S(1)}, bf16[256,512]{1,0:T(8,128)(2,1)S(1)}, u32[]{:S(2)}, u32[]{:S(2)}) collective-permute-start(bf16[256,512]{1,0:T(8,128)(2,1)S(1)} %collective-permute-done.refs_0_.refs_4_.refs_5_.refs_7_), channel_id=1, source_target_pairs={{0,1},{1,3},{3,2},{2,0},{4,5},{5,7},{7,6},{6,4},{8,9},{9,11},{11,1... | collective-permute-start | bytes 786440 | tf_op jit(solution)/shard_map/ppermute | solution.py:46
  19.4 0.0 collective-permute-done.2.refs_7_
  19.4 0.0 collective-permute-done.3.refs_8_
  19.4 0.0 collective-permute-done.4.refs_9_
  19.4 0.0 collective-permute-done.1.refs_5_.refs_6_.refs_8_
  19.5 0.0 copy-done
  19.5 0.0 copy-done.1
  19.5 3.6 %first_shards.1 = (f32[4,1024,256]{2,1,0:T(8,128)S(1)}, f32[4,128,128]{2,1,0:T(8,128)S(1)}, f32[4,128,256]{2,1,0:T(8,128)S(1)}, f32[4,128,128]{2,1,0:T(8,128)S(1...) custom-call(s32[18]{0:T(128)S(1)} %copy-done.1, ...), custom_call_target="tpu_custom_call" | custom-call | flops 6442450944 | bytes 2097152 | tf_op jit(solution)/shard_map/first_shards/pallas_call | solution.py:439
  23.1 0.1 compare_reduce_fusion.2
  23.2 1.5 %collective-permute-done.5.refs_7_.refs_9_ = bf16[256,512]{1,0:T(8,128)(2,1)S(1)} collective-permute-done((bf16[256,512]{1,0:T(8,128)(2,1)S(1)}, bf16[256,512]{1,0:T(8,128)(2,1)S(1)}, u32[]{:S(2)}, u32[]{:S(2)}) %collective-permute-start.5) | collective-permute-done | bytes 262176 | tf_op jit(solution)/shard_map/ppermute | solution.py:46
  24.7 2.1 %last_shard_decode.1 = bf16[16,4096]{1,0:T(8,128)(2,1)S(1)} custom-call(f32[4,128,256]{2,1,0:T(8,128)S(1)} %get-tuple-element.25.refs_0_, f32[4,128,128]{2,1,0:T(8,128)S(1)} %get-tuple-element.26.refs_1_, f32[8,128]{1,0:T(8,128)S(1)} %get-tuple-element.22.refs_2_, bf16[16,4096]{1,0:T(8,128)(2,1)S(1)} %get-tuple-element.27.refs_3_, ...), custom_call_target="tpu_custom_call" | custom-call | flops 268435456 | bytes 262144 | tf_op jit(solution)/shard_map/last_shard_decode/pallas_call | solution.py:452
  26.9 0.1 fusion
  26.9 1.2 %collective-permute-start.6 = (bf16[2,4096]{1,0:T(2,128)(2,1)S(1)}, bf16[2,4096]{1,0:T(2,128)(2,1)S(1)}, u32[]{:S(2)}, u32[]{:S(2)}) collective-permute-start(bf16[2,4096]{1,0:T(2,128)(2,1)S(1)} %get-tuple-element.34), channel_id=1, source_target_pairs={{0,12},{4,8},{8,4},{12,0},{1,13},{5,9},{9,5},{13,1},{2,14},{6,10},... | collective-permute-start | bytes 49160 | tf_op jit(solution)/shard_map/ppermute | solution.py:496
  28.1 0.5 %collective-permute-start.7 = (bf16[2,4096]{1,0:T(2,128)(2,1)S(1)}, bf16[2,4096]{1,0:T(2,128)(2,1)S(1)}, u32[]{:S(2)}, u32[]{:S(2)}) collective-permute-start(bf16[2,4096]{1,0:T(2,128)(2,1)S(1)} %get-tuple-element.37), channel_id=1, source_target_pairs={{0,8},{4,12},{8,0},{12,4},{1,9},{5,13},{9,1},{13,5},{2,10},{6,14},... | collective-permute-start | bytes 49160 | tf_op jit(solution)/shard_map/ppermute | solution.py:496
  28.6 0.2 collective-permute-start.8
  28.8 7.6 %last_shard_prefill.1 = bf16[128,4096]{1,0:T(8,128)(2,1)} custom-call(f32[4,1024,256]{2,1,0:T(8,128)S(1)} %get-tuple-element.20.refs_0_, f32[4,128,128]{2,1,0:T(8,128)S(1)} %get-tuple-element.21.refs_1_, f32[8,128]{1,0:T(8,128)S(1)} %get-tuple-element.22.refs_2_, bf16[128,4096]{1,0:T(8,128)(2,1)S(1)} %copy-done, ...), custom_call_target="tpu_custom_call" | custom-call | flops 2147483648 | bytes 2097152 | tf_op jit(solution)/shard_map/last_shard_prefill/pallas_call | solution.py:465
  36.5 0.0 collective-permute-done.6
  36.5 0.0 collective-permute-done.7
  36.5 0.0 collective-permute-done.8
  36.5 0.8 %broadcast_select_fusion.2 = bf16[4,2,4096]{2,1,0:T(2,128)(2,1)} fusion(pred[4]{0:T(512)(128)(4,1)S(1)} %get-tuple-element.33, pred[4]{0:T(512)(128)(4,1)S(1)} %get-tuple-element.32, pred[4]{0:T(512)(128)(4,1)S(1)} %get-tuple-element.31, pred[4]{0:T(512)(128)(4,1)S(1)} %get-tuple-element.30, bf16[2,4096]{1,0:T(2,128)(2,1)S(1)} %get-tuple-element.35, ...), kind=kLoop, calls=%fused_computation.3 | loop fusion | flops 131072 | bytes 131088 | tf_op jit(solution)/shard_map/jit(_where)/select_n | solution.py:540
  (2 shorter events, 0.0 us)
Async XLA Ops:
  1.6 10.5 %collective-permute-start = (bf16[256,512]{1,0:T(8,128)(2,1)S(1)}, bf16[256,512]{1,0:T(8,128)(2,1)S(1)}, u32[]{:S(2)}, u32[]{:S(2)}) collective-permute-start(bf16[256,512]{1,0:T(8,128)(2,1)S(1)} %pad_maximum_fusion.refs_3_.refs_4_.refs_6_), channel_id=1, source_target_pairs={{0,1},{1,3},{3,2},{2,0},{4,5},{5,7},{7,6},{6,4},{8,9},{9,11},{11,1... | collective-permute-start | bytes 786440 | tf_op jit(solution)/shard_map/ppermute | solution.py:46
  5.7 13.7 %collective-permute-start.2 = (bf16[8,5120]{1,0:T(8,128)(2,1)S(1)}, bf16[8,5120]{1,0:T(8,128)(2,1)S(1)}, u32[]{:S(2)}, u32[]{:S(2)}) collective-permute-start(bf16[8,5120]{1,0:T(8,128)(2,1)S(1)} %reshape.39.refs_6_), channel_id=1, source_target_pairs={{0,4},{4,0},{8,12},{12,8},{1,5},{5,1},{9,13},{13,9},{2,6},{6,2},{1... | collective-permute-start | bytes 245768 | tf_op jit(solution)/shard_map/ppermute | solution.py:496
  5.8 13.7 %collective-permute-start.3 = (bf16[8,5120]{1,0:T(8,128)(2,1)S(1)}, bf16[8,5120]{1,0:T(8,128)(2,1)S(1)}, u32[]{:S(2)}, u32[]{:S(2)}) collective-permute-start(bf16[8,5120]{1,0:T(8,128)(2,1)S(1)} %reshape.39.refs_6_), channel_id=1, source_target_pairs={{0,8},{4,12},{8,0},{12,4},{1,9},{5,13},{9,1},{13,5},{2,10},{6,14},... | collective-permute-start | bytes 245768 | tf_op jit(solution)/shard_map/ppermute | solution.py:496
  7.3 12.1 %collective-permute-start.4 = (bf16[8,5120]{1,0:T(8,128)(2,1)S(1)}, bf16[8,5120]{1,0:T(8,128)(2,1)S(1)}, u32[]{:S(2)}, u32[]{:S(2)}) collective-permute-start(bf16[8,5120]{1,0:T(8,128)(2,1)S(1)} %reshape.39.refs_6_), channel_id=1, source_target_pairs={{0,12},{4,8},{8,4},{12,0},{1,13},{5,9},{9,5},{13,1},{2,14},{6,10},... | collective-permute-start | bytes 245768 | tf_op jit(solution)/shard_map/ppermute | solution.py:496
  7.6 11.8 %collective-permute-start.1 = (bf16[256,512]{1,0:T(8,128)(2,1)S(1)}, bf16[256,512]{1,0:T(8,128)(2,1)S(1)}, u32[]{:S(2)}, u32[]{:S(2)}) collective-permute-start(bf16[256,512]{1,0:T(8,128)(2,1)S(1)} %pad_maximum_fusion.refs_3_.refs_4_.refs_6_), channel_id=1, source_target_pairs={{1,0},{3,1},{2,3},{0,2},{5,4},{7,5},{6,7},{4,6},{9,8},{11,9},{10,1... | collective-permute-start | bytes 786440 | tf_op jit(solution)/shard_map/ppermute | solution.py:46
  10.0 9.4 %copy-start = (bf16[128,4096]{1,0:T(8,128)(2,1)S(1)}, bf16[128,4096]{1,0:T(8,128)(2,1)}, u32[]{:S(2)}) copy-start(bf16[128,4096]{1,0:T(8,128)(2,1)} %refs_3_.1) | copy-start | bytes 3145732
  10.1 9.4 %copy-start.1 = (s32[18]{0:T(128)S(1)}, s32[18]{0:T(128)}, u32[]{:S(2)}) copy-start(s32[18]{0:T(128)} %facts.1.refs_0_) | copy-start | bytes 220
  12.1 12.7 %collective-permute-start.5 = (bf16[256,512]{1,0:T(8,128)(2,1)S(1)}, bf16[256,512]{1,0:T(8,128)(2,1)S(1)}, u32[]{:S(2)}, u32[]{:S(2)}) collective-permute-start(bf16[256,512]{1,0:T(8,128)(2,1)S(1)} %collective-permute-done.refs_0_.refs_4_.refs_5_.refs_7_), channel_id=1, source_target_pairs={{0,1},{1,3},{3,2},{2,0},{4,5},{5,7},{7,6},{6,4},{8,9},{9,11},{11,1... | collective-permute-start | bytes 786440 | tf_op jit(solution)/shard_map/ppermute | solution.py:46
  26.9 9.5 %collective-permute-start.6 = (bf16[2,4096]{1,0:T(2,128)(2,1)S(1)}, bf16[2,4096]{1,0:T(2,128)(2,1)S(1)}, u32[]{:S(2)}, u32[]{:S(2)}) collective-permute-start(bf16[2,4096]{1,0:T(2,128)(2,1)S(1)} %get-tuple-element.34), channel_id=1, source_target_pairs={{0,12},{4,8},{8,4},{12,0},{1,13},{5,9},{9,5},{13,1},{2,14},{6,10},... | collective-permute-start | bytes 49160 | tf_op jit(solution)/shard_map/ppermute | solution.py:496
  28.1 8.4 %collective-permute-start.7 = (bf16[2,4096]{1,0:T(2,128)(2,1)S(1)}, bf16[2,4096]{1,0:T(2,128)(2,1)S(1)}, u32[]{:S(2)}, u32[]{:S(2)}) collective-permute-start(bf16[2,4096]{1,0:T(2,128)(2,1)S(1)} %get-tuple-element.37), channel_id=1, source_target_pairs={{0,8},{4,12},{8,0},{12,4},{1,9},{5,13},{9,1},{13,5},{2,10},{6,14},... | collective-permute-start | bytes 49160 | tf_op jit(solution)/shard_map/ppermute | solution.py:496
  28.6 7.8 %collective-permute-start.8 = (bf16[2,4096]{1,0:T(2,128)(2,1)S(1)}, bf16[2,4096]{1,0:T(2,128)(2,1)S(1)}, u32[]{:S(2)}, u32[]{:S(2)}) collective-permute-start(bf16[2,4096]{1,0:T(2,128)(2,1)S(1)} %get-tuple-element.36), channel_id=1, source_target_pairs={{0,4},{4,0},{8,12},{12,8},{1,5},{5,1},{9,13},{13,9},{2,6},{6,2},{1... | collective-permute-start | bytes 49160 | tf_op jit(solution)/shard_map/ppermute | solution.py:496

commit v13 on v12

--- a/solution.py
+++ b/solution.py
@@ -208,13 +208,13 @@
 
 def first_kernel(plan, pd_size, facts_ref, maxima_ref, q_ref, *refs):
     width = plan.size
-    kv_refs, refs = refs[: width - 1], refs[width - 1 :]
+    kv_refs, refs = refs[: width - 2], refs[width - 2 :]
     block_refs, refs = refs[:pd_size], refs[pd_size:]
     acc_ref, bias_ref, dec_acc_ref, dec_bias_ref, worst_ref, queries_ref, fresh_ref, pick_ref, owner_ref = refs
     tokens = q_ref.shape[0]
     half = tokens // 2
     facts = Facts(facts_ref, width)
-    sources = facts.source[:-1]
+    sources = facts.source[:-2]
     pick_ref[...] = pick_matrix(facts)
     slot = iota((8, HEAD_SIZE), 0)
     owner = jnp.zeros_like(slot)
@@ -276,6 +276,32 @@
     each_kv_head(width, step)
 
 
+def middle_kernel(plan, acc_ref, bias_ref, dec_acc_ref, dec_bias_ref, worst_ref, queries_ref, q_ref, kv_ref, *refs):
+    new_acc_ref, new_dec_acc_ref, new_worst_ref = refs
+    piece = plan.size - 2
+    tokens = q_ref.shape[0]
+    half = tokens // 2
+    worst = worst_ref[...]
+    for h in range(KEY_VALUE_HEADS):
+        columns = slice(h * HEAD_SIZE, (h + 1) * HEAD_SIZE)
+        keys, values = kv_ref[:tokens, columns], with_ones(kv_ref[tokens:, columns])
+        queries = stacked_heads(queries_ref, slice(None), h * Q_BLOCK, HEADS_PER_KV)
+        exponents = scores_of(queries, keys) * EXPONENT + dec_bias_ref[piece]
+        worst = jnp.maximum(worst, peak(exponents))
+        new_dec_acc_ref[h] = dec_acc_ref[h] + product(jnp.exp2(exponents).astype(jnp.bfloat16), values)
+        for start in (0, half):
+            bias = bias_ref[piece, start : start + half, :]
+            queries = stacked_heads(q_ref, slice(start, start + half), h * Q_BLOCK, HEADS_PER_KV)
+            scores = scores_of(queries, keys).reshape(HEADS_PER_KV, half, tokens)
+            exponents = (scores * EXPONENT + bias[None]).reshape(HEADS_PER_KV * half, tokens)
+            worst = jnp.maximum(worst, peak(exponents))
+            rows = slice(start * HEADS_PER_KV, (start + half) * HEADS_PER_KV)
+            new_acc_ref[h, rows, :] = acc_ref[h, rows, :] + product(
+                jnp.exp2(exponents).astype(jnp.bfloat16), values
+            )
+    new_worst_ref[...] = worst
+
+
 def divided(acc):
     return (acc[:, :HEAD_SIZE] * pl.reciprocal(acc[:, HEAD_SIZE:], approx=True)).astype(jnp.bfloat16)
 
@@ -424,7 +450,7 @@
     tokens, width = query.shape[0], plan.size
     rows = HEADS_PER_KV * tokens
     f32, bf16 = jnp.float32, jnp.bfloat16
-    every = (width - 1) * tokens
+    every = (width - 2) * tokens
     shapes = [
         jax.ShapeDtypeStruct((KEY_VALUE_HEADS, rows, 2 * HEAD_SIZE), f32),
         jax.ShapeDtypeStruct((width, tokens, tokens), f32),
@@ -438,13 +464,29 @@
     ]
     return pl.pallas_call(
         lambda *refs: first_kernel(plan, len(blocks), *refs),
-        in_specs=[SMEM] + [VMEM] * (2 + len(blocks) + width - 1),
+        in_specs=[SMEM] + [VMEM] * (len(blocks) + width),
         out_specs=[VMEM] * len(shapes),
         out_shape=shapes,
         compiler_params=pltpu.CompilerParams(vmem_limit_bytes=(28 + width) * MIB),
         cost_estimate=cost(tokens, every, tokens * every * QUERY_HEADS),
         name="first_shards",
     )(facts, maxima, query, *pieces, *blocks)
+
+
+def call_middle(plan, state, query, piece):
+    acc, bias, dec_acc, dec_bias, worst, queries = state[:6]
+    tokens = query.shape[0]
+    new_acc, new_dec_acc, new_worst = pl.pallas_call(
+        lambda *refs: middle_kernel(plan, *refs),
+        in_specs=[VMEM] * 8,
+        out_specs=[VMEM] * 3,
+        out_shape=[jax.ShapeDtypeStruct(a.shape, a.dtype) for a in (acc, dec_acc, worst)],
+        input_output_aliases={0: 0, 2: 1, 4: 2},
+        compiler_params=pltpu.CompilerParams(vmem_limit_bytes=32 * MIB),
+        cost_estimate=cost(tokens, tokens, tokens * tokens * QUERY_HEADS),
+        name="middle_shard",
+    )(acc, bias, dec_acc, dec_bias, worst, queries, query, piece)
+    return [new_acc, bias, new_dec_acc, dec_bias, new_worst] + list(state[5:])
 
 
 def call_decode(plan, state, pieces):
@@ -515,7 +557,7 @@
     kv, decoded_query = lax.optimization_barrier(
         (jnp.concatenate([prompt_key, prompt_value], axis=0), decoded_query)
     )
-    later_kv, own = lax.optimization_barrier((kv, own))
+    later_kv, own, facts = lax.optimization_barrier((kv, own, facts))
     pieces, maxima, up, down = [kv], None, kv, later_kv
     for d in range(1, plan.size // 2 + 1):
         if d == 2:
@@ -527,7 +569,8 @@
     blocks = [own] + [paired(own, k) for k in range(1, pd_size)]
     maxima = start_maxima(pieces[1])
 
-    state = call_first(plan, facts, maxima, prompt_query, blocks, pieces[:-1])
+    state = call_first(plan, facts, maxima, prompt_query, blocks, pieces[:-2])
+    state = call_middle(plan, state, prompt_query, pieces[-2])
     outgoing = call_decode(plan, state, pieces)
     arrived = [outgoing[:DECODE_STEPS]]
     for k in range(1, pd_size):

time: 37.6 us -> 38.8 us (1.032)
  Pallas kernels: 14.6 us -> 16.2 us
    pallas_call x0 -> x1, Pallas kernels: none -> 2.22 us  [call_middle(): pl.pallas_call(lambda *refs: middle_kernel(plan, *refs), in_specs=[VMEM]...]
    pallas_call x1, Pallas kernels: 3.61 us -> 2.92 us  [call_first(): pl.pallas_call(lambda *refs: first_kernel(plan, len(blocks), *refs), in_s...]
  transfers between devices with their start and end apart: 9 -> 9, of which waited for: 2 -> 2; matrix products, arithmetic and copies ran while one was open for 3% -> 3% of each run, Pallas kernels for 34% -> 36%
where the time goes in v13:
time: 38.8 us; the launch traced here: 38.6 us
  Pallas kernels  16.2 us (42%)
  starting transfers between devices  15.3 us (39%)
  waiting for transfers between devices  3.39 us (9%)
  other arithmetic  2.88 us (7%)
  between operations  0.77 us (2%)
    ppermute x3, starting transfers between devices, step(): lax.ppermute(array, 'tp', self.pairs if up else [(b, a) for a, b in self....  11.4 us
    pallas_call x1, Pallas kernels, call_prefill(): pl.pallas_call(lambda *refs: prefill_kernel(plan, *refs), in_specs=[VMEM]...  7.58 us
    ppermute x6, starting transfers between devices, paired(): lax.ppermute(array, 'pd', [(g, g ^ k) for g in range(lax.axis_size('pd'))])  3.86 us
    ppermute x3, waiting for transfers between devices, step(): lax.ppermute(array, 'tp', self.pairs if up else [(b, a) for a, b in self....  3.37 us
    pallas_call x1, Pallas kernels, call_first(): pl.pallas_call(lambda *refs: first_kernel(plan, len(blocks), *refs), in_s...  2.92 us
    pallas_call x1, Pallas kernels, call_middle(): pl.pallas_call(lambda *refs: middle_kernel(plan, *refs), in_specs=[VMEM]...  2.22 us
    pallas_call x1, Pallas kernels, call_decode(): pl.pallas_call(lambda *refs: decode_kernel(plan, *refs), in_specs=[VMEM]...  2.13 us
    pallas_call x1, Pallas kernels, facts_row(): pl.pallas_call(kernel, in_specs=[SMEM, SMEM], out_specs=SMEM, out_shape=j...  1.3 us
  transfers between devices with their start and end apart: 9, of which 2 were waited for; matrix products, arithmetic and copies ran while one was open for 3% of the time, Pallas kernels for 36%

profile of v13, /device:TPU:0, one launch (start us, length us, event | category | flops | bytes accessed | tf_op | source)
XLA Modules:
  0.0 38.6 jit_solution(17624892691963435939)
XLA Ops:
  0.6 1.0 %pad_maximum_fusion.refs_3_.refs_4_.refs_6_ = bf16[256,512]{1,0:T(8,128)(2,1)S(1)} fusion(bf16[128,512]{1,0:T(8,128)(2,1)} %param.10, bf16[128,512]{1,0:T(8,128)(2,1)} %param.9), kind=kLoop, calls=%fused_computation | loop fusion | flops 524288 | bytes 524288 | tf_op jit(solution)/shard_map/concatenate | solution.py:558
  1.6 3.1 %collective-permute-start = (bf16[256,512]{1,0:T(8,128)(2,1)S(1)}, bf16[256,512]{1,0:T(8,128)(2,1)S(1)}, u32[]{:S(2)}, u32[]{:S(2)}) collective-permute-start(bf16[256,512]{1,0:T(8,128)(2,1)S(1)} %pad_maximum_fusion.refs_3_.refs_4_.refs_6_), channel_id=1, source_target_pairs={{0,1},{1,3},{3,2},{2,0},{4,5},{5,7},{7,6},{6,4},{8,9},{9,11},{11,1... | collective-permute-start | bytes 786440 | tf_op jit(solution)/shard_map/ppermute | solution.py:46
  4.7 0.9 %pad_maximum_fusion.1 = bf16[4,2,5120]{2,1,0:T(2,128)(2,1)S(1)} fusion(bf16[4,2,512]{2,1,0:T(2,128)(2,1)} %param.15, bf16[4,2,512]{2,1,0:T(2,128)(2,1)} %param.14, bf16[4,2,4096]{2,1,0:T(2,128)(2,1)} %param.13), kind=kLoop, calls=%fused_computation.5 | loop fusion | flops 245760 | bytes 163840 | tf_op jit(solution)/shard_map/concatenate | solution.py:553
  5.7 1.3 %facts.1.refs_0_ = s32[18]{0:T(128)} custom-call(s32[4,4]{1,0:T(4,128)} %lengths_ref.1, s32[16]{0:T(128)} %slots_ref.1), custom_call_target="tpu_custom_call" | custom-call | flops 5000000000 | tf_op jit(solution)/shard_map/facts/pallas_call | solution.py:126
  7.0 0.0 copy-start
  7.0 0.0 copy-start.1
  7.0 0.1 collective-permute-start.1
  7.1 1.6 %collective-permute-start.2 = (bf16[8,5120]{1,0:T(8,128)(2,1)S(1)}, bf16[8,5120]{1,0:T(8,128)(2,1)S(1)}, u32[]{:S(2)}, u32[]{:S(2)}) collective-permute-start(bf16[8,5120]{1,0:T(8,128)(2,1)S(1)} %reshape.39.refs_5_), channel_id=1, source_target_pairs={{0,8},{4,12},{8,0},{12,4},{1,9},{5,13},{9,1},{13,5},{2,10},{6,14},... | collective-permute-start | bytes 245768 | tf_op jit(solution)/shard_map/ppermute | solution.py:538
  8.7 0.3 collective-permute-start.3
  9.0 1.1 %collective-permute-start.4 = (bf16[256,512]{1,0:T(8,128)(2,1)S(1)}, bf16[256,512]{1,0:T(8,128)(2,1)S(1)}, u32[]{:S(2)}, u32[]{:S(2)}) collective-permute-start(bf16[256,512]{1,0:T(8,128)(2,1)S(1)} %pad_maximum_fusion.refs_3_.refs_4_.refs_6_), channel_id=1, source_target_pairs={{1,0},{3,1},{2,3},{0,2},{5,4},{7,5},{6,7},{4,6},{9,8},{11,9},{10,1... | collective-permute-start | bytes 786440 | tf_op jit(solution)/shard_map/ppermute | solution.py:46
  10.1 1.9 %collective-permute-done.refs_0_.refs_4_.refs_5_.refs_7_ = bf16[256,512]{1,0:T(8,128)(2,1)S(1)} collective-permute-done((bf16[256,512]{1,0:T(8,128)(2,1)S(1)}, bf16[256,512]{1,0:T(8,128)(2,1)S(1)}, u32[]{:S(2)}, u32[]{:S(2)}) %collective-permute-start) | collective-permute-done | bytes 262176 | tf_op jit(solution)/shard_map/ppermute | solution.py:46
  12.0 7.2 %collective-permute-start.5 = (bf16[256,512]{1,0:T(8,128)(2,1)S(1)}, bf16[256,512]{1,0:T(8,128)(2,1)S(1)}, u32[]{:S(2)}, u32[]{:S(2)}) collective-permute-start(bf16[256,512]{1,0:T(8,128)(2,1)S(1)} %collective-permute-done.refs_0_.refs_4_.refs_5_.refs_7_), channel_id=1, source_target_pairs={{0,1},{1,3},{3,2},{2,0},{4,5},{5,7},{7,6},{6,4},{8,9},{9,11},{11,1... | collective-permute-start | bytes 786440 | tf_op jit(solution)/shard_map/ppermute | solution.py:46
  19.2 0.0 collective-permute-done.1.refs_6_
  19.2 0.0 collective-permute-done.2.refs_7_
  19.3 0.0 collective-permute-done.3.refs_8_
  19.3 0.0 copy-done
  19.3 0.0 copy-done.1
  19.3 2.9 %first_shards.1 = (f32[4,1024,256]{2,1,0:T(8,128)S(1)}, f32[4,128,128]{2,1,0:T(8,128)S(1)}, f32[4,128,256]{2,1,0:T(8,128)S(1)}, f32[4,128,128]{2,1,0:T(8,128)S(1...) custom-call(s32[18]{0:T(128)S(1)} %copy-done.1, ...), custom_call_target="tpu_custom_call" | custom-call | flops 4294967296 | bytes 2097152 | tf_op jit(solution)/shard_map/first_shards/pallas_call | solution.py:465
  22.2 0.1 compare_reduce_fusion.2
  22.4 0.0 collective-permute-done.4.refs_7_.refs_6_.refs_8_
  22.4 2.2 %middle_shard.1 = (f32[4,1024,256]{2,1,0:T(8,128)S(1)}, f32[4,128,256]{2,1,0:T(8,128)S(1)}, f32[8,128]{1,0:T(8,128)S(1)}) custom-call(f32[4,1024,256]{2,1,0:T(8,128)S(1)} %get-tuple-element.24.refs_0_, f32[4,128,128]{2,1,0:T(8,128)S(1)} %get-tuple-element.25.refs_1_, ...), custom_call_target="tpu_custom_call", output_to_operand_aliasing={{0}: (0, {}), {1}: (2, {}), {2}: (4, {})} | custom-call | flops 2147483648 | bytes 2097152 | tf_op jit(solution)/shard_map/middle_shard/pallas_call | solution.py:479
  24.6 1.4 %collective-permute-done.5.refs_7_.refs_9_ = bf16[256,512]{1,0:T(8,128)(2,1)S(1)} collective-permute-done((bf16[256,512]{1,0:T(8,128)(2,1)S(1)}, bf16[256,512]{1,0:T(8,128)(2,1)S(1)}, u32[]{:S(2)}, u32[]{:S(2)}) %collective-permute-start.5) | collective-permute-done | bytes 262176 | tf_op jit(solution)/shard_map/ppermute | solution.py:46
  26.0 2.1 %last_shard_decode.1 = bf16[16,4096]{1,0:T(8,128)(2,1)S(1)} custom-call(f32[4,128,256]{2,1,0:T(8,128)S(1)} %get-tuple-element.35.refs_0_, f32[4,128,128]{2,1,0:T(8,128)S(1)} %get-tuple-element.27.refs_3_.refs_1_, f32[8,128]{1,0:T(8,128)S(1)} %get-tuple-element.32.refs_2_, bf16[16,4096]{1,0:T(8,128)(2,1)S(1)} %get-tuple-element.29.refs_5_.refs_3_, ...), custom_call_target="tpu_custom_call" | custom-call | flops 268435456 | bytes 262144 | tf_op jit(solution)/shard_map/last_shard_decode/pallas_call | solution.py:494
  28.2 0.1 fusion
  28.2 0.5 %collective-permute-start.6 = (bf16[2,4096]{1,0:T(2,128)(2,1)S(1)}, bf16[2,4096]{1,0:T(2,128)(2,1)S(1)}, u32[]{:S(2)}, u32[]{:S(2)}) collective-permute-start(bf16[2,4096]{1,0:T(2,128)(2,1)S(1)} %get-tuple-element.42), channel_id=1, source_target_pairs={{0,12},{4,8},{8,4},{12,0},{1,13},{5,9},{9,5},{13,1},{2,14},{6,10},... | collective-permute-start | bytes 49160 | tf_op jit(solution)/shard_map/ppermute | solution.py:538
  28.8 1.1 %collective-permute-start.7 = (bf16[2,4096]{1,0:T(2,128)(2,1)S(1)}, bf16[2,4096]{1,0:T(2,128)(2,1)S(1)}, u32[]{:S(2)}, u32[]{:S(2)}) collective-permute-start(bf16[2,4096]{1,0:T(2,128)(2,1)S(1)} %get-tuple-element.45), channel_id=1, source_target_pairs={{0,8},{4,12},{8,0},{12,4},{1,9},{5,13},{9,1},{13,5},{2,10},{6,14},... | collective-permute-start | bytes 49160 | tf_op jit(solution)/shard_map/ppermute | solution.py:538
  29.9 0.3 collective-permute-start.8
  30.1 7.6 %last_shard_prefill.1 = bf16[128,4096]{1,0:T(8,128)(2,1)} custom-call(f32[4,1024,256]{2,1,0:T(8,128)S(1)} %get-tuple-element.31.refs_0_, f32[4,128,128]{2,1,0:T(8,128)S(1)} %get-tuple-element.25.refs_1_, f32[8,128]{1,0:T(8,128)S(1)} %get-tuple-element.32.refs_2_, bf16[128,4096]{1,0:T(8,128)(2,1)S(1)} %copy-done, ...), custom_call_target="tpu_custom_call" | custom-call | flops 2147483648 | bytes 2097152 | tf_op jit(solution)/shard_map/last_shard_prefill/pallas_call | solution.py:507
  37.7 0.0 collective-permute-done.6
  37.7 0.0 collective-permute-done.7
  37.8 0.0 collective-permute-done.8
  37.8 0.8 %broadcast_select_fusion.2 = bf16[4,2,4096]{2,1,0:T(2,128)(2,1)} fusion(pred[4]{0:T(512)(128)(4,1)S(1)} %get-tuple-element.41, pred[4]{0:T(512)(128)(4,1)S(1)} %get-tuple-element.40, pred[4]{0:T(512)(128)(4,1)S(1)} %get-tuple-element.39, pred[4]{0:T(512)(128)(4,1)S(1)} %get-tuple-element.38, bf16[2,4096]{1,0:T(2,128)(2,1)S(1)} %get-tuple-element.43, ...), kind=kLoop, calls=%fused_computation.3 | loop fusion | flops 131072 | bytes 131088 | tf_op jit(solution)/shard_map/jit(_where)/select_n | solution.py:583
  (2 shorter events, 0.0 us)
Async XLA Ops:
  1.6 10.4 %collective-permute-start = (bf16[256,512]{1,0:T(8,128)(2,1)S(1)}, bf16[256,512]{1,0:T(8,128)(2,1)S(1)}, u32[]{:S(2)}, u32[]{:S(2)}) collective-permute-start(bf16[256,512]{1,0:T(8,128)(2,1)S(1)} %pad_maximum_fusion.refs_3_.refs_4_.refs_6_), channel_id=1, source_target_pairs={{0,1},{1,3},{3,2},{2,0},{4,5},{5,7},{7,6},{6,4},{8,9},{9,11},{11,1... | collective-permute-start | bytes 786440 | tf_op jit(solution)/shard_map/ppermute | solution.py:46
  7.0 12.3 %copy-start = (bf16[128,4096]{1,0:T(8,128)(2,1)S(1)}, bf16[128,4096]{1,0:T(8,128)(2,1)}, u32[]{:S(2)}) copy-start(bf16[128,4096]{1,0:T(8,128)(2,1)} %refs_3_.1) | copy-start | bytes 3145732
  7.0 12.3 %copy-start.1 = (s32[18]{0:T(128)S(1)}, s32[18]{0:T(128)}, u32[]{:S(2)}) copy-start(s32[18]{0:T(128)} %facts.1.refs_0_) | copy-start | bytes 220
  7.0 12.2 %collective-permute-start.1 = (bf16[8,5120]{1,0:T(8,128)(2,1)S(1)}, bf16[8,5120]{1,0:T(8,128)(2,1)S(1)}, u32[]{:S(2)}, u32[]{:S(2)}) collective-permute-start(bf16[8,5120]{1,0:T(8,128)(2,1)S(1)} %reshape.39.refs_5_), channel_id=1, source_target_pairs={{0,4},{4,0},{8,12},{12,8},{1,5},{5,1},{9,13},{13,9},{2,6},{6,2},{1... | collective-permute-start | bytes 245768 | tf_op jit(solution)/shard_map/ppermute | solution.py:538
  7.1 12.2 %collective-permute-start.2 = (bf16[8,5120]{1,0:T(8,128)(2,1)S(1)}, bf16[8,5120]{1,0:T(8,128)(2,1)S(1)}, u32[]{:S(2)}, u32[]{:S(2)}) collective-permute-start(bf16[8,5120]{1,0:T(8,128)(2,1)S(1)} %reshape.39.refs_5_), channel_id=1, source_target_pairs={{0,8},{4,12},{8,0},{12,4},{1,9},{5,13},{9,1},{13,5},{2,10},{6,14},... | collective-permute-start | bytes 245768 | tf_op jit(solution)/shard_map/ppermute | solution.py:538
  8.7 10.6 %collective-permute-start.3 = (bf16[8,5120]{1,0:T(8,128)(2,1)S(1)}, bf16[8,5120]{1,0:T(8,128)(2,1)S(1)}, u32[]{:S(2)}, u32[]{:S(2)}) collective-permute-start(bf16[8,5120]{1,0:T(8,128)(2,1)S(1)} %reshape.39.refs_5_), channel_id=1, source_target_pairs={{0,12},{4,8},{8,4},{12,0},{1,13},{5,9},{9,5},{13,1},{2,14},{6,10},... | collective-permute-start | bytes 245768 | tf_op jit(solution)/shard_map/ppermute | solution.py:538
  9.0 13.4 %collective-permute-start.4 = (bf16[256,512]{1,0:T(8,128)(2,1)S(1)}, bf16[256,512]{1,0:T(8,128)(2,1)S(1)}, u32[]{:S(2)}, u32[]{:S(2)}) collective-permute-start(bf16[256,512]{1,0:T(8,128)(2,1)S(1)} %pad_maximum_fusion.refs_3_.refs_4_.refs_6_), channel_id=1, source_target_pairs={{1,0},{3,1},{2,3},{0,2},{5,4},{7,5},{6,7},{4,6},{9,8},{11,9},{10,1... | collective-permute-start | bytes 786440 | tf_op jit(solution)/shard_map/ppermute | solution.py:46
  12.0 14.0 %collective-permute-start.5 = (bf16[256,512]{1,0:T(8,128)(2,1)S(1)}, bf16[256,512]{1,0:T(8,128)(2,1)S(1)}, u32[]{:S(2)}, u32[]{:S(2)}) collective-permute-start(bf16[256,512]{1,0:T(8,128)(2,1)S(1)} %collective-permute-done.refs_0_.refs_4_.refs_5_.refs_7_), channel_id=1, source_target_pairs={{0,1},{1,3},{3,2},{2,0},{4,5},{5,7},{7,6},{6,4},{8,9},{9,11},{11,1... | collective-permute-start | bytes 786440 | tf_op jit(solution)/shard_map/ppermute | solution.py:46
  28.2 9.5 %collective-permute-start.6 = (bf16[2,4096]{1,0:T(2,128)(2,1)S(1)}, bf16[2,4096]{1,0:T(2,128)(2,1)S(1)}, u32[]{:S(2)}, u32[]{:S(2)}) collective-permute-start(bf16[2,4096]{1,0:T(2,128)(2,1)S(1)} %get-tuple-element.42), channel_id=1, source_target_pairs={{0,12},{4,8},{8,4},{12,0},{1,13},{5,9},{9,5},{13,1},{2,14},{6,10},... | collective-permute-start | bytes 49160 | tf_op jit(solution)/shard_map/ppermute | solution.py:538
  28.8 9.0 %collective-permute-start.7 = (bf16[2,4096]{1,0:T(2,128)(2,1)S(1)}, bf16[2,4096]{1,0:T(2,128)(2,1)S(1)}, u32[]{:S(2)}, u32[]{:S(2)}) collective-permute-start(bf16[2,4096]{1,0:T(2,128)(2,1)S(1)} %get-tuple-element.45), channel_id=1, source_target_pairs={{0,8},{4,12},{8,0},{12,4},{1,9},{5,13},{9,1},{13,5},{2,10},{6,14},... | collective-permute-start | bytes 49160 | tf_op jit(solution)/shard_map/ppermute | solution.py:538
  29.9 7.9 %collective-permute-start.8 = (bf16[2,4096]{1,0:T(2,128)(2,1)S(1)}, bf16[2,4096]{1,0:T(2,128)(2,1)S(1)}, u32[]{:S(2)}, u32[]{:S(2)}) collective-permute-start(bf16[2,4096]{1,0:T(2,128)(2,1)S(1)} %get-tuple-element.44), channel_id=1, source_target_pairs={{0,4},{4,0},{8,12},{12,8},{1,5},{5,1},{9,13},{13,9},{2,6},{6,2},{1... | collective-permute-start | bytes 49160 | tf_op jit(solution)/shard_map/ppermute | solution.py:538

commit v14 on v11

--- a/solution.py
+++ b/solution.py
@@ -37,9 +37,13 @@
         self.size = size
         order = [0] + list(range(1, size, 2)) + [i for i in range(size - 1, 0, -1) if i % 2 == 0]
         self.pairs = [(order[i], order[(i + 1) % size]) for i in range(size)]
-
-    def step(self, array):
-        return lax.ppermute(array, "tp", self.pairs)
+        self.offsets = [0]
+        for d in range(1, size // 2 + 1):
+            self.offsets += [-d, d]
+        self.offsets = self.offsets[:size]
+
+    def step(self, array, up):
+        return lax.ppermute(array, "tp", self.pairs if up else [(b, a) for a, b in self.pairs])
 
 
 def scores_of(queries, keys):
@@ -105,8 +109,8 @@
         values += [slots_ref[group * GROUP_REQUESTS + r] for r in range(GROUP_REQUESTS)]
         values += [lengths_ref[group, r] for r in range(GROUP_REQUESTS)]
         place = jnp.where(member % 2 == 1, (member + 1) // 2, width - member // 2)
-        for s in range(width):
-            before = (place + width - s) % width
+        for offset in plan.offsets:
+            before = (place + width + offset) % width
             up = 2 * before - 1
             values.append(jnp.where(before == 0, 0, jnp.where(before <= width // 2, up, 2 * (width - before))))
         for i, value in enumerate(values):
@@ -204,13 +208,13 @@
 
 def first_kernel(plan, pd_size, facts_ref, maxima_ref, q_ref, *refs):
     width = plan.size
-    k_refs, v_refs, refs = refs[: width - 1], refs[width - 1 : 2 * width - 2], refs[2 * width - 2 :]
+    k_refs, v_refs, refs = refs[: width - 2], refs[width - 2 : 2 * width - 4], refs[2 * width - 4 :]
     block_refs, refs = refs[:pd_size], refs[pd_size:]
     acc_ref, bias_ref, dec_acc_ref, dec_bias_ref, worst_ref, queries_ref, fresh_ref, pick_ref, owner_ref = refs
     tokens = q_ref.shape[0]
     half = tokens // 2
     facts = Facts(facts_ref, width)
-    sources = facts.source[:-1]
+    sources = facts.source[:-2]
     pick_ref[...] = pick_matrix(facts)
     slot = iota((8, HEAD_SIZE), 0)
     owner = jnp.zeros_like(slot)
@@ -270,6 +274,32 @@
     each_kv_head(width, step)
 
 
+def middle_kernel(plan, acc_ref, bias_ref, dec_acc_ref, dec_bias_ref, worst_ref, queries_ref, q_ref, k_ref, v_ref, *refs):
+    new_acc_ref, new_dec_acc_ref, new_worst_ref = refs
+    piece = plan.size - 2
+    tokens = q_ref.shape[0]
+    half = tokens // 2
+    worst = worst_ref[...]
+    for h in range(KEY_VALUE_HEADS):
+        columns = slice(h * HEAD_SIZE, (h + 1) * HEAD_SIZE)
+        keys, values = k_ref[:, columns], with_ones(v_ref[:, columns])
+        queries = stacked_heads(queries_ref, slice(None), h * Q_BLOCK, HEADS_PER_KV)
+        exponents = scores_of(queries, keys) * EXPONENT + dec_bias_ref[piece]
+        worst = jnp.maximum(worst, peak(exponents))
+        new_dec_acc_ref[h] = dec_acc_ref[h] + product(jnp.exp2(exponents).astype(jnp.bfloat16), values)
+        for start in (0, half):
+            bias = bias_ref[piece, start : start + half, :]
+            queries = stacked_heads(q_ref, slice(start, start + half), h * Q_BLOCK, HEADS_PER_KV)
+            scores = scores_of(queries, keys).reshape(HEADS_PER_KV, half, tokens)
+            exponents = (scores * EXPONENT + bias[None]).reshape(HEADS_PER_KV * half, tokens)
+            worst = jnp.maximum(worst, peak(exponents))
+            rows = slice(start * HEADS_PER_KV, (start + half) * HEADS_PER_KV)
+            new_acc_ref[h, rows, :] = acc_ref[h, rows, :] + product(
+                jnp.exp2(exponents).astype(jnp.bfloat16), values
+            )
+    new_worst_ref[...] = worst
+
+
 def divided(acc):
     return (acc[:, :HEAD_SIZE] * pl.reciprocal(acc[:, HEAD_SIZE:], approx=True)).astype(jnp.bfloat16)
 
@@ -417,7 +447,7 @@
     tokens, width = query.shape[0], plan.size
     rows = HEADS_PER_KV * tokens
     f32, bf16 = jnp.float32, jnp.bfloat16
-    every = (width - 1) * tokens
+    every = (width - 2) * tokens
     shapes = [
         jax.ShapeDtypeStruct((KEY_VALUE_HEADS, rows, 2 * HEAD_SIZE), f32),
         jax.ShapeDtypeStruct((width, tokens, tokens), f32),
@@ -431,13 +461,29 @@
     ]
     return pl.pallas_call(
         lambda *refs: first_kernel(plan, len(blocks), *refs),
-        in_specs=[SMEM] + [VMEM] * (2 + len(blocks) + 2 * (width - 1)),
+        in_specs=[SMEM] + [VMEM] * (2 + len(blocks) + 2 * (width - 2)),
         out_specs=[VMEM] * len(shapes),
         out_shape=shapes,
         compiler_params=pltpu.CompilerParams(vmem_limit_bytes=(28 + width) * MIB),
         cost_estimate=cost(tokens, every, tokens * every * QUERY_HEADS),
         name="first_shards",
     )(facts, maxima, query, *keys, *values, *blocks)
+
+
+def call_middle(plan, state, query, key, value):
+    acc, bias, dec_acc, dec_bias, worst, queries = state[:6]
+    tokens = query.shape[0]
+    new_acc, new_dec_acc, new_worst = pl.pallas_call(
+        lambda *refs: middle_kernel(plan, *refs),
+        in_specs=[VMEM] * 9,
+        out_specs=[VMEM] * 3,
+        out_shape=[jax.ShapeDtypeStruct(a.shape, a.dtype) for a in (acc, dec_acc, worst)],
+        input_output_aliases={0: 0, 2: 1, 4: 2},
+        compiler_params=pltpu.CompilerParams(vmem_limit_bytes=32 * MIB),
+        cost_estimate=cost(tokens, tokens, tokens * tokens * QUERY_HEADS),
+        name="middle_shard",
+    )(acc, bias, dec_acc, dec_bias, worst, queries, query, key, value)
+    return [new_acc, bias, new_dec_acc, dec_bias, new_worst] + list(state[5:])
 
 
 def call_decode(plan, state, keys, values):
@@ -506,20 +552,21 @@
     )
     facts = facts_row(plan, prompt_lengths, decode_slot)
     prompt_key, decoded_query = lax.optimization_barrier((prompt_key, decoded_query))
-    prompt_value, own = lax.optimization_barrier((prompt_value, own))
-    keys, values, maxima = [prompt_key], [prompt_value], None
-    for s in range(1, plan.size):
-        if s == 2:
-            keys[1], own, facts = lax.optimization_barrier((keys[1], own, facts))
-        if s == plan.size - 1:
-            maxima = start_maxima(keys[-1])
-            keys[-1], maxima = lax.optimization_barrier((keys[-1], maxima))
-        keys.append(plan.step(keys[-1]))
-        values.append(plan.step(values[-1]))
-        if s == 2:
-            blocks = [own] + [paired(own, k) for k in range(1, pd_size)]
-
-    state = call_first(plan, facts, maxima, prompt_query, blocks, keys[:-1], values[:-1])
+    later_key, later_value, own, facts = lax.optimization_barrier((prompt_key, prompt_value, own, facts))
+    chains = []
+    for up, down in ((prompt_key, later_key), (prompt_value, later_value)):
+        pieces = [up]
+        for d in range(1, plan.size // 2 + 1):
+            up = plan.step(up, True)
+            down = plan.step(down, False) if 2 * d < plan.size else None
+            pieces += [up, down]
+        chains.append(pieces[: plan.size])
+    keys, values = chains
+    blocks = [own] + [paired(own, k) for k in range(1, pd_size)]
+    maxima = start_maxima(keys[1], values[1])
+
+    state = call_first(plan, facts, maxima, prompt_query, blocks, keys[:-2], values[:-2])
+    state = call_middle(plan, state, prompt_query, keys[-2], values[-2])
     outgoing = call_decode(plan, state, keys, values)
     arrived = [outgoing[:DECODE_STEPS]]
     for k in range(1, pd_size):

time: 38.9 us -> 38.7 us (level)
  starting transfers between devices: 17.9 us -> 14.5 us
  Pallas kernels: 14.6 us -> 16.3 us
  waiting for transfers between devices: 3.3 us -> 4.92 us
    ppermute x6, starting transfers between devices: 13.9 us -> 10.4 us  [step(): lax.ppermute(array, 'tp', self.pairs if up else [(b, a) for a, b in self....]
    pallas_call x0 -> x1, Pallas kernels: none -> 2.22 us  [call_middle(): pl.pallas_call(lambda *refs: middle_kernel(plan, *refs), in_specs=[VMEM]...]
    ppermute x6, waiting for transfers between devices: 3.29 us -> 4.67 us  [step(): lax.ppermute(array, 'tp', self.pairs if up else [(b, a) for a, b in self....]
    pallas_call x1, Pallas kernels: 3.62 us -> 2.93 us  [call_first(): pl.pallas_call(lambda *refs: first_kernel(plan, len(blocks), *refs), in_s...]
  transfers between devices with their start and end apart: 12 -> 12, of which waited for: 2 -> 4; matrix products, arithmetic and copies ran while one was open for 3% -> 3% of each run, Pallas kernels for 32% -> 37%
where the time goes in v14:
time: 38.7 us; the launch traced here: 38.5 us
  Pallas kernels  16.3 us (42%)
  starting transfers between devices  14.5 us (37%)
  waiting for transfers between devices  4.92 us (13%)
  other arithmetic  1.89 us (5%)
  between operations  0.77 us (2%)
    ppermute x6, starting transfers between devices, step(): lax.ppermute(array, 'tp', self.pairs if up else [(b, a) for a, b in self....  10.4 us
    pallas_call x1, Pallas kernels, call_prefill(): pl.pallas_call(lambda *refs: prefill_kernel(plan, *refs), in_specs=[VMEM]...  7.58 us
    ppermute x6, waiting for transfers between devices, step(): lax.ppermute(array, 'tp', self.pairs if up else [(b, a) for a, b in self....  4.67 us
    ppermute x6, starting transfers between devices, paired(): lax.ppermute(array, 'pd', [(g, g ^ k) for g in range(lax.axis_size('pd'))])  4.14 us
    pallas_call x1, Pallas kernels, call_first(): pl.pallas_call(lambda *refs: first_kernel(plan, len(blocks), *refs), in_s...  2.93 us
    pallas_call x1, Pallas kernels, call_middle(): pl.pallas_call(lambda *refs: middle_kernel(plan, *refs), in_specs=[VMEM]...  2.22 us
    pallas_call x1, Pallas kernels, call_decode(): pl.pallas_call(lambda *refs: decode_kernel(plan, *refs), in_specs=[VMEM]...  2.13 us
    pallas_call x1, Pallas kernels, facts_row(): pl.pallas_call(kernel, in_specs=[SMEM, SMEM], out_specs=SMEM, out_shape=j...  1.43 us
  transfers between devices with their start and end apart: 12, of which 4 were waited for; matrix products, arithmetic and copies ran while one was open for 3% of the time, Pallas kernels for 37%

profile of v14, /device:TPU:0, one launch (start us, length us, event | category | flops | bytes accessed | tf_op | source)
XLA Modules:
  0.0 38.5 jit_solution(10730109453150031172)
XLA Ops:
  0.6 3.1 %collective-permute-start = (bf16[128,512]{1,0:T(8,128)(2,1)}, bf16[128,512]{1,0:T(8,128)(2,1)S(1)}, u32[]{:S(2)}, u32[]{:S(2)}) collective-permute-start(bf16[128,512]{1,0:T(8,128)(2,1)} %refs_6_.2), channel_id=1, source_target_pairs={{0,1},{1,3},{3,2},{2,0},{4,5},{5,7},{7,6},{6,4},{8,9},{9,11},{11,1... | collective-permute-start | bytes 393224 | tf_op jit(solution)/shard_map/ppermute | solution.py:46
  3.7 2.6 %collective-permute-start.1 = (bf16[128,512]{1,0:T(8,128)(2,1)}, bf16[128,512]{1,0:T(8,128)(2,1)S(1)}, u32[]{:S(2)}, u32[]{:S(2)}) collective-permute-start(bf16[128,512]{1,0:T(8,128)(2,1)} %refs_10_.1), channel_id=1, source_target_pairs={{0,1},{1,3},{3,2},{2,0},{4,5},{5,7},{7,6},{6,4},{8,9},{9,11},{11,1... | collective-permute-start | bytes 393224 | tf_op jit(solution)/shard_map/ppermute | solution.py:46
  6.3 0.9 %pad_maximum_fusion = bf16[4,2,5120]{2,1,0:T(2,128)(2,1)S(1)} fusion(bf16[4,2,512]{2,1,0:T(2,128)(2,1)} %param.15, bf16[4,2,512]{2,1,0:T(2,128)(2,1)} %param.14, bf16[4,2,4096]{2,1,0:T(2,128)(2,1)} %param.13), kind=kLoop, calls=%fused_computation.4 | loop fusion | flops 245760 | bytes 163840 | tf_op jit(solution)/shard_map/concatenate | solution.py:550
  7.2 0.0 copy-start
  7.3 0.0 copy-start.1
  7.3 1.4 %facts.1.refs_0_ = s32[18]{0:T(128)} custom-call(s32[4,4]{1,0:T(4,128)} %lengths_ref.1, s32[16]{0:T(128)} %slots_ref.1), custom_call_target="tpu_custom_call" | custom-call | flops 5000000000 | tf_op jit(solution)/shard_map/facts/pallas_call | solution.py:126
  8.8 0.0 copy-start.2
  8.8 0.0 copy-start.3
  8.8 0.1 collective-permute-start.2
  8.9 1.6 %collective-permute-start.3 = (bf16[8,5120]{1,0:T(8,128)(2,1)S(1)}, bf16[8,5120]{1,0:T(8,128)(2,1)S(1)}, u32[]{:S(2)}, u32[]{:S(2)}) collective-permute-start(bf16[8,5120]{1,0:T(8,128)(2,1)S(1)} %reshape.39.refs_7_), channel_id=1, source_target_pairs={{0,8},{4,12},{8,0},{12,4},{1,9},{5,13},{9,1},{13,5},{2,10},{6,14},... | collective-permute-start | bytes 245768 | tf_op jit(solution)/shard_map/ppermute | solution.py:535
  10.4 0.3 collective-permute-start.4
  10.7 0.0 collective-permute-done.refs_0_.refs_4_.refs_5_.refs_7_
  10.7 0.0 copy-done
  10.7 0.6 %collective-permute-start.5 = (bf16[128,512]{1,0:T(8,128)(2,1)S(1)}, bf16[128,512]{1,0:T(8,128)(2,1)S(1)}, u32[]{:S(2)}, u32[]{:S(2)}) collective-permute-start(bf16[128,512]{1,0:T(8,128)(2,1)S(1)} %copy-done), channel_id=1, source_target_pairs={{1,0},{3,1},{2,3},{0,2},{5,4},{7,5},{6,7},{4,6},{9,8},{11,9},{10,1... | collective-permute-start | bytes 393224 | tf_op jit(solution)/shard_map/ppermute | solution.py:46
  11.3 0.0 collective-permute-done.1.refs_1_.refs_6_.refs_9_.refs_11_
  11.3 0.0 copy-done.1
  11.3 2.5 %collective-permute-start.6 = (bf16[128,512]{1,0:T(8,128)(2,1)S(1)}, bf16[128,512]{1,0:T(8,128)(2,1)S(1)}, u32[]{:S(2)}, u32[]{:S(2)}) collective-permute-start(bf16[128,512]{1,0:T(8,128)(2,1)S(1)} %copy-done.1), channel_id=1, source_target_pairs={{1,0},{3,1},{2,3},{0,2},{5,4},{7,5},{6,7},{4,6},{9,8},{11,9},{10,1... | collective-permute-start | bytes 393224 | tf_op jit(solution)/shard_map/ppermute | solution.py:46
  13.8 0.0 collective-permute-done.2.refs_8_
  13.8 0.0 collective-permute-start.7
  13.8 0.2 collective-permute-done.3.refs_9_
  14.0 1.6 %collective-permute-start.8 = (bf16[128,512]{1,0:T(8,128)(2,1)S(1)}, bf16[128,512]{1,0:T(8,128)(2,1)S(1)}, u32[]{:S(2)}, u32[]{:S(2)}) collective-permute-start(bf16[128,512]{1,0:T(8,128)(2,1)S(1)} %collective-permute-done.1.refs_1_.refs_6_.refs_9_.refs_11_), channel_id=1, source_target_pairs={{0,1},{1,3},{3,2},{2,0},{4,5},{5,7},{7,6},{6,4},{8,9},{9,11},{11,1... | collective-permute-start | bytes 393224 | tf_op jit(solution)/shard_map/ppermute | solution.py:46
  15.7 0.0 collective-permute-done.4.refs_10_
  15.7 0.0 copy-done.2
  15.7 0.0 copy-done.3
  15.7 2.9 %first_shards.1 = (f32[4,1024,256]{2,1,0:T(8,128)S(1)}, f32[4,128,128]{2,1,0:T(8,128)S(1)}, f32[4,128,256]{2,1,0:T(8,128)S(1)}, f32[4,128,128]{2,1,0:T(8,128)S(1...) custom-call(s32[18]{0:T(128)S(1)} %copy-done.3, ...), custom_call_target="tpu_custom_call" | custom-call | flops 4294967296 | bytes 2097152 | tf_op jit(solution)/shard_map/first_shards/pallas_call | solution.py:462
  18.6 0.0 collective-permute-done.5.refs_7_.refs_6_.refs_8_
  18.6 0.7 %collective-permute-done.6.refs_8_.refs_10_.refs_12_ = bf16[128,512]{1,0:T(8,128)(2,1)S(1)} collective-permute-done((bf16[128,512]{1,0:T(8,128)(2,1)S(1)}, bf16[128,512]{1,0:T(8,128)(2,1)S(1)}, u32[]{:S(2)}, u32[]{:S(2)}) %collective-permute-start.6) | collective-permute-done | bytes 131104 | tf_op jit(solution)/shard_map/ppermute | solution.py:46
  19.4 2.2 %middle_shard.1 = (f32[4,1024,256]{2,1,0:T(8,128)S(1)}, f32[4,128,256]{2,1,0:T(8,128)S(1)}, f32[8,128]{1,0:T(8,128)S(1)}) custom-call(f32[4,1024,256]{2,1,0:T(8,128)S(1)} %get-tuple-element.22.refs_0_, f32[4,128,128]{2,1,0:T(8,128)S(1)} %get-tuple-element.23.refs_1_, ...), custom_call_target="tpu_custom_call", output_to_operand_aliasing={{0}: (0, {}), {1}: (2, {}), {2}: (4, {})} | custom-call | flops 2147483648 | bytes 2097152 | tf_op jit(solution)/shard_map/middle_shard/pallas_call | solution.py:476
  21.6 0.1 compare_reduce_fusion.2
  21.8 1.2 %collective-permute-done.7.refs_7_.refs_9_ = bf16[128,512]{1,0:T(8,128)(2,1)S(1)} collective-permute-done((bf16[128,512]{1,0:T(8,128)(2,1)S(1)}, bf16[128,512]{1,0:T(8,128)(2,1)S(1)}, u32[]{:S(2)}, u32[]{:S(2)}) %collective-permute-start.7) | collective-permute-done | bytes 131104 | tf_op jit(solution)/shard_map/ppermute | solution.py:46
  23.0 2.7 %collective-permute-done.8.refs_11_.refs_13_ = bf16[128,512]{1,0:T(8,128)(2,1)S(1)} collective-permute-done((bf16[128,512]{1,0:T(8,128)(2,1)S(1)}, bf16[128,512]{1,0:T(8,128)(2,1)S(1)}, u32[]{:S(2)}, u32[]{:S(2)}) %collective-permute-start.8) | collective-permute-done | bytes 131104 | tf_op jit(solution)/shard_map/ppermute | solution.py:46
  25.7 2.1 %last_shard_decode.1 = bf16[16,4096]{1,0:T(8,128)(2,1)S(1)} custom-call(f32[4,128,256]{2,1,0:T(8,128)S(1)} %get-tuple-element.33.refs_0_, f32[4,128,128]{2,1,0:T(8,128)S(1)} %get-tuple-element.25.refs_3_.refs_1_, f32[8,128]{1,0:T(8,128)S(1)} %get-tuple-element.31.refs_2_, bf16[16,4096]{1,0:T(8,128)(2,1)S(1)} %get-tuple-element.27.refs_5_.refs_3_, ...), custom_call_target="tpu_custom_call" | custom-call | flops 268435456 | bytes 262144 | tf_op jit(solution)/shard_map/last_shard_decode/pallas_call | solution.py:491
  27.8 0.1 fusion
  27.9 1.6 %collective-permute-start.10 = (bf16[2,4096]{1,0:T(2,128)(2,1)S(1)}, bf16[2,4096]{1,0:T(2,128)(2,1)S(1)}, u32[]{:S(2)}, u32[]{:S(2)}) collective-permute-start(bf16[2,4096]{1,0:T(2,128)(2,1)S(1)} %get-tuple-element.43), channel_id=1, source_target_pairs={{0,8},{4,12},{8,0},{12,4},{1,9},{5,13},{9,1},{13,5},{2,10},{6,14},... | collective-permute-start | bytes 49160 | tf_op jit(solution)/shard_map/ppermute | solution.py:535
  29.4 0.0 collective-permute-start.11
  29.4 0.6 %collective-permute-start.9 = (bf16[2,4096]{1,0:T(2,128)(2,1)S(1)}, bf16[2,4096]{1,0:T(2,128)(2,1)S(1)}, u32[]{:S(2)}, u32[]{:S(2)}) collective-permute-start(bf16[2,4096]{1,0:T(2,128)(2,1)S(1)} %get-tuple-element.40), channel_id=1, source_target_pairs={{0,12},{4,8},{8,4},{12,0},{1,13},{5,9},{9,5},{13,1},{2,14},{6,10},... | collective-permute-start | bytes 49160 | tf_op jit(solution)/shard_map/ppermute | solution.py:535
  30.1 7.6 %last_shard_prefill.1 = bf16[128,4096]{1,0:T(8,128)(2,1)} custom-call(f32[4,1024,256]{2,1,0:T(8,128)S(1)} %get-tuple-element.30.refs_0_, f32[4,128,128]{2,1,0:T(8,128)S(1)} %get-tuple-element.23.refs_1_, f32[8,128]{1,0:T(8,128)S(1)} %get-tuple-element.31.refs_2_, bf16[128,4096]{1,0:T(8,128)(2,1)S(1)} %copy-done.2, bf16[128,512]{1,0:T(8,128)(2,1)S(1)} %copy-done, ...), custom_call_target="tpu_custom_call" | custom-call | flops 2147483648 | bytes 2097152 | tf_op jit(solution)/shard_map/last_shard_prefill/pallas_call | solution.py:504
  37.7 0.0 collective-permute-done.10
  37.7 0.0 collective-permute-done.11
  37.7 0.0 collective-permute-done.9
  37.7 0.8 %broadcast_select_fusion.2 = bf16[4,2,4096]{2,1,0:T(2,128)(2,1)} fusion(pred[4]{0:T(512)(128)(4,1)S(1)} %get-tuple-element.39, pred[4]{0:T(512)(128)(4,1)S(1)} %get-tuple-element.38, pred[4]{0:T(512)(128)(4,1)S(1)} %get-tuple-element.37, pred[4]{0:T(512)(128)(4,1)S(1)} %get-tuple-element.36, bf16[2,4096]{1,0:T(2,128)(2,1)S(1)} %get-tuple-element.41, ...), kind=kLoop, calls=%fused_computation.2 | loop fusion | flops 131072 | bytes 131088 | tf_op jit(solution)/shard_map/jit(_where)/select_n | solution.py:579
  (2 shorter events, 0.0 us)
Async XLA Ops:
  0.6 10.1 %collective-permute-start = (bf16[128,512]{1,0:T(8,128)(2,1)}, bf16[128,512]{1,0:T(8,128)(2,1)S(1)}, u32[]{:S(2)}, u32[]{:S(2)}) collective-permute-start(bf16[128,512]{1,0:T(8,128)(2,1)} %refs_6_.2), channel_id=1, source_target_pairs={{0,1},{1,3},{3,2},{2,0},{4,5},{5,7},{7,6},{6,4},{8,9},{9,11},{11,1... | collective-permute-start | bytes 393224 | tf_op jit(solution)/shard_map/ppermute | solution.py:46
  3.7 7.6 %collective-permute-start.1 = (bf16[128,512]{1,0:T(8,128)(2,1)}, bf16[128,512]{1,0:T(8,128)(2,1)S(1)}, u32[]{:S(2)}, u32[]{:S(2)}) collective-permute-start(bf16[128,512]{1,0:T(8,128)(2,1)} %refs_10_.1), channel_id=1, source_target_pairs={{0,1},{1,3},{3,2},{2,0},{4,5},{5,7},{7,6},{6,4},{8,9},{9,11},{11,1... | collective-permute-start | bytes 393224 | tf_op jit(solution)/shard_map/ppermute | solution.py:46
  7.2 3.5 %copy-start = (bf16[128,512]{1,0:T(8,128)(2,1)S(1)}, bf16[128,512]{1,0:T(8,128)(2,1)}, u32[]{:S(2)}) copy-start(bf16[128,512]{1,0:T(8,128)(2,1)} %refs_6_.2) | copy-start | bytes 393220
  7.3 4.1 %copy-start.1 = (bf16[128,512]{1,0:T(8,128)(2,1)S(1)}, bf16[128,512]{1,0:T(8,128)(2,1)}, u32[]{:S(2)}) copy-start(bf16[128,512]{1,0:T(8,128)(2,1)} %refs_10_.1) | copy-start | bytes 393220
  8.8 6.9 %copy-start.2 = (bf16[128,4096]{1,0:T(8,128)(2,1)S(1)}, bf16[128,4096]{1,0:T(8,128)(2,1)}, u32[]{:S(2)}) copy-start(bf16[128,4096]{1,0:T(8,128)(2,1)} %refs_3_.2) | copy-start | bytes 3145732
  8.8 6.9 %copy-start.3 = (s32[18]{0:T(128)S(1)}, s32[18]{0:T(128)}, u32[]{:S(2)}) copy-start(s32[18]{0:T(128)} %facts.1.refs_0_) | copy-start | bytes 220
  8.8 5.0 %collective-permute-start.2 = (bf16[8,5120]{1,0:T(8,128)(2,1)S(1)}, bf16[8,5120]{1,0:T(8,128)(2,1)S(1)}, u32[]{:S(2)}, u32[]{:S(2)}) collective-permute-start(bf16[8,5120]{1,0:T(8,128)(2,1)S(1)} %reshape.39.refs_7_), channel_id=1, source_target_pairs={{0,4},{4,0},{8,12},{12,8},{1,5},{5,1},{9,13},{13,9},{2,6},{6,2},{1... | collective-permute-start | bytes 245768 | tf_op jit(solution)/shard_map/ppermute | solution.py:535
  8.9 5.2 %collective-permute-start.3 = (bf16[8,5120]{1,0:T(8,128)(2,1)S(1)}, bf16[8,5120]{1,0:T(8,128)(2,1)S(1)}, u32[]{:S(2)}, u32[]{:S(2)}) collective-permute-start(bf16[8,5120]{1,0:T(8,128)(2,1)S(1)} %reshape.39.refs_7_), channel_id=1, source_target_pairs={{0,8},{4,12},{8,0},{12,4},{1,9},{5,13},{9,1},{13,5},{2,10},{6,14},... | collective-permute-start | bytes 245768 | tf_op jit(solution)/shard_map/ppermute | solution.py:535
  10.4 5.3 %collective-permute-start.4 = (bf16[8,5120]{1,0:T(8,128)(2,1)S(1)}, bf16[8,5120]{1,0:T(8,128)(2,1)S(1)}, u32[]{:S(2)}, u32[]{:S(2)}) collective-permute-start(bf16[8,5120]{1,0:T(8,128)(2,1)S(1)} %reshape.39.refs_7_), channel_id=1, source_target_pairs={{0,12},{4,8},{8,4},{12,0},{1,13},{5,9},{9,5},{13,1},{2,14},{6,10},... | collective-permute-start | bytes 245768 | tf_op jit(solution)/shard_map/ppermute | solution.py:535
  10.7 7.9 %collective-permute-start.5 = (bf16[128,512]{1,0:T(8,128)(2,1)S(1)}, bf16[128,512]{1,0:T(8,128)(2,1)S(1)}, u32[]{:S(2)}, u32[]{:S(2)}) collective-permute-start(bf16[128,512]{1,0:T(8,128)(2,1)S(1)} %copy-done), channel_id=1, source_target_pairs={{1,0},{3,1},{2,3},{0,2},{5,4},{7,5},{6,7},{4,6},{9,8},{11,9},{10,1... | collective-permute-start | bytes 393224 | tf_op jit(solution)/shard_map/ppermute | solution.py:46
  11.3 8.1 %collective-permute-start.6 = (bf16[128,512]{1,0:T(8,128)(2,1)S(1)}, bf16[128,512]{1,0:T(8,128)(2,1)S(1)}, u32[]{:S(2)}, u32[]{:S(2)}) collective-permute-start(bf16[128,512]{1,0:T(8,128)(2,1)S(1)} %copy-done.1), channel_id=1, source_target_pairs={{1,0},{3,1},{2,3},{0,2},{5,4},{7,5},{6,7},{4,6},{9,8},{11,9},{10,1... | collective-permute-start | bytes 393224 | tf_op jit(solution)/shard_map/ppermute | solution.py:46
  13.8 9.2 %collective-permute-start.7 = (bf16[128,512]{1,0:T(8,128)(2,1)S(1)}, bf16[128,512]{1,0:T(8,128)(2,1)S(1)}, u32[]{:S(2)}, u32[]{:S(2)}) collective-permute-start(bf16[128,512]{1,0:T(8,128)(2,1)S(1)} %collective-permute-done.refs_0_.refs_4_.refs_5_.refs_7_), channel_id=1, source_target_pairs={{0,1},{1,3},{3,2},{2,0},{4,5},{5,7},{7,6},{6,4},{8,9},{9,11},{11,1... | collective-permute-start | bytes 393224 | tf_op jit(solution)/shard_map/ppermute | solution.py:46
  14.0 11.6 %collective-permute-start.8 = (bf16[128,512]{1,0:T(8,128)(2,1)S(1)}, bf16[128,512]{1,0:T(8,128)(2,1)S(1)}, u32[]{:S(2)}, u32[]{:S(2)}) collective-permute-start(bf16[128,512]{1,0:T(8,128)(2,1)S(1)} %collective-permute-done.1.refs_1_.refs_6_.refs_9_.refs_11_), channel_id=1, source_target_pairs={{0,1},{1,3},{3,2},{2,0},{4,5},{5,7},{7,6},{6,4},{8,9},{9,11},{11,1... | collective-permute-start | bytes 393224 | tf_op jit(solution)/shard_map/ppermute | solution.py:46
  27.9 9.8 %collective-permute-start.10 = (bf16[2,4096]{1,0:T(2,128)(2,1)S(1)}, bf16[2,4096]{1,0:T(2,128)(2,1)S(1)}, u32[]{:S(2)}, u32[]{:S(2)}) collective-permute-start(bf16[2,4096]{1,0:T(2,128)(2,1)S(1)} %get-tuple-element.43), channel_id=1, source_target_pairs={{0,8},{4,12},{8,0},{12,4},{1,9},{5,13},{9,1},{13,5},{2,10},{6,14},... | collective-permute-start | bytes 49160 | tf_op jit(solution)/shard_map/ppermute | solution.py:535
  29.4 8.3 %collective-permute-start.11 = (bf16[2,4096]{1,0:T(2,128)(2,1)S(1)}, bf16[2,4096]{1,0:T(2,128)(2,1)S(1)}, u32[]{:S(2)}, u32[]{:S(2)}) collective-permute-start(bf16[2,4096]{1,0:T(2,128)(2,1)S(1)} %get-tuple-element.42), channel_id=1, source_target_pairs={{0,4},{4,0},{8,12},{12,8},{1,5},{5,1},{9,13},{13,9},{2,6},{6,2},{1... | collective-permute-start | bytes 49160 | tf_op jit(solution)/shard_map/ppermute | solution.py:535
  29.4 8.3 %collective-permute-start.9 = (bf16[2,4096]{1,0:T(2,128)(2,1)S(1)}, bf16[2,4096]{1,0:T(2,128)(2,1)S(1)}, u32[]{:S(2)}, u32[]{:S(2)}) collective-permute-start(bf16[2,4096]{1,0:T(2,128)(2,1)S(1)} %get-tuple-element.40), channel_id=1, source_target_pairs={{0,12},{4,8},{8,4},{12,0},{1,13},{5,9},{9,5},{13,1},{2,14},{6,10},... | collective-permute-start | bytes 49160 | tf_op jit(solution)/shard_map/ppermute | solution.py:535

commit v15 on v14

--- a/solution.py
+++ b/solution.py
@@ -35,7 +35,7 @@
 class Ring:
     def __init__(self, size):
         self.size = size
-        order = [0] + list(range(1, size, 2)) + [i for i in range(size - 1, 0, -1) if i % 2 == 0]
+        order = list(range(0, size, 2)) + [i for i in range(size - 1, 0, -1) if i % 2 == 1]
         self.pairs = [(order[i], order[(i + 1) % size]) for i in range(size)]
         self.offsets = [0]
         for d in range(1, size // 2 + 1):
@@ -108,11 +108,10 @@
         values = [group, member]
         values += [slots_ref[group * GROUP_REQUESTS + r] for r in range(GROUP_REQUESTS)]
         values += [lengths_ref[group, r] for r in range(GROUP_REQUESTS)]
-        place = jnp.where(member % 2 == 1, (member + 1) // 2, width - member // 2)
+        place = jnp.where(member % 2 == 0, member // 2, width - (member + 1) // 2)
         for offset in plan.offsets:
             before = (place + width + offset) % width
-            up = 2 * before - 1
-            values.append(jnp.where(before == 0, 0, jnp.where(before <= width // 2, up, 2 * (width - before))))
+            values.append(jnp.where(2 * before < width, 2 * before, 2 * (width - before) - 1))
         for i, value in enumerate(values):
             out_ref[i] = value.astype(jnp.int32)
         for q in range(requests):

time: 38.7 us -> 41.3 us (1.067)
  waiting for transfers between devices: 4.92 us -> 6.99 us
  starting transfers between devices: 14.5 us -> 15 us
    ppermute x6, waiting for transfers between devices: 4.67 us -> 6.98 us  [step(): lax.ppermute(array, 'tp', self.pairs if up else [(b, a) for a, b in self....]
    ppermute x6, starting transfers between devices: 10.4 us -> 10.8 us  [step(): lax.ppermute(array, 'tp', self.pairs if up else [(b, a) for a, b in self....]
  transfers between devices with their start and end apart: 12 -> 12, of which waited for: 4 -> 1; matrix products, arithmetic and copies ran while one was open for 3% -> 3% of each run, Pallas kernels for 37% -> 34%
where the time goes in v15:
time: 41.3 us; the launch traced here: 41.1 us
  Pallas kernels  16.3 us (39%)
  starting transfers between devices  15 us (36%)
  waiting for transfers between devices  6.99 us (17%)
  other arithmetic  1.89 us (5%)
  between operations  0.78 us (2%)
    ppermute x6, starting transfers between devices, step(): lax.ppermute(array, 'tp', self.pairs if up else [(b, a) for a, b in self....  10.8 us
    pallas_call x1, Pallas kernels, call_prefill(): pl.pallas_call(lambda *refs: prefill_kernel(plan, *refs), in_specs=[VMEM]...  7.58 us
    ppermute x6, waiting for transfers between devices, step(): lax.ppermute(array, 'tp', self.pairs if up else [(b, a) for a, b in self....  6.98 us
    ppermute x6, starting transfers between devices, paired(): lax.ppermute(array, 'pd', [(g, g ^ k) for g in range(lax.axis_size('pd'))])  4.14 us
    pallas_call x1, Pallas kernels, call_first(): pl.pallas_call(lambda *refs: first_kernel(plan, len(blocks), *refs), in_s...  2.93 us
    pallas_call x1, Pallas kernels, call_middle(): pl.pallas_call(lambda *refs: middle_kernel(plan, *refs), in_specs=[VMEM]...  2.22 us
    pallas_call x1, Pallas kernels, call_decode(): pl.pallas_call(lambda *refs: decode_kernel(plan, *refs), in_specs=[VMEM]...  2.13 us
    pallas_call x1, Pallas kernels, facts_row(): pl.pallas_call(kernel, in_specs=[SMEM, SMEM], out_specs=SMEM, out_shape=j...  1.43 us
  transfers between devices with their start and end apart: 12, of which 1 were waited for; matrix products, arithmetic and copies ran while one was open for 3% of the time, Pallas kernels for 34%

profile of v15, /device:TPU:0, one launch (start us, length us, event | category | flops | bytes accessed | tf_op | source)
XLA Modules:
  0.0 41.1 jit_solution(18324603255407819165)
XLA Ops:
  0.6 4.1 %collective-permute-start = (bf16[128,512]{1,0:T(8,128)(2,1)}, bf16[128,512]{1,0:T(8,128)(2,1)S(1)}, u32[]{:S(2)}, u32[]{:S(2)}) collective-permute-start(bf16[128,512]{1,0:T(8,128)(2,1)} %refs_6_.2), channel_id=1, source_target_pairs={{0,2},{2,3},{3,1},{1,0},{4,6},{6,7},{7,5},{5,4},{8,10},{10,11},{11... | collective-permute-start | bytes 393224 | tf_op jit(solution)/shard_map/ppermute | solution.py:46
  4.7 1.6 %collective-permute-start.1 = (bf16[128,512]{1,0:T(8,128)(2,1)}, bf16[128,512]{1,0:T(8,128)(2,1)S(1)}, u32[]{:S(2)}, u32[]{:S(2)}) collective-permute-start(bf16[128,512]{1,0:T(8,128)(2,1)} %refs_10_.1), channel_id=1, source_target_pairs={{0,2},{2,3},{3,1},{1,0},{4,6},{6,7},{7,5},{5,4},{8,10},{10,11},{11... | collective-permute-start | bytes 393224 | tf_op jit(solution)/shard_map/ppermute | solution.py:46
  6.3 0.9 %pad_maximum_fusion = bf16[4,2,5120]{2,1,0:T(2,128)(2,1)S(1)} fusion(bf16[4,2,512]{2,1,0:T(2,128)(2,1)} %param.15, bf16[4,2,512]{2,1,0:T(2,128)(2,1)} %param.14, bf16[4,2,4096]{2,1,0:T(2,128)(2,1)} %param.13), kind=kLoop, calls=%fused_computation.4 | loop fusion | flops 245760 | bytes 163840 | tf_op jit(solution)/shard_map/concatenate | solution.py:549
  7.2 0.0 copy-start
  7.3 0.0 copy-start.1
  7.3 1.4 %facts.1.refs_0_ = s32[18]{0:T(128)} custom-call(s32[4,4]{1,0:T(4,128)} %lengths_ref.1, s32[16]{0:T(128)} %slots_ref.1), custom_call_target="tpu_custom_call" | custom-call | flops 5000000000 | tf_op jit(solution)/shard_map/facts/pallas_call | solution.py:125
  8.7 0.0 copy-start.2
  8.8 0.0 copy-start.3
  8.8 0.1 collective-permute-start.2
  8.9 1.6 %collective-permute-start.3 = (bf16[8,5120]{1,0:T(8,128)(2,1)S(1)}, bf16[8,5120]{1,0:T(8,128)(2,1)S(1)}, u32[]{:S(2)}, u32[]{:S(2)}) collective-permute-start(bf16[8,5120]{1,0:T(8,128)(2,1)S(1)} %reshape.39.refs_7_), channel_id=1, source_target_pairs={{0,8},{4,12},{8,0},{12,4},{1,9},{5,13},{9,1},{13,5},{2,10},{6,14},... | collective-permute-start | bytes 245768 | tf_op jit(solution)/shard_map/ppermute | solution.py:534
  10.4 0.3 collective-permute-start.4
  10.7 0.0 collective-permute-done.refs_0_.refs_4_.refs_5_.refs_7_
  10.7 0.0 copy-done
  10.7 0.5 %collective-permute-start.5 = (bf16[128,512]{1,0:T(8,128)(2,1)S(1)}, bf16[128,512]{1,0:T(8,128)(2,1)S(1)}, u32[]{:S(2)}, u32[]{:S(2)}) collective-permute-start(bf16[128,512]{1,0:T(8,128)(2,1)S(1)} %copy-done), channel_id=1, source_target_pairs={{2,0},{3,2},{1,3},{0,1},{6,4},{7,6},{5,7},{4,5},{10,8},{11,10},{9,... | collective-permute-start | bytes 393224 | tf_op jit(solution)/shard_map/ppermute | solution.py:46
  11.2 0.0 collective-permute-done.1.refs_1_.refs_6_.refs_9_.refs_11_
  11.2 0.0 copy-done.1
  11.2 1.7 %collective-permute-start.6 = (bf16[128,512]{1,0:T(8,128)(2,1)S(1)}, bf16[128,512]{1,0:T(8,128)(2,1)S(1)}, u32[]{:S(2)}, u32[]{:S(2)}) collective-permute-start(bf16[128,512]{1,0:T(8,128)(2,1)S(1)} %copy-done.1), channel_id=1, source_target_pairs={{2,0},{3,2},{1,3},{0,1},{6,4},{7,6},{5,7},{4,5},{10,8},{11,10},{9,... | collective-permute-start | bytes 393224 | tf_op jit(solution)/shard_map/ppermute | solution.py:46
  12.9 0.0 collective-permute-done.2.refs_8_
  12.9 1.2 %collective-permute-start.7 = (bf16[128,512]{1,0:T(8,128)(2,1)S(1)}, bf16[128,512]{1,0:T(8,128)(2,1)S(1)}, u32[]{:S(2)}, u32[]{:S(2)}) collective-permute-start(bf16[128,512]{1,0:T(8,128)(2,1)S(1)} %collective-permute-done.refs_0_.refs_4_.refs_5_.refs_7_), channel_id=1, source_target_pairs={{0,2},{2,3},{3,1},{1,0},{4,6},{6,7},{7,5},{5,4},{8,10},{10,11},{11... | collective-permute-start | bytes 393224 | tf_op jit(solution)/shard_map/ppermute | solution.py:46
  14.1 0.0 collective-permute-done.3.refs_9_
  14.1 1.8 %collective-permute-start.8 = (bf16[128,512]{1,0:T(8,128)(2,1)S(1)}, bf16[128,512]{1,0:T(8,128)(2,1)S(1)}, u32[]{:S(2)}, u32[]{:S(2)}) collective-permute-start(bf16[128,512]{1,0:T(8,128)(2,1)S(1)} %collective-permute-done.1.refs_1_.refs_6_.refs_9_.refs_11_), channel_id=1, source_target_pairs={{0,2},{2,3},{3,1},{1,0},{4,6},{6,7},{7,5},{5,4},{8,10},{10,11},{11... | collective-permute-start | bytes 393224 | tf_op jit(solution)/shard_map/ppermute | solution.py:46
  15.9 0.0 collective-permute-done.4.refs_10_
  15.9 0.0 copy-done.2
  15.9 0.0 copy-done.3
  15.9 2.9 %first_shards.1 = (f32[4,1024,256]{2,1,0:T(8,128)S(1)}, f32[4,128,128]{2,1,0:T(8,128)S(1)}, f32[4,128,256]{2,1,0:T(8,128)S(1)}, f32[4,128,128]{2,1,0:T(8,128)S(1...) custom-call(s32[18]{0:T(128)S(1)} %copy-done.3, ...), custom_call_target="tpu_custom_call" | custom-call | flops 4294967296 | bytes 2097152 | tf_op jit(solution)/shard_map/first_shards/pallas_call | solution.py:461
  18.9 0.0 collective-permute-done.5.refs_7_.refs_6_.refs_8_
  18.9 7.0 %collective-permute-done.6.refs_8_.refs_10_.refs_12_ = bf16[128,512]{1,0:T(8,128)(2,1)S(1)} collective-permute-done((bf16[128,512]{1,0:T(8,128)(2,1)S(1)}, bf16[128,512]{1,0:T(8,128)(2,1)S(1)}, u32[]{:S(2)}, u32[]{:S(2)}) %collective-permute-start.6) | collective-permute-done | bytes 131104 | tf_op jit(solution)/shard_map/ppermute | solution.py:46
  25.8 2.2 %middle_shard.1 = (f32[4,1024,256]{2,1,0:T(8,128)S(1)}, f32[4,128,256]{2,1,0:T(8,128)S(1)}, f32[8,128]{1,0:T(8,128)S(1)}) custom-call(f32[4,1024,256]{2,1,0:T(8,128)S(1)} %get-tuple-element.22.refs_0_, f32[4,128,128]{2,1,0:T(8,128)S(1)} %get-tuple-element.23.refs_1_, ...), custom_call_target="tpu_custom_call", output_to_operand_aliasing={{0}: (0, {}), {1}: (2, {}), {2}: (4, {})} | custom-call | flops 2147483648 | bytes 2097152 | tf_op jit(solution)/shard_map/middle_shard/pallas_call | solution.py:475
  28.1 0.1 compare_reduce_fusion.2
  28.2 0.0 collective-permute-done.7.refs_7_.refs_9_
  28.2 0.0 collective-permute-done.8.refs_11_.refs_13_
  28.2 2.1 %last_shard_decode.1 = bf16[16,4096]{1,0:T(8,128)(2,1)S(1)} custom-call(f32[4,128,256]{2,1,0:T(8,128)S(1)} %get-tuple-element.33.refs_0_, f32[4,128,128]{2,1,0:T(8,128)S(1)} %get-tuple-element.25.refs_3_.refs_1_, f32[8,128]{1,0:T(8,128)S(1)} %get-tuple-element.31.refs_2_, bf16[16,4096]{1,0:T(8,128)(2,1)S(1)} %get-tuple-element.27.refs_5_.refs_3_, ...), custom_call_target="tpu_custom_call" | custom-call | flops 268435456 | bytes 262144 | tf_op jit(solution)/shard_map/last_shard_decode/pallas_call | solution.py:490
  30.4 0.1 fusion
  30.4 1.6 %collective-permute-start.10 = (bf16[2,4096]{1,0:T(2,128)(2,1)S(1)}, bf16[2,4096]{1,0:T(2,128)(2,1)S(1)}, u32[]{:S(2)}, u32[]{:S(2)}) collective-permute-start(bf16[2,4096]{1,0:T(2,128)(2,1)S(1)} %get-tuple-element.43), channel_id=1, source_target_pairs={{0,8},{4,12},{8,0},{12,4},{1,9},{5,13},{9,1},{13,5},{2,10},{6,14},... | collective-permute-start | bytes 49160 | tf_op jit(solution)/shard_map/ppermute | solution.py:534
  32.0 0.0 collective-permute-start.11
  32.0 0.6 %collective-permute-start.9 = (bf16[2,4096]{1,0:T(2,128)(2,1)S(1)}, bf16[2,4096]{1,0:T(2,128)(2,1)S(1)}, u32[]{:S(2)}, u32[]{:S(2)}) collective-permute-start(bf16[2,4096]{1,0:T(2,128)(2,1)S(1)} %get-tuple-element.40), channel_id=1, source_target_pairs={{0,12},{4,8},{8,4},{12,0},{1,13},{5,9},{9,5},{13,1},{2,14},{6,10},... | collective-permute-start | bytes 49160 | tf_op jit(solution)/shard_map/ppermute | solution.py:534
  32.6 7.6 %last_shard_prefill.1 = bf16[128,4096]{1,0:T(8,128)(2,1)} custom-call(f32[4,1024,256]{2,1,0:T(8,128)S(1)} %get-tuple-element.30.refs_0_, f32[4,128,128]{2,1,0:T(8,128)S(1)} %get-tuple-element.23.refs_1_, f32[8,128]{1,0:T(8,128)S(1)} %get-tuple-element.31.refs_2_, bf16[128,4096]{1,0:T(8,128)(2,1)S(1)} %copy-done.2, bf16[128,512]{1,0:T(8,128)(2,1)S(1)} %copy-done, ...), custom_call_target="tpu_custom_call" | custom-call | flops 2147483648 | bytes 2097152 | tf_op jit(solution)/shard_map/last_shard_prefill/pallas_call | solution.py:503
  40.2 0.0 collective-permute-done.10
  40.2 0.0 collective-permute-done.11
  40.2 0.0 collective-permute-done.9
  40.3 0.8 %broadcast_select_fusion.2 = bf16[4,2,4096]{2,1,0:T(2,128)(2,1)} fusion(pred[4]{0:T(512)(128)(4,1)S(1)} %get-tuple-element.39, pred[4]{0:T(512)(128)(4,1)S(1)} %get-tuple-element.38, pred[4]{0:T(512)(128)(4,1)S(1)} %get-tuple-element.37, pred[4]{0:T(512)(128)(4,1)S(1)} %get-tuple-element.36, bf16[2,4096]{1,0:T(2,128)(2,1)S(1)} %get-tuple-element.41, ...), kind=kLoop, calls=%fused_computation.2 | loop fusion | flops 131072 | bytes 131088 | tf_op jit(solution)/shard_map/jit(_where)/select_n | solution.py:578
  (2 shorter events, 0.0 us)
Async XLA Ops:
  0.6 10.1 %collective-permute-start = (bf16[128,512]{1,0:T(8,128)(2,1)}, bf16[128,512]{1,0:T(8,128)(2,1)S(1)}, u32[]{:S(2)}, u32[]{:S(2)}) collective-permute-start(bf16[128,512]{1,0:T(8,128)(2,1)} %refs_6_.2), channel_id=1, source_target_pairs={{0,2},{2,3},{3,1},{1,0},{4,6},{6,7},{7,5},{5,4},{8,10},{10,11},{11... | collective-permute-start | bytes 393224 | tf_op jit(solution)/shard_map/ppermute | solution.py:46
  4.7 6.5 %collective-permute-start.1 = (bf16[128,512]{1,0:T(8,128)(2,1)}, bf16[128,512]{1,0:T(8,128)(2,1)S(1)}, u32[]{:S(2)}, u32[]{:S(2)}) collective-permute-start(bf16[128,512]{1,0:T(8,128)(2,1)} %refs_10_.1), channel_id=1, source_target_pairs={{0,2},{2,3},{3,1},{1,0},{4,6},{6,7},{7,5},{5,4},{8,10},{10,11},{11... | collective-permute-start | bytes 393224 | tf_op jit(solution)/shard_map/ppermute | solution.py:46
  7.2 3.5 %copy-start = (bf16[128,512]{1,0:T(8,128)(2,1)S(1)}, bf16[128,512]{1,0:T(8,128)(2,1)}, u32[]{:S(2)}) copy-start(bf16[128,512]{1,0:T(8,128)(2,1)} %refs_6_.2) | copy-start | bytes 393220
  7.3 4.0 %copy-start.1 = (bf16[128,512]{1,0:T(8,128)(2,1)S(1)}, bf16[128,512]{1,0:T(8,128)(2,1)}, u32[]{:S(2)}) copy-start(bf16[128,512]{1,0:T(8,128)(2,1)} %refs_10_.1) | copy-start | bytes 393220
  8.7 7.2 %copy-start.2 = (bf16[128,4096]{1,0:T(8,128)(2,1)S(1)}, bf16[128,4096]{1,0:T(8,128)(2,1)}, u32[]{:S(2)}) copy-start(bf16[128,4096]{1,0:T(8,128)(2,1)} %refs_3_.2) | copy-start | bytes 3145732
  8.8 7.2 %copy-start.3 = (s32[18]{0:T(128)S(1)}, s32[18]{0:T(128)}, u32[]{:S(2)}) copy-start(s32[18]{0:T(128)} %facts.1.refs_0_) | copy-start | bytes 220
  8.8 4.1 %collective-permute-start.2 = (bf16[8,5120]{1,0:T(8,128)(2,1)S(1)}, bf16[8,5120]{1,0:T(8,128)(2,1)S(1)}, u32[]{:S(2)}, u32[]{:S(2)}) collective-permute-start(bf16[8,5120]{1,0:T(8,128)(2,1)S(1)} %reshape.39.refs_7_), channel_id=1, source_target_pairs={{0,4},{4,0},{8,12},{12,8},{1,5},{5,1},{9,13},{13,9},{2,6},{6,2},{1... | collective-permute-start | bytes 245768 | tf_op jit(solution)/shard_map/ppermute | solution.py:534
  8.9 5.3 %collective-permute-start.3 = (bf16[8,5120]{1,0:T(8,128)(2,1)S(1)}, bf16[8,5120]{1,0:T(8,128)(2,1)S(1)}, u32[]{:S(2)}, u32[]{:S(2)}) collective-permute-start(bf16[8,5120]{1,0:T(8,128)(2,1)S(1)} %reshape.39.refs_7_), channel_id=1, source_target_pairs={{0,8},{4,12},{8,0},{12,4},{1,9},{5,13},{9,1},{13,5},{2,10},{6,14},... | collective-permute-start | bytes 245768 | tf_op jit(solution)/shard_map/ppermute | solution.py:534
  10.4 5.5 %collective-permute-start.4 = (bf16[8,5120]{1,0:T(8,128)(2,1)S(1)}, bf16[8,5120]{1,0:T(8,128)(2,1)S(1)}, u32[]{:S(2)}, u32[]{:S(2)}) collective-permute-start(bf16[8,5120]{1,0:T(8,128)(2,1)S(1)} %reshape.39.refs_7_), channel_id=1, source_target_pairs={{0,12},{4,8},{8,4},{12,0},{1,13},{5,9},{9,5},{13,1},{2,14},{6,10},... | collective-permute-start | bytes 245768 | tf_op jit(solution)/shard_map/ppermute | solution.py:534
  10.7 8.1 %collective-permute-start.5 = (bf16[128,512]{1,0:T(8,128)(2,1)S(1)}, bf16[128,512]{1,0:T(8,128)(2,1)S(1)}, u32[]{:S(2)}, u32[]{:S(2)}) collective-permute-start(bf16[128,512]{1,0:T(8,128)(2,1)S(1)} %copy-done), channel_id=1, source_target_pairs={{2,0},{3,2},{1,3},{0,1},{6,4},{7,6},{5,7},{4,5},{10,8},{11,10},{9,... | collective-permute-start | bytes 393224 | tf_op jit(solution)/shard_map/ppermute | solution.py:46
  11.2 14.6 %collective-permute-start.6 = (bf16[128,512]{1,0:T(8,128)(2,1)S(1)}, bf16[128,512]{1,0:T(8,128)(2,1)S(1)}, u32[]{:S(2)}, u32[]{:S(2)}) collective-permute-start(bf16[128,512]{1,0:T(8,128)(2,1)S(1)} %copy-done.1), channel_id=1, source_target_pairs={{2,0},{3,2},{1,3},{0,1},{6,4},{7,6},{5,7},{4,5},{10,8},{11,10},{9,... | collective-permute-start | bytes 393224 | tf_op jit(solution)/shard_map/ppermute | solution.py:46
  12.9 15.3 %collective-permute-start.7 = (bf16[128,512]{1,0:T(8,128)(2,1)S(1)}, bf16[128,512]{1,0:T(8,128)(2,1)S(1)}, u32[]{:S(2)}, u32[]{:S(2)}) collective-permute-start(bf16[128,512]{1,0:T(8,128)(2,1)S(1)} %collective-permute-done.refs_0_.refs_4_.refs_5_.refs_7_), channel_id=1, source_target_pairs={{0,2},{2,3},{3,1},{1,0},{4,6},{6,7},{7,5},{5,4},{8,10},{10,11},{11... | collective-permute-start | bytes 393224 | tf_op jit(solution)/shard_map/ppermute | solution.py:46
  14.1 14.1 %collective-permute-start.8 = (bf16[128,512]{1,0:T(8,128)(2,1)S(1)}, bf16[128,512]{1,0:T(8,128)(2,1)S(1)}, u32[]{:S(2)}, u32[]{:S(2)}) collective-permute-start(bf16[128,512]{1,0:T(8,128)(2,1)S(1)} %collective-permute-done.1.refs_1_.refs_6_.refs_9_.refs_11_), channel_id=1, source_target_pairs={{0,2},{2,3},{3,1},{1,0},{4,6},{6,7},{7,5},{5,4},{8,10},{10,11},{11... | collective-permute-start | bytes 393224 | tf_op jit(solution)/shard_map/ppermute | solution.py:46
  30.4 9.8 %collective-permute-start.10 = (bf16[2,4096]{1,0:T(2,128)(2,1)S(1)}, bf16[2,4096]{1,0:T(2,128)(2,1)S(1)}, u32[]{:S(2)}, u32[]{:S(2)}) collective-permute-start(bf16[2,4096]{1,0:T(2,128)(2,1)S(1)} %get-tuple-element.43), channel_id=1, source_target_pairs={{0,8},{4,12},{8,0},{12,4},{1,9},{5,13},{9,1},{13,5},{2,10},{6,14},... | collective-permute-start | bytes 49160 | tf_op jit(solution)/shard_map/ppermute | solution.py:534
  32.0 8.2 %collective-permute-start.11 = (bf16[2,4096]{1,0:T(2,128)(2,1)S(1)}, bf16[2,4096]{1,0:T(2,128)(2,1)S(1)}, u32[]{:S(2)}, u32[]{:S(2)}) collective-permute-start(bf16[2,4096]{1,0:T(2,128)(2,1)S(1)} %get-tuple-element.42), channel_id=1, source_target_pairs={{0,4},{4,0},{8,12},{12,8},{1,5},{5,1},{9,13},{13,9},{2,6},{6,2},{1... | collective-permute-start | bytes 49160 | tf_op jit(solution)/shard_map/ppermute | solution.py:534
  32.0 8.3 %collective-permute-start.9 = (bf16[2,4096]{1,0:T(2,128)(2,1)S(1)}, bf16[2,4096]{1,0:T(2,128)(2,1)S(1)}, u32[]{:S(2)}, u32[]{:S(2)}) collective-permute-start(bf16[2,4096]{1,0:T(2,128)(2,1)S(1)} %get-tuple-element.40), channel_id=1, source_target_pairs={{0,12},{4,8},{8,4},{12,0},{1,13},{5,9},{9,5},{13,1},{2,14},{6,10},... | collective-permute-start | bytes 49160 | tf_op jit(solution)/shard_map/ppermute | solution.py:534

commit v16 on v14

--- a/solution.py
+++ b/solution.py
@@ -552,7 +552,7 @@
     )
     facts = facts_row(plan, prompt_lengths, decode_slot)
     prompt_key, decoded_query = lax.optimization_barrier((prompt_key, decoded_query))
-    later_key, later_value, own, facts = lax.optimization_barrier((prompt_key, prompt_value, own, facts))
+    later_key, later_value = prompt_key, prompt_value
     chains = []
     for up, down in ((prompt_key, later_key), (prompt_value, later_value)):
         pieces = [up]
@@ -563,7 +563,7 @@
         chains.append(pieces[: plan.size])
     keys, values = chains
     blocks = [own] + [paired(own, k) for k in range(1, pd_size)]
-    maxima = start_maxima(keys[1], values[1])
+    maxima = start_maxima(keys[1], values[1], keys[2], values[2])
 
     state = call_first(plan, facts, maxima, prompt_query, blocks, keys[:-2], values[:-2])
     state = call_middle(plan, state, prompt_query, keys[-2], values[-2])

time: 38.7 us -> 39.6 us (1.023)
  starting transfers between devices: 14.5 us -> 18.9 us
  waiting for transfers between devices: 4.92 us -> 1.43 us
    ppermute x6, starting transfers between devices: 10.4 us -> 13.9 us  [step(): lax.ppermute(array, 'tp', self.pairs if up else [(b, a) for a, b in self....]
    ppermute x6, waiting for transfers between devices: 4.67 us -> 1.42 us  [step(): lax.ppermute(array, 'tp', self.pairs if up else [(b, a) for a, b in self....]
    ppermute x6, starting transfers between devices: 4.14 us -> 4.96 us  [paired(): lax.ppermute(array, 'pd', [(g, g ^ k) for g in range(lax.axis_size('pd'))])]
  transfers between devices with their start and end apart: 12 -> 12, of which waited for: 4 -> 1; matrix products, arithmetic and copies ran while one was open for 3% -> 3% of each run, Pallas kernels for 37% -> 36%
where the time goes in v16:
time: 39.6 us; the launch traced here: 39.3 us
  starting transfers between devices  18.9 us (48%)
  Pallas kernels  16.2 us (41%)
  other arithmetic  1.89 us (5%)
  waiting for transfers between devices  1.43 us (4%)
  between operations  0.81 us (2%)
    ppermute x6, starting transfers between devices, step(): lax.ppermute(array, 'tp', self.pairs if up else [(b, a) for a, b in self....  13.9 us
    pallas_call x1, Pallas kernels, call_prefill(): pl.pallas_call(lambda *refs: prefill_kernel(plan, *refs), in_specs=[VMEM]...  7.63 us
    ppermute x6, starting transfers between devices, paired(): lax.ppermute(array, 'pd', [(g, g ^ k) for g in range(lax.axis_size('pd'))])  4.96 us
    pallas_call x1, Pallas kernels, call_first(): pl.pallas_call(lambda *refs: first_kernel(plan, len(blocks), *refs), in_s...  2.93 us
    pallas_call x1, Pallas kernels, call_middle(): pl.pallas_call(lambda *refs: middle_kernel(plan, *refs), in_specs=[VMEM]...  2.22 us
    pallas_call x1, Pallas kernels, call_decode(): pl.pallas_call(lambda *refs: decode_kernel(plan, *refs), in_specs=[VMEM]...  2.13 us
    ppermute x6, waiting for transfers between devices, step(): lax.ppermute(array, 'tp', self.pairs if up else [(b, a) for a, b in self....  1.42 us
    pallas_call x1, Pallas kernels, facts_row(): pl.pallas_call(kernel, in_specs=[SMEM, SMEM], out_specs=SMEM, out_shape=j...  1.3 us
  transfers between devices with their start and end apart: 12, of which 1 were waited for; matrix products, arithmetic and copies ran while one was open for 3% of the time, Pallas kernels for 36%

profile of v16, /device:TPU:0, one launch (start us, length us, event | category | flops | bytes accessed | tf_op | source)
XLA Modules:
  0.0 39.3 jit_solution(2988348264695624194)
XLA Ops:
  0.6 3.1 %collective-permute-start = (bf16[128,512]{1,0:T(8,128)(2,1)}, bf16[128,512]{1,0:T(8,128)(2,1)S(1)}, u32[]{:S(2)}, u32[]{:S(2)}) collective-permute-start(bf16[128,512]{1,0:T(8,128)(2,1)} %refs_6_.2), channel_id=1, source_target_pairs={{0,1},{1,3},{3,2},{2,0},{4,5},{5,7},{7,6},{6,4},{8,9},{9,11},{11,1... | collective-permute-start | bytes 393224 | tf_op jit(solution)/shard_map/ppermute | solution.py:46
  3.7 1.1 %collective-permute-start.2 = (bf16[128,512]{1,0:T(8,128)(2,1)}, bf16[128,512]{1,0:T(8,128)(2,1)S(1)}, u32[]{:S(2)}, u32[]{:S(2)}) collective-permute-start(bf16[128,512]{1,0:T(8,128)(2,1)} %refs_6_.2), channel_id=1, source_target_pairs={{1,0},{3,1},{2,3},{0,2},{5,4},{7,5},{6,7},{4,6},{9,8},{11,9},{10,1... | collective-permute-start | bytes 393224 | tf_op jit(solution)/shard_map/ppermute | solution.py:46
  4.8 1.5 %collective-permute-start.1 = (bf16[128,512]{1,0:T(8,128)(2,1)}, bf16[128,512]{1,0:T(8,128)(2,1)S(1)}, u32[]{:S(2)}, u32[]{:S(2)}) collective-permute-start(bf16[128,512]{1,0:T(8,128)(2,1)} %refs_10_.1), channel_id=1, source_target_pairs={{0,1},{1,3},{3,2},{2,0},{4,5},{5,7},{7,6},{6,4},{8,9},{9,11},{11,1... | collective-permute-start | bytes 393224 | tf_op jit(solution)/shard_map/ppermute | solution.py:46
  6.3 1.4 %collective-permute-start.3 = (bf16[128,512]{1,0:T(8,128)(2,1)}, bf16[128,512]{1,0:T(8,128)(2,1)S(1)}, u32[]{:S(2)}, u32[]{:S(2)}) collective-permute-start(bf16[128,512]{1,0:T(8,128)(2,1)} %refs_10_.1), channel_id=1, source_target_pairs={{1,0},{3,1},{2,3},{0,2},{5,4},{7,5},{6,7},{4,6},{9,8},{11,9},{10,1... | collective-permute-start | bytes 393224 | tf_op jit(solution)/shard_map/ppermute | solution.py:46
  7.7 0.9 %pad_maximum_fusion = bf16[4,2,5120]{2,1,0:T(2,128)(2,1)S(1)} fusion(bf16[4,2,512]{2,1,0:T(2,128)(2,1)} %param.15, bf16[4,2,512]{2,1,0:T(2,128)(2,1)} %param.14, bf16[4,2,4096]{2,1,0:T(2,128)(2,1)} %param.13), kind=kLoop, calls=%fused_computation.4 | loop fusion | flops 245760 | bytes 163840 | tf_op jit(solution)/shard_map/concatenate | solution.py:550
  8.7 0.1 collective-permute-start.4
  8.8 1.3 %facts.1.refs_0_ = s32[18]{0:T(128)} custom-call(s32[4,4]{1,0:T(4,128)} %lengths_ref.1, s32[16]{0:T(128)} %slots_ref.1), custom_call_target="tpu_custom_call" | custom-call | flops 5000000000 | tf_op jit(solution)/shard_map/facts/pallas_call | solution.py:126
  10.1 0.0 copy-start
  10.1 0.0 copy-start.1
  10.1 0.0 copy-start.2
  10.1 0.0 copy-start.3
  10.1 0.0 collective-permute-done.refs_0_.refs_4_.refs_5_.refs_7_
  10.2 1.8 %collective-permute-start.5 = (bf16[8,5120]{1,0:T(8,128)(2,1)S(1)}, bf16[8,5120]{1,0:T(8,128)(2,1)S(1)}, u32[]{:S(2)}, u32[]{:S(2)}) collective-permute-start(bf16[8,5120]{1,0:T(8,128)(2,1)S(1)} %reshape.39.refs_7_), channel_id=1, source_target_pairs={{0,8},{4,12},{8,0},{12,4},{1,9},{5,13},{9,1},{13,5},{2,10},{6,14},... | collective-permute-start | bytes 245768 | tf_op jit(solution)/shard_map/ppermute | solution.py:535
  12.0 1.4 %collective-permute-done.2.refs_2_.refs_7_.refs_6_.refs_8_ = bf16[128,512]{1,0:T(8,128)(2,1)S(1)} collective-permute-done((bf16[128,512]{1,0:T(8,128)(2,1)}, bf16[128,512]{1,0:T(8,128)(2,1)S(1)}, u32[]{:S(2)}, u32[]{:S(2)}) %collective-permute-start.2) | collective-permute-done | bytes 131104 | tf_op jit(solution)/shard_map/ppermute | solution.py:46
  13.4 0.9 %collective-permute-start.6 = (bf16[8,5120]{1,0:T(8,128)(2,1)S(1)}, bf16[8,5120]{1,0:T(8,128)(2,1)S(1)}, u32[]{:S(2)}, u32[]{:S(2)}) collective-permute-start(bf16[8,5120]{1,0:T(8,128)(2,1)S(1)} %reshape.39.refs_7_), channel_id=1, source_target_pairs={{0,12},{4,8},{8,4},{12,0},{1,13},{5,9},{9,5},{13,1},{2,14},{6,10},... | collective-permute-start | bytes 245768 | tf_op jit(solution)/shard_map/ppermute | solution.py:535
  14.2 0.0 collective-permute-done.1.refs_1_.refs_6_.refs_9_.refs_11_
  14.2 3.5 %collective-permute-start.7 = (bf16[128,512]{1,0:T(8,128)(2,1)S(1)}, bf16[128,512]{1,0:T(8,128)(2,1)S(1)}, u32[]{:S(2)}, u32[]{:S(2)}) collective-permute-start(bf16[128,512]{1,0:T(8,128)(2,1)S(1)} %collective-permute-done.refs_0_.refs_4_.refs_5_.refs_7_), channel_id=1, source_target_pairs={{0,1},{1,3},{3,2},{2,0},{4,5},{5,7},{7,6},{6,4},{8,9},{9,11},{11,1... | collective-permute-start | bytes 393224 | tf_op jit(solution)/shard_map/ppermute | solution.py:46
  17.8 0.0 collective-permute-done.3.refs_3_.refs_8_.refs_10_.refs_12_
  17.8 3.3 %collective-permute-start.8 = (bf16[128,512]{1,0:T(8,128)(2,1)S(1)}, bf16[128,512]{1,0:T(8,128)(2,1)S(1)}, u32[]{:S(2)}, u32[]{:S(2)}) collective-permute-start(bf16[128,512]{1,0:T(8,128)(2,1)S(1)} %collective-permute-done.1.refs_1_.refs_6_.refs_9_.refs_11_), channel_id=1, source_target_pairs={{0,1},{1,3},{3,2},{2,0},{4,5},{5,7},{7,6},{6,4},{8,9},{9,11},{11,1... | collective-permute-start | bytes 393224 | tf_op jit(solution)/shard_map/ppermute | solution.py:46
  21.1 0.0 collective-permute-done.4.refs_8_
  21.1 0.0 collective-permute-done.5.refs_9_
  21.1 0.0 collective-permute-done.6.refs_10_
  21.1 0.0 copy-done
  21.1 0.0 copy-done.1
  21.1 0.0 copy-done.2
  21.1 0.0 copy-done.3
  21.1 2.9 %first_shards.1 = (f32[4,1024,256]{2,1,0:T(8,128)S(1)}, f32[4,128,128]{2,1,0:T(8,128)S(1)}, f32[4,128,256]{2,1,0:T(8,128)S(1)}, f32[4,128,128]{2,1,0:T(8,128)S(1...) custom-call(s32[18]{0:T(128)S(1)} %copy-done.3, ...), custom_call_target="tpu_custom_call" | custom-call | flops 4294967296 | bytes 2097152 | tf_op jit(solution)/shard_map/first_shards/pallas_call | solution.py:462
  24.1 2.2 %middle_shard.1 = (f32[4,1024,256]{2,1,0:T(8,128)S(1)}, f32[4,128,256]{2,1,0:T(8,128)S(1)}, f32[8,128]{1,0:T(8,128)S(1)}) custom-call(f32[4,1024,256]{2,1,0:T(8,128)S(1)} %get-tuple-element.16.refs_0_, f32[4,128,128]{2,1,0:T(8,128)S(1)} %get-tuple-element.17.refs_1_, ...), custom_call_target="tpu_custom_call", output_to_operand_aliasing={{0}: (0, {}), {1}: (2, {}), {2}: (4, {})} | custom-call | flops 2147483648 | bytes 2097152 | tf_op jit(solution)/shard_map/middle_shard/pallas_call | solution.py:476
  26.3 0.1 compare_reduce_fusion.2
  26.4 0.0 collective-permute-done.7.refs_7_.refs_9_
  26.5 0.0 collective-permute-done.8.refs_11_.refs_13_
  26.5 2.1 %last_shard_decode.1 = bf16[16,4096]{1,0:T(8,128)(2,1)S(1)} custom-call(f32[4,128,256]{2,1,0:T(8,128)S(1)} %get-tuple-element.25.refs_0_, f32[4,128,128]{2,1,0:T(8,128)S(1)} %get-tuple-element.19.refs_3_.refs_1_, f32[8,128]{1,0:T(8,128)S(1)} %get-tuple-element.23.refs_2_, bf16[16,4096]{1,0:T(8,128)(2,1)S(1)} %get-tuple-element.21.refs_5_.refs_3_, ...), custom_call_target="tpu_custom_call" | custom-call | flops 268435456 | bytes 262144 | tf_op jit(solution)/shard_map/last_shard_decode/pallas_call | solution.py:491
  28.6 0.1 fusion
  28.7 1.6 %collective-permute-start.10 = (bf16[2,4096]{1,0:T(2,128)(2,1)S(1)}, bf16[2,4096]{1,0:T(2,128)(2,1)S(1)}, u32[]{:S(2)}, u32[]{:S(2)}) collective-permute-start(bf16[2,4096]{1,0:T(2,128)(2,1)S(1)} %get-tuple-element.35), channel_id=1, source_target_pairs={{0,8},{4,12},{8,0},{12,4},{1,9},{5,13},{9,1},{13,5},{2,10},{6,14},... | collective-permute-start | bytes 49160 | tf_op jit(solution)/shard_map/ppermute | solution.py:535
  30.2 0.0 collective-permute-start.11
  30.2 0.6 %collective-permute-start.9 = (bf16[2,4096]{1,0:T(2,128)(2,1)S(1)}, bf16[2,4096]{1,0:T(2,128)(2,1)S(1)}, u32[]{:S(2)}, u32[]{:S(2)}) collective-permute-start(bf16[2,4096]{1,0:T(2,128)(2,1)S(1)} %get-tuple-element.32), channel_id=1, source_target_pairs={{0,12},{4,8},{8,4},{12,0},{1,13},{5,9},{9,5},{13,1},{2,14},{6,10},... | collective-permute-start | bytes 49160 | tf_op jit(solution)/shard_map/ppermute | solution.py:535
  30.9 7.6 %last_shard_prefill.1 = bf16[128,4096]{1,0:T(8,128)(2,1)} custom-call(f32[4,1024,256]{2,1,0:T(8,128)S(1)} %get-tuple-element.22.refs_0_, f32[4,128,128]{2,1,0:T(8,128)S(1)} %get-tuple-element.17.refs_1_, f32[8,128]{1,0:T(8,128)S(1)} %get-tuple-element.23.refs_2_, bf16[128,4096]{1,0:T(8,128)(2,1)S(1)} %copy-done.2, bf16[128,512]{1,0:T(8,128)(2,1)S(1)} %copy-done, ...), custom_call_target="tpu_custom_call" | custom-call | flops 2147483648 | bytes 2097152 | tf_op jit(solution)/shard_map/last_shard_prefill/pallas_call | solution.py:504
  38.5 0.0 collective-permute-done.10
  38.5 0.0 collective-permute-done.11
  38.5 0.0 collective-permute-done.9
  38.5 0.8 %broadcast_select_fusion.2 = bf16[4,2,4096]{2,1,0:T(2,128)(2,1)} fusion(pred[4]{0:T(512)(128)(4,1)S(1)} %get-tuple-element.31, pred[4]{0:T(512)(128)(4,1)S(1)} %get-tuple-element.30, pred[4]{0:T(512)(128)(4,1)S(1)} %get-tuple-element.29, pred[4]{0:T(512)(128)(4,1)S(1)} %get-tuple-element.28, bf16[2,4096]{1,0:T(2,128)(2,1)S(1)} %get-tuple-element.33, ...), kind=kLoop, calls=%fused_computation.2 | loop fusion | flops 131072 | bytes 131088 | tf_op jit(solution)/shard_map/jit(_where)/select_n | solution.py:579
  (2 shorter events, 0.0 us)
Async XLA Ops:
  0.6 9.5 %collective-permute-start = (bf16[128,512]{1,0:T(8,128)(2,1)}, bf16[128,512]{1,0:T(8,128)(2,1)S(1)}, u32[]{:S(2)}, u32[]{:S(2)}) collective-permute-start(bf16[128,512]{1,0:T(8,128)(2,1)} %refs_6_.2), channel_id=1, source_target_pairs={{0,1},{1,3},{3,2},{2,0},{4,5},{5,7},{7,6},{6,4},{8,9},{9,11},{11,1... | collective-permute-start | bytes 393224 | tf_op jit(solution)/shard_map/ppermute | solution.py:46
  3.7 9.7 %collective-permute-start.2 = (bf16[128,512]{1,0:T(8,128)(2,1)}, bf16[128,512]{1,0:T(8,128)(2,1)S(1)}, u32[]{:S(2)}, u32[]{:S(2)}) collective-permute-start(bf16[128,512]{1,0:T(8,128)(2,1)} %refs_6_.2), channel_id=1, source_target_pairs={{1,0},{3,1},{2,3},{0,2},{5,4},{7,5},{6,7},{4,6},{9,8},{11,9},{10,1... | collective-permute-start | bytes 393224 | tf_op jit(solution)/shard_map/ppermute | solution.py:46
  4.8 9.5 %collective-permute-start.1 = (bf16[128,512]{1,0:T(8,128)(2,1)}, bf16[128,512]{1,0:T(8,128)(2,1)S(1)}, u32[]{:S(2)}, u32[]{:S(2)}) collective-permute-start(bf16[128,512]{1,0:T(8,128)(2,1)} %refs_10_.1), channel_id=1, source_target_pairs={{0,1},{1,3},{3,2},{2,0},{4,5},{5,7},{7,6},{6,4},{8,9},{9,11},{11,1... | collective-permute-start | bytes 393224 | tf_op jit(solution)/shard_map/ppermute | solution.py:46
  6.3 11.5 %collective-permute-start.3 = (bf16[128,512]{1,0:T(8,128)(2,1)}, bf16[128,512]{1,0:T(8,128)(2,1)S(1)}, u32[]{:S(2)}, u32[]{:S(2)}) collective-permute-start(bf16[128,512]{1,0:T(8,128)(2,1)} %refs_10_.1), channel_id=1, source_target_pairs={{1,0},{3,1},{2,3},{0,2},{5,4},{7,5},{6,7},{4,6},{9,8},{11,9},{10,1... | collective-permute-start | bytes 393224 | tf_op jit(solution)/shard_map/ppermute | solution.py:46
  8.7 12.4 %collective-permute-start.4 = (bf16[8,5120]{1,0:T(8,128)(2,1)S(1)}, bf16[8,5120]{1,0:T(8,128)(2,1)S(1)}, u32[]{:S(2)}, u32[]{:S(2)}) collective-permute-start(bf16[8,5120]{1,0:T(8,128)(2,1)S(1)} %reshape.39.refs_7_), channel_id=1, source_target_pairs={{0,4},{4,0},{8,12},{12,8},{1,5},{5,1},{9,13},{13,9},{2,6},{6,2},{1... | collective-permute-start | bytes 245768 | tf_op jit(solution)/shard_map/ppermute | solution.py:535
  10.1 11.0 %copy-start = (bf16[128,512]{1,0:T(8,128)(2,1)S(1)}, bf16[128,512]{1,0:T(8,128)(2,1)}, u32[]{:S(2)}) copy-start(bf16[128,512]{1,0:T(8,128)(2,1)} %refs_6_.2) | copy-start | bytes 393220
  10.1 11.0 %copy-start.1 = (bf16[128,512]{1,0:T(8,128)(2,1)S(1)}, bf16[128,512]{1,0:T(8,128)(2,1)}, u32[]{:S(2)}) copy-start(bf16[128,512]{1,0:T(8,128)(2,1)} %refs_10_.1) | copy-start | bytes 393220
  10.1 11.0 %copy-start.2 = (bf16[128,4096]{1,0:T(8,128)(2,1)S(1)}, bf16[128,4096]{1,0:T(8,128)(2,1)}, u32[]{:S(2)}) copy-start(bf16[128,4096]{1,0:T(8,128)(2,1)} %refs_3_.2) | copy-start | bytes 3145732
  10.1 11.0 %copy-start.3 = (s32[18]{0:T(128)S(1)}, s32[18]{0:T(128)}, u32[]{:S(2)}) copy-start(s32[18]{0:T(128)} %facts.1.refs_0_) | copy-start | bytes 220
  10.2 10.9 %collective-permute-start.5 = (bf16[8,5120]{1,0:T(8,128)(2,1)S(1)}, bf16[8,5120]{1,0:T(8,128)(2,1)S(1)}, u32[]{:S(2)}, u32[]{:S(2)}) collective-permute-start(bf16[8,5120]{1,0:T(8,128)(2,1)S(1)} %reshape.39.refs_7_), channel_id=1, source_target_pairs={{0,8},{4,12},{8,0},{12,4},{1,9},{5,13},{9,1},{13,5},{2,10},{6,14},... | collective-permute-start | bytes 245768 | tf_op jit(solution)/shard_map/ppermute | solution.py:535
  13.4 7.7 %collective-permute-start.6 = (bf16[8,5120]{1,0:T(8,128)(2,1)S(1)}, bf16[8,5120]{1,0:T(8,128)(2,1)S(1)}, u32[]{:S(2)}, u32[]{:S(2)}) collective-permute-start(bf16[8,5120]{1,0:T(8,128)(2,1)S(1)} %reshape.39.refs_7_), channel_id=1, source_target_pairs={{0,12},{4,8},{8,4},{12,0},{1,13},{5,9},{9,5},{13,1},{2,14},{6,10},... | collective-permute-start | bytes 245768 | tf_op jit(solution)/shard_map/ppermute | solution.py:535
  14.2 12.2 %collective-permute-start.7 = (bf16[128,512]{1,0:T(8,128)(2,1)S(1)}, bf16[128,512]{1,0:T(8,128)(2,1)S(1)}, u32[]{:S(2)}, u32[]{:S(2)}) collective-permute-start(bf16[128,512]{1,0:T(8,128)(2,1)S(1)} %collective-permute-done.refs_0_.refs_4_.refs_5_.refs_7_), channel_id=1, source_target_pairs={{0,1},{1,3},{3,2},{2,0},{4,5},{5,7},{7,6},{6,4},{8,9},{9,11},{11,1... | collective-permute-start | bytes 393224 | tf_op jit(solution)/shard_map/ppermute | solution.py:46
  17.8 8.7 %collective-permute-start.8 = (bf16[128,512]{1,0:T(8,128)(2,1)S(1)}, bf16[128,512]{1,0:T(8,128)(2,1)S(1)}, u32[]{:S(2)}, u32[]{:S(2)}) collective-permute-start(bf16[128,512]{1,0:T(8,128)(2,1)S(1)} %collective-permute-done.1.refs_1_.refs_6_.refs_9_.refs_11_), channel_id=1, source_target_pairs={{0,1},{1,3},{3,2},{2,0},{4,5},{5,7},{7,6},{6,4},{8,9},{9,11},{11,1... | collective-permute-start | bytes 393224 | tf_op jit(solution)/shard_map/ppermute | solution.py:46
  28.7 9.8 %collective-permute-start.10 = (bf16[2,4096]{1,0:T(2,128)(2,1)S(1)}, bf16[2,4096]{1,0:T(2,128)(2,1)S(1)}, u32[]{:S(2)}, u32[]{:S(2)}) collective-permute-start(bf16[2,4096]{1,0:T(2,128)(2,1)S(1)} %get-tuple-element.35), channel_id=1, source_target_pairs={{0,8},{4,12},{8,0},{12,4},{1,9},{5,13},{9,1},{13,5},{2,10},{6,14},... | collective-permute-start | bytes 49160 | tf_op jit(solution)/shard_map/ppermute | solution.py:535
  30.2 8.3 %collective-permute-start.11 = (bf16[2,4096]{1,0:T(2,128)(2,1)S(1)}, bf16[2,4096]{1,0:T(2,128)(2,1)S(1)}, u32[]{:S(2)}, u32[]{:S(2)}) collective-permute-start(bf16[2,4096]{1,0:T(2,128)(2,1)S(1)} %get-tuple-element.34), channel_id=1, source_target_pairs={{0,4},{4,0},{8,12},{12,8},{1,5},{5,1},{9,13},{13,9},{2,6},{6,2},{1... | collective-permute-start | bytes 49160 | tf_op jit(solution)/shard_map/ppermute | solution.py:535
  30.2 8.3 %collective-permute-start.9 = (bf16[2,4096]{1,0:T(2,128)(2,1)S(1)}, bf16[2,4096]{1,0:T(2,128)(2,1)S(1)}, u32[]{:S(2)}, u32[]{:S(2)}) collective-permute-start(bf16[2,4096]{1,0:T(2,128)(2,1)S(1)} %get-tuple-element.32), channel_id=1, source_target_pairs={{0,12},{4,8},{8,4},{12,0},{1,13},{5,9},{9,5},{13,1},{2,14},{6,10},... | collective-permute-start | bytes 49160 | tf_op jit(solution)/shard_map/ppermute | solution.py:535

commit v17 on v14

--- a/solution.py
+++ b/solution.py
@@ -206,60 +206,36 @@
     )
 
 
-def first_kernel(plan, pd_size, facts_ref, maxima_ref, q_ref, *refs):
+def bias_kernel(plan, facts, bias_ref):
+    for s in range(plan.size):
+        tokens = bias_ref.shape[1]
+        bias_ref[s] = causal_bias(
+            0, tokens, tokens, facts.source[s : s + 1], facts.ends, facts.member, plan.size
+        )
+
+
+def first_kernel(plan, facts_ref, maxima_ref, q_ref, *refs):
     width = plan.size
     k_refs, v_refs, refs = refs[: width - 2], refs[width - 2 : 2 * width - 4], refs[2 * width - 4 :]
-    block_refs, refs = refs[:pd_size], refs[pd_size:]
-    acc_ref, bias_ref, dec_acc_ref, dec_bias_ref, worst_ref, queries_ref, fresh_ref, pick_ref, owner_ref = refs
+    acc_ref, bias_ref, worst_ref = refs
     tokens = q_ref.shape[0]
     half = tokens // 2
     facts = Facts(facts_ref, width)
     sources = facts.source[:-2]
-    pick_ref[...] = pick_matrix(facts)
-    slot = iota((8, HEAD_SIZE), 0)
-    owner = jnp.zeros_like(slot)
-    for p in range(GROUP_REQUESTS):
-        owner = jnp.where(slot == p, facts.owner[p], owner)
-    owner_ref[...] = owner
-    for s in range(width):
-        bias_ref[s] = causal_bias(0, tokens, tokens, facts.source[s : s + 1], facts.ends, facts.member, width)
-        dec_bias_ref[s] = jnp.where(
-            request_mask(facts.ends, tokens, facts.source[s : s + 1], width), 0.0, MASKED
-        )
-    rows = picked_rows(facts, pd_size, block_refs)
-    queries_ref[...] = rows[:, :Q_WIDTH]
-    fresh_ref[...] = rows[:, Q_WIDTH:]
+    bias_kernel(plan, facts, bias_ref)
     worst_ref[...] = maxima_ref[...]
-    new_mask = fresh_mask()
-    mask = request_mask(facts.ends, tokens, sources, width)
     spans = ((0, half), (half, tokens))
     biases = [
         causal_bias(s, half, keys, sources, facts.ends, facts.member, width) for s, keys in spans
     ]
     together = max(1, min(HEADS_PER_KV, HEADS_PER_KV * 4 // width))
 
-    def weigh(exponents):
-        top = jnp.max(peak(exponents), axis=1, keepdims=True)
-        worst_ref[...] = jnp.maximum(worst_ref[...], top)
-        return jnp.exp2(exponents).astype(jnp.bfloat16)
-
     def step(h):
         columns = span(h * HEAD_SIZE, HEAD_SIZE)
         first = h * Q_BLOCK
-        queries = stacked_heads(queries_ref, slice(None), first, HEADS_PER_KV)
-        k_all = jnp.concatenate([ref[:, columns] for ref in k_refs], axis=0)
-        v_all = with_ones(jnp.concatenate([ref[:, columns] for ref in v_refs], axis=0))
-        new_scores = scores_of(queries, fresh_ref[:, columns]) * EXPONENT
-        new_weights = weigh(jnp.where(new_mask, new_scores, MASKED))
-        new_values = fresh_ref[:, span(KV_WIDTH + h * HEAD_SIZE, HEAD_SIZE)]
-        weights = weigh(jnp.where(mask, scores_of(queries, k_all) * EXPONENT, MASKED))
-        dec_acc_ref[h] = product(weights, v_all) + product(new_weights, with_ones(new_values))
         for (start, keys), bias in zip(spans, biases):
-            if keys < tokens:
-                k_part = jnp.concatenate([ref[:keys, columns] for ref in k_refs], axis=0)
-                v_part = with_ones(jnp.concatenate([ref[:keys, columns] for ref in v_refs], axis=0))
-            else:
-                k_part, v_part = k_all, v_all
+            k_part = jnp.concatenate([ref[:keys, columns] for ref in k_refs], axis=0)
+            v_part = with_ones(jnp.concatenate([ref[:keys, columns] for ref in v_refs], axis=0))
             for g in range(0, HEADS_PER_KV, together):
                 queries = stacked_heads(
                     q_ref, slice(start, start + half), first + g * HEAD_SIZE, together
@@ -269,13 +245,15 @@
                 rows = slice(
                     start * HEADS_PER_KV + g * half, start * HEADS_PER_KV + (g + together) * half
                 )
-                acc_ref[h, rows, :] = product(weigh(exponents), v_part)
+                worst_ref[...] = jnp.maximum(
+                    worst_ref[...], jnp.max(peak(exponents), axis=1, keepdims=True)
+                )
+                acc_ref[h, rows, :] = product(jnp.exp2(exponents).astype(jnp.bfloat16), v_part)
 
     each_kv_head(width, step)
 
 
-def middle_kernel(plan, acc_ref, bias_ref, dec_acc_ref, dec_bias_ref, worst_ref, queries_ref, q_ref, k_ref, v_ref, *refs):
-    new_acc_ref, new_dec_acc_ref, new_worst_ref = refs
+def middle_kernel(plan, acc_ref, bias_ref, worst_ref, q_ref, k_ref, v_ref, new_acc_ref, new_worst_ref):
     piece = plan.size - 2
     tokens = q_ref.shape[0]
     half = tokens // 2
@@ -283,10 +261,6 @@
     for h in range(KEY_VALUE_HEADS):
         columns = slice(h * HEAD_SIZE, (h + 1) * HEAD_SIZE)
         keys, values = k_ref[:, columns], with_ones(v_ref[:, columns])
-        queries = stacked_heads(queries_ref, slice(None), h * Q_BLOCK, HEADS_PER_KV)
-        exponents = scores_of(queries, keys) * EXPONENT + dec_bias_ref[piece]
-        worst = jnp.maximum(worst, peak(exponents))
-        new_dec_acc_ref[h] = dec_acc_ref[h] + product(jnp.exp2(exponents).astype(jnp.bfloat16), values)
         for start in (0, half):
             bias = bias_ref[piece, start : start + half, :]
             queries = stacked_heads(q_ref, slice(start, start + half), h * Q_BLOCK, HEADS_PER_KV)
@@ -297,6 +271,47 @@
             new_acc_ref[h, rows, :] = acc_ref[h, rows, :] + product(
                 jnp.exp2(exponents).astype(jnp.bfloat16), values
             )
+    new_worst_ref[...] = worst
+
+
+def first_decode_kernel(plan, pd_size, facts_ref, worst_ref, *refs):
+    width = plan.size
+    k_refs, v_refs, refs = refs[: width - 1], refs[width - 1 : 2 * width - 2], refs[2 * width - 2 :]
+    block_refs, refs = refs[:pd_size], refs[pd_size:]
+    acc_ref, bias_ref, new_worst_ref, queries_ref, fresh_ref, pick_ref, owner_ref = refs
+    tokens = k_refs[0].shape[0]
+    facts = Facts(facts_ref, width)
+    pick_ref[...] = pick_matrix(facts)
+    slot = iota((8, HEAD_SIZE), 0)
+    owner = jnp.zeros_like(slot)
+    for p in range(GROUP_REQUESTS):
+        owner = jnp.where(slot == p, facts.owner[p], owner)
+    owner_ref[...] = owner
+    for s in range(width):
+        bias_ref[s] = jnp.where(
+            request_mask(facts.ends, tokens, facts.source[s : s + 1], width), 0.0, MASKED
+        )
+    rows = picked_rows(facts, pd_size, block_refs)
+    queries_ref[...] = rows[:, :Q_WIDTH]
+    fresh_ref[...] = rows[:, Q_WIDTH:]
+    new_mask = fresh_mask()
+    worst = worst_ref[...]
+    for h in range(KEY_VALUE_HEADS):
+        columns = slice(h * HEAD_SIZE, (h + 1) * HEAD_SIZE)
+        queries = stacked_heads(rows, slice(None), h * Q_BLOCK, HEADS_PER_KV)
+        new_columns = slice(Q_WIDTH + h * HEAD_SIZE, Q_WIDTH + (h + 1) * HEAD_SIZE)
+        exponents = jnp.where(new_mask, scores_of(queries, rows[:, new_columns]) * EXPONENT, MASKED)
+        worst = jnp.maximum(worst, jnp.max(peak(exponents), axis=1, keepdims=True))
+        new_columns = slice(Q_WIDTH + KV_WIDTH + h * HEAD_SIZE, Q_WIDTH + KV_WIDTH + (h + 1) * HEAD_SIZE)
+        acc = product(jnp.exp2(exponents).astype(jnp.bfloat16), with_ones(rows[:, new_columns]))
+        for parts in parts_in(width - 1):
+            k_part = jnp.concatenate([k_refs[s][:, columns] for s in parts], axis=0)
+            v_part = jnp.concatenate([v_refs[s][:, columns] for s in parts], axis=0)
+            bias = jnp.concatenate([bias_ref[s] for s in parts], axis=1)
+            exponents = scores_of(queries, k_part) * EXPONENT + bias
+            worst = jnp.maximum(worst, jnp.max(peak(exponents), axis=1, keepdims=True))
+            acc += product(jnp.exp2(exponents).astype(jnp.bfloat16), with_ones(v_part))
+        acc_ref[h] = acc
     new_worst_ref[...] = worst
 
 
@@ -443,14 +458,44 @@
     )
 
 
-def call_first(plan, facts, maxima, query, blocks, keys, values):
+def call_first(plan, facts, maxima, query, keys, values):
     tokens, width = query.shape[0], plan.size
     rows = HEADS_PER_KV * tokens
-    f32, bf16 = jnp.float32, jnp.bfloat16
     every = (width - 2) * tokens
     shapes = [
-        jax.ShapeDtypeStruct((KEY_VALUE_HEADS, rows, 2 * HEAD_SIZE), f32),
-        jax.ShapeDtypeStruct((width, tokens, tokens), f32),
+        jax.ShapeDtypeStruct((KEY_VALUE_HEADS, rows, 2 * HEAD_SIZE), jnp.float32),
+        jax.ShapeDtypeStruct((width, tokens, tokens), jnp.float32),
+        jax.ShapeDtypeStruct((8, HEAD_SIZE), jnp.float32),
+    ]
+    return pl.pallas_call(
+        lambda *refs: first_kernel(plan, *refs),
+        in_specs=[SMEM] + [VMEM] * (2 + 2 * (width - 2)),
+        out_specs=[VMEM] * len(shapes),
+        out_shape=shapes,
+        compiler_params=pltpu.CompilerParams(vmem_limit_bytes=(28 + width) * MIB),
+        cost_estimate=cost(tokens, every, tokens * every * QUERY_HEADS),
+        name="first_shards",
+    )(facts, maxima, query, *keys, *values)
+
+
+def call_middle(plan, acc, bias, worst, query, key, value):
+    tokens = query.shape[0]
+    return pl.pallas_call(
+        lambda *refs: middle_kernel(plan, *refs),
+        in_specs=[VMEM] * 6,
+        out_specs=[VMEM] * 2,
+        out_shape=[jax.ShapeDtypeStruct(a.shape, a.dtype) for a in (acc, worst)],
+        input_output_aliases={0: 0, 2: 1},
+        compiler_params=pltpu.CompilerParams(vmem_limit_bytes=32 * MIB),
+        cost_estimate=cost(1, 1, 1),
+        name="middle_shard",
+    )(acc, bias, worst, query, key, value)
+
+
+def call_first_decode(plan, facts, worst, keys, values, blocks):
+    tokens, width = keys[0].shape[0], plan.size
+    f32, bf16 = jnp.float32, jnp.bfloat16
+    shapes = [
         jax.ShapeDtypeStruct((KEY_VALUE_HEADS, STACKED, 2 * HEAD_SIZE), f32),
         jax.ShapeDtypeStruct((width, STACKED, tokens), f32),
         jax.ShapeDtypeStruct((8, HEAD_SIZE), f32),
@@ -460,30 +505,14 @@
         jax.ShapeDtypeStruct((8, HEAD_SIZE), jnp.int32),
     ]
     return pl.pallas_call(
-        lambda *refs: first_kernel(plan, len(blocks), *refs),
-        in_specs=[SMEM] + [VMEM] * (2 + len(blocks) + 2 * (width - 2)),
+        lambda *refs: first_decode_kernel(plan, len(blocks), *refs),
+        in_specs=[SMEM] + [VMEM] * (1 + len(blocks) + 2 * (width - 1)),
         out_specs=[VMEM] * len(shapes),
         out_shape=shapes,
         compiler_params=pltpu.CompilerParams(vmem_limit_bytes=(28 + width) * MIB),
-        cost_estimate=cost(tokens, every, tokens * every * QUERY_HEADS),
-        name="first_shards",
-    )(facts, maxima, query, *keys, *values, *blocks)
-
-
-def call_middle(plan, state, query, key, value):
-    acc, bias, dec_acc, dec_bias, worst, queries = state[:6]
-    tokens = query.shape[0]
-    new_acc, new_dec_acc, new_worst = pl.pallas_call(
-        lambda *refs: middle_kernel(plan, *refs),
-        in_specs=[VMEM] * 9,
-        out_specs=[VMEM] * 3,
-        out_shape=[jax.ShapeDtypeStruct(a.shape, a.dtype) for a in (acc, dec_acc, worst)],
-        input_output_aliases={0: 0, 2: 1, 4: 2},
-        compiler_params=pltpu.CompilerParams(vmem_limit_bytes=32 * MIB),
-        cost_estimate=cost(tokens, tokens, tokens * tokens * QUERY_HEADS),
-        name="middle_shard",
-    )(acc, bias, dec_acc, dec_bias, worst, queries, query, key, value)
-    return [new_acc, bias, new_dec_acc, dec_bias, new_worst] + list(state[5:])
+        cost_estimate=cost(1, 1, 1),
+        name="first_decode",
+    )(facts, worst, *keys, *values, *blocks)
 
 
 def call_decode(plan, state, keys, values):
@@ -496,10 +525,10 @@
         compiler_params=pltpu.CompilerParams(vmem_limit_bytes=(28 + width) * MIB),
         cost_estimate=cost(PADDED_ROWS, tokens, PADDED_ROWS * tokens * QUERY_HEADS),
         name="last_shard_decode",
-    )(*state[2:8], *keys, *values)
-
-
-def call_prefill(plan, state, query, keys, values):
+    )(*state[:6], *keys, *values)
+
+
+def call_prefill(plan, acc, bias, worst, query, keys, values):
     tokens, width = query.shape[0], plan.size
     return pl.pallas_call(
         lambda *refs: prefill_kernel(plan, *refs),
@@ -513,7 +542,7 @@
         compiler_params=pltpu.CompilerParams(vmem_limit_bytes=(28 + width) * MIB),
         cost_estimate=cost(tokens, tokens, tokens * tokens * QUERY_HEADS),
         name="last_shard_prefill",
-    )(*state[:2], state[4], query, *keys, *values)
+    )(acc, bias, worst, query, *keys, *values)
 
 
 def start_maxima(*arrays, flops=5 * 10**9):
@@ -562,18 +591,20 @@
             pieces += [up, down]
         chains.append(pieces[: plan.size])
     keys, values = chains
+    own, _ = lax.optimization_barrier((own, (keys[1], values[1])))
     blocks = [own] + [paired(own, k) for k in range(1, pd_size)]
     maxima = start_maxima(keys[1], values[1])
 
-    state = call_first(plan, facts, maxima, prompt_query, blocks, keys[:-2], values[:-2])
-    state = call_middle(plan, state, prompt_query, keys[-2], values[-2])
+    acc, bias, worst = call_first(plan, facts, maxima, prompt_query, keys[:-2], values[:-2])
+    acc, worst = call_middle(plan, acc, bias, worst, prompt_query, keys[-2], values[-2])
+    state = call_first_decode(plan, facts, worst, keys[:-1], values[:-1], blocks)
     outgoing = call_decode(plan, state, keys, values)
     arrived = [outgoing[:DECODE_STEPS]]
     for k in range(1, pd_size):
         arrived.append(paired(outgoing[k * DECODE_STEPS : (k + 1) * DECODE_STEPS], k))
-    pre_out = call_prefill(plan, state, prompt_query, keys, values)
-
-    from_block = state[8][:GROUP_REQUESTS, 0]
+    pre_out = call_prefill(plan, acc, bias, state[2], prompt_query, keys, values)
+
+    from_block = state[6][:GROUP_REQUESTS, 0]
     dec_out = jnp.zeros((GROUP_REQUESTS, DECODE_STEPS, Q_WIDTH), jnp.bfloat16)
     for k in range(pd_size):
         dec_out = jnp.where((from_block == k)[:, None, None], arrived[k][None], dec_out)

time: 38.7 us -> 41.7 us (1.078)
  starting transfers between devices: 14.5 us -> 18 us
  waiting for transfers between devices: 4.92 us -> 4.08 us
    ppermute x6, starting transfers between devices: 10.4 us -> 13.9 us  [step(): lax.ppermute(array, 'tp', self.pairs if up else [(b, a) for a, b in self....]
    pallas_call x1 -> x2, Pallas kernels: 2.93 us -> 3.59 us  [the longest x1 1.97 us: call_first(): pl.pallas_call(lambda *refs: first_kernel(plan, *refs), in_specs=[SMEM] +...]
    ppermute x6, waiting for transfers between devices: 4.67 us -> 4.06 us  [step(): lax.ppermute(array, 'tp', self.pairs if up else [(b, a) for a, b in self....]
    pallas_call x1, Pallas kernels: 2.22 us -> 1.75 us  [call_middle(): pl.pallas_call(lambda *refs: middle_kernel(plan, *refs), in_specs=[VMEM]...]
  transfers between devices with their start and end apart: 12 -> 12, of which waited for: 4 -> 2; matrix products, arithmetic and copies ran while one was open for 3% -> 3% of each run, Pallas kernels for 37% -> 35%
where the time goes in v17:
time: 41.7 us; the launch traced here: 41.5 us
  starting transfers between devices  18 us (43%)
  Pallas kernels  16.6 us (40%)
  waiting for transfers between devices  4.08 us (10%)
  other arithmetic  1.89 us (5%)
  between operations  0.8 us (2%)
    ppermute x6, starting transfers between devices, step(): lax.ppermute(array, 'tp', self.pairs if up else [(b, a) for a, b in self....  13.9 us
    pallas_call x1, Pallas kernels, call_prefill(): pl.pallas_call(lambda *refs: prefill_kernel(plan, *refs), in_specs=[VMEM]...  7.67 us
    ppermute x6, starting transfers between devices, paired(): lax.ppermute(array, 'pd', [(g, g ^ k) for g in range(lax.axis_size('pd'))])  4.07 us
    ppermute x6, waiting for transfers between devices, step(): lax.ppermute(array, 'tp', self.pairs if up else [(b, a) for a, b in self....  4.06 us
    pallas_call x1, Pallas kernels, call_decode(): pl.pallas_call(lambda *refs: decode_kernel(plan, *refs), in_specs=[VMEM]...  2.13 us
    pallas_call x1, Pallas kernels, call_first(): pl.pallas_call(lambda *refs: first_kernel(plan, *refs), in_specs=[SMEM] +...  1.97 us
    pallas_call x1, Pallas kernels, call_middle(): pl.pallas_call(lambda *refs: middle_kernel(plan, *refs), in_specs=[VMEM]...  1.75 us
    pallas_call x1, Pallas kernels, call_first_decode(): pl.pallas_call(lambda *refs: first_decode_kernel(plan, len(blocks), *refs...  1.61 us
  transfers between devices with their start and end apart: 12, of which 2 were waited for; matrix products, arithmetic and copies ran while one was open for 3% of the time, Pallas kernels for 35%

profile of v17, /device:TPU:0, one launch (start us, length us, event | category | flops | bytes accessed | tf_op | source)
XLA Modules:
  0.0 41.5 jit_solution(9377673155599551569)
XLA Ops:
  0.6 3.1 %collective-permute-start = (bf16[128,512]{1,0:T(8,128)(2,1)}, bf16[128,512]{1,0:T(8,128)(2,1)S(1)}, u32[]{:S(2)}, u32[]{:S(2)}) collective-permute-start(bf16[128,512]{1,0:T(8,128)(2,1)} %refs_6_), channel_id=1, source_target_pairs={{0,1},{1,3},{3,2},{2,0},{4,5},{5,7},{7,6},{6,4},{8,9},{9,11},{11,1... | collective-permute-start | bytes 393224 | tf_op jit(solution)/shard_map/ppermute | solution.py:46
  3.7 2.6 %collective-permute-start.1 = (bf16[128,512]{1,0:T(8,128)(2,1)}, bf16[128,512]{1,0:T(8,128)(2,1)S(1)}, u32[]{:S(2)}, u32[]{:S(2)}) collective-permute-start(bf16[128,512]{1,0:T(8,128)(2,1)} %refs_10_.1), channel_id=1, source_target_pairs={{0,1},{1,3},{3,2},{2,0},{4,5},{5,7},{7,6},{6,4},{8,9},{9,11},{11,1... | collective-permute-start | bytes 393224 | tf_op jit(solution)/shard_map/ppermute | solution.py:46
  6.3 0.9 %pad_maximum_fusion = bf16[4,2,5120]{2,1,0:T(2,128)(2,1)S(1)} fusion(bf16[4,2,512]{2,1,0:T(2,128)(2,1)} %param.15, bf16[4,2,512]{2,1,0:T(2,128)(2,1)} %param.14, bf16[4,2,4096]{2,1,0:T(2,128)(2,1)} %param.13), kind=kLoop, calls=%fused_computation.4 | loop fusion | flops 245760 | bytes 163840 | tf_op jit(solution)/shard_map/concatenate | solution.py:579
  7.2 0.0 copy-start.1
  7.3 0.0 copy-start.2
  7.3 1.4 %facts.1.refs_0_ = s32[18]{0:T(128)} custom-call(s32[4,4]{1,0:T(4,128)} %lengths_ref.1, s32[16]{0:T(128)} %slots_ref.1), custom_call_target="tpu_custom_call" | custom-call | flops 5000000000 | tf_op jit(solution)/shard_map/facts/pallas_call | solution.py:126
  8.8 0.0 copy-done.1
  8.8 0.0 copy-start
  8.8 0.0 copy-start.3
  8.8 0.4 collective-permute-start.2
  9.2 0.0 copy-done.2
  9.2 0.2 collective-permute-start.3
  9.4 0.0 collective-permute-done.refs_0_.refs_4_.refs_3_.refs_5_.refs_7_
  9.4 1.9 %collective-permute-done.1.refs_1_.refs_6_.refs_9_.refs_11_ = bf16[128,512]{1,0:T(8,128)(2,1)S(1)} collective-permute-done((bf16[128,512]{1,0:T(8,128)(2,1)}, bf16[128,512]{1,0:T(8,128)(2,1)S(1)}, u32[]{:S(2)}, u32[]{:S(2)}) %collective-permute-start.1) | collective-permute-done | bytes 131104 | tf_op jit(solution)/shard_map/ppermute | solution.py:46
  11.3 0.0 collective-permute-start.4
  11.3 1.5 %collective-permute-start.5 = (bf16[8,5120]{1,0:T(8,128)(2,1)S(1)}, bf16[8,5120]{1,0:T(8,128)(2,1)S(1)}, u32[]{:S(2)}, u32[]{:S(2)}) collective-permute-start(bf16[8,5120]{1,0:T(8,128)(2,1)S(1)} %reshape.39.refs_8_), channel_id=1, source_target_pairs={{0,8},{4,12},{8,0},{12,4},{1,9},{5,13},{9,1},{13,5},{2,10},{6,14},... | collective-permute-start | bytes 245768 | tf_op jit(solution)/shard_map/ppermute | solution.py:564
  12.8 0.3 collective-permute-start.6
  13.2 2.1 %collective-permute-done.2.refs_4_.refs_6_.refs_8_ = bf16[128,512]{1,0:T(8,128)(2,1)S(1)} collective-permute-done((bf16[128,512]{1,0:T(8,128)(2,1)S(1)}, bf16[128,512]{1,0:T(8,128)(2,1)S(1)}, u32[]{:S(2)}, u32[]{:S(2)}) %collective-permute-start.2) | collective-permute-done | bytes 131104 | tf_op jit(solution)/shard_map/ppermute | solution.py:46
  15.3 4.4 %collective-permute-start.7 = (bf16[128,512]{1,0:T(8,128)(2,1)S(1)}, bf16[128,512]{1,0:T(8,128)(2,1)S(1)}, u32[]{:S(2)}, u32[]{:S(2)}) collective-permute-start(bf16[128,512]{1,0:T(8,128)(2,1)S(1)} %collective-permute-done.refs_0_.refs_4_.refs_3_.refs_5_.refs_7_), channel_id=1, source_target_pairs={{0,1},{1,3},{3,2},{2,0},{4,5},{5,7},{7,6},{6,4},{8,9},{9,11},{11,1... | collective-permute-start | bytes 393224 | tf_op jit(solution)/shard_map/ppermute | solution.py:46
  19.7 0.0 collective-permute-done.3.refs_5_.refs_7_.refs_10_.refs_12_
  19.7 3.3 %collective-permute-start.8 = (bf16[128,512]{1,0:T(8,128)(2,1)S(1)}, bf16[128,512]{1,0:T(8,128)(2,1)S(1)}, u32[]{:S(2)}, u32[]{:S(2)}) collective-permute-start(bf16[128,512]{1,0:T(8,128)(2,1)S(1)} %collective-permute-done.1.refs_1_.refs_6_.refs_9_.refs_11_), channel_id=1, source_target_pairs={{0,1},{1,3},{3,2},{2,0},{4,5},{5,7},{7,6},{6,4},{8,9},{9,11},{11,1... | collective-permute-start | bytes 393224 | tf_op jit(solution)/shard_map/ppermute | solution.py:46
  23.0 0.0 copy-done
  23.0 0.0 copy-done.3
  23.0 2.0 %first_shards.1 = (f32[4,1024,256]{2,1,0:T(8,128)S(1)}, f32[4,128,128]{2,1,0:T(8,128)S(1)}, f32[8,128]{1,0:T(8,128)S(1)}) custom-call(s32[18]{0:T(128)S(1)} %copy-done.3, f32[8,128]{1,0:T(8,128)S(1)} %start_maxima.1.refs_1_, bf16[128,4096]{1,0:T(8,128)(2,1)S(1)} %copy-done, bf16[128,512]{1,0:T(8,128)(2,1)S(1)} %copy-done.1, ...), custom_call_target="tpu_custom_call" | custom-call | flops 4294967296 | bytes 2097152 | tf_op jit(solution)/shard_map/first_shards/pallas_call | solution.py:470
  25.0 1.7 %middle_shard.1 = (f32[4,1024,256]{2,1,0:T(8,128)S(1)}, f32[8,128]{1,0:T(8,128)S(1)}) custom-call(f32[4,1024,256]{2,1,0:T(8,128)S(1)} %get-tuple-element.22.refs_0_, f32[4,128,128]{2,1,0:T(8,128)S(1)} %get-tuple-element.23.refs_1_, f32[8,128]{1,0:T(8,128)S(1)} %get-tuple-element.24.refs_2_, ...), custom_call_target="tpu_custom_call", output_to_operand_aliasing={{0}: (0, {}), {1}: (2, {})} | custom-call | flops 131072 | bytes 16384 | tf_op jit(solution)/shard_map/middle_shard/pallas_call | solution.py:483
  26.7 0.0 collective-permute-done.4.refs_9_
  26.7 0.0 collective-permute-done.5.refs_10_
  26.7 0.0 collective-permute-done.6.refs_11_
  26.8 1.6 %first_decode.1 = (f32[4,128,256]{2,1,0:T(8,128)S(1)}, f32[4,128,128]{2,1,0:T(8,128)S(1)}, f32[8,128]{1,0:T(8,128)S(1)}, bf16[16,4096]{1,0:T(8,128)(2,1)S(1)}, b...) custom-call(s32[18]{0:T(128)S(1)} %copy-done.3, ...), custom_call_target="tpu_custom_call" | custom-call | flops 131072 | bytes 16384 | tf_op jit(solution)/shard_map/first_decode/pallas_call | solution.py:507
  28.4 0.1 compare_reduce_fusion.2
  28.5 0.0 collective-permute-done.7.refs_7_.refs_9_
  28.5 0.0 collective-permute-done.8.refs_11_.refs_13_
  28.5 2.1 %last_shard_decode.1 = bf16[16,4096]{1,0:T(8,128)(2,1)S(1)} custom-call(f32[4,128,256]{2,1,0:T(8,128)S(1)} %get-tuple-element.33.refs_0_, f32[4,128,128]{2,1,0:T(8,128)S(1)} %get-tuple-element.34.refs_1_, f32[8,128]{1,0:T(8,128)S(1)} %get-tuple-element.31.refs_2_, bf16[16,4096]{1,0:T(8,128)(2,1)S(1)} %get-tuple-element.35.refs_3_, ...), custom_call_target="tpu_custom_call" | custom-call | flops 268435456 | bytes 262144 | tf_op jit(solution)/shard_map/last_shard_decode/pallas_call | solution.py:520
  30.7 0.1 fusion
  30.7 1.6 %collective-permute-start.10 = (bf16[2,4096]{1,0:T(2,128)(2,1)S(1)}, bf16[2,4096]{1,0:T(2,128)(2,1)S(1)}, u32[]{:S(2)}, u32[]{:S(2)}) collective-permute-start(bf16[2,4096]{1,0:T(2,128)(2,1)S(1)} %get-tuple-element.45), channel_id=1, source_target_pairs={{0,8},{4,12},{8,0},{12,4},{1,9},{5,13},{9,1},{13,5},{2,10},{6,14},... | collective-permute-start | bytes 49160 | tf_op jit(solution)/shard_map/ppermute | solution.py:564
  32.3 0.0 collective-permute-start.11
  32.3 0.6 %collective-permute-start.9 = (bf16[2,4096]{1,0:T(2,128)(2,1)S(1)}, bf16[2,4096]{1,0:T(2,128)(2,1)S(1)}, u32[]{:S(2)}, u32[]{:S(2)}) collective-permute-start(bf16[2,4096]{1,0:T(2,128)(2,1)S(1)} %get-tuple-element.42), channel_id=1, source_target_pairs={{0,12},{4,8},{8,4},{12,0},{1,13},{5,9},{9,5},{13,1},{2,14},{6,10},... | collective-permute-start | bytes 49160 | tf_op jit(solution)/shard_map/ppermute | solution.py:564
  32.9 7.7 %last_shard_prefill.1 = bf16[128,4096]{1,0:T(8,128)(2,1)} custom-call(f32[4,1024,256]{2,1,0:T(8,128)S(1)} %get-tuple-element.27.refs_0_, f32[4,128,128]{2,1,0:T(8,128)S(1)} %get-tuple-element.23.refs_1_, f32[8,128]{1,0:T(8,128)S(1)} %get-tuple-element.31.refs_2_, bf16[128,4096]{1,0:T(8,128)(2,1)S(1)} %copy-done, bf16[128,512]{1,0:T(8,128)(2,1)S(1)} %copy-done.1, ...), custom_call_target="tpu_custom_call" | custom-call | flops 2147483648 | bytes 2097152 | tf_op jit(solution)/shard_map/last_shard_prefill/pallas_call | solution.py:533
  40.6 0.0 collective-permute-done.10
  40.6 0.0 collective-permute-done.11
  40.6 0.0 collective-permute-done.9
  40.7 0.8 %broadcast_select_fusion.2 = bf16[4,2,4096]{2,1,0:T(2,128)(2,1)} fusion(pred[4]{0:T(512)(128)(4,1)S(1)} %get-tuple-element.41, pred[4]{0:T(512)(128)(4,1)S(1)} %get-tuple-element.40, pred[4]{0:T(512)(128)(4,1)S(1)} %get-tuple-element.39, pred[4]{0:T(512)(128)(4,1)S(1)} %get-tuple-element.38, bf16[2,4096]{1,0:T(2,128)(2,1)S(1)} %get-tuple-element.43, ...), kind=kLoop, calls=%fused_computation.2 | loop fusion | flops 131072 | bytes 131088 | tf_op jit(solution)/shard_map/jit(_where)/select_n | solution.py:610
  (2 shorter events, 0.0 us)
Async XLA Ops:
  0.6 8.7 %collective-permute-start = (bf16[128,512]{1,0:T(8,128)(2,1)}, bf16[128,512]{1,0:T(8,128)(2,1)S(1)}, u32[]{:S(2)}, u32[]{:S(2)}) collective-permute-start(bf16[128,512]{1,0:T(8,128)(2,1)} %refs_6_), channel_id=1, source_target_pairs={{0,1},{1,3},{3,2},{2,0},{4,5},{5,7},{7,6},{6,4},{8,9},{9,11},{11,1... | collective-permute-start | bytes 393224 | tf_op jit(solution)/shard_map/ppermute | solution.py:46
  3.7 7.6 %collective-permute-start.1 = (bf16[128,512]{1,0:T(8,128)(2,1)}, bf16[128,512]{1,0:T(8,128)(2,1)S(1)}, u32[]{:S(2)}, u32[]{:S(2)}) collective-permute-start(bf16[128,512]{1,0:T(8,128)(2,1)} %refs_10_.1), channel_id=1, source_target_pairs={{0,1},{1,3},{3,2},{2,0},{4,5},{5,7},{7,6},{6,4},{8,9},{9,11},{11,1... | collective-permute-start | bytes 393224 | tf_op jit(solution)/shard_map/ppermute | solution.py:46
  7.2 1.5 %copy-start.1 = (bf16[128,512]{1,0:T(8,128)(2,1)S(1)}, bf16[128,512]{1,0:T(8,128)(2,1)}, u32[]{:S(2)}) copy-start(bf16[128,512]{1,0:T(8,128)(2,1)} %refs_6_) | copy-start | bytes 393220
  7.3 1.9 %copy-start.2 = (bf16[128,512]{1,0:T(8,128)(2,1)S(1)}, bf16[128,512]{1,0:T(8,128)(2,1)}, u32[]{:S(2)}) copy-start(bf16[128,512]{1,0:T(8,128)(2,1)} %refs_10_.1) | copy-start | bytes 393220
  8.8 14.2 %copy-start = (bf16[128,4096]{1,0:T(8,128)(2,1)S(1)}, bf16[128,4096]{1,0:T(8,128)(2,1)}, u32[]{:S(2)}) copy-start(bf16[128,4096]{1,0:T(8,128)(2,1)} %refs_3_.4) | copy-start | bytes 3145732
  8.8 14.2 %copy-start.3 = (s32[18]{0:T(128)S(1)}, s32[18]{0:T(128)}, u32[]{:S(2)}) copy-start(s32[18]{0:T(128)} %facts.1.refs_0_) | copy-start | bytes 220
  8.8 6.5 %collective-permute-start.2 = (bf16[128,512]{1,0:T(8,128)(2,1)S(1)}, bf16[128,512]{1,0:T(8,128)(2,1)S(1)}, u32[]{:S(2)}, u32[]{:S(2)}) collective-permute-start(bf16[128,512]{1,0:T(8,128)(2,1)S(1)} %copy-done.1), channel_id=1, source_target_pairs={{1,0},{3,1},{2,3},{0,2},{5,4},{7,5},{6,7},{4,6},{9,8},{11,9},{10,1... | collective-permute-start | bytes 393224 | tf_op jit(solution)/shard_map/ppermute | solution.py:46
  9.2 10.5 %collective-permute-start.3 = (bf16[128,512]{1,0:T(8,128)(2,1)S(1)}, bf16[128,512]{1,0:T(8,128)(2,1)S(1)}, u32[]{:S(2)}, u32[]{:S(2)}) collective-permute-start(bf16[128,512]{1,0:T(8,128)(2,1)S(1)} %copy-done.2), channel_id=1, source_target_pairs={{1,0},{3,1},{2,3},{0,2},{5,4},{7,5},{6,7},{4,6},{9,8},{11,9},{10,1... | collective-permute-start | bytes 393224 | tf_op jit(solution)/shard_map/ppermute | solution.py:46
  11.3 15.4 %collective-permute-start.4 = (bf16[8,5120]{1,0:T(8,128)(2,1)S(1)}, bf16[8,5120]{1,0:T(8,128)(2,1)S(1)}, u32[]{:S(2)}, u32[]{:S(2)}) collective-permute-start(bf16[8,5120]{1,0:T(8,128)(2,1)S(1)} %reshape.39.refs_8_), channel_id=1, source_target_pairs={{0,4},{4,0},{8,12},{12,8},{1,5},{5,1},{9,13},{13,9},{2,6},{6,2},{1... | collective-permute-start | bytes 245768 | tf_op jit(solution)/shard_map/ppermute | solution.py:564
  11.3 15.4 %collective-permute-start.5 = (bf16[8,5120]{1,0:T(8,128)(2,1)S(1)}, bf16[8,5120]{1,0:T(8,128)(2,1)S(1)}, u32[]{:S(2)}, u32[]{:S(2)}) collective-permute-start(bf16[8,5120]{1,0:T(8,128)(2,1)S(1)} %reshape.39.refs_8_), channel_id=1, source_target_pairs={{0,8},{4,12},{8,0},{12,4},{1,9},{5,13},{9,1},{13,5},{2,10},{6,14},... | collective-permute-start | bytes 245768 | tf_op jit(solution)/shard_map/ppermute | solution.py:564
  12.8 13.9 %collective-permute-start.6 = (bf16[8,5120]{1,0:T(8,128)(2,1)S(1)}, bf16[8,5120]{1,0:T(8,128)(2,1)S(1)}, u32[]{:S(2)}, u32[]{:S(2)}) collective-permute-start(bf16[8,5120]{1,0:T(8,128)(2,1)S(1)} %reshape.39.refs_8_), channel_id=1, source_target_pairs={{0,12},{4,8},{8,4},{12,0},{1,13},{5,9},{9,5},{13,1},{2,14},{6,10},... | collective-permute-start | bytes 245768 | tf_op jit(solution)/shard_map/ppermute | solution.py:564
  15.3 13.2 %collective-permute-start.7 = (bf16[128,512]{1,0:T(8,128)(2,1)S(1)}, bf16[128,512]{1,0:T(8,128)(2,1)S(1)}, u32[]{:S(2)}, u32[]{:S(2)}) collective-permute-start(bf16[128,512]{1,0:T(8,128)(2,1)S(1)} %collective-permute-done.refs_0_.refs_4_.refs_3_.refs_5_.refs_7_), channel_id=1, source_target_pairs={{0,1},{1,3},{3,2},{2,0},{4,5},{5,7},{7,6},{6,4},{8,9},{9,11},{11,1... | collective-permute-start | bytes 393224 | tf_op jit(solution)/shard_map/ppermute | solution.py:46
  19.7 8.8 %collective-permute-start.8 = (bf16[128,512]{1,0:T(8,128)(2,1)S(1)}, bf16[128,512]{1,0:T(8,128)(2,1)S(1)}, u32[]{:S(2)}, u32[]{:S(2)}) collective-permute-start(bf16[128,512]{1,0:T(8,128)(2,1)S(1)} %collective-permute-done.1.refs_1_.refs_6_.refs_9_.refs_11_), channel_id=1, source_target_pairs={{0,1},{1,3},{3,2},{2,0},{4,5},{5,7},{7,6},{6,4},{8,9},{9,11},{11,1... | collective-permute-start | bytes 393224 | tf_op jit(solution)/shard_map/ppermute | solution.py:46
  30.7 9.9 %collective-permute-start.10 = (bf16[2,4096]{1,0:T(2,128)(2,1)S(1)}, bf16[2,4096]{1,0:T(2,128)(2,1)S(1)}, u32[]{:S(2)}, u32[]{:S(2)}) collective-permute-start(bf16[2,4096]{1,0:T(2,128)(2,1)S(1)} %get-tuple-element.45), channel_id=1, source_target_pairs={{0,8},{4,12},{8,0},{12,4},{1,9},{5,13},{9,1},{13,5},{2,10},{6,14},... | collective-permute-start | bytes 49160 | tf_op jit(solution)/shard_map/ppermute | solution.py:564
  32.3 8.3 %collective-permute-start.11 = (bf16[2,4096]{1,0:T(2,128)(2,1)S(1)}, bf16[2,4096]{1,0:T(2,128)(2,1)S(1)}, u32[]{:S(2)}, u32[]{:S(2)}) collective-permute-start(bf16[2,4096]{1,0:T(2,128)(2,1)S(1)} %get-tuple-element.44), channel_id=1, source_target_pairs={{0,4},{4,0},{8,12},{12,8},{1,5},{5,1},{9,13},{13,9},{2,6},{6,2},{1... | collective-permute-start | bytes 49160 | tf_op jit(solution)/shard_map/ppermute | solution.py:564
  32.3 8.4 %collective-permute-start.9 = (bf16[2,4096]{1,0:T(2,128)(2,1)S(1)}, bf16[2,4096]{1,0:T(2,128)(2,1)S(1)}, u32[]{:S(2)}, u32[]{:S(2)}) collective-permute-start(bf16[2,4096]{1,0:T(2,128)(2,1)S(1)} %get-tuple-element.42), channel_id=1, source_target_pairs={{0,12},{4,8},{8,4},{12,0},{1,13},{5,9},{9,5},{13,1},{2,14},{6,10},... | collective-permute-start | bytes 49160 | tf_op jit(solution)/shard_map/ppermute | solution.py:564

commit v18 on v14

--- a/solution.py
+++ b/solution.py
@@ -208,13 +208,13 @@
 
 def first_kernel(plan, pd_size, facts_ref, maxima_ref, q_ref, *refs):
     width = plan.size
-    k_refs, v_refs, refs = refs[: width - 2], refs[width - 2 : 2 * width - 4], refs[2 * width - 4 :]
+    k_refs, v_refs, refs = refs[:1], refs[1:2], refs[2:]
     block_refs, refs = refs[:pd_size], refs[pd_size:]
     acc_ref, bias_ref, dec_acc_ref, dec_bias_ref, worst_ref, queries_ref, fresh_ref, pick_ref, owner_ref = refs
     tokens = q_ref.shape[0]
     half = tokens // 2
     facts = Facts(facts_ref, width)
-    sources = facts.source[:-2]
+    sources = facts.source[:1]
     pick_ref[...] = pick_matrix(facts)
     slot = iota((8, HEAD_SIZE), 0)
     owner = jnp.zeros_like(slot)
@@ -274,29 +274,38 @@
     each_kv_head(width, step)
 
 
-def middle_kernel(plan, acc_ref, bias_ref, dec_acc_ref, dec_bias_ref, worst_ref, queries_ref, q_ref, k_ref, v_ref, *refs):
+def middle_kernel(plan, acc_ref, bias_ref, dec_acc_ref, dec_bias_ref, worst_ref, queries_ref, q_ref, *refs):
+    count = plan.size - 2
+    k_refs, v_refs, refs = refs[:count], refs[count : 2 * count], refs[2 * count :]
     new_acc_ref, new_dec_acc_ref, new_worst_ref = refs
-    piece = plan.size - 2
     tokens = q_ref.shape[0]
     half = tokens // 2
     worst = worst_ref[...]
     for h in range(KEY_VALUE_HEADS):
         columns = slice(h * HEAD_SIZE, (h + 1) * HEAD_SIZE)
-        keys, values = k_ref[:, columns], with_ones(v_ref[:, columns])
-        queries = stacked_heads(queries_ref, slice(None), h * Q_BLOCK, HEADS_PER_KV)
-        exponents = scores_of(queries, keys) * EXPONENT + dec_bias_ref[piece]
-        worst = jnp.maximum(worst, peak(exponents))
-        new_dec_acc_ref[h] = dec_acc_ref[h] + product(jnp.exp2(exponents).astype(jnp.bfloat16), values)
-        for start in (0, half):
-            bias = bias_ref[piece, start : start + half, :]
-            queries = stacked_heads(q_ref, slice(start, start + half), h * Q_BLOCK, HEADS_PER_KV)
-            scores = scores_of(queries, keys).reshape(HEADS_PER_KV, half, tokens)
-            exponents = (scores * EXPONENT + bias[None]).reshape(HEADS_PER_KV * half, tokens)
-            worst = jnp.maximum(worst, peak(exponents))
-            rows = slice(start * HEADS_PER_KV, (start + half) * HEADS_PER_KV)
-            new_acc_ref[h, rows, :] = acc_ref[h, rows, :] + product(
+        for parts in parts_in(count):
+            keys = jnp.concatenate([k_refs[s][:, columns] for s in parts], axis=0)
+            values = with_ones(jnp.concatenate([v_refs[s][:, columns] for s in parts], axis=0))
+            old_acc_ref, old_dec_acc_ref = acc_ref, dec_acc_ref
+            if parts[0] > 0:
+                old_acc_ref, old_dec_acc_ref = new_acc_ref, new_dec_acc_ref
+            queries = stacked_heads(queries_ref, slice(None), h * Q_BLOCK, HEADS_PER_KV)
+            bias = jnp.concatenate([dec_bias_ref[s + 1] for s in parts], axis=1)
+            exponents = scores_of(queries, keys) * EXPONENT + bias
+            worst = jnp.maximum(worst, jnp.max(peak(exponents), axis=1, keepdims=True))
+            new_dec_acc_ref[h] = old_dec_acc_ref[h] + product(
                 jnp.exp2(exponents).astype(jnp.bfloat16), values
             )
+            for start in (0, half):
+                bias = jnp.concatenate([bias_ref[s + 1, start : start + half, :] for s in parts], axis=1)
+                queries = stacked_heads(q_ref, slice(start, start + half), h * Q_BLOCK, HEADS_PER_KV)
+                scores = scores_of(queries, keys).reshape(HEADS_PER_KV, half, bias.shape[1])
+                exponents = (scores * EXPONENT + bias[None]).reshape(HEADS_PER_KV * half, bias.shape[1])
+                worst = jnp.maximum(worst, jnp.max(peak(exponents), axis=1, keepdims=True))
+                rows = slice(start * HEADS_PER_KV, (start + half) * HEADS_PER_KV)
+                new_acc_ref[h, rows, :] = old_acc_ref[h, rows, :] + product(
+                    jnp.exp2(exponents).astype(jnp.bfloat16), values
+                )
     new_worst_ref[...] = worst
 
 
@@ -447,7 +456,7 @@
     tokens, width = query.shape[0], plan.size
     rows = HEADS_PER_KV * tokens
     f32, bf16 = jnp.float32, jnp.bfloat16
-    every = (width - 2) * tokens
+    every = tokens
     shapes = [
         jax.ShapeDtypeStruct((KEY_VALUE_HEADS, rows, 2 * HEAD_SIZE), f32),
         jax.ShapeDtypeStruct((width, tokens, tokens), f32),
@@ -461,7 +470,7 @@
     ]
     return pl.pallas_call(
         lambda *refs: first_kernel(plan, len(blocks), *refs),
-        in_specs=[SMEM] + [VMEM] * (2 + len(blocks) + 2 * (width - 2)),
+        in_specs=[SMEM] + [VMEM] * (4 + len(blocks)),
         out_specs=[VMEM] * len(shapes),
         out_shape=shapes,
         compiler_params=pltpu.CompilerParams(vmem_limit_bytes=(28 + width) * MIB),
@@ -470,19 +479,19 @@
     )(facts, maxima, query, *keys, *values, *blocks)
 
 
-def call_middle(plan, state, query, key, value):
+def call_middle(plan, state, query, keys, values):
     acc, bias, dec_acc, dec_bias, worst, queries = state[:6]
     tokens = query.shape[0]
     new_acc, new_dec_acc, new_worst = pl.pallas_call(
         lambda *refs: middle_kernel(plan, *refs),
-        in_specs=[VMEM] * 9,
+        in_specs=[VMEM] * (7 + 2 * len(keys)),
         out_specs=[VMEM] * 3,
         out_shape=[jax.ShapeDtypeStruct(a.shape, a.dtype) for a in (acc, dec_acc, worst)],
         input_output_aliases={0: 0, 2: 1, 4: 2},
         compiler_params=pltpu.CompilerParams(vmem_limit_bytes=32 * MIB),
         cost_estimate=cost(tokens, tokens, tokens * tokens * QUERY_HEADS),
         name="middle_shard",
-    )(acc, bias, dec_acc, dec_bias, worst, queries, query, key, value)
+    )(acc, bias, dec_acc, dec_bias, worst, queries, query, *keys, *values)
     return [new_acc, bias, new_dec_acc, dec_bias, new_worst] + list(state[5:])
 
 
@@ -554,19 +563,19 @@
     prompt_key, decoded_query = lax.optimization_barrier((prompt_key, decoded_query))
     later_key, later_value, own, facts = lax.optimization_barrier((prompt_key, prompt_value, own, facts))
     chains = []
-    for up, down in ((prompt_key, later_key), (prompt_value, later_value)):
-        pieces = [up]
+    for first, later, way in ((prompt_key, later_key, True), (prompt_value, later_value, False)):
+        pieces = [first]
         for d in range(1, plan.size // 2 + 1):
-            up = plan.step(up, True)
-            down = plan.step(down, False) if 2 * d < plan.size else None
-            pieces += [up, down]
-        chains.append(pieces[: plan.size])
+            first = plan.step(first, way)
+            later = plan.step(later, not way) if 2 * d < plan.size else None
+            pieces += [first, later] if way else [later, first]
+        chains.append(pieces[: plan.size - 1] + [first])
     keys, values = chains
     blocks = [own] + [paired(own, k) for k in range(1, pd_size)]
-    maxima = start_maxima(keys[1], values[1])
-
-    state = call_first(plan, facts, maxima, prompt_query, blocks, keys[:-2], values[:-2])
-    state = call_middle(plan, state, prompt_query, keys[-2], values[-2])
+    maxima = start_maxima(keys[1], values[2])
+
+    state = call_first(plan, facts, maxima, prompt_query, blocks, keys[:1], values[:1])
+    state = call_middle(plan, state, prompt_query, keys[1:-1], values[1:-1])
     outgoing = call_decode(plan, state, keys, values)
     arrived = [outgoing[:DECODE_STEPS]]
     for k in range(1, pd_size):

time: 38.7 us -> 38.1 us (0.984)
  Pallas kernels: 16.3 us -> 15.7 us
  waiting for transfers between devices: 4.92 us -> 4.49 us
  starting transfers between devices: 14.5 us -> 14.9 us
  transfers between devices with their start and end apart: 12 -> 12, of which waited for: 4 -> 4; matrix products, arithmetic and copies ran while one was open for 3% -> 3% of each run, Pallas kernels for 37% -> 36%
where the time goes in v18:
time: 38.1 us; the launch traced here: 37.9 us
  Pallas kernels  15.7 us (41%)
  starting transfers between devices  14.9 us (39%)
  waiting for transfers between devices  4.49 us (12%)
  other arithmetic  1.89 us (5%)
  between operations  0.76 us (2%)
    ppermute x6, starting transfers between devices, step(): lax.ppermute(array, 'tp', self.pairs if up else [(b, a) for a, b in self....  10.7 us
    pallas_call x1, Pallas kernels, call_prefill(): pl.pallas_call(lambda *refs: prefill_kernel(plan, *refs), in_specs=[VMEM]...  7.62 us
    ppermute x6, waiting for transfers between devices, step(): lax.ppermute(array, 'tp', self.pairs if up else [(b, a) for a, b in self....  4.47 us
    ppermute x6, starting transfers between devices, paired(): lax.ppermute(array, 'pd', [(g, g ^ k) for g in range(lax.axis_size('pd'))])  4.17 us
    pallas_call x1, Pallas kernels, call_first(): pl.pallas_call(lambda *refs: first_kernel(plan, len(blocks), *refs), in_s...  2.67 us
    pallas_call x1, Pallas kernels, call_decode(): pl.pallas_call(lambda *refs: decode_kernel(plan, *refs), in_specs=[VMEM]...  2.13 us
    pallas_call x1, Pallas kernels, call_middle(): pl.pallas_call(lambda *refs: middle_kernel(plan, *refs), in_specs=[VMEM]...  1.9 us
    pallas_call x1, Pallas kernels, facts_row(): pl.pallas_call(kernel, in_specs=[SMEM, SMEM], out_specs=SMEM, out_shape=j...  1.43 us
  transfers between devices with their start and end apart: 12, of which 4 were waited for; matrix products, arithmetic and copies ran while one was open for 3% of the time, Pallas kernels for 36%

profile of v18, /device:TPU:0, one launch (start us, length us, event | category | flops | bytes accessed | tf_op | source)
XLA Modules:
  0.0 37.9 jit_solution(4668900602685871995)
XLA Ops:
  0.6 3.1 %collective-permute-start = (bf16[128,512]{1,0:T(8,128)(2,1)}, bf16[128,512]{1,0:T(8,128)(2,1)S(1)}, u32[]{:S(2)}, u32[]{:S(2)}) collective-permute-start(bf16[128,512]{1,0:T(8,128)(2,1)} %refs_6_.2), channel_id=1, source_target_pairs={{0,1},{1,3},{3,2},{2,0},{4,5},{5,7},{7,6},{6,4},{8,9},{9,11},{11,1... | collective-permute-start | bytes 393224 | tf_op jit(solution)/shard_map/ppermute | solution.py:46
  3.7 1.1 %collective-permute-start.1 = (bf16[128,512]{1,0:T(8,128)(2,1)}, bf16[128,512]{1,0:T(8,128)(2,1)S(1)}, u32[]{:S(2)}, u32[]{:S(2)}) collective-permute-start(bf16[128,512]{1,0:T(8,128)(2,1)} %refs_10_.1), channel_id=1, source_target_pairs={{1,0},{3,1},{2,3},{0,2},{5,4},{7,5},{6,7},{4,6},{9,8},{11,9},{10,1... | collective-permute-start | bytes 393224 | tf_op jit(solution)/shard_map/ppermute | solution.py:46
  4.8 0.9 %pad_maximum_fusion = bf16[4,2,5120]{2,1,0:T(2,128)(2,1)S(1)} fusion(bf16[4,2,512]{2,1,0:T(2,128)(2,1)} %param.15, bf16[4,2,512]{2,1,0:T(2,128)(2,1)} %param.14, bf16[4,2,4096]{2,1,0:T(2,128)(2,1)} %param.13), kind=kLoop, calls=%fused_computation.4 | loop fusion | flops 245760 | bytes 163840 | tf_op jit(solution)/shard_map/concatenate | solution.py:559
  5.7 0.0 copy-start
  5.7 0.0 copy-start.1
  5.8 1.4 %facts.1.refs_0_ = s32[18]{0:T(128)} custom-call(s32[4,4]{1,0:T(4,128)} %lengths_ref.1, s32[16]{0:T(128)} %slots_ref.1), custom_call_target="tpu_custom_call" | custom-call | flops 5000000000 | tf_op jit(solution)/shard_map/facts/pallas_call | solution.py:126
  7.2 0.0 copy-start.2
  7.3 0.0 copy-start.3
  7.3 0.1 collective-permute-start.2
  7.3 1.8 %collective-permute-start.3 = (bf16[8,5120]{1,0:T(8,128)(2,1)S(1)}, bf16[8,5120]{1,0:T(8,128)(2,1)S(1)}, u32[]{:S(2)}, u32[]{:S(2)}) collective-permute-start(bf16[8,5120]{1,0:T(8,128)(2,1)S(1)} %reshape.39.refs_5_), channel_id=1, source_target_pairs={{0,8},{4,12},{8,0},{12,4},{1,9},{5,13},{9,1},{13,5},{2,10},{6,14},... | collective-permute-start | bytes 245768 | tf_op jit(solution)/shard_map/ppermute | solution.py:544
  9.2 0.1 collective-permute-start.4
  9.2 0.0 collective-permute-done.refs_0_.refs_7_.refs_5_
  9.2 0.0 copy-done
  9.2 1.9 %collective-permute-start.5 = (bf16[128,512]{1,0:T(8,128)(2,1)S(1)}, bf16[128,512]{1,0:T(8,128)(2,1)S(1)}, u32[]{:S(2)}, u32[]{:S(2)}) collective-permute-start(bf16[128,512]{1,0:T(8,128)(2,1)S(1)} %copy-done), channel_id=1, source_target_pairs={{1,0},{3,1},{2,3},{0,2},{5,4},{7,5},{6,7},{4,6},{9,8},{11,9},{10,1... | collective-permute-start | bytes 393224 | tf_op jit(solution)/shard_map/ppermute | solution.py:46
  11.2 0.1 collective-permute-done.1.refs_1_.refs_10_.refs_12_
  11.2 0.0 copy-done.1
  11.2 1.7 %collective-permute-start.6 = (bf16[128,512]{1,0:T(8,128)(2,1)S(1)}, bf16[128,512]{1,0:T(8,128)(2,1)S(1)}, u32[]{:S(2)}, u32[]{:S(2)}) collective-permute-start(bf16[128,512]{1,0:T(8,128)(2,1)S(1)} %copy-done.1), channel_id=1, source_target_pairs={{0,1},{1,3},{3,2},{2,0},{4,5},{5,7},{7,6},{6,4},{8,9},{9,11},{11,1... | collective-permute-start | bytes 393224 | tf_op jit(solution)/shard_map/ppermute | solution.py:46
  13.0 0.0 collective-permute-done.2.refs_6_
  13.0 2.5 %collective-permute-start.7 = (bf16[128,512]{1,0:T(8,128)(2,1)S(1)}, bf16[128,512]{1,0:T(8,128)(2,1)S(1)}, u32[]{:S(2)}, u32[]{:S(2)}) collective-permute-start(bf16[128,512]{1,0:T(8,128)(2,1)S(1)} %collective-permute-done.refs_0_.refs_7_.refs_5_), channel_id=1, source_target_pairs={{0,1},{1,3},{3,2},{2,0},{4,5},{5,7},{7,6},{6,4},{8,9},{9,11},{11,1... | collective-permute-start | bytes 393224 | tf_op jit(solution)/shard_map/ppermute | solution.py:46
  15.5 0.0 collective-permute-done.3.refs_7_
  15.5 0.4 collective-permute-start.8
  15.9 0.0 collective-permute-done.4.refs_8_
  15.9 0.0 copy-done.2
  15.9 0.0 copy-done.3
  15.9 2.7 %first_shards.1 = (f32[4,1024,256]{2,1,0:T(8,128)S(1)}, f32[4,128,128]{2,1,0:T(8,128)S(1)}, f32[4,128,256]{2,1,0:T(8,128)S(1)}, f32[4,128,128]{2,1,0:T(8,128)S(1...) custom-call(s32[18]{0:T(128)S(1)} %copy-done.3, ...), custom_call_target="tpu_custom_call" | custom-call | flops 2147483648 | bytes 2097152 | tf_op jit(solution)/shard_map/first_shards/pallas_call | solution.py:471
  18.6 0.0 collective-permute-done.5.refs_8_.refs_6_
  18.6 2.4 %collective-permute-done.6.refs_9_.refs_11_ = bf16[128,512]{1,0:T(8,128)(2,1)S(1)} collective-permute-done((bf16[128,512]{1,0:T(8,128)(2,1)S(1)}, bf16[128,512]{1,0:T(8,128)(2,1)S(1)}, u32[]{:S(2)}, u32[]{:S(2)}) %collective-permute-start.6) | collective-permute-done | bytes 131104 | tf_op jit(solution)/shard_map/ppermute | solution.py:46
  21.0 1.9 %middle_shard.1 = (f32[4,1024,256]{2,1,0:T(8,128)S(1)}, f32[4,128,256]{2,1,0:T(8,128)S(1)}, f32[8,128]{1,0:T(8,128)S(1)}) custom-call(f32[4,1024,256]{2,1,0:T(8,128)S(1)} %get-tuple-element.22.refs_0_, f32[4,128,128]{2,1,0:T(8,128)S(1)} %get-tuple-element.23.refs_1_, ...), custom_call_target="tpu_custom_call", output_to_operand_aliasing={{0}: (0, {}), {1}: (2, {}), {2}: (4, {})} | custom-call | flops 2147483648 | bytes 2097152 | tf_op jit(solution)/shard_map/middle_shard/pallas_call | solution.py:485
  22.9 0.1 compare_reduce_fusion.2
  23.1 1.8 %collective-permute-done.7.refs_7_.refs_9_ = bf16[128,512]{1,0:T(8,128)(2,1)S(1)} collective-permute-done((bf16[128,512]{1,0:T(8,128)(2,1)S(1)}, bf16[128,512]{1,0:T(8,128)(2,1)S(1)}, u32[]{:S(2)}, u32[]{:S(2)}) %collective-permute-start.7) | collective-permute-done | bytes 131104 | tf_op jit(solution)/shard_map/ppermute | solution.py:46
  24.8 0.2 collective-permute-done.8.refs_11_.refs_13_
  25.1 2.1 %last_shard_decode.1 = bf16[16,4096]{1,0:T(8,128)(2,1)S(1)} custom-call(f32[4,128,256]{2,1,0:T(8,128)S(1)} %get-tuple-element.33.refs_0_, f32[4,128,128]{2,1,0:T(8,128)S(1)} %get-tuple-element.25.refs_3_.refs_1_, f32[8,128]{1,0:T(8,128)S(1)} %get-tuple-element.31.refs_2_, bf16[16,4096]{1,0:T(8,128)(2,1)S(1)} %get-tuple-element.27.refs_5_.refs_3_, ...), custom_call_target="tpu_custom_call" | custom-call | flops 268435456 | bytes 262144 | tf_op jit(solution)/shard_map/last_shard_decode/pallas_call | solution.py:500
  27.2 0.1 fusion
  27.3 1.6 %collective-permute-start.10 = (bf16[2,4096]{1,0:T(2,128)(2,1)S(1)}, bf16[2,4096]{1,0:T(2,128)(2,1)S(1)}, u32[]{:S(2)}, u32[]{:S(2)}) collective-permute-start(bf16[2,4096]{1,0:T(2,128)(2,1)S(1)} %get-tuple-element.43), channel_id=1, source_target_pairs={{0,8},{4,12},{8,0},{12,4},{1,9},{5,13},{9,1},{13,5},{2,10},{6,14},... | collective-permute-start | bytes 49160 | tf_op jit(solution)/shard_map/ppermute | solution.py:544
  28.8 0.0 collective-permute-start.11
  28.8 0.6 %collective-permute-start.9 = (bf16[2,4096]{1,0:T(2,128)(2,1)S(1)}, bf16[2,4096]{1,0:T(2,128)(2,1)S(1)}, u32[]{:S(2)}, u32[]{:S(2)}) collective-permute-start(bf16[2,4096]{1,0:T(2,128)(2,1)S(1)} %get-tuple-element.40), channel_id=1, source_target_pairs={{0,12},{4,8},{8,4},{12,0},{1,13},{5,9},{9,5},{13,1},{2,14},{6,10},... | collective-permute-start | bytes 49160 | tf_op jit(solution)/shard_map/ppermute | solution.py:544
  29.5 7.6 %last_shard_prefill.1 = bf16[128,4096]{1,0:T(8,128)(2,1)} custom-call(f32[4,1024,256]{2,1,0:T(8,128)S(1)} %get-tuple-element.30.refs_0_, f32[4,128,128]{2,1,0:T(8,128)S(1)} %get-tuple-element.23.refs_1_, f32[8,128]{1,0:T(8,128)S(1)} %get-tuple-element.31.refs_2_, bf16[128,4096]{1,0:T(8,128)(2,1)S(1)} %copy-done.2, bf16[128,512]{1,0:T(8,128)(2,1)S(1)} %copy-done, ...), custom_call_target="tpu_custom_call" | custom-call | flops 2147483648 | bytes 2097152 | tf_op jit(solution)/shard_map/last_shard_prefill/pallas_call | solution.py:513
  37.1 0.0 collective-permute-done.10
  37.1 0.0 collective-permute-done.11
  37.1 0.0 collective-permute-done.9
  37.1 0.8 %broadcast_select_fusion.2 = bf16[4,2,4096]{2,1,0:T(2,128)(2,1)} fusion(pred[4]{0:T(512)(128)(4,1)S(1)} %get-tuple-element.39, pred[4]{0:T(512)(128)(4,1)S(1)} %get-tuple-element.38, pred[4]{0:T(512)(128)(4,1)S(1)} %get-tuple-element.37, pred[4]{0:T(512)(128)(4,1)S(1)} %get-tuple-element.36, bf16[2,4096]{1,0:T(2,128)(2,1)S(1)} %get-tuple-element.41, ...), kind=kLoop, calls=%fused_computation.2 | loop fusion | flops 131072 | bytes 131088 | tf_op jit(solution)/shard_map/jit(_where)/select_n | solution.py:588
  (2 shorter events, 0.0 us)
Async XLA Ops:
  0.6 8.6 %collective-permute-start = (bf16[128,512]{1,0:T(8,128)(2,1)}, bf16[128,512]{1,0:T(8,128)(2,1)S(1)}, u32[]{:S(2)}, u32[]{:S(2)}) collective-permute-start(bf16[128,512]{1,0:T(8,128)(2,1)} %refs_6_.2), channel_id=1, source_target_pairs={{0,1},{1,3},{3,2},{2,0},{4,5},{5,7},{7,6},{6,4},{8,9},{9,11},{11,1... | collective-permute-start | bytes 393224 | tf_op jit(solution)/shard_map/ppermute | solution.py:46
  3.7 7.5 %collective-permute-start.1 = (bf16[128,512]{1,0:T(8,128)(2,1)}, bf16[128,512]{1,0:T(8,128)(2,1)S(1)}, u32[]{:S(2)}, u32[]{:S(2)}) collective-permute-start(bf16[128,512]{1,0:T(8,128)(2,1)} %refs_10_.1), channel_id=1, source_target_pairs={{1,0},{3,1},{2,3},{0,2},{5,4},{7,5},{6,7},{4,6},{9,8},{11,9},{10,1... | collective-permute-start | bytes 393224 | tf_op jit(solution)/shard_map/ppermute | solution.py:46
  5.7 3.5 %copy-start = (bf16[128,512]{1,0:T(8,128)(2,1)S(1)}, bf16[128,512]{1,0:T(8,128)(2,1)}, u32[]{:S(2)}) copy-start(bf16[128,512]{1,0:T(8,128)(2,1)} %refs_6_.2) | copy-start | bytes 393220
  5.7 5.5 %copy-start.1 = (bf16[128,512]{1,0:T(8,128)(2,1)S(1)}, bf16[128,512]{1,0:T(8,128)(2,1)}, u32[]{:S(2)}) copy-start(bf16[128,512]{1,0:T(8,128)(2,1)} %refs_10_.1) | copy-start | bytes 393220
  7.2 8.7 %copy-start.2 = (bf16[128,4096]{1,0:T(8,128)(2,1)S(1)}, bf16[128,4096]{1,0:T(8,128)(2,1)}, u32[]{:S(2)}) copy-start(bf16[128,4096]{1,0:T(8,128)(2,1)} %refs_3_.2) | copy-start | bytes 3145732
  7.3 8.7 %copy-start.3 = (s32[18]{0:T(128)S(1)}, s32[18]{0:T(128)}, u32[]{:S(2)}) copy-start(s32[18]{0:T(128)} %facts.1.refs_0_) | copy-start | bytes 220
  7.3 5.7 %collective-permute-start.2 = (bf16[8,5120]{1,0:T(8,128)(2,1)S(1)}, bf16[8,5120]{1,0:T(8,128)(2,1)S(1)}, u32[]{:S(2)}, u32[]{:S(2)}) collective-permute-start(bf16[8,5120]{1,0:T(8,128)(2,1)S(1)} %reshape.39.refs_5_), channel_id=1, source_target_pairs={{0,4},{4,0},{8,12},{12,8},{1,5},{5,1},{9,13},{13,9},{2,6},{6,2},{1... | collective-permute-start | bytes 245768 | tf_op jit(solution)/shard_map/ppermute | solution.py:544
  7.3 8.2 %collective-permute-start.3 = (bf16[8,5120]{1,0:T(8,128)(2,1)S(1)}, bf16[8,5120]{1,0:T(8,128)(2,1)S(1)}, u32[]{:S(2)}, u32[]{:S(2)}) collective-permute-start(bf16[8,5120]{1,0:T(8,128)(2,1)S(1)} %reshape.39.refs_5_), channel_id=1, source_target_pairs={{0,8},{4,12},{8,0},{12,4},{1,9},{5,13},{9,1},{13,5},{2,10},{6,14},... | collective-permute-start | bytes 245768 | tf_op jit(solution)/shard_map/ppermute | solution.py:544
  9.2 6.7 %collective-permute-start.4 = (bf16[8,5120]{1,0:T(8,128)(2,1)S(1)}, bf16[8,5120]{1,0:T(8,128)(2,1)S(1)}, u32[]{:S(2)}, u32[]{:S(2)}) collective-permute-start(bf16[8,5120]{1,0:T(8,128)(2,1)S(1)} %reshape.39.refs_5_), channel_id=1, source_target_pairs={{0,12},{4,8},{8,4},{12,0},{1,13},{5,9},{9,5},{13,1},{2,14},{6,10},... | collective-permute-start | bytes 245768 | tf_op jit(solution)/shard_map/ppermute | solution.py:544
  9.2 9.4 %collective-permute-start.5 = (bf16[128,512]{1,0:T(8,128)(2,1)S(1)}, bf16[128,512]{1,0:T(8,128)(2,1)S(1)}, u32[]{:S(2)}, u32[]{:S(2)}) collective-permute-start(bf16[128,512]{1,0:T(8,128)(2,1)S(1)} %copy-done), channel_id=1, source_target_pairs={{1,0},{3,1},{2,3},{0,2},{5,4},{7,5},{6,7},{4,6},{9,8},{11,9},{10,1... | collective-permute-start | bytes 393224 | tf_op jit(solution)/shard_map/ppermute | solution.py:46
  11.2 9.8 %collective-permute-start.6 = (bf16[128,512]{1,0:T(8,128)(2,1)S(1)}, bf16[128,512]{1,0:T(8,128)(2,1)S(1)}, u32[]{:S(2)}, u32[]{:S(2)}) collective-permute-start(bf16[128,512]{1,0:T(8,128)(2,1)S(1)} %copy-done.1), channel_id=1, source_target_pairs={{0,1},{1,3},{3,2},{2,0},{4,5},{5,7},{7,6},{6,4},{8,9},{9,11},{11,1... | collective-permute-start | bytes 393224 | tf_op jit(solution)/shard_map/ppermute | solution.py:46
  13.0 11.9 %collective-permute-start.7 = (bf16[128,512]{1,0:T(8,128)(2,1)S(1)}, bf16[128,512]{1,0:T(8,128)(2,1)S(1)}, u32[]{:S(2)}, u32[]{:S(2)}) collective-permute-start(bf16[128,512]{1,0:T(8,128)(2,1)S(1)} %collective-permute-done.refs_0_.refs_7_.refs_5_), channel_id=1, source_target_pairs={{0,1},{1,3},{3,2},{2,0},{4,5},{5,7},{7,6},{6,4},{8,9},{9,11},{11,1... | collective-permute-start | bytes 393224 | tf_op jit(solution)/shard_map/ppermute | solution.py:46
  15.5 9.5 %collective-permute-start.8 = (bf16[128,512]{1,0:T(8,128)(2,1)S(1)}, bf16[128,512]{1,0:T(8,128)(2,1)S(1)}, u32[]{:S(2)}, u32[]{:S(2)}) collective-permute-start(bf16[128,512]{1,0:T(8,128)(2,1)S(1)} %collective-permute-done.1.refs_1_.refs_10_.refs_12_), channel_id=1, source_target_pairs={{1,0},{3,1},{2,3},{0,2},{5,4},{7,5},{6,7},{4,6},{9,8},{11,9},{10,1... | collective-permute-start | bytes 393224 | tf_op jit(solution)/shard_map/ppermute | solution.py:46
  27.3 9.8 %collective-permute-start.10 = (bf16[2,4096]{1,0:T(2,128)(2,1)S(1)}, bf16[2,4096]{1,0:T(2,128)(2,1)S(1)}, u32[]{:S(2)}, u32[]{:S(2)}) collective-permute-start(bf16[2,4096]{1,0:T(2,128)(2,1)S(1)} %get-tuple-element.43), channel_id=1, source_target_pairs={{0,8},{4,12},{8,0},{12,4},{1,9},{5,13},{9,1},{13,5},{2,10},{6,14},... | collective-permute-start | bytes 49160 | tf_op jit(solution)/shard_map/ppermute | solution.py:544
  28.8 8.3 %collective-permute-start.11 = (bf16[2,4096]{1,0:T(2,128)(2,1)S(1)}, bf16[2,4096]{1,0:T(2,128)(2,1)S(1)}, u32[]{:S(2)}, u32[]{:S(2)}) collective-permute-start(bf16[2,4096]{1,0:T(2,128)(2,1)S(1)} %get-tuple-element.42), channel_id=1, source_target_pairs={{0,4},{4,0},{8,12},{12,8},{1,5},{5,1},{9,13},{13,9},{2,6},{6,2},{1... | collective-permute-start | bytes 49160 | tf_op jit(solution)/shard_map/ppermute | solution.py:544
  28.8 8.3 %collective-permute-start.9 = (bf16[2,4096]{1,0:T(2,128)(2,1)S(1)}, bf16[2,4096]{1,0:T(2,128)(2,1)S(1)}, u32[]{:S(2)}, u32[]{:S(2)}) collective-permute-start(bf16[2,4096]{1,0:T(2,128)(2,1)S(1)} %get-tuple-element.40), channel_id=1, source_target_pairs={{0,12},{4,8},{8,4},{12,0},{1,13},{5,9},{9,5},{13,1},{2,14},{6,10},... | collective-permute-start | bytes 49160 | tf_op jit(solution)/shard_map/ppermute | solution.py:544

commit v19 on v18

--- a/solution.py
+++ b/solution.py
@@ -562,17 +562,25 @@
     facts = facts_row(plan, prompt_lengths, decode_slot)
     prompt_key, decoded_query = lax.optimization_barrier((prompt_key, decoded_query))
     later_key, later_value, own, facts = lax.optimization_barrier((prompt_key, prompt_value, own, facts))
-    chains = []
-    for first, later, way in ((prompt_key, later_key, True), (prompt_value, later_value, False)):
-        pieces = [first]
-        for d in range(1, plan.size // 2 + 1):
-            first = plan.step(first, way)
-            later = plan.step(later, not way) if 2 * d < plan.size else None
-            pieces += [first, later] if way else [later, first]
-        chains.append(pieces[: plan.size - 1] + [first])
-    keys, values = chains
     blocks = [own] + [paired(own, k) for k in range(1, pd_size)]
-    maxima = start_maxima(keys[1], values[2])
+    firsts = [prompt_key, prompt_value]
+    laters = [later_key, later_value]
+    ways = (True, False)
+    keys, values = [prompt_key], [prompt_value]
+    maxima = None
+    for d in range(1, plan.size // 2 + 1):
+        firsts = [plan.step(a, way) for a, way in zip(firsts, ways)]
+        if 2 * d < plan.size:
+            laters = [plan.step(a, not way) for a, way in zip(laters, ways)]
+        if d == 1:
+            firsts, blocks = lax.optimization_barrier((firsts, blocks))
+            maxima = start_maxima(*firsts)
+        if 2 * d < plan.size:
+            keys += [firsts[0], laters[0]]
+            values += [laters[1], firsts[1]]
+        else:
+            keys.append(firsts[0])
+            values.append(firsts[1])
 
     state = call_first(plan, facts, maxima, prompt_query, blocks, keys[:1], values[:1])
     state = call_middle(plan, state, prompt_query, keys[1:-1], values[1:-1])

time: 38.1 us -> 38.6 us (1.013)
    ppermute x6, waiting for transfers between devices: 0.02 us -> 1.07 us  [paired(): lax.ppermute(array, 'pd', [(g, g ^ k) for g in range(lax.axis_size('pd'))])]
    ppermute x6, waiting for transfers between devices: 4.47 us -> 3.74 us  [step(): lax.ppermute(array, 'tp', self.pairs if up else [(b, a) for a, b in self....]
  transfers between devices with their start and end apart: 12 -> 12, of which waited for: 4 -> 4; matrix products, arithmetic and copies ran while one was open for 3% -> 3% of each run, Pallas kernels for 36% -> 35%
where the time goes in v19:
time: 38.6 us; the launch traced here: 38.4 us
  Pallas kernels  15.7 us (41%)
  starting transfers between devices  15 us (39%)
  waiting for transfers between devices  4.81 us (12%)
  other arithmetic  1.89 us (5%)
  between operations  0.76 us (2%)
    ppermute x6, starting transfers between devices, step(): lax.ppermute(array, 'tp', self.pairs if up else [(b, a) for a, b in self....  10.9 us
    pallas_call x1, Pallas kernels, call_prefill(): pl.pallas_call(lambda *refs: prefill_kernel(plan, *refs), in_specs=[VMEM]...  7.63 us
    ppermute x6, starting transfers between devices, paired(): lax.ppermute(array, 'pd', [(g, g ^ k) for g in range(lax.axis_size('pd'))])  4.17 us
    ppermute x6, waiting for transfers between devices, step(): lax.ppermute(array, 'tp', self.pairs if up else [(b, a) for a, b in self....  3.74 us
    pallas_call x1, Pallas kernels, call_first(): pl.pallas_call(lambda *refs: first_kernel(plan, len(blocks), *refs), in_s...  2.66 us
    pallas_call x1, Pallas kernels, call_decode(): pl.pallas_call(lambda *refs: decode_kernel(plan, *refs), in_specs=[VMEM]...  2.12 us
    pallas_call x1, Pallas kernels, call_middle(): pl.pallas_call(lambda *refs: middle_kernel(plan, *refs), in_specs=[VMEM]...  1.9 us
    pallas_call x1, Pallas kernels, facts_row(): pl.pallas_call(kernel, in_specs=[SMEM, SMEM], out_specs=SMEM, out_shape=j...  1.43 us
  transfers between devices with their start and end apart: 12, of which 4 were waited for; matrix products, arithmetic and copies ran while one was open for 3% of the time, Pallas kernels for 35%

profile of v19, /device:TPU:0, one launch (start us, length us, event | category | flops | bytes accessed | tf_op | source)
XLA Modules:
  0.0 38.4 jit_solution(6340088917577498959)
XLA Ops:
  0.6 3.1 %collective-permute-start = (bf16[128,512]{1,0:T(8,128)(2,1)}, bf16[128,512]{1,0:T(8,128)(2,1)S(1)}, u32[]{:S(2)}, u32[]{:S(2)}) collective-permute-start(bf16[128,512]{1,0:T(8,128)(2,1)} %refs_6_.2), channel_id=1, source_target_pairs={{0,1},{1,3},{3,2},{2,0},{4,5},{5,7},{7,6},{6,4},{8,9},{9,11},{11,1... | collective-permute-start | bytes 393224 | tf_op jit(solution)/shard_map/ppermute | solution.py:46
  3.7 1.1 %collective-permute-start.1 = (bf16[128,512]{1,0:T(8,128)(2,1)}, bf16[128,512]{1,0:T(8,128)(2,1)S(1)}, u32[]{:S(2)}, u32[]{:S(2)}) collective-permute-start(bf16[128,512]{1,0:T(8,128)(2,1)} %refs_10_.1), channel_id=1, source_target_pairs={{1,0},{3,1},{2,3},{0,2},{5,4},{7,5},{6,7},{4,6},{9,8},{11,9},{10,1... | collective-permute-start | bytes 393224 | tf_op jit(solution)/shard_map/ppermute | solution.py:46
  4.8 0.9 %pad_maximum_fusion = bf16[4,2,5120]{2,1,0:T(2,128)(2,1)S(1)} fusion(bf16[4,2,512]{2,1,0:T(2,128)(2,1)} %param.15, bf16[4,2,512]{2,1,0:T(2,128)(2,1)} %param.14, bf16[4,2,4096]{2,1,0:T(2,128)(2,1)} %param.13), kind=kLoop, calls=%fused_computation.4 | loop fusion | flops 245760 | bytes 163840 | tf_op jit(solution)/shard_map/concatenate | solution.py:559
  5.7 0.0 copy-start
  5.7 0.0 copy-start.1
  5.8 1.4 %facts.1.refs_0_ = s32[18]{0:T(128)} custom-call(s32[4,4]{1,0:T(4,128)} %lengths_ref.1, s32[16]{0:T(128)} %slots_ref.1), custom_call_target="tpu_custom_call" | custom-call | flops 5000000000 | tf_op jit(solution)/shard_map/facts/pallas_call | solution.py:126
  7.2 0.0 copy-start.2
  7.3 0.0 copy-start.3
  7.3 0.1 collective-permute-start.2
  7.3 1.8 %collective-permute-start.3 = (bf16[8,5120]{1,0:T(8,128)(2,1)S(1)}, bf16[8,5120]{1,0:T(8,128)(2,1)S(1)}, u32[]{:S(2)}, u32[]{:S(2)}) collective-permute-start(bf16[8,5120]{1,0:T(8,128)(2,1)S(1)} %reshape.39.refs_5_), channel_id=1, source_target_pairs={{0,8},{4,12},{8,0},{12,4},{1,9},{5,13},{9,1},{13,5},{2,10},{6,14},... | collective-permute-start | bytes 245768 | tf_op jit(solution)/shard_map/ppermute | solution.py:544
  9.2 0.1 collective-permute-start.4
  9.2 0.0 collective-permute-done.2.refs_6_
  9.2 0.0 copy-done
  9.2 1.9 %collective-permute-start.5 = (bf16[128,512]{1,0:T(8,128)(2,1)S(1)}, bf16[128,512]{1,0:T(8,128)(2,1)S(1)}, u32[]{:S(2)}, u32[]{:S(2)}) collective-permute-start(bf16[128,512]{1,0:T(8,128)(2,1)S(1)} %copy-done), channel_id=1, source_target_pairs={{1,0},{3,1},{2,3},{0,2},{5,4},{7,5},{6,7},{4,6},{9,8},{11,9},{10,1... | collective-permute-start | bytes 393224 | tf_op jit(solution)/shard_map/ppermute | solution.py:46
  11.2 1.1 %collective-permute-done.3.refs_7_ = bf16[8,5120]{1,0:T(8,128)(2,1)S(1)} collective-permute-done((bf16[8,5120]{1,0:T(8,128)(2,1)S(1)}, bf16[8,5120]{1,0:T(8,128)(2,1)S(1)}, u32[]{:S(2)}, u32[]{:S(2)}) %collective-permute-start.3) | collective-permute-done | bytes 81952 | tf_op jit(solution)/shard_map/ppermute | solution.py:544
  12.2 0.0 copy-done.1
  12.2 1.8 %collective-permute-start.6 = (bf16[128,512]{1,0:T(8,128)(2,1)S(1)}, bf16[128,512]{1,0:T(8,128)(2,1)S(1)}, u32[]{:S(2)}, u32[]{:S(2)}) collective-permute-start(bf16[128,512]{1,0:T(8,128)(2,1)S(1)} %copy-done.1), channel_id=1, source_target_pairs={{0,1},{1,3},{3,2},{2,0},{4,5},{5,7},{7,6},{6,4},{8,9},{9,11},{11,1... | collective-permute-start | bytes 393224 | tf_op jit(solution)/shard_map/ppermute | solution.py:46
  14.1 0.0 collective-permute-done.4.refs_8_
  14.1 0.0 collective-permute-done.refs_0_.refs_7_.refs_5_
  14.1 0.0 collective-permute-done.1.refs_1_.refs_10_.refs_12_
  14.1 3.0 %collective-permute-start.7 = (bf16[128,512]{1,0:T(8,128)(2,1)S(1)}, bf16[128,512]{1,0:T(8,128)(2,1)S(1)}, u32[]{:S(2)}, u32[]{:S(2)}) collective-permute-start(bf16[128,512]{1,0:T(8,128)(2,1)S(1)} %collective-permute-done.refs_0_.refs_7_.refs_5_), channel_id=1, source_target_pairs={{0,1},{1,3},{3,2},{2,0},{4,5},{5,7},{7,6},{6,4},{8,9},{9,11},{11,1... | collective-permute-start | bytes 393224 | tf_op jit(solution)/shard_map/ppermute | solution.py:46
  17.0 0.0 collective-permute-start.8
  17.0 0.0 copy-done.2
  17.0 0.0 copy-done.3
  17.1 2.7 %first_shards.1 = (f32[4,1024,256]{2,1,0:T(8,128)S(1)}, f32[4,128,128]{2,1,0:T(8,128)S(1)}, f32[4,128,256]{2,1,0:T(8,128)S(1)}, f32[4,128,128]{2,1,0:T(8,128)S(1...) custom-call(s32[18]{0:T(128)S(1)} %copy-done.3, ...), custom_call_target="tpu_custom_call" | custom-call | flops 2147483648 | bytes 2097152 | tf_op jit(solution)/shard_map/first_shards/pallas_call | solution.py:471
  19.7 0.0 collective-permute-done.5.refs_8_.refs_6_
  19.7 0.4 collective-permute-done.6.refs_9_.refs_11_
  20.1 1.9 %middle_shard.1 = (f32[4,1024,256]{2,1,0:T(8,128)S(1)}, f32[4,128,256]{2,1,0:T(8,128)S(1)}, f32[8,128]{1,0:T(8,128)S(1)}) custom-call(f32[4,1024,256]{2,1,0:T(8,128)S(1)} %get-tuple-element.34.refs_0_, f32[4,128,128]{2,1,0:T(8,128)S(1)} %get-tuple-element.35.refs_1_, ...), custom_call_target="tpu_custom_call", output_to_operand_aliasing={{0}: (0, {}), {1}: (2, {}), {2}: (4, {})} | custom-call | flops 2147483648 | bytes 2097152 | tf_op jit(solution)/shard_map/middle_shard/pallas_call | solution.py:485
  22.0 0.1 compare_reduce_fusion.2
  22.1 1.5 %collective-permute-done.7.refs_7_.refs_9_ = bf16[128,512]{1,0:T(8,128)(2,1)S(1)} collective-permute-done((bf16[128,512]{1,0:T(8,128)(2,1)S(1)}, bf16[128,512]{1,0:T(8,128)(2,1)S(1)}, u32[]{:S(2)}, u32[]{:S(2)}) %collective-permute-start.7) | collective-permute-done | bytes 131104 | tf_op jit(solution)/shard_map/ppermute | solution.py:46
  23.7 1.8 %collective-permute-done.8.refs_11_.refs_13_ = bf16[128,512]{1,0:T(8,128)(2,1)S(1)} collective-permute-done((bf16[128,512]{1,0:T(8,128)(2,1)S(1)}, bf16[128,512]{1,0:T(8,128)(2,1)S(1)}, u32[]{:S(2)}, u32[]{:S(2)}) %collective-permute-start.8) | collective-permute-done | bytes 131104 | tf_op jit(solution)/shard_map/ppermute | solution.py:46
  25.5 2.1 %last_shard_decode.1 = bf16[16,4096]{1,0:T(8,128)(2,1)S(1)} custom-call(f32[4,128,256]{2,1,0:T(8,128)S(1)} %get-tuple-element.45.refs_0_, f32[4,128,128]{2,1,0:T(8,128)S(1)} %get-tuple-element.37.refs_3_.refs_1_, f32[8,128]{1,0:T(8,128)S(1)} %get-tuple-element.43.refs_2_, bf16[16,4096]{1,0:T(8,128)(2,1)S(1)} %get-tuple-element.39.refs_5_.refs_3_, ...), custom_call_target="tpu_custom_call" | custom-call | flops 268435456 | bytes 262144 | tf_op jit(solution)/shard_map/last_shard_decode/pallas_call | solution.py:500
  27.6 0.1 fusion
  27.7 1.6 %collective-permute-start.10 = (bf16[2,4096]{1,0:T(2,128)(2,1)S(1)}, bf16[2,4096]{1,0:T(2,128)(2,1)S(1)}, u32[]{:S(2)}, u32[]{:S(2)}) collective-permute-start(bf16[2,4096]{1,0:T(2,128)(2,1)S(1)} %get-tuple-element.55), channel_id=1, source_target_pairs={{0,8},{4,12},{8,0},{12,4},{1,9},{5,13},{9,1},{13,5},{2,10},{6,14},... | collective-permute-start | bytes 49160 | tf_op jit(solution)/shard_map/ppermute | solution.py:544
  29.3 0.0 collective-permute-start.11
  29.3 0.6 %collective-permute-start.9 = (bf16[2,4096]{1,0:T(2,128)(2,1)S(1)}, bf16[2,4096]{1,0:T(2,128)(2,1)S(1)}, u32[]{:S(2)}, u32[]{:S(2)}) collective-permute-start(bf16[2,4096]{1,0:T(2,128)(2,1)S(1)} %get-tuple-element.52), channel_id=1, source_target_pairs={{0,12},{4,8},{8,4},{12,0},{1,13},{5,9},{9,5},{13,1},{2,14},{6,10},... | collective-permute-start | bytes 49160 | tf_op jit(solution)/shard_map/ppermute | solution.py:544
  29.9 7.6 %last_shard_prefill.1 = bf16[128,4096]{1,0:T(8,128)(2,1)} custom-call(f32[4,1024,256]{2,1,0:T(8,128)S(1)} %get-tuple-element.42.refs_0_, f32[4,128,128]{2,1,0:T(8,128)S(1)} %get-tuple-element.35.refs_1_, f32[8,128]{1,0:T(8,128)S(1)} %get-tuple-element.43.refs_2_, bf16[128,4096]{1,0:T(8,128)(2,1)S(1)} %copy-done.2, bf16[128,512]{1,0:T(8,128)(2,1)S(1)} %copy-done, ...), custom_call_target="tpu_custom_call" | custom-call | flops 2147483648 | bytes 2097152 | tf_op jit(solution)/shard_map/last_shard_prefill/pallas_call | solution.py:513
  37.5 0.0 collective-permute-done.10
  37.6 0.0 collective-permute-done.11
  37.6 0.0 collective-permute-done.9
  37.6 0.8 %broadcast_select_fusion.2 = bf16[4,2,4096]{2,1,0:T(2,128)(2,1)} fusion(pred[4]{0:T(512)(128)(4,1)S(1)} %get-tuple-element.51, pred[4]{0:T(512)(128)(4,1)S(1)} %get-tuple-element.50, pred[4]{0:T(512)(128)(4,1)S(1)} %get-tuple-element.49, pred[4]{0:T(512)(128)(4,1)S(1)} %get-tuple-element.48, bf16[2,4096]{1,0:T(2,128)(2,1)S(1)} %get-tuple-element.53, ...), kind=kLoop, calls=%fused_computation.2 | loop fusion | flops 131072 | bytes 131088 | tf_op jit(solution)/shard_map/jit(_where)/select_n | solution.py:596
  (2 shorter events, 0.0 us)
Async XLA Ops:
  0.6 13.4 %collective-permute-start = (bf16[128,512]{1,0:T(8,128)(2,1)}, bf16[128,512]{1,0:T(8,128)(2,1)S(1)}, u32[]{:S(2)}, u32[]{:S(2)}) collective-permute-start(bf16[128,512]{1,0:T(8,128)(2,1)} %refs_6_.2), channel_id=1, source_target_pairs={{0,1},{1,3},{3,2},{2,0},{4,5},{5,7},{7,6},{6,4},{8,9},{9,11},{11,1... | collective-permute-start | bytes 393224 | tf_op jit(solution)/shard_map/ppermute | solution.py:46
  3.7 10.4 %collective-permute-start.1 = (bf16[128,512]{1,0:T(8,128)(2,1)}, bf16[128,512]{1,0:T(8,128)(2,1)S(1)}, u32[]{:S(2)}, u32[]{:S(2)}) collective-permute-start(bf16[128,512]{1,0:T(8,128)(2,1)} %refs_10_.1), channel_id=1, source_target_pairs={{1,0},{3,1},{2,3},{0,2},{5,4},{7,5},{6,7},{4,6},{9,8},{11,9},{10,1... | collective-permute-start | bytes 393224 | tf_op jit(solution)/shard_map/ppermute | solution.py:46
  5.7 3.5 %copy-start = (bf16[128,512]{1,0:T(8,128)(2,1)S(1)}, bf16[128,512]{1,0:T(8,128)(2,1)}, u32[]{:S(2)}) copy-start(bf16[128,512]{1,0:T(8,128)(2,1)} %refs_6_.2) | copy-start | bytes 393220
  5.7 6.5 %copy-start.1 = (bf16[128,512]{1,0:T(8,128)(2,1)S(1)}, bf16[128,512]{1,0:T(8,128)(2,1)}, u32[]{:S(2)}) copy-start(bf16[128,512]{1,0:T(8,128)(2,1)} %refs_10_.1) | copy-start | bytes 393220
  7.2 9.8 %copy-start.2 = (bf16[128,4096]{1,0:T(8,128)(2,1)S(1)}, bf16[128,4096]{1,0:T(8,128)(2,1)}, u32[]{:S(2)}) copy-start(bf16[128,4096]{1,0:T(8,128)(2,1)} %refs_3_.2) | copy-start | bytes 3145732
  7.3 9.8 %copy-start.3 = (s32[18]{0:T(128)S(1)}, s32[18]{0:T(128)}, u32[]{:S(2)}) copy-start(s32[18]{0:T(128)} %facts.1.refs_0_) | copy-start | bytes 220
  7.3 2.0 %collective-permute-start.2 = (bf16[8,5120]{1,0:T(8,128)(2,1)S(1)}, bf16[8,5120]{1,0:T(8,128)(2,1)S(1)}, u32[]{:S(2)}, u32[]{:S(2)}) collective-permute-start(bf16[8,5120]{1,0:T(8,128)(2,1)S(1)} %reshape.39.refs_5_), channel_id=1, source_target_pairs={{0,4},{4,0},{8,12},{12,8},{1,5},{5,1},{9,13},{13,9},{2,6},{6,2},{1... | collective-permute-start | bytes 245768 | tf_op jit(solution)/shard_map/ppermute | solution.py:544
  7.3 4.9 %collective-permute-start.3 = (bf16[8,5120]{1,0:T(8,128)(2,1)S(1)}, bf16[8,5120]{1,0:T(8,128)(2,1)S(1)}, u32[]{:S(2)}, u32[]{:S(2)}) collective-permute-start(bf16[8,5120]{1,0:T(8,128)(2,1)S(1)} %reshape.39.refs_5_), channel_id=1, source_target_pairs={{0,8},{4,12},{8,0},{12,4},{1,9},{5,13},{9,1},{13,5},{2,10},{6,14},... | collective-permute-start | bytes 245768 | tf_op jit(solution)/shard_map/ppermute | solution.py:544
  9.2 4.9 %collective-permute-start.4 = (bf16[8,5120]{1,0:T(8,128)(2,1)S(1)}, bf16[8,5120]{1,0:T(8,128)(2,1)S(1)}, u32[]{:S(2)}, u32[]{:S(2)}) collective-permute-start(bf16[8,5120]{1,0:T(8,128)(2,1)S(1)} %reshape.39.refs_5_), channel_id=1, source_target_pairs={{0,12},{4,8},{8,4},{12,0},{1,13},{5,9},{9,5},{13,1},{2,14},{6,10},... | collective-permute-start | bytes 245768 | tf_op jit(solution)/shard_map/ppermute | solution.py:544
  9.2 10.5 %collective-permute-start.5 = (bf16[128,512]{1,0:T(8,128)(2,1)S(1)}, bf16[128,512]{1,0:T(8,128)(2,1)S(1)}, u32[]{:S(2)}, u32[]{:S(2)}) collective-permute-start(bf16[128,512]{1,0:T(8,128)(2,1)S(1)} %copy-done), channel_id=1, source_target_pairs={{1,0},{3,1},{2,3},{0,2},{5,4},{7,5},{6,7},{4,6},{9,8},{11,9},{10,1... | collective-permute-start | bytes 393224 | tf_op jit(solution)/shard_map/ppermute | solution.py:46
  12.2 7.9 %collective-permute-start.6 = (bf16[128,512]{1,0:T(8,128)(2,1)S(1)}, bf16[128,512]{1,0:T(8,128)(2,1)S(1)}, u32[]{:S(2)}, u32[]{:S(2)}) collective-permute-start(bf16[128,512]{1,0:T(8,128)(2,1)S(1)} %copy-done.1), channel_id=1, source_target_pairs={{0,1},{1,3},{3,2},{2,0},{4,5},{5,7},{7,6},{6,4},{8,9},{9,11},{11,1... | collective-permute-start | bytes 393224 | tf_op jit(solution)/shard_map/ppermute | solution.py:46
  14.1 9.6 %collective-permute-start.7 = (bf16[128,512]{1,0:T(8,128)(2,1)S(1)}, bf16[128,512]{1,0:T(8,128)(2,1)S(1)}, u32[]{:S(2)}, u32[]{:S(2)}) collective-permute-start(bf16[128,512]{1,0:T(8,128)(2,1)S(1)} %collective-permute-done.refs_0_.refs_7_.refs_5_), channel_id=1, source_target_pairs={{0,1},{1,3},{3,2},{2,0},{4,5},{5,7},{7,6},{6,4},{8,9},{9,11},{11,1... | collective-permute-start | bytes 393224 | tf_op jit(solution)/shard_map/ppermute | solution.py:46
  17.0 8.5 %collective-permute-start.8 = (bf16[128,512]{1,0:T(8,128)(2,1)S(1)}, bf16[128,512]{1,0:T(8,128)(2,1)S(1)}, u32[]{:S(2)}, u32[]{:S(2)}) collective-permute-start(bf16[128,512]{1,0:T(8,128)(2,1)S(1)} %collective-permute-done.1.refs_1_.refs_10_.refs_12_), channel_id=1, source_target_pairs={{1,0},{3,1},{2,3},{0,2},{5,4},{7,5},{6,7},{4,6},{9,8},{11,9},{10,1... | collective-permute-start | bytes 393224 | tf_op jit(solution)/shard_map/ppermute | solution.py:46
  27.7 9.8 %collective-permute-start.10 = (bf16[2,4096]{1,0:T(2,128)(2,1)S(1)}, bf16[2,4096]{1,0:T(2,128)(2,1)S(1)}, u32[]{:S(2)}, u32[]{:S(2)}) collective-permute-start(bf16[2,4096]{1,0:T(2,128)(2,1)S(1)} %get-tuple-element.55), channel_id=1, source_target_pairs={{0,8},{4,12},{8,0},{12,4},{1,9},{5,13},{9,1},{13,5},{2,10},{6,14},... | collective-permute-start | bytes 49160 | tf_op jit(solution)/shard_map/ppermute | solution.py:544
  29.3 8.3 %collective-permute-start.11 = (bf16[2,4096]{1,0:T(2,128)(2,1)S(1)}, bf16[2,4096]{1,0:T(2,128)(2,1)S(1)}, u32[]{:S(2)}, u32[]{:S(2)}) collective-permute-start(bf16[2,4096]{1,0:T(2,128)(2,1)S(1)} %get-tuple-element.54), channel_id=1, source_target_pairs={{0,4},{4,0},{8,12},{12,8},{1,5},{5,1},{9,13},{13,9},{2,6},{6,2},{1... | collective-permute-start | bytes 49160 | tf_op jit(solution)/shard_map/ppermute | solution.py:544
  29.3 8.3 %collective-permute-start.9 = (bf16[2,4096]{1,0:T(2,128)(2,1)S(1)}, bf16[2,4096]{1,0:T(2,128)(2,1)S(1)}, u32[]{:S(2)}, u32[]{:S(2)}) collective-permute-start(bf16[2,4096]{1,0:T(2,128)(2,1)S(1)} %get-tuple-element.52), channel_id=1, source_target_pairs={{0,12},{4,8},{8,4},{12,0},{1,13},{5,9},{9,5},{13,1},{2,14},{6,10},... | collective-permute-start | bytes 49160 | tf_op jit(solution)/shard_map/ppermute | solution.py:544

commit v20 on v19

--- a/solution.py
+++ b/solution.py
@@ -562,7 +562,6 @@
     facts = facts_row(plan, prompt_lengths, decode_slot)
     prompt_key, decoded_query = lax.optimization_barrier((prompt_key, decoded_query))
     later_key, later_value, own, facts = lax.optimization_barrier((prompt_key, prompt_value, own, facts))
-    blocks = [own] + [paired(own, k) for k in range(1, pd_size)]
     firsts = [prompt_key, prompt_value]
     laters = [later_key, later_value]
     ways = (True, False)
@@ -570,10 +569,12 @@
     maxima = None
     for d in range(1, plan.size // 2 + 1):
         firsts = [plan.step(a, way) for a, way in zip(firsts, ways)]
+        if d == 1:
+            firsts[0], own, laters[1] = lax.optimization_barrier((firsts[0], own, laters[1]))
+            blocks = [own] + [paired(own, k) for k in range(1, pd_size)]
         if 2 * d < plan.size:
             laters = [plan.step(a, not way) for a, way in zip(laters, ways)]
         if d == 1:
-            firsts, blocks = lax.optimization_barrier((firsts, blocks))
             maxima = start_maxima(*firsts)
         if 2 * d < plan.size:
             keys += [firsts[0], laters[0]]

time: 38.6 us -> 41.9 us (1.085)
  the two profiles are of different devices: /device:TPU:0 before, /device:TPU:31 now
where the time goes in v20:
time: 41.9 us; the launch traced here: 41.7 us
  Pallas kernels  15.7 us (37%)
  waiting for transfers between devices  14.9 us (36%)
  starting transfers between devices  8.23 us (20%)
  other arithmetic  1.89 us (5%)
  between operations  0.81 us (2%)
    ppermute x6, waiting for transfers between devices, step(): lax.ppermute(array, 'tp', self.pairs if up else [(b, a) for a, b in self....  10.5 us
    pallas_call x1, Pallas kernels, call_prefill(): pl.pallas_call(lambda *refs: prefill_kernel(plan, *refs), in_specs=[VMEM]...  7.63 us
    ppermute x6, starting transfers between devices, paired(): lax.ppermute(array, 'pd', [(g, g ^ k) for g in range(lax.axis_size('pd'))])  5.64 us
    ppermute x6, waiting for transfers between devices, paired(): lax.ppermute(array, 'pd', [(g, g ^ k) for g in range(lax.axis_size('pd'))])  4.43 us
    pallas_call x1, Pallas kernels, call_first(): pl.pallas_call(lambda *refs: first_kernel(plan, len(blocks), *refs), in_s...  2.66 us
    ppermute x6, starting transfers between devices, step(): lax.ppermute(array, 'tp', self.pairs if up else [(b, a) for a, b in self....  2.6 us
    pallas_call x1, Pallas kernels, call_decode(): pl.pallas_call(lambda *refs: decode_kernel(plan, *refs), in_specs=[VMEM]...  2.13 us
    pallas_call x1, Pallas kernels, call_middle(): pl.pallas_call(lambda *refs: middle_kernel(plan, *refs), in_specs=[VMEM]...  1.9 us
  transfers between devices with their start and end apart: 12, of which 4 were waited for; matrix products, arithmetic and copies ran while one was open for 3% of the time, Pallas kernels for 33%

profile of v20, /device:TPU:31, one launch (start us, length us, event | category | flops | bytes accessed | tf_op | source)
XLA Modules:
  0.0 41.7 jit_solution(17795358319785857681)
XLA Ops:
  0.6 0.2 collective-permute-start
  0.9 2.2 %collective-permute-start.1 = (bf16[128,512]{1,0:T(8,128)(2,1)}, bf16[128,512]{1,0:T(8,128)(2,1)S(1)}, u32[]{:S(2)}, u32[]{:S(2)}) collective-permute-start(bf16[128,512]{1,0:T(8,128)(2,1)} %refs_10_.1), channel_id=1, source_target_pairs={{1,0},{3,1},{2,3},{0,2},{5,4},{7,5},{6,7},{4,6},{9,8},{11,9},{10,1... | collective-permute-start | bytes 393224 | tf_op jit(solution)/shard_map/ppermute | solution.py:46
  3.0 0.9 %pad_maximum_fusion = bf16[4,2,5120]{2,1,0:T(2,128)(2,1)S(1)} fusion(bf16[4,2,512]{2,1,0:T(2,128)(2,1)} %param.15, bf16[4,2,512]{2,1,0:T(2,128)(2,1)} %param.14, bf16[4,2,4096]{2,1,0:T(2,128)(2,1)} %param.13), kind=kLoop, calls=%fused_computation.4 | loop fusion | flops 245760 | bytes 163840 | tf_op jit(solution)/shard_map/concatenate | solution.py:559
  4.0 0.0 copy-start
  4.0 1.4 %facts.1.refs_0_ = s32[18]{0:T(128)} custom-call(s32[4,4]{1,0:T(4,128)} %lengths_ref.1, s32[16]{0:T(128)} %slots_ref.1), custom_call_target="tpu_custom_call" | custom-call | flops 5000000000 | tf_op jit(solution)/shard_map/facts/pallas_call | solution.py:126
  5.5 0.0 copy-done
  5.5 0.0 copy-start.1
  5.5 0.0 copy-start.2
  5.5 0.0 copy-start.3
  5.5 0.1 collective-permute-start.5
  5.6 6.5 %collective-permute-done.refs_0_.refs_7_.refs_5_ = bf16[128,512]{1,0:T(8,128)(2,1)S(1)} collective-permute-done((bf16[128,512]{1,0:T(8,128)(2,1)}, bf16[128,512]{1,0:T(8,128)(2,1)S(1)}, u32[]{:S(2)}, u32[]{:S(2)}) %collective-permute-start) | collective-permute-done | bytes 131104 | tf_op jit(solution)/shard_map/ppermute | solution.py:46
  12.1 1.2 %collective-permute-start.2 = (bf16[8,5120]{1,0:T(8,128)(2,1)S(1)}, bf16[8,5120]{1,0:T(8,128)(2,1)S(1)}, u32[]{:S(2)}, u32[]{:S(2)}) collective-permute-start(bf16[8,5120]{1,0:T(8,128)(2,1)S(1)} %reshape.39.refs_5_), channel_id=1, source_target_pairs={{0,4},{4,0},{8,12},{12,8},{1,5},{5,1},{9,13},{13,9},{2,6},{6,2},{1... | collective-permute-start | bytes 245768 | tf_op jit(solution)/shard_map/ppermute | solution.py:544
  13.3 0.3 collective-permute-start.3
  13.6 1.4 %collective-permute-start.4 = (bf16[8,5120]{1,0:T(8,128)(2,1)S(1)}, bf16[8,5120]{1,0:T(8,128)(2,1)S(1)}, u32[]{:S(2)}, u32[]{:S(2)}) collective-permute-start(bf16[8,5120]{1,0:T(8,128)(2,1)S(1)} %reshape.39.refs_5_), channel_id=1, source_target_pairs={{0,12},{4,8},{8,4},{12,0},{1,13},{5,9},{9,5},{13,1},{2,14},{6,10},... | collective-permute-start | bytes 245768 | tf_op jit(solution)/shard_map/ppermute | solution.py:544
  15.0 0.0 collective-permute-done.1.refs_1_.refs_10_.refs_12_
  15.0 0.0 collective-permute-start.7
  15.0 0.0 collective-permute-done.2.refs_6_
  15.0 0.0 copy-done.1
  15.0 0.1 collective-permute-start.6
  15.1 2.3 %collective-permute-done.3.refs_7_ = bf16[8,5120]{1,0:T(8,128)(2,1)S(1)} collective-permute-done((bf16[8,5120]{1,0:T(8,128)(2,1)S(1)}, bf16[8,5120]{1,0:T(8,128)(2,1)S(1)}, u32[]{:S(2)}, u32[]{:S(2)}) %collective-permute-start.3) | collective-permute-done | bytes 81952 | tf_op jit(solution)/shard_map/ppermute | solution.py:544
  17.4 0.1 collective-permute-start.8
  17.5 2.1 %collective-permute-done.4.refs_8_ = bf16[8,5120]{1,0:T(8,128)(2,1)S(1)} collective-permute-done((bf16[8,5120]{1,0:T(8,128)(2,1)S(1)}, bf16[8,5120]{1,0:T(8,128)(2,1)S(1)}, u32[]{:S(2)}, u32[]{:S(2)}) %collective-permute-start.4) | collective-permute-done | bytes 81952 | tf_op jit(solution)/shard_map/ppermute | solution.py:544
  19.5 0.0 copy-done.2
  19.5 0.0 copy-done.3
  19.5 2.7 %first_shards.1 = (f32[4,1024,256]{2,1,0:T(8,128)S(1)}, f32[4,128,128]{2,1,0:T(8,128)S(1)}, f32[4,128,256]{2,1,0:T(8,128)S(1)}, f32[4,128,128]{2,1,0:T(8,128)S(1...) custom-call(s32[18]{0:T(128)S(1)} %copy-done.3, ...), custom_call_target="tpu_custom_call" | custom-call | flops 2147483648 | bytes 2097152 | tf_op jit(solution)/shard_map/first_shards/pallas_call | solution.py:471
  22.2 0.1 compare_reduce_fusion.2
  22.4 0.0 collective-permute-done.5.refs_8_.refs_6_
  22.4 4.0 %collective-permute-done.6.refs_9_.refs_11_ = bf16[128,512]{1,0:T(8,128)(2,1)S(1)} collective-permute-done((bf16[128,512]{1,0:T(8,128)(2,1)S(1)}, bf16[128,512]{1,0:T(8,128)(2,1)S(1)}, u32[]{:S(2)}, u32[]{:S(2)}) %collective-permute-start.6) | collective-permute-done | bytes 131104 | tf_op jit(solution)/shard_map/ppermute | solution.py:46
  26.3 1.9 %middle_shard.1 = (f32[4,1024,256]{2,1,0:T(8,128)S(1)}, f32[4,128,256]{2,1,0:T(8,128)S(1)}, f32[8,128]{1,0:T(8,128)S(1)}) custom-call(f32[4,1024,256]{2,1,0:T(8,128)S(1)} %get-tuple-element.28.refs_0_, f32[4,128,128]{2,1,0:T(8,128)S(1)} %get-tuple-element.29.refs_1_, ...), custom_call_target="tpu_custom_call", output_to_operand_aliasing={{0}: (0, {}), {1}: (2, {}), {2}: (4, {})} | custom-call | flops 2147483648 | bytes 2097152 | tf_op jit(solution)/shard_map/middle_shard/pallas_call | solution.py:485
  28.2 0.0 collective-permute-done.7.refs_7_.refs_9_
  28.3 0.0 collective-permute-done.8.refs_11_.refs_13_
  28.3 2.1 %last_shard_decode.1 = bf16[16,4096]{1,0:T(8,128)(2,1)S(1)} custom-call(f32[4,128,256]{2,1,0:T(8,128)S(1)} %get-tuple-element.39.refs_0_, f32[4,128,128]{2,1,0:T(8,128)S(1)} %get-tuple-element.31.refs_3_.refs_1_, f32[8,128]{1,0:T(8,128)S(1)} %get-tuple-element.37.refs_2_, bf16[16,4096]{1,0:T(8,128)(2,1)S(1)} %get-tuple-element.33.refs_5_.refs_3_, ...), custom_call_target="tpu_custom_call" | custom-call | flops 268435456 | bytes 262144 | tf_op jit(solution)/shard_map/last_shard_decode/pallas_call | solution.py:500
  30.4 0.1 fusion
  30.5 0.3 collective-permute-start.10
  30.8 1.3 %collective-permute-start.11 = (bf16[2,4096]{1,0:T(2,128)(2,1)S(1)}, bf16[2,4096]{1,0:T(2,128)(2,1)S(1)}, u32[]{:S(2)}, u32[]{:S(2)}) collective-permute-start(bf16[2,4096]{1,0:T(2,128)(2,1)S(1)} %get-tuple-element.48), channel_id=1, source_target_pairs={{0,4},{4,0},{8,12},{12,8},{1,5},{5,1},{9,13},{13,9},{2,6},{6,2},{1... | collective-permute-start | bytes 49160 | tf_op jit(solution)/shard_map/ppermute | solution.py:544
  32.1 1.1 %collective-permute-start.9 = (bf16[2,4096]{1,0:T(2,128)(2,1)S(1)}, bf16[2,4096]{1,0:T(2,128)(2,1)S(1)}, u32[]{:S(2)}, u32[]{:S(2)}) collective-permute-start(bf16[2,4096]{1,0:T(2,128)(2,1)S(1)} %get-tuple-element.46), channel_id=1, source_target_pairs={{0,12},{4,8},{8,4},{12,0},{1,13},{5,9},{9,5},{13,1},{2,14},{6,10},... | collective-permute-start | bytes 49160 | tf_op jit(solution)/shard_map/ppermute | solution.py:544
  33.2 7.6 %last_shard_prefill.1 = bf16[128,4096]{1,0:T(8,128)(2,1)} custom-call(f32[4,1024,256]{2,1,0:T(8,128)S(1)} %get-tuple-element.36.refs_0_, f32[4,128,128]{2,1,0:T(8,128)S(1)} %get-tuple-element.29.refs_1_, f32[8,128]{1,0:T(8,128)S(1)} %get-tuple-element.37.refs_2_, bf16[128,4096]{1,0:T(8,128)(2,1)S(1)} %copy-done.2, bf16[128,512]{1,0:T(8,128)(2,1)S(1)} %copy-done, ...), custom_call_target="tpu_custom_call" | custom-call | flops 2147483648 | bytes 2097152 | tf_op jit(solution)/shard_map/last_shard_prefill/pallas_call | solution.py:513
  40.9 0.0 collective-permute-done.10
  40.9 0.0 collective-permute-done.11
  40.9 0.0 collective-permute-done.9
  40.9 0.8 %broadcast_select_fusion.2 = bf16[4,2,4096]{2,1,0:T(2,128)(2,1)} fusion(pred[4]{0:T(512)(128)(4,1)S(1)} %get-tuple-element.45, pred[4]{0:T(512)(128)(4,1)S(1)} %get-tuple-element.44, pred[4]{0:T(512)(128)(4,1)S(1)} %get-tuple-element.43, pred[4]{0:T(512)(128)(4,1)S(1)} %get-tuple-element.42, bf16[2,4096]{1,0:T(2,128)(2,1)S(1)} %get-tuple-element.47, ...), kind=kLoop, calls=%fused_computation.2 | loop fusion | flops 131072 | bytes 131088 | tf_op jit(solution)/shard_map/jit(_where)/select_n | solution.py:597
  (2 shorter events, 0.0 us)
Async XLA Ops:
  0.6 11.4 %collective-permute-start = (bf16[128,512]{1,0:T(8,128)(2,1)}, bf16[128,512]{1,0:T(8,128)(2,1)S(1)}, u32[]{:S(2)}, u32[]{:S(2)}) collective-permute-start(bf16[128,512]{1,0:T(8,128)(2,1)} %refs_6_.2), channel_id=1, source_target_pairs={{0,1},{1,3},{3,2},{2,0},{4,5},{5,7},{7,6},{6,4},{8,9},{9,11},{11,1... | collective-permute-start | bytes 393224 | tf_op jit(solution)/shard_map/ppermute | solution.py:46
  0.9 14.1 %collective-permute-start.1 = (bf16[128,512]{1,0:T(8,128)(2,1)}, bf16[128,512]{1,0:T(8,128)(2,1)S(1)}, u32[]{:S(2)}, u32[]{:S(2)}) collective-permute-start(bf16[128,512]{1,0:T(8,128)(2,1)} %refs_10_.1), channel_id=1, source_target_pairs={{1,0},{3,1},{2,3},{0,2},{5,4},{7,5},{6,7},{4,6},{9,8},{11,9},{10,1... | collective-permute-start | bytes 393224 | tf_op jit(solution)/shard_map/ppermute | solution.py:46
  4.0 1.5 %copy-start = (bf16[128,512]{1,0:T(8,128)(2,1)S(1)}, bf16[128,512]{1,0:T(8,128)(2,1)}, u32[]{:S(2)}) copy-start(bf16[128,512]{1,0:T(8,128)(2,1)} %refs_6_.2) | copy-start | bytes 393220
  5.5 9.5 %copy-start.1 = (bf16[128,512]{1,0:T(8,128)(2,1)S(1)}, bf16[128,512]{1,0:T(8,128)(2,1)}, u32[]{:S(2)}) copy-start(bf16[128,512]{1,0:T(8,128)(2,1)} %refs_10_.1) | copy-start | bytes 393220
  5.5 14.0 %copy-start.2 = (bf16[128,4096]{1,0:T(8,128)(2,1)S(1)}, bf16[128,4096]{1,0:T(8,128)(2,1)}, u32[]{:S(2)}) copy-start(bf16[128,4096]{1,0:T(8,128)(2,1)} %refs_3_.2) | copy-start | bytes 3145732
  5.5 14.0 %copy-start.3 = (s32[18]{0:T(128)S(1)}, s32[18]{0:T(128)}, u32[]{:S(2)}) copy-start(s32[18]{0:T(128)} %facts.1.refs_0_) | copy-start | bytes 220
  5.5 16.8 %collective-permute-start.5 = (bf16[128,512]{1,0:T(8,128)(2,1)S(1)}, bf16[128,512]{1,0:T(8,128)(2,1)S(1)}, u32[]{:S(2)}, u32[]{:S(2)}) collective-permute-start(bf16[128,512]{1,0:T(8,128)(2,1)S(1)} %copy-done), channel_id=1, source_target_pairs={{1,0},{3,1},{2,3},{0,2},{5,4},{7,5},{6,7},{4,6},{9,8},{11,9},{10,1... | collective-permute-start | bytes 393224 | tf_op jit(solution)/shard_map/ppermute | solution.py:46
  12.1 2.9 %collective-permute-start.2 = (bf16[8,5120]{1,0:T(8,128)(2,1)S(1)}, bf16[8,5120]{1,0:T(8,128)(2,1)S(1)}, u32[]{:S(2)}, u32[]{:S(2)}) collective-permute-start(bf16[8,5120]{1,0:T(8,128)(2,1)S(1)} %reshape.39.refs_5_), channel_id=1, source_target_pairs={{0,4},{4,0},{8,12},{12,8},{1,5},{5,1},{9,13},{13,9},{2,6},{6,2},{1... | collective-permute-start | bytes 245768 | tf_op jit(solution)/shard_map/ppermute | solution.py:544
  13.3 4.1 %collective-permute-start.3 = (bf16[8,5120]{1,0:T(8,128)(2,1)S(1)}, bf16[8,5120]{1,0:T(8,128)(2,1)S(1)}, u32[]{:S(2)}, u32[]{:S(2)}) collective-permute-start(bf16[8,5120]{1,0:T(8,128)(2,1)S(1)} %reshape.39.refs_5_), channel_id=1, source_target_pairs={{0,8},{4,12},{8,0},{12,4},{1,9},{5,13},{9,1},{13,5},{2,10},{6,14},... | collective-permute-start | bytes 245768 | tf_op jit(solution)/shard_map/ppermute | solution.py:544
  13.6 6.0 %collective-permute-start.4 = (bf16[8,5120]{1,0:T(8,128)(2,1)S(1)}, bf16[8,5120]{1,0:T(8,128)(2,1)S(1)}, u32[]{:S(2)}, u32[]{:S(2)}) collective-permute-start(bf16[8,5120]{1,0:T(8,128)(2,1)S(1)} %reshape.39.refs_5_), channel_id=1, source_target_pairs={{0,12},{4,8},{8,4},{12,0},{1,13},{5,9},{9,5},{13,1},{2,14},{6,10},... | collective-permute-start | bytes 245768 | tf_op jit(solution)/shard_map/ppermute | solution.py:544
  15.0 13.3 %collective-permute-start.7 = (bf16[128,512]{1,0:T(8,128)(2,1)S(1)}, bf16[128,512]{1,0:T(8,128)(2,1)S(1)}, u32[]{:S(2)}, u32[]{:S(2)}) collective-permute-start(bf16[128,512]{1,0:T(8,128)(2,1)S(1)} %collective-permute-done.refs_0_.refs_7_.refs_5_), channel_id=1, source_target_pairs={{0,1},{1,3},{3,2},{2,0},{4,5},{5,7},{7,6},{6,4},{8,9},{9,11},{11,1... | collective-permute-start | bytes 393224 | tf_op jit(solution)/shard_map/ppermute | solution.py:46
  15.0 11.4 %collective-permute-start.6 = (bf16[128,512]{1,0:T(8,128)(2,1)S(1)}, bf16[128,512]{1,0:T(8,128)(2,1)S(1)}, u32[]{:S(2)}, u32[]{:S(2)}) collective-permute-start(bf16[128,512]{1,0:T(8,128)(2,1)S(1)} %copy-done.1), channel_id=1, source_target_pairs={{0,1},{1,3},{3,2},{2,0},{4,5},{5,7},{7,6},{6,4},{8,9},{9,11},{11,1... | collective-permute-start | bytes 393224 | tf_op jit(solution)/shard_map/ppermute | solution.py:46
  17.4 10.9 %collective-permute-start.8 = (bf16[128,512]{1,0:T(8,128)(2,1)S(1)}, bf16[128,512]{1,0:T(8,128)(2,1)S(1)}, u32[]{:S(2)}, u32[]{:S(2)}) collective-permute-start(bf16[128,512]{1,0:T(8,128)(2,1)S(1)} %collective-permute-done.1.refs_1_.refs_10_.refs_12_), channel_id=1, source_target_pairs={{1,0},{3,1},{2,3},{0,2},{5,4},{7,5},{6,7},{4,6},{9,8},{11,9},{10,1... | collective-permute-start | bytes 393224 | tf_op jit(solution)/shard_map/ppermute | solution.py:46
  30.5 10.4 %collective-permute-start.10 = (bf16[2,4096]{1,0:T(2,128)(2,1)S(1)}, bf16[2,4096]{1,0:T(2,128)(2,1)S(1)}, u32[]{:S(2)}, u32[]{:S(2)}) collective-permute-start(bf16[2,4096]{1,0:T(2,128)(2,1)S(1)} %get-tuple-element.49), channel_id=1, source_target_pairs={{0,8},{4,12},{8,0},{12,4},{1,9},{5,13},{9,1},{13,5},{2,10},{6,14},... | collective-permute-start | bytes 49160 | tf_op jit(solution)/shard_map/ppermute | solution.py:544
  30.8 10.1 %collective-permute-start.11 = (bf16[2,4096]{1,0:T(2,128)(2,1)S(1)}, bf16[2,4096]{1,0:T(2,128)(2,1)S(1)}, u32[]{:S(2)}, u32[]{:S(2)}) collective-permute-start(bf16[2,4096]{1,0:T(2,128)(2,1)S(1)} %get-tuple-element.48), channel_id=1, source_target_pairs={{0,4},{4,0},{8,12},{12,8},{1,5},{5,1},{9,13},{13,9},{2,6},{6,2},{1... | collective-permute-start | bytes 49160 | tf_op jit(solution)/shard_map/ppermute | solution.py:544
  32.1 8.8 %collective-permute-start.9 = (bf16[2,4096]{1,0:T(2,128)(2,1)S(1)}, bf16[2,4096]{1,0:T(2,128)(2,1)S(1)}, u32[]{:S(2)}, u32[]{:S(2)}) collective-permute-start(bf16[2,4096]{1,0:T(2,128)(2,1)S(1)} %get-tuple-element.46), channel_id=1, source_target_pairs={{0,12},{4,8},{8,4},{12,0},{1,13},{5,9},{9,5},{13,1},{2,14},{6,10},... | collective-permute-start | bytes 49160 | tf_op jit(solution)/shard_map/ppermute | solution.py:544

commit v21 on v13

--- a/solution.py
+++ b/solution.py
@@ -557,12 +557,14 @@
     kv, decoded_query = lax.optimization_barrier(
         (jnp.concatenate([prompt_key, prompt_value], axis=0), decoded_query)
     )
-    later_kv, own, facts = lax.optimization_barrier((kv, own, facts))
-    pieces, maxima, up, down = [kv], None, kv, later_kv
+    own, facts = lax.optimization_barrier((own, facts))
+    pieces, maxima, up, down = [kv], None, kv, kv
     for d in range(1, plan.size // 2 + 1):
         if d == 2:
             up, facts = lax.optimization_barrier((up, facts))
         up = plan.step(up, True)
+        if d == 1:
+            up, down = lax.optimization_barrier((up, down))
         down = plan.step(down, False) if 2 * d < plan.size else None
         pieces += [up, down]
     pieces = pieces[: plan.size]

time: 38.8 us -> 39.5 us (1.018)
  waiting for transfers between devices: 3.39 us -> 10.4 us
  starting transfers between devices: 15.3 us -> 8.96 us
    ppermute x3, waiting for transfers between devices: 3.37 us -> 10.4 us  [step(): lax.ppermute(array, 'tp', self.pairs if up else [(b, a) for a, b in self....]
    ppermute x3, starting transfers between devices: 11.4 us -> 5.1 us  [step(): lax.ppermute(array, 'tp', self.pairs if up else [(b, a) for a, b in self....]
  transfers between devices with their start and end apart: 9 -> 9, of which waited for: 2 -> 3; matrix products, arithmetic and copies ran while one was open for 3% -> 3% of each run, Pallas kernels for 36% -> 36%
where the time goes in v21:
time: 39.5 us; the launch traced here: 39.3 us
  Pallas kernels  16.1 us (41%)
  waiting for transfers between devices  10.4 us (26%)
  starting transfers between devices  8.96 us (23%)
  other arithmetic  2.88 us (7%)
  between operations  0.75 us (2%)
    ppermute x3, waiting for transfers between devices, step(): lax.ppermute(array, 'tp', self.pairs if up else [(b, a) for a, b in self....  10.4 us
    pallas_call x1, Pallas kernels, call_prefill(): pl.pallas_call(lambda *refs: prefill_kernel(plan, *refs), in_specs=[VMEM]...  7.58 us
    ppermute x3, starting transfers between devices, step(): lax.ppermute(array, 'tp', self.pairs if up else [(b, a) for a, b in self....  5.1 us
    ppermute x6, starting transfers between devices, paired(): lax.ppermute(array, 'pd', [(g, g ^ k) for g in range(lax.axis_size('pd'))])  3.86 us
    pallas_call x1, Pallas kernels, call_first(): pl.pallas_call(lambda *refs: first_kernel(plan, len(blocks), *refs), in_s...  2.92 us
    pallas_call x1, Pallas kernels, call_middle(): pl.pallas_call(lambda *refs: middle_kernel(plan, *refs), in_specs=[VMEM]...  2.22 us
    pallas_call x1, Pallas kernels, call_decode(): pl.pallas_call(lambda *refs: decode_kernel(plan, *refs), in_specs=[VMEM]...  2.13 us
    pallas_call x1, Pallas kernels, facts_row(): pl.pallas_call(kernel, in_specs=[SMEM, SMEM], out_specs=SMEM, out_shape=j...  1.3 us
  transfers between devices with their start and end apart: 9, of which 3 were waited for; matrix products, arithmetic and copies ran while one was open for 3% of the time, Pallas kernels for 36%

profile of v21, /device:TPU:0, one launch (start us, length us, event | category | flops | bytes accessed | tf_op | source)
XLA Modules:
  0.0 39.3 jit_solution(4881229977103309710)
XLA Ops:
  0.6 1.0 %pad_maximum_fusion.refs_3_.refs_4_.refs_6_ = bf16[256,512]{1,0:T(8,128)(2,1)S(1)} fusion(bf16[128,512]{1,0:T(8,128)(2,1)} %param.10, bf16[128,512]{1,0:T(8,128)(2,1)} %param.9), kind=kLoop, calls=%fused_computation | loop fusion | flops 524288 | bytes 524288 | tf_op jit(solution)/shard_map/concatenate | solution.py:558
  1.6 3.1 %collective-permute-start = (bf16[256,512]{1,0:T(8,128)(2,1)S(1)}, bf16[256,512]{1,0:T(8,128)(2,1)S(1)}, u32[]{:S(2)}, u32[]{:S(2)}) collective-permute-start(bf16[256,512]{1,0:T(8,128)(2,1)S(1)} %pad_maximum_fusion.refs_3_.refs_4_.refs_6_), channel_id=1, source_target_pairs={{0,1},{1,3},{3,2},{2,0},{4,5},{5,7},{7,6},{6,4},{8,9},{9,11},{11,1... | collective-permute-start | bytes 786440 | tf_op jit(solution)/shard_map/ppermute | solution.py:46
  4.7 0.9 %pad_maximum_fusion.1 = bf16[4,2,5120]{2,1,0:T(2,128)(2,1)S(1)} fusion(bf16[4,2,512]{2,1,0:T(2,128)(2,1)} %param.15, bf16[4,2,512]{2,1,0:T(2,128)(2,1)} %param.14, bf16[4,2,4096]{2,1,0:T(2,128)(2,1)} %param.13), kind=kLoop, calls=%fused_computation.5 | loop fusion | flops 245760 | bytes 163840 | tf_op jit(solution)/shard_map/concatenate | solution.py:553
  5.7 1.3 %facts.1.refs_0_ = s32[18]{0:T(128)} custom-call(s32[4,4]{1,0:T(4,128)} %lengths_ref.1, s32[16]{0:T(128)} %slots_ref.1), custom_call_target="tpu_custom_call" | custom-call | flops 5000000000 | tf_op jit(solution)/shard_map/facts/pallas_call | solution.py:126
  7.0 0.0 copy-start
  7.0 0.0 copy-start.1
  7.0 0.1 collective-permute-start.1
  7.1 1.6 %collective-permute-start.2 = (bf16[8,5120]{1,0:T(8,128)(2,1)S(1)}, bf16[8,5120]{1,0:T(8,128)(2,1)S(1)}, u32[]{:S(2)}, u32[]{:S(2)}) collective-permute-start(bf16[8,5120]{1,0:T(8,128)(2,1)S(1)} %reshape.39.refs_5_), channel_id=1, source_target_pairs={{0,8},{4,12},{8,0},{12,4},{1,9},{5,13},{9,1},{13,5},{2,10},{6,14},... | collective-permute-start | bytes 245768 | tf_op jit(solution)/shard_map/ppermute | solution.py:538
  8.7 0.3 collective-permute-start.3
  9.0 3.1 %collective-permute-done.refs_0_.refs_4_.refs_5_.refs_7_ = bf16[256,512]{1,0:T(8,128)(2,1)S(1)} collective-permute-done((bf16[256,512]{1,0:T(8,128)(2,1)S(1)}, bf16[256,512]{1,0:T(8,128)(2,1)S(1)}, u32[]{:S(2)}, u32[]{:S(2)}) %collective-permute-start) | collective-permute-done | bytes 262176 | tf_op jit(solution)/shard_map/ppermute | solution.py:46
  12.0 1.7 %collective-permute-start.4 = (bf16[256,512]{1,0:T(8,128)(2,1)S(1)}, bf16[256,512]{1,0:T(8,128)(2,1)S(1)}, u32[]{:S(2)}, u32[]{:S(2)}) collective-permute-start(bf16[256,512]{1,0:T(8,128)(2,1)S(1)} %pad_maximum_fusion.refs_3_.refs_4_.refs_6_), channel_id=1, source_target_pairs={{1,0},{3,1},{2,3},{0,2},{5,4},{7,5},{6,7},{4,6},{9,8},{11,9},{10,1... | collective-permute-start | bytes 786440 | tf_op jit(solution)/shard_map/ppermute | solution.py:46
  13.8 0.3 collective-permute-start.5
  14.0 0.0 collective-permute-done.1.refs_6_
  14.0 0.0 collective-permute-done.2.refs_7_
  14.1 0.0 collective-permute-done.3.refs_8_
  14.1 0.0 copy-done
  14.1 0.0 copy-done.1
  14.1 2.9 %first_shards.1 = (f32[4,1024,256]{2,1,0:T(8,128)S(1)}, f32[4,128,128]{2,1,0:T(8,128)S(1)}, f32[4,128,256]{2,1,0:T(8,128)S(1)}, f32[4,128,128]{2,1,0:T(8,128)S(1...) custom-call(s32[18]{0:T(128)S(1)} %copy-done.1, ...), custom_call_target="tpu_custom_call" | custom-call | flops 4294967296 | bytes 2097152 | tf_op jit(solution)/shard_map/first_shards/pallas_call | solution.py:465
  17.0 0.1 compare_reduce_fusion.2
  17.2 3.4 %collective-permute-done.4.refs_7_.refs_6_.refs_8_ = bf16[256,512]{1,0:T(8,128)(2,1)S(1)} collective-permute-done((bf16[256,512]{1,0:T(8,128)(2,1)S(1)}, bf16[256,512]{1,0:T(8,128)(2,1)S(1)}, u32[]{:S(2)}, u32[]{:S(2)}) %collective-permute-start.4) | collective-permute-done | bytes 262176 | tf_op jit(solution)/shard_map/ppermute | solution.py:46
  20.6 2.2 %middle_shard.1 = (f32[4,1024,256]{2,1,0:T(8,128)S(1)}, f32[4,128,256]{2,1,0:T(8,128)S(1)}, f32[8,128]{1,0:T(8,128)S(1)}) custom-call(f32[4,1024,256]{2,1,0:T(8,128)S(1)} %get-tuple-element.26.refs_0_, f32[4,128,128]{2,1,0:T(8,128)S(1)} %get-tuple-element.27.refs_1_, ...), custom_call_target="tpu_custom_call", output_to_operand_aliasing={{0}: (0, {}), {1}: (2, {}), {2}: (4, {})} | custom-call | flops 2147483648 | bytes 2097152 | tf_op jit(solution)/shard_map/middle_shard/pallas_call | solution.py:479
  22.8 3.9 %collective-permute-done.5.refs_7_.refs_9_ = bf16[256,512]{1,0:T(8,128)(2,1)S(1)} collective-permute-done((bf16[256,512]{1,0:T(8,128)(2,1)S(1)}, bf16[256,512]{1,0:T(8,128)(2,1)S(1)}, u32[]{:S(2)}, u32[]{:S(2)}) %collective-permute-start.5) | collective-permute-done | bytes 262176 | tf_op jit(solution)/shard_map/ppermute | solution.py:46
  26.7 2.1 %last_shard_decode.1 = bf16[16,4096]{1,0:T(8,128)(2,1)S(1)} custom-call(f32[4,128,256]{2,1,0:T(8,128)S(1)} %get-tuple-element.37.refs_0_, f32[4,128,128]{2,1,0:T(8,128)S(1)} %get-tuple-element.29.refs_3_.refs_1_, f32[8,128]{1,0:T(8,128)S(1)} %get-tuple-element.34.refs_2_, bf16[16,4096]{1,0:T(8,128)(2,1)S(1)} %get-tuple-element.31.refs_5_.refs_3_, ...), custom_call_target="tpu_custom_call" | custom-call | flops 268435456 | bytes 262144 | tf_op jit(solution)/shard_map/last_shard_decode/pallas_call | solution.py:494
  28.8 0.1 fusion
  28.9 1.2 %collective-permute-start.6 = (bf16[2,4096]{1,0:T(2,128)(2,1)S(1)}, bf16[2,4096]{1,0:T(2,128)(2,1)S(1)}, u32[]{:S(2)}, u32[]{:S(2)}) collective-permute-start(bf16[2,4096]{1,0:T(2,128)(2,1)S(1)} %get-tuple-element.44), channel_id=1, source_target_pairs={{0,12},{4,8},{8,4},{12,0},{1,13},{5,9},{9,5},{13,1},{2,14},{6,10},... | collective-permute-start | bytes 49160 | tf_op jit(solution)/shard_map/ppermute | solution.py:538
  30.1 0.5 %collective-permute-start.7 = (bf16[2,4096]{1,0:T(2,128)(2,1)S(1)}, bf16[2,4096]{1,0:T(2,128)(2,1)S(1)}, u32[]{:S(2)}, u32[]{:S(2)}) collective-permute-start(bf16[2,4096]{1,0:T(2,128)(2,1)S(1)} %get-tuple-element.47), channel_id=1, source_target_pairs={{0,8},{4,12},{8,0},{12,4},{1,9},{5,13},{9,1},{13,5},{2,10},{6,14},... | collective-permute-start | bytes 49160 | tf_op jit(solution)/shard_map/ppermute | solution.py:538
  30.6 0.2 collective-permute-start.8
  30.8 7.6 %last_shard_prefill.1 = bf16[128,4096]{1,0:T(8,128)(2,1)} custom-call(f32[4,1024,256]{2,1,0:T(8,128)S(1)} %get-tuple-element.33.refs_0_, f32[4,128,128]{2,1,0:T(8,128)S(1)} %get-tuple-element.27.refs_1_, f32[8,128]{1,0:T(8,128)S(1)} %get-tuple-element.34.refs_2_, bf16[128,4096]{1,0:T(8,128)(2,1)S(1)} %copy-done, ...), custom_call_target="tpu_custom_call" | custom-call | flops 2147483648 | bytes 2097152 | tf_op jit(solution)/shard_map/last_shard_prefill/pallas_call | solution.py:507
  38.4 0.0 collective-permute-done.6
  38.4 0.0 collective-permute-done.7
  38.5 0.0 collective-permute-done.8
  38.5 0.8 %broadcast_select_fusion.2 = bf16[4,2,4096]{2,1,0:T(2,128)(2,1)} fusion(pred[4]{0:T(512)(128)(4,1)S(1)} %get-tuple-element.43, pred[4]{0:T(512)(128)(4,1)S(1)} %get-tuple-element.42, pred[4]{0:T(512)(128)(4,1)S(1)} %get-tuple-element.41, pred[4]{0:T(512)(128)(4,1)S(1)} %get-tuple-element.40, bf16[2,4096]{1,0:T(2,128)(2,1)S(1)} %get-tuple-element.45, ...), kind=kLoop, calls=%fused_computation.3 | loop fusion | flops 131072 | bytes 131088 | tf_op jit(solution)/shard_map/jit(_where)/select_n | solution.py:585
  (2 shorter events, 0.0 us)
Async XLA Ops:
  1.6 10.4 %collective-permute-start = (bf16[256,512]{1,0:T(8,128)(2,1)S(1)}, bf16[256,512]{1,0:T(8,128)(2,1)S(1)}, u32[]{:S(2)}, u32[]{:S(2)}) collective-permute-start(bf16[256,512]{1,0:T(8,128)(2,1)S(1)} %pad_maximum_fusion.refs_3_.refs_4_.refs_6_), channel_id=1, source_target_pairs={{0,1},{1,3},{3,2},{2,0},{4,5},{5,7},{7,6},{6,4},{8,9},{9,11},{11,1... | collective-permute-start | bytes 786440 | tf_op jit(solution)/shard_map/ppermute | solution.py:46
  7.0 7.1 %copy-start = (bf16[128,4096]{1,0:T(8,128)(2,1)S(1)}, bf16[128,4096]{1,0:T(8,128)(2,1)}, u32[]{:S(2)}) copy-start(bf16[128,4096]{1,0:T(8,128)(2,1)} %refs_3_.1) | copy-start | bytes 3145732
  7.0 7.1 %copy-start.1 = (s32[18]{0:T(128)S(1)}, s32[18]{0:T(128)}, u32[]{:S(2)}) copy-start(s32[18]{0:T(128)} %facts.1.refs_0_) | copy-start | bytes 220
  7.0 7.0 %collective-permute-start.1 = (bf16[8,5120]{1,0:T(8,128)(2,1)S(1)}, bf16[8,5120]{1,0:T(8,128)(2,1)S(1)}, u32[]{:S(2)}, u32[]{:S(2)}) collective-permute-start(bf16[8,5120]{1,0:T(8,128)(2,1)S(1)} %reshape.39.refs_5_), channel_id=1, source_target_pairs={{0,4},{4,0},{8,12},{12,8},{1,5},{5,1},{9,13},{13,9},{2,6},{6,2},{1... | collective-permute-start | bytes 245768 | tf_op jit(solution)/shard_map/ppermute | solution.py:538
  7.1 7.0 %collective-permute-start.2 = (bf16[8,5120]{1,0:T(8,128)(2,1)S(1)}, bf16[8,5120]{1,0:T(8,128)(2,1)S(1)}, u32[]{:S(2)}, u32[]{:S(2)}) collective-permute-start(bf16[8,5120]{1,0:T(8,128)(2,1)S(1)} %reshape.39.refs_5_), channel_id=1, source_target_pairs={{0,8},{4,12},{8,0},{12,4},{1,9},{5,13},{9,1},{13,5},{2,10},{6,14},... | collective-permute-start | bytes 245768 | tf_op jit(solution)/shard_map/ppermute | solution.py:538
  8.7 5.4 %collective-permute-start.3 = (bf16[8,5120]{1,0:T(8,128)(2,1)S(1)}, bf16[8,5120]{1,0:T(8,128)(2,1)S(1)}, u32[]{:S(2)}, u32[]{:S(2)}) collective-permute-start(bf16[8,5120]{1,0:T(8,128)(2,1)S(1)} %reshape.39.refs_5_), channel_id=1, source_target_pairs={{0,12},{4,8},{8,4},{12,0},{1,13},{5,9},{9,5},{13,1},{2,14},{6,10},... | collective-permute-start | bytes 245768 | tf_op jit(solution)/shard_map/ppermute | solution.py:538
  12.0 8.5 %collective-permute-start.4 = (bf16[256,512]{1,0:T(8,128)(2,1)S(1)}, bf16[256,512]{1,0:T(8,128)(2,1)S(1)}, u32[]{:S(2)}, u32[]{:S(2)}) collective-permute-start(bf16[256,512]{1,0:T(8,128)(2,1)S(1)} %pad_maximum_fusion.refs_3_.refs_4_.refs_6_), channel_id=1, source_target_pairs={{1,0},{3,1},{2,3},{0,2},{5,4},{7,5},{6,7},{4,6},{9,8},{11,9},{10,1... | collective-permute-start | bytes 786440 | tf_op jit(solution)/shard_map/ppermute | solution.py:46
  13.8 13.0 %collective-permute-start.5 = (bf16[256,512]{1,0:T(8,128)(2,1)S(1)}, bf16[256,512]{1,0:T(8,128)(2,1)S(1)}, u32[]{:S(2)}, u32[]{:S(2)}) collective-permute-start(bf16[256,512]{1,0:T(8,128)(2,1)S(1)} %collective-permute-done.refs_0_.refs_4_.refs_5_.refs_7_), channel_id=1, source_target_pairs={{0,1},{1,3},{3,2},{2,0},{4,5},{5,7},{7,6},{6,4},{8,9},{9,11},{11,1... | collective-permute-start | bytes 786440 | tf_op jit(solution)/shard_map/ppermute | solution.py:46
  28.9 9.5 %collective-permute-start.6 = (bf16[2,4096]{1,0:T(2,128)(2,1)S(1)}, bf16[2,4096]{1,0:T(2,128)(2,1)S(1)}, u32[]{:S(2)}, u32[]{:S(2)}) collective-permute-start(bf16[2,4096]{1,0:T(2,128)(2,1)S(1)} %get-tuple-element.44), channel_id=1, source_target_pairs={{0,12},{4,8},{8,4},{12,0},{1,13},{5,9},{9,5},{13,1},{2,14},{6,10},... | collective-permute-start | bytes 49160 | tf_op jit(solution)/shard_map/ppermute | solution.py:538
  30.1 8.4 %collective-permute-start.7 = (bf16[2,4096]{1,0:T(2,128)(2,1)S(1)}, bf16[2,4096]{1,0:T(2,128)(2,1)S(1)}, u32[]{:S(2)}, u32[]{:S(2)}) collective-permute-start(bf16[2,4096]{1,0:T(2,128)(2,1)S(1)} %get-tuple-element.47), channel_id=1, source_target_pairs={{0,8},{4,12},{8,0},{12,4},{1,9},{5,13},{9,1},{13,5},{2,10},{6,14},... | collective-permute-start | bytes 49160 | tf_op jit(solution)/shard_map/ppermute | solution.py:538
  30.6 7.8 %collective-permute-start.8 = (bf16[2,4096]{1,0:T(2,128)(2,1)S(1)}, bf16[2,4096]{1,0:T(2,128)(2,1)S(1)}, u32[]{:S(2)}, u32[]{:S(2)}) collective-permute-start(bf16[2,4096]{1,0:T(2,128)(2,1)S(1)} %get-tuple-element.46), channel_id=1, source_target_pairs={{0,4},{4,0},{8,12},{12,8},{1,5},{5,1},{9,13},{13,9},{2,6},{6,2},{1... | collective-permute-start | bytes 49160 | tf_op jit(solution)/shard_map/ppermute | solution.py:538

commit v22 on v12

--- a/solution.py
+++ b/solution.py
@@ -477,6 +477,30 @@
     )(*state[:2], state[4], query, *pieces)
 
 
+def stacked(key, value):
+    tokens, width = key.shape
+
+    def kernel(k_ref, v_ref, out_ref, sem):
+        copies = [
+            pltpu.make_async_copy(ref, out_ref.at[pl.ds(i * tokens, tokens), :], sem.at[i])
+            for i, ref in enumerate((k_ref, v_ref))
+        ]
+        for copy in copies:
+            copy.start()
+        for copy in copies:
+            copy.wait()
+
+    return pl.pallas_call(
+        kernel,
+        in_specs=[HBM, HBM],
+        out_specs=HBM,
+        out_shape=jax.ShapeDtypeStruct((2 * tokens, width), key.dtype),
+        scratch_shapes=[pltpu.SemaphoreType.DMA((2,))],
+        compiler_params=pltpu.CompilerParams(vmem_limit_bytes=60 * MIB),
+        name="stacked",
+    )(key, value)
+
+
 def start_maxima(*arrays, flops=5 * 10**9):
     def kernel(*refs):
         refs[-1][...] = jnp.full((8, HEAD_SIZE), MASKED, jnp.float32)
@@ -513,7 +537,7 @@
     )
     facts = facts_row(plan, prompt_lengths, decode_slot)
     kv, decoded_query = lax.optimization_barrier(
-        (jnp.concatenate([prompt_key, prompt_value], axis=0), decoded_query)
+        (stacked(prompt_key, prompt_value), decoded_query)
     )
     later_kv, own = lax.optimization_barrier((kv, own))
     pieces, maxima, up, down = [kv], None, kv, later_kv

time: 37.6 us -> 45.9 us (1.22)
  Pallas kernels: 14.6 us -> 23.7 us
  other arithmetic: 2.88 us -> 1.89 us
    pallas_call x0 -> x1, Pallas kernels: none -> 9.06 us  [stacked(): pl.pallas_call(kernel, in_specs=[HBM, HBM], out_specs=HBM, out_shape=jax....]
    concatenate x1 -> x0, other arithmetic: 0.99 us -> none  [body(): jnp.concatenate([prompt_key, prompt_value], axis=0)]
  transfers between devices with their start and end apart: 9 -> 9, of which waited for: 2 -> 2; matrix products, arithmetic and copies ran while one was open for 3% -> 2% of each run, Pallas kernels for 34% -> 27%
where the time goes in v22:
time: 45.9 us; the launch traced here: 45.6 us
  Pallas kernels  23.7 us (52%)
  starting transfers between devices  15.5 us (34%)
  waiting for transfers between devices  3.59 us (8%)
  other arithmetic  1.89 us (4%)
  between operations  0.78 us (2%)
    ppermute x3, starting transfers between devices, step(): lax.ppermute(array, 'tp', self.pairs if up else [(b, a) for a, b in self....  11.6 us
    pallas_call x1, Pallas kernels, stacked(): pl.pallas_call(kernel, in_specs=[HBM, HBM], out_specs=HBM, out_shape=jax....  9.06 us
    pallas_call x1, Pallas kernels, call_prefill(): pl.pallas_call(lambda *refs: prefill_kernel(plan, *refs), in_specs=[VMEM]...  7.58 us
    ppermute x6, starting transfers between devices, paired(): lax.ppermute(array, 'pd', [(g, g ^ k) for g in range(lax.axis_size('pd'))])  3.86 us
    pallas_call x1, Pallas kernels, call_first(): pl.pallas_call(lambda *refs: first_kernel(plan, len(blocks), *refs), in_s...  3.61 us
    ppermute x3, waiting for transfers between devices, step(): lax.ppermute(array, 'tp', self.pairs if up else [(b, a) for a, b in self....  3.57 us
    pallas_call x1, Pallas kernels, call_decode(): pl.pallas_call(lambda *refs: decode_kernel(plan, *refs), in_specs=[VMEM]...  2.13 us
    pallas_call x1, Pallas kernels, facts_row(): pl.pallas_call(kernel, in_specs=[SMEM, SMEM], out_specs=SMEM, out_shape=j...  1.29 us
  transfers between devices with their start and end apart: 9, of which 2 were waited for; matrix products, arithmetic and copies ran while one was open for 2% of the time, Pallas kernels for 27%

profile of v22, /device:TPU:0, one launch (start us, length us, event | category | flops | bytes accessed | tf_op | source)
XLA Modules:
  0.0 45.6 jit_solution(7701170308031141884)
XLA Ops:
  0.6 9.1 %stacked.1.refs_3_.refs_4_.refs_6_ = bf16[256,512]{1,0:T(8,128)(2,1)} custom-call(bf16[128,512]{1,0:T(8,128)(2,1)} %k_ref.1, bf16[128,512]{1,0:T(8,128)(2,1)} %v_ref.1), custom_call_target="tpu_custom_call" | custom-call | tf_op jit(solution)/shard_map/stacked/pallas_call | solution.py:493
  9.7 3.1 %collective-permute-start = (bf16[256,512]{1,0:T(8,128)(2,1)}, bf16[256,512]{1,0:T(8,128)(2,1)S(1)}, u32[]{:S(2)}, u32[]{:S(2)}) collective-permute-start(bf16[256,512]{1,0:T(8,128)(2,1)} %stacked.1.refs_3_.refs_4_.refs_6_), channel_id=1, source_target_pairs={{0,1},{1,3},{3,2},{2,0},{4,5},{5,7},{7,6},{6,4},{8,9},{9,11},{11,1... | collective-permute-start | bytes 786440 | tf_op jit(solution)/shard_map/ppermute | solution.py:46
  12.8 0.9 %pad_maximum_fusion = bf16[4,2,5120]{2,1,0:T(2,128)(2,1)S(1)} fusion(bf16[4,2,512]{2,1,0:T(2,128)(2,1)} %param.15, bf16[4,2,512]{2,1,0:T(2,128)(2,1)} %param.14, bf16[4,2,4096]{2,1,0:T(2,128)(2,1)} %param.13), kind=kLoop, calls=%fused_computation.4 | loop fusion | flops 245760 | bytes 163840 | tf_op jit(solution)/shard_map/concatenate | solution.py:535
  13.8 0.1 collective-permute-start.2
  13.8 1.6 %collective-permute-start.3 = (bf16[8,5120]{1,0:T(8,128)(2,1)S(1)}, bf16[8,5120]{1,0:T(8,128)(2,1)S(1)}, u32[]{:S(2)}, u32[]{:S(2)}) collective-permute-start(bf16[8,5120]{1,0:T(8,128)(2,1)S(1)} %reshape.39.refs_6_), channel_id=1, source_target_pairs={{0,8},{4,12},{8,0},{12,4},{1,9},{5,13},{9,1},{13,5},{2,10},{6,14},... | collective-permute-start | bytes 245768 | tf_op jit(solution)/shard_map/ppermute | solution.py:520
  15.4 0.3 collective-permute-start.4
  15.7 1.1 %collective-permute-start.1 = (bf16[256,512]{1,0:T(8,128)(2,1)}, bf16[256,512]{1,0:T(8,128)(2,1)S(1)}, u32[]{:S(2)}, u32[]{:S(2)}) collective-permute-start(bf16[256,512]{1,0:T(8,128)(2,1)} %stacked.1.refs_3_.refs_4_.refs_6_), channel_id=1, source_target_pairs={{1,0},{3,1},{2,3},{0,2},{5,4},{7,5},{6,7},{4,6},{9,8},{11,9},{10,1... | collective-permute-start | bytes 786440 | tf_op jit(solution)/shard_map/ppermute | solution.py:46
  16.8 1.3 %facts.1.refs_0_ = s32[18]{0:T(128)} custom-call(s32[4,4]{1,0:T(4,128)} %lengths_ref.1, s32[16]{0:T(128)} %slots_ref.1), custom_call_target="tpu_custom_call" | custom-call | flops 5000000000 | tf_op jit(solution)/shard_map/facts/pallas_call | solution.py:126
  18.1 0.0 copy-start
  18.1 0.0 copy-start.1
  18.1 0.0 copy-start.2
  18.2 2.2 %collective-permute-done.refs_0_.refs_4_.refs_5_.refs_7_ = bf16[256,512]{1,0:T(8,128)(2,1)S(1)} collective-permute-done((bf16[256,512]{1,0:T(8,128)(2,1)}, bf16[256,512]{1,0:T(8,128)(2,1)S(1)}, u32[]{:S(2)}, u32[]{:S(2)}) %collective-permute-start) | collective-permute-done | bytes 262176 | tf_op jit(solution)/shard_map/ppermute | solution.py:46
  20.4 7.5 %collective-permute-start.5 = (bf16[256,512]{1,0:T(8,128)(2,1)S(1)}, bf16[256,512]{1,0:T(8,128)(2,1)S(1)}, u32[]{:S(2)}, u32[]{:S(2)}) collective-permute-start(bf16[256,512]{1,0:T(8,128)(2,1)S(1)} %collective-permute-done.refs_0_.refs_4_.refs_5_.refs_7_), channel_id=1, source_target_pairs={{0,1},{1,3},{3,2},{2,0},{4,5},{5,7},{7,6},{6,4},{8,9},{9,11},{11,1... | collective-permute-start | bytes 786440 | tf_op jit(solution)/shard_map/ppermute | solution.py:46
  27.8 0.0 collective-permute-done.2.refs_7_
  27.8 0.0 collective-permute-done.3.refs_8_
  27.8 0.0 collective-permute-done.4.refs_9_
  27.8 0.0 collective-permute-done.1.refs_5_.refs_6_.refs_8_
  27.9 0.0 copy-done
  27.9 0.0 copy-done.1
  27.9 0.0 copy-done.2
  27.9 3.6 %first_shards.1 = (f32[4,1024,256]{2,1,0:T(8,128)S(1)}, f32[4,128,128]{2,1,0:T(8,128)S(1)}, f32[4,128,256]{2,1,0:T(8,128)S(1)}, f32[4,128,128]{2,1,0:T(8,128)S(1...) custom-call(s32[18]{0:T(128)S(1)} %copy-done.2, ...), custom_call_target="tpu_custom_call" | custom-call | flops 6442450944 | bytes 2097152 | tf_op jit(solution)/shard_map/first_shards/pallas_call | solution.py:439
  31.5 0.1 compare_reduce_fusion.2
  31.6 1.4 %collective-permute-done.5.refs_7_.refs_9_ = bf16[256,512]{1,0:T(8,128)(2,1)S(1)} collective-permute-done((bf16[256,512]{1,0:T(8,128)(2,1)S(1)}, bf16[256,512]{1,0:T(8,128)(2,1)S(1)}, u32[]{:S(2)}, u32[]{:S(2)}) %collective-permute-start.5) | collective-permute-done | bytes 262176 | tf_op jit(solution)/shard_map/ppermute | solution.py:46
  33.0 2.1 %last_shard_decode.1 = bf16[16,4096]{1,0:T(8,128)(2,1)S(1)} custom-call(f32[4,128,256]{2,1,0:T(8,128)S(1)} %get-tuple-element.25.refs_0_, f32[4,128,128]{2,1,0:T(8,128)S(1)} %get-tuple-element.26.refs_1_, f32[8,128]{1,0:T(8,128)S(1)} %get-tuple-element.22.refs_2_, bf16[16,4096]{1,0:T(8,128)(2,1)S(1)} %get-tuple-element.27.refs_3_, ...), custom_call_target="tpu_custom_call" | custom-call | flops 268435456 | bytes 262144 | tf_op jit(solution)/shard_map/last_shard_decode/pallas_call | solution.py:452
  35.1 0.1 fusion
  35.2 1.2 %collective-permute-start.6 = (bf16[2,4096]{1,0:T(2,128)(2,1)S(1)}, bf16[2,4096]{1,0:T(2,128)(2,1)S(1)}, u32[]{:S(2)}, u32[]{:S(2)}) collective-permute-start(bf16[2,4096]{1,0:T(2,128)(2,1)S(1)} %get-tuple-element.34), channel_id=1, source_target_pairs={{0,12},{4,8},{8,4},{12,0},{1,13},{5,9},{9,5},{13,1},{2,14},{6,10},... | collective-permute-start | bytes 49160 | tf_op jit(solution)/shard_map/ppermute | solution.py:520
  36.4 0.5 %collective-permute-start.7 = (bf16[2,4096]{1,0:T(2,128)(2,1)S(1)}, bf16[2,4096]{1,0:T(2,128)(2,1)S(1)}, u32[]{:S(2)}, u32[]{:S(2)}) collective-permute-start(bf16[2,4096]{1,0:T(2,128)(2,1)S(1)} %get-tuple-element.37), channel_id=1, source_target_pairs={{0,8},{4,12},{8,0},{12,4},{1,9},{5,13},{9,1},{13,5},{2,10},{6,14},... | collective-permute-start | bytes 49160 | tf_op jit(solution)/shard_map/ppermute | solution.py:520
  36.9 0.2 collective-permute-start.8
  37.1 7.6 %last_shard_prefill.1 = bf16[128,4096]{1,0:T(8,128)(2,1)} custom-call(f32[4,1024,256]{2,1,0:T(8,128)S(1)} %get-tuple-element.20.refs_0_, f32[4,128,128]{2,1,0:T(8,128)S(1)} %get-tuple-element.21.refs_1_, f32[8,128]{1,0:T(8,128)S(1)} %get-tuple-element.22.refs_2_, bf16[128,4096]{1,0:T(8,128)(2,1)S(1)} %copy-done.1, bf16[256,512]{1,0:T(8,128)(2,1)S(1)} %copy-done, ...), custom_call_target="tpu_custom_call" | custom-call | flops 2147483648 | bytes 2097152 | tf_op jit(solution)/shard_map/last_shard_prefill/pallas_call | solution.py:465
  44.7 0.0 collective-permute-done.6
  44.7 0.0 collective-permute-done.7
  44.8 0.0 collective-permute-done.8
  44.8 0.8 %broadcast_select_fusion.2 = bf16[4,2,4096]{2,1,0:T(2,128)(2,1)} fusion(pred[4]{0:T(512)(128)(4,1)S(1)} %get-tuple-element.33, pred[4]{0:T(512)(128)(4,1)S(1)} %get-tuple-element.32, pred[4]{0:T(512)(128)(4,1)S(1)} %get-tuple-element.31, pred[4]{0:T(512)(128)(4,1)S(1)} %get-tuple-element.30, bf16[2,4096]{1,0:T(2,128)(2,1)S(1)} %get-tuple-element.35, ...), kind=kLoop, calls=%fused_computation.2 | loop fusion | flops 131072 | bytes 131088 | tf_op jit(solution)/shard_map/jit(_where)/select_n | solution.py:564
  (2 shorter events, 0.0 us)
Async XLA Ops:
  9.7 10.7 %collective-permute-start = (bf16[256,512]{1,0:T(8,128)(2,1)}, bf16[256,512]{1,0:T(8,128)(2,1)S(1)}, u32[]{:S(2)}, u32[]{:S(2)}) collective-permute-start(bf16[256,512]{1,0:T(8,128)(2,1)} %stacked.1.refs_3_.refs_4_.refs_6_), channel_id=1, source_target_pairs={{0,1},{1,3},{3,2},{2,0},{4,5},{5,7},{7,6},{6,4},{8,9},{9,11},{11,1... | collective-permute-start | bytes 786440 | tf_op jit(solution)/shard_map/ppermute | solution.py:46
  13.8 14.1 %collective-permute-start.2 = (bf16[8,5120]{1,0:T(8,128)(2,1)S(1)}, bf16[8,5120]{1,0:T(8,128)(2,1)S(1)}, u32[]{:S(2)}, u32[]{:S(2)}) collective-permute-start(bf16[8,5120]{1,0:T(8,128)(2,1)S(1)} %reshape.39.refs_6_), channel_id=1, source_target_pairs={{0,4},{4,0},{8,12},{12,8},{1,5},{5,1},{9,13},{13,9},{2,6},{6,2},{1... | collective-permute-start | bytes 245768 | tf_op jit(solution)/shard_map/ppermute | solution.py:520
  13.8 14.0 %collective-permute-start.3 = (bf16[8,5120]{1,0:T(8,128)(2,1)S(1)}, bf16[8,5120]{1,0:T(8,128)(2,1)S(1)}, u32[]{:S(2)}, u32[]{:S(2)}) collective-permute-start(bf16[8,5120]{1,0:T(8,128)(2,1)S(1)} %reshape.39.refs_6_), channel_id=1, source_target_pairs={{0,8},{4,12},{8,0},{12,4},{1,9},{5,13},{9,1},{13,5},{2,10},{6,14},... | collective-permute-start | bytes 245768 | tf_op jit(solution)/shard_map/ppermute | solution.py:520
  15.4 12.4 %collective-permute-start.4 = (bf16[8,5120]{1,0:T(8,128)(2,1)S(1)}, bf16[8,5120]{1,0:T(8,128)(2,1)S(1)}, u32[]{:S(2)}, u32[]{:S(2)}) collective-permute-start(bf16[8,5120]{1,0:T(8,128)(2,1)S(1)} %reshape.39.refs_6_), channel_id=1, source_target_pairs={{0,12},{4,8},{8,4},{12,0},{1,13},{5,9},{9,5},{13,1},{2,14},{6,10},... | collective-permute-start | bytes 245768 | tf_op jit(solution)/shard_map/ppermute | solution.py:520
  15.7 12.1 %collective-permute-start.1 = (bf16[256,512]{1,0:T(8,128)(2,1)}, bf16[256,512]{1,0:T(8,128)(2,1)S(1)}, u32[]{:S(2)}, u32[]{:S(2)}) collective-permute-start(bf16[256,512]{1,0:T(8,128)(2,1)} %stacked.1.refs_3_.refs_4_.refs_6_), channel_id=1, source_target_pairs={{1,0},{3,1},{2,3},{0,2},{5,4},{7,5},{6,7},{4,6},{9,8},{11,9},{10,1... | collective-permute-start | bytes 786440 | tf_op jit(solution)/shard_map/ppermute | solution.py:46
  18.1 9.7 %copy-start = (bf16[256,512]{1,0:T(8,128)(2,1)S(1)}, bf16[256,512]{1,0:T(8,128)(2,1)}, u32[]{:S(2)}) copy-start(bf16[256,512]{1,0:T(8,128)(2,1)} %stacked.1.refs_3_.refs_4_.refs_6_) | copy-start | bytes 786436
  18.1 9.7 %copy-start.1 = (bf16[128,4096]{1,0:T(8,128)(2,1)S(1)}, bf16[128,4096]{1,0:T(8,128)(2,1)}, u32[]{:S(2)}) copy-start(bf16[128,4096]{1,0:T(8,128)(2,1)} %refs_3_.1) | copy-start | bytes 3145732
  18.1 9.7 %copy-start.2 = (s32[18]{0:T(128)S(1)}, s32[18]{0:T(128)}, u32[]{:S(2)}) copy-start(s32[18]{0:T(128)} %facts.1.refs_0_) | copy-start | bytes 220
  20.4 12.7 %collective-permute-start.5 = (bf16[256,512]{1,0:T(8,128)(2,1)S(1)}, bf16[256,512]{1,0:T(8,128)(2,1)S(1)}, u32[]{:S(2)}, u32[]{:S(2)}) collective-permute-start(bf16[256,512]{1,0:T(8,128)(2,1)S(1)} %collective-permute-done.refs_0_.refs_4_.refs_5_.refs_7_), channel_id=1, source_target_pairs={{0,1},{1,3},{3,2},{2,0},{4,5},{5,7},{7,6},{6,4},{8,9},{9,11},{11,1... | collective-permute-start | bytes 786440 | tf_op jit(solution)/shard_map/ppermute | solution.py:46
  35.2 9.5 %collective-permute-start.6 = (bf16[2,4096]{1,0:T(2,128)(2,1)S(1)}, bf16[2,4096]{1,0:T(2,128)(2,1)S(1)}, u32[]{:S(2)}, u32[]{:S(2)}) collective-permute-start(bf16[2,4096]{1,0:T(2,128)(2,1)S(1)} %get-tuple-element.34), channel_id=1, source_target_pairs={{0,12},{4,8},{8,4},{12,0},{1,13},{5,9},{9,5},{13,1},{2,14},{6,10},... | collective-permute-start | bytes 49160 | tf_op jit(solution)/shard_map/ppermute | solution.py:520
  36.4 8.4 %collective-permute-start.7 = (bf16[2,4096]{1,0:T(2,128)(2,1)S(1)}, bf16[2,4096]{1,0:T(2,128)(2,1)S(1)}, u32[]{:S(2)}, u32[]{:S(2)}) collective-permute-start(bf16[2,4096]{1,0:T(2,128)(2,1)S(1)} %get-tuple-element.37), channel_id=1, source_target_pairs={{0,8},{4,12},{8,0},{12,4},{1,9},{5,13},{9,1},{13,5},{2,10},{6,14},... | collective-permute-start | bytes 49160 | tf_op jit(solution)/shard_map/ppermute | solution.py:520
  36.9 7.8 %collective-permute-start.8 = (bf16[2,4096]{1,0:T(2,128)(2,1)S(1)}, bf16[2,4096]{1,0:T(2,128)(2,1)S(1)}, u32[]{:S(2)}, u32[]{:S(2)}) collective-permute-start(bf16[2,4096]{1,0:T(2,128)(2,1)S(1)} %get-tuple-element.36), channel_id=1, source_target_pairs={{0,4},{4,0},{8,12},{12,8},{1,5},{5,1},{9,13},{13,9},{2,6},{6,2},{1... | collective-permute-start | bytes 49160 | tf_op jit(solution)/shard_map/ppermute | solution.py:520
